TPU v7x, 32 devices: a whole 2x2x4 slice. The times are simulated.
32 devices in a mesh: expert: 16 (over z, y, x), tensor: 2 (over core).
Axes of the slice: x: 2, y: 2, z: 4, core: 2. Of those that a mesh axis runs over, the one named last changes fastest.
Arguments:
- tokens: bfloat16 [16384, 1536], P('expert'), may hold values from -6 to 6
- cotangent: bfloat16 [16384, 1536], P('expert'), may hold values from -6 to 6
- norm_gain: float32 [1536], replicated, may hold values from 0.5 to 1.5
- ffn_gain: float32 [1536], replicated, may hold values from 0.5 to 1.5
- w_query: bfloat16 [1536, 1536], P(None, 'tensor'), may hold values from -0.15625 to 0.15625
- w_key: bfloat16 [1536, 256], P(None, 'tensor'), may hold values from -0.15625 to 0.15625
- w_value: bfloat16 [1536, 256], P(None, 'tensor'), may hold values from -0.15625 to 0.15625
- w_out: bfloat16 [1536, 1536], P('tensor'), may hold values from -1.25 to 1.25
- w_router: bfloat16 [1536, 16], replicated, may hold values from -0.078125 to 0.078125
- w_gate: bfloat16 [16, 1536, 768], P('expert', None, 'tensor'), may hold values from -0.15625 to 0.15625
- w_up: bfloat16 [16, 1536, 768], P('expert', None, 'tensor'), may hold values from -0.15625 to 0.15625
- w_down: bfloat16 [16, 768, 1536], P('expert', 'tensor'), may hold values from -0.625 to 0.625
- routes: int32 [16384, 4], P('expert'), may hold values from 0 to 15, all different within a row
- order: int32 [16, 4096], P('expert'), may hold values from 0 to 4095, each once within a row
- segments: int32 [16, 1024], P('expert'), may hold values from 0 to 5, never falling along the last dimension, each value on 1 to 256 neighbouring positions
Outputs:
- output: bfloat16 [16384, 1536], P('expert')
- input_grad: float32 [16384, 1536], P('expert')
- norm_gain_grad: float32 [1536], P('expert')
- ffn_gain_grad: float32 [1536], P('expert')
- query_grad: float32 [1536, 1536], P('expert', 'tensor')
- key_grad: float32 [1536, 256], P('expert', 'tensor')
- value_grad: float32 [1536, 256], P('expert', 'tensor')
- out_grad: float32 [1536, 1536], P('tensor', 'expert')
- router_grad: float32 [1536, 16], P('expert')
- gate_grad: float32 [16, 1536, 768], P('expert', None, 'tensor')
- up_grad: float32 [16, 1536, 768], P('expert', None, 'tensor')
- down_grad: float32 [16, 768, 1536], P('expert', 'tensor')
Inputs may be any that keep to these rules, and one draw needn't show every extreme that they name: `routes`: each row names 4 different experts; every expert is named by some row. `order`: each row holds each rank once; entry t * 4 + k belongs to pair k of token t. `segments`: never falls along a row; each value covers 1 to 256 positions of its row, some one exactly 256.
All inputs are finite; a program needn't handle non-finite values.
Results may differ from a plain program's by a relative error of at most 0.025.
Values may be sent and summed in bfloat16 or wider, within the bound.
No kernel may reach another device: no remote copies, remote signals or barrier semaphores. Data moves between devices by JAX's collectives and lax.ppermute only.
A program may use at most 384 MiB of HBM per device.

v0:
```python
import math

import jax
import jax.numpy as jnp
from jax import lax
from jax.sharding import PartitionSpec as P

epsilon = 1e-06
rope_base = 1000000.0
masked_score = -1e30


def rope_tables(seq_length, head_width):
    half_width = head_width // 2
    exponent = jnp.arange(half_width, dtype=jnp.float32) * (2.0 / head_width)
    frequency = jnp.exp(-math.log(rope_base) * exponent)
    angle = jnp.arange(seq_length, dtype=jnp.float32)[:, None] * frequency[None, :]
    return (jnp.cos(angle), jnp.sin(angle))


def rotate(inputs, cosine_table, sine_table):
    half_width = inputs.shape[-1] // 2
    first_part = inputs[..., :half_width]
    second_part = inputs[..., half_width:]
    cosine_wide = cosine_table[:, None, :]
    sine_wide = sine_table[:, None, :]
    return jnp.concatenate(
        [
            first_part * cosine_wide - second_part * sine_wide,
            second_part * cosine_wide + first_part * sine_wide,
        ],
        axis=-1,
    )


def rotate_back(grads_in, cosine_table, sine_table):
    half_width = grads_in.shape[-1] // 2
    first_part = grads_in[..., :half_width]
    second_part = grads_in[..., half_width:]
    cosine_wide = cosine_table[:, None, :]
    sine_wide = sine_table[:, None, :]
    return jnp.concatenate(
        [
            first_part * cosine_wide + second_part * sine_wide,
            second_part * cosine_wide - first_part * sine_wide,
        ],
        axis=-1,
    )


def rms_scale(inputs):
    return lax.rsqrt(jnp.mean(inputs * inputs, axis=-1, keepdims=True) + epsilon)


def slot_table(route_rows, order_row, expert_count, capacity):
    seq_length, pick_count = route_rows.shape
    pair_count = seq_length * pick_count
    flat_routes = route_rows.reshape(pair_count)
    pair_ids = jnp.arange(pair_count, dtype=jnp.int32)
    by_rank = jnp.zeros((pair_count,), jnp.int32).at[order_row].set(pair_ids)
    ranked = flat_routes[by_rank]
    expert_ids = jnp.arange(expert_count, dtype=jnp.int32)
    ranked_hits = (ranked[:, None] == expert_ids[None, :]).astype(jnp.int32)
    earlier = jnp.cumsum(ranked_hits, axis=0) - ranked_hits
    place_ranked = jnp.sum(earlier * ranked_hits, axis=1)
    placement = place_ranked[order_row]
    sink_slot = expert_count * capacity
    pair_slot = jnp.where(placement < capacity, flat_routes * capacity + placement, sink_slot)
    slot_owner = (
        jnp.full((sink_slot + 1,), seq_length, jnp.int32).at[pair_slot].set(pair_ids // pick_count)
    )
    return (pair_slot.reshape(seq_length, pick_count), slot_owner[:sink_slot])


def contract_rows(left, right):
    return lax.dot_general(
        left, right, (((0,), (0,)), ((), ())), preferred_element_type=jnp.float32
    )


def times_transposed(left, right):
    return lax.dot_general(
        left, right, (((1,), (1,)), ((), ())), preferred_element_type=jnp.float32
    )


def attention_scores(query, keys, allowed, score_scale):
    raw_scores = jnp.einsum("qhd,kd->hqk", query, keys, preferred_element_type=jnp.float32)
    return jnp.where(allowed[None], raw_scores * score_scale, masked_score)


def expert_front(expert_rows, gate_matrix, up_matrix):
    gate_pre = jnp.dot(expert_rows, gate_matrix, preferred_element_type=jnp.float32)
    up_pre = jnp.dot(expert_rows, up_matrix, preferred_element_type=jnp.float32)
    activation = (jax.nn.silu(gate_pre) * up_pre).astype(jnp.bfloat16)
    return (gate_pre, up_pre, activation)


def on_device(
    tokens,
    cotangent,
    norm_gain,
    ffn_gain,
    w_query,
    w_key,
    w_value,
    w_out,
    w_router,
    w_gate,
    w_up,
    w_down,
    routes,
    order,
    segments,
):
    seq_length, model_width = tokens.shape
    expert_count = w_router.shape[1]
    pick_count = routes.shape[1]
    capacity = 9 * seq_length * pick_count // (8 * expert_count)
    head_width = w_key.shape[1]
    local_heads = w_query.shape[1] // head_width
    score_scale = 1.0 / math.sqrt(head_width)
    slot_total = expert_count * capacity
    pair_slot, slot_owner = slot_table(routes, order[0], expert_count, capacity)
    cosine_table, sine_table = rope_tables(seq_length, head_width)
    allowed = segments[0][None, :] <= segments[0][:, None]
    zero_row = jnp.zeros((1, model_width), jnp.bfloat16)
    source = tokens.astype(jnp.float32)
    inverse_first = rms_scale(source)
    normed_first = source * inverse_first
    first_in = (normed_first * norm_gain).astype(jnp.bfloat16)
    query_pre = jnp.dot(first_in, w_query, preferred_element_type=jnp.float32).reshape(
        seq_length, local_heads, head_width
    )
    query = rotate(query_pre, cosine_table, sine_table).astype(jnp.bfloat16)
    key_pre = jnp.dot(first_in, w_key, preferred_element_type=jnp.float32)[:, None, :]
    keys = rotate(key_pre, cosine_table, sine_table)[:, 0, :].astype(jnp.bfloat16)
    values = jnp.dot(first_in, w_value, preferred_element_type=jnp.float32).astype(jnp.bfloat16)
    scores = attention_scores(query, keys, allowed, score_scale)
    log_total = jax.nn.logsumexp(scores, axis=-1, keepdims=True)
    weights = jnp.exp(scores - log_total).astype(jnp.bfloat16)
    mixed = jnp.einsum("hqk,kd->qhd", weights, values, preferred_element_type=jnp.float32)
    mixed = mixed.astype(jnp.bfloat16).reshape(seq_length, local_heads * head_width)
    attention_part = jnp.dot(mixed, w_out, preferred_element_type=jnp.float32)
    hidden = source + lax.psum(attention_part.astype(jnp.bfloat16), "tensor").astype(jnp.float32)
    inverse_second = rms_scale(hidden)
    normed_second = hidden * inverse_second
    second_in = (normed_second * ffn_gain).astype(jnp.bfloat16)
    logits = jnp.dot(second_in, w_router, preferred_element_type=jnp.float32)
    picked = routes[:, :, None] == jnp.arange(expert_count, dtype=jnp.int32)[None, None, :]
    chosen = jnp.sum(jnp.where(picked, logits[:, None, :], 0.0), axis=-1)
    gate_weights = jax.nn.softmax(chosen, axis=-1)
    outgoing = jnp.concatenate([second_in, zero_row], axis=0)[slot_owner].reshape(
        expert_count, capacity, model_width
    )
    arrived = lax.all_to_all(outgoing, "expert", split_axis=0, concat_axis=0, tiled=True)
    expert_rows = arrived.reshape(slot_total, model_width)
    gate_pre, up_pre, activation = expert_front(expert_rows, w_gate[0], w_up[0])
    expert_part = jnp.dot(activation, w_down[0], preferred_element_type=jnp.float32).astype(
        jnp.bfloat16
    )
    expert_part = expert_part.reshape(expert_count, capacity, model_width)
    summed_half = lax.psum_scatter(
        expert_part.astype(jnp.float32).astype(jnp.bfloat16),
        "tensor",
        scatter_dimension=2,
        tiled=True,
    )
    summed_whole = lax.all_gather(summed_half, "tensor", axis=2, tiled=True)
    returned = lax.all_to_all(summed_whole, "expert", split_axis=0, concat_axis=0, tiled=True)
    returned_pad = jnp.concatenate([returned.reshape(slot_total, model_width), zero_row], axis=0)
    pair_rows = [returned_pad[pair_slot[:, pick_rank]] for pick_rank in range(pick_count)]
    combined = jnp.zeros_like(hidden)
    for pick_rank in range(pick_count):
        combined = combined + gate_weights[:, pick_rank : pick_rank + 1] * pair_rows[
            pick_rank
        ].astype(jnp.float32)
    output = (hidden + combined).astype(jnp.bfloat16)
    upstream = cotangent.astype(jnp.float32)
    gate_total = jnp.stack(
        [
            jnp.sum(upstream * pair_rows[pick_rank].astype(jnp.float32), axis=-1)
            for pick_rank in range(pick_count)
        ],
        axis=-1,
    )
    slot_gate = (
        jnp.zeros((slot_total + 1,), jnp.float32)
        .at[pair_slot.reshape(-1)]
        .set(gate_weights.reshape(-1))[:slot_total]
    )
    cotangent_rows = jnp.concatenate([cotangent, zero_row], axis=0)[slot_owner]
    grad_out = (cotangent_rows.astype(jnp.float32) * slot_gate[:, None]).astype(jnp.bfloat16)
    grad_out = grad_out.reshape(expert_count, capacity, model_width)
    grad_arrived = lax.all_to_all(grad_out, "expert", split_axis=0, concat_axis=0, tiled=True)
    grad_rows = grad_arrived.reshape(slot_total, model_width)
    d_act = times_transposed(grad_rows, w_down[0])
    down_grad = contract_rows(activation, grad_rows)[None]
    sigmoid_gate = jax.nn.sigmoid(gate_pre)
    silu_gate = gate_pre * sigmoid_gate
    d_gate = (d_act * up_pre * sigmoid_gate * (1.0 + gate_pre * (1.0 - sigmoid_gate))).astype(
        jnp.bfloat16
    )
    d_up = (d_act * silu_gate).astype(jnp.bfloat16)
    gate_grad = contract_rows(expert_rows, d_gate)[None]
    up_grad = contract_rows(expert_rows, d_up)[None]
    row_part = (times_transposed(d_gate, w_gate[0]) + times_transposed(d_up, w_up[0])).astype(
        jnp.bfloat16
    )
    row_part = row_part.reshape(expert_count, capacity, model_width)
    row_half = lax.psum_scatter(
        row_part.astype(jnp.float32).astype(jnp.bfloat16), "tensor", scatter_dimension=2, tiled=True
    )
    row_whole = lax.all_gather(row_half, "tensor", axis=2, tiled=True)
    back_rows = lax.all_to_all(row_whole, "expert", split_axis=0, concat_axis=0, tiled=True)
    back_pad = jnp.concatenate([back_rows.reshape(slot_total, model_width), zero_row], axis=0)
    row_total = jnp.zeros_like(hidden)
    for pick_rank in range(pick_count):
        row_total = row_total + back_pad[pair_slot[:, pick_rank]].astype(jnp.float32)
    d_chosen = gate_weights * (
        gate_total - jnp.sum(gate_weights * gate_total, axis=-1, keepdims=True)
    )
    d_logits = jnp.sum(jnp.where(picked, d_chosen[:, :, None], 0.0), axis=1).astype(jnp.bfloat16)
    router_grad = contract_rows(second_in, d_logits)
    d_second = row_total + times_transposed(d_logits, w_router)
    scaled_second = d_second * ffn_gain
    ffn_gain_grad = jnp.sum(d_second * normed_second, axis=0)
    d_hidden = upstream + inverse_second * (
        scaled_second
        - normed_second * jnp.mean(scaled_second * normed_second, axis=-1, keepdims=True)
    )
    d_branch = d_hidden.astype(jnp.bfloat16)
    out_grad = contract_rows(mixed, d_branch)
    d_mixed = (
        times_transposed(d_branch, w_out)
        .astype(jnp.bfloat16)
        .reshape(seq_length, local_heads, head_width)
    )
    scores = attention_scores(query, keys, allowed, score_scale)
    probs = jnp.exp(scores - log_total)
    d_probs = jnp.einsum("qhd,kd->hqk", d_mixed, values, preferred_element_type=jnp.float32)
    row_dot = jnp.sum(probs * d_probs, axis=-1, keepdims=True)
    d_scores = (score_scale * probs * (d_probs - row_dot)).astype(jnp.bfloat16)
    d_query_turned = jnp.einsum("hqk,kd->qhd", d_scores, keys, preferred_element_type=jnp.float32)
    d_keys_turned = jnp.einsum("hqk,qhd->kd", d_scores, query, preferred_element_type=jnp.float32)
    d_values = jnp.einsum(
        "hqk,qhd->kd", probs.astype(jnp.bfloat16), d_mixed, preferred_element_type=jnp.float32
    ).astype(jnp.bfloat16)
    d_query = (
        rotate_back(d_query_turned, cosine_table, sine_table)
        .astype(jnp.bfloat16)
        .reshape(seq_length, local_heads * head_width)
    )
    d_keys = rotate_back(d_keys_turned[:, None, :], cosine_table, sine_table)[:, 0, :].astype(
        jnp.bfloat16
    )
    query_grad = contract_rows(first_in, d_query)
    key_grad = contract_rows(first_in, d_keys)
    value_grad = contract_rows(first_in, d_values)
    d_first = (
        times_transposed(d_query, w_query)
        + times_transposed(d_keys, w_key)
        + times_transposed(d_values, w_value)
    )
    d_first = lax.psum(d_first.astype(jnp.bfloat16), "tensor").astype(jnp.float32)
    scaled_first = d_first * norm_gain
    norm_gain_grad = jnp.sum(d_first * normed_first, axis=0)
    input_grad = d_hidden + inverse_first * (
        scaled_first - normed_first * jnp.mean(scaled_first * normed_first, axis=-1, keepdims=True)
    )
    reduced = (
        lax.psum_scatter(query_grad, "expert", scatter_dimension=0, tiled=True),
        lax.psum_scatter(key_grad, "expert", scatter_dimension=0, tiled=True),
        lax.psum_scatter(value_grad, "expert", scatter_dimension=0, tiled=True),
        lax.psum_scatter(out_grad, "expert", scatter_dimension=1, tiled=True),
        lax.psum_scatter(router_grad, "expert", scatter_dimension=0, tiled=True),
        lax.psum_scatter(norm_gain_grad, "expert", scatter_dimension=0, tiled=True),
        lax.psum_scatter(ffn_gain_grad, "expert", scatter_dimension=0, tiled=True),
    )
    return (
        output,
        input_grad,
        reduced[5],
        reduced[6],
        reduced[0],
        reduced[1],
        reduced[2],
        reduced[3],
        reduced[4],
        gate_grad,
        up_grad,
        down_grad,
    )


def solution(mesh):
    placed = (
        P("expert", None),
        P("expert", None),
        P(),
        P(),
        P(None, "tensor"),
        P(None, "tensor"),
        P(None, "tensor"),
        P("tensor", None),
        P(),
        P("expert", None, "tensor"),
        P("expert", None, "tensor"),
        P("expert", "tensor", None),
        P("expert", None),
        P("expert", None),
        P("expert", None),
    )
    return jax.shard_map(
        on_device,
        mesh=mesh,
        in_specs=placed,
        out_specs=(
            P("expert", None),
            P("expert", None),
            P("expert"),
            P("expert"),
            P("expert", "tensor"),
            P("expert", "tensor"),
            P("expert", "tensor"),
            P("tensor", "expert"),
            P("expert", None),
            P("expert", None, "tensor"),
            P("expert", None, "tensor"),
            P("expert", "tensor", None),
        ),
        check_vma=False,
    )
```

profile of v0, /device:TPU:9, one launch (start us, length us, event | category | flops | bytes accessed | tf_op | source)
XLA Modules:
  0.0 2533.9 jit_solution(14066000749593828386)
XLA Ops:
  31.7 3.9 subtract_convert_fusion.1
  35.7 11.2 fusion.5
  46.8 11.3 exponential_reduce_fusion
  58.2 12.2 convolution_convert_fusion.2
  71.6 4.1 convolution_convert_fusion.1
  76.4 15.5 scatter_custom_fusion
  91.9 23.0 gather_fusion
  115.0 4.6 reduce-window.6
  120.6 23.0 gather_fusion.1
  148.4 15.9 scatter_custom_fusion.1
  164.4 4.1 multiply_reduce_fusion.2
  173.8 30.6 %gather_fusion.2 = bf16[4608,1536]{1,0:T(8,128)(2,1)} fusion(bf16[1025,1536]{1,0:T(8,128)(2,1)} %concatenate.34, s32[5120]{0:T(1024)S(1)} %pad_clamp_fusion), kind=kCustom, calls=%fused_computation.2 | custom fusion | bytes 28329984 | tf_op jit(solution)/shard_map/gather | solution.py:153
  204.4 312.5 %all_to_all.20 = bf16[16,288,1536]{2,1,0:T(8,128)(2,1)S(1)} all-to-all(bf16[16,288,1536]{2,1,0:T(8,128)(2,1)} %bitcast.175), channel_id=1, replica_groups=mesh['expert'=16,'tensor'=2] {'expert'}, dimensions={0} | all-to-all | bytes 28311552 | tf_op jit(solution)/shard_map/all_to_all | solution.py:156
  517.0 9.5 fusion.40
  526.4 12.0 multiply_convert_fusion.2
  538.4 12.1 convolution_convert_fusion
  550.6 24.2 reduce-scatter.10.cloned.1.call-done
  574.8 29.2 %all-gather.3.cloned.1.call-done = bf16[16,288,1536]{2,1,0:T(8,128)(2,1)} async-done(((bf16[16,288,768]{2,1,0:T(8,128)(2,1)}), bf16[16,288,1536]{2,1,0:T(8,128)(2,1)}) %all-gather.3.cloned.1.call-update) | async-done | bytes 14155792 | tf_op jit(solution)/shard_map/all_gather | solution.py:169
  604.0 6.6 all-to-all-start.1
  614.4 30.6 %gather_fusion.7 = bf16[4608,1536]{1,0:T(8,128)(2,1)} fusion(bf16[1025,1536]{1,0:T(8,128)(2,1)} %concatenate.36, s32[5120]{0:T(1024)S(1)} %pad_clamp_fusion), kind=kCustom, calls=%fused_computation.7 | custom fusion | bytes 28329984 | tf_op jit(solution)/shard_map/gather | solution.py:192
  649.1 265.8 %all-to-all-done.1 = bf16[16,288,1536]{2,1,0:T(8,128)(2,1)} async-done(((bf16[16,288,1536]{2,1,0:T(8,128)(2,1)}), bf16[16,288,1536]{2,1,0:T(8,128)(2,1)}, u32[]{:S(2)}, u32[]{:S(2)}) %all-to-all-start.1) | async-done | bytes 14155808 | tf_op jit(solution)/shard_map/all_to_all | solution.py:170
  914.8 12.8 concatenate.35
  927.6 14.1 gather_fusion.6
  941.8 14.1 gather_fusion.5
  955.9 14.5 gather_fusion.4
  970.4 14.1 gather_fusion.3
  984.5 7.0 fusion.23
  992.1 15.7 scatter_custom_fusion.2
  1007.9 7.5 fusion
  1015.3 330.3 %all_to_all.21 = bf16[16,288,1536]{2,1,0:T(8,128)(2,1)} all-to-all(bf16[16,288,1536]{2,1,0:T(8,128)(2,1)S(1)} %fusion), channel_id=1, replica_groups=mesh['expert'=16,'tensor'=2] {'expert'}, dimensions={0} | all-to-all | bytes 28311552 | tf_op jit(solution)/shard_map/all_to_all | solution.py:195
  1345.6 15.7 multiply_convert_fusion
  1361.4 12.9 fusion.38
  1374.3 18.4 add_convert_fusion
  1392.7 25.1 reduce-scatter.12.cloned.1.call-done
  1417.8 29.2 %all-gather.5.cloned.1.call-done = bf16[16,288,1536]{2,1,0:T(8,128)(2,1)} async-done(((bf16[16,288,768]{2,1,0:T(8,128)(2,1)}), bf16[16,288,1536]{2,1,0:T(8,128)(2,1)}) %all-gather.5.cloned.1.call-update) | async-done | bytes 14155792 | tf_op jit(solution)/shard_map/all_gather | solution.py:214
  1447.0 6.4 all-to-all-start.3
  1453.6 4.2 fusion.88
  1457.9 303.9 %all-to-all-done.3 = bf16[16,288,1536]{2,1,0:T(8,128)(2,1)} async-done(((bf16[16,288,1536]{2,1,0:T(8,128)(2,1)}), bf16[16,288,1536]{2,1,0:T(8,128)(2,1)}, u32[]{:S(2)}, u32[]{:S(2)}) %all-to-all-start.3) | async-done | bytes 14155808 | tf_op jit(solution)/shard_map/all_to_all | solution.py:215
  1761.8 13.0 concatenate.37
  1774.8 14.1 gather_fusion.11
  1788.9 14.1 gather_fusion.10
  1803.0 14.1 gather_fusion.9
  1817.2 14.2 gather_fusion.8
  1831.5 10.4 multiply_reduce_fusion
  1846.5 9.5 convert_add_fusion
  1856.0 5.5 convolution_convert_fusion.3
  1862.7 11.7 fusion.31
  1874.4 17.5 fusion.1
  1891.9 22.5 fusion.3
  1914.4 9.0 convolution_bitcast_fusion.6
  1923.5 8.2 convolution_bitcast_fusion.3
  1938.6 4.8 fusion.85
  1955.1 8.1 fusion.28
  1963.3 7.2 fusion.86
  1973.3 12.1 convolution_bitcast_fusion
  1985.4 13.0 convolution_bitcast_fusion.1
  1998.5 9.0 convolution_bitcast_fusion.2
  2007.4 4.1 fusion.21
  2011.6 69.3 %all-reduce.6 = (f32[1536]{0:T(1024)S(1)}, f32[1536]{0:T(1024)S(1)}) all-reduce(f32[1536]{0:T(1024)S(1)} %get-tuple-element.14, f32[1536]{0:T(1024)S(1)} %get-tuple-element.12), channel_id=4, replica_groups=mesh['expert'=16,'tensor'=2] {'expert'}, use_global_device_ids=true, to_apply=%region_27.28.clone | all-reduce | flops 3072 | bytes 24576
  2082.0 7.2 fusion.13
  2089.2 27.8 %reduce-scatter.18.cloned.1.call-done = f32[96,128]{1,0:T(8,128)} async-done(((f32[1536,128]{1,0:T(8,128)}), f32[96,128]{1,0:T(8,128)}) %reduce-scatter.18.cloned.1.call-update) | async-done | bytes 49168 | tf_op jit(solution)/shard_map/reduce_scatter | solution.py:274
  2117.1 126.6 %reduce-scatter.16.cloned.1.call-done = f32[96,128]{1,0:T(8,128)} async-done(((f32[1536,128]{1,0:T(8,128)}), f32[96,128]{1,0:T(8,128)}) %reduce-scatter.16.cloned.1.call-update) | async-done | bytes 49168 | tf_op jit(solution)/shard_map/reduce_scatter | solution.py:273
  2243.6 141.0 %reduce-scatter.20.cloned.1.call-done = f32[768,96]{0,1:T(8,128)} async-done(((f32[768,1536]{0,1:T(8,128)}), f32[768,96]{0,1:T(8,128)}) %reduce-scatter.20.cloned.1.call-update) | async-done | bytes 294928 | tf_op jit(solution)/shard_map/reduce_scatter | solution.py:275
  2384.6 142.4 %reduce-scatter.14.cloned.1.call-done = f32[96,768]{1,0:T(8,128)} async-done(((f32[1536,768]{1,0:T(8,128)}), f32[96,768]{1,0:T(8,128)}) %reduce-scatter.14.cloned.1.call-update) | async-done | bytes 294928 | tf_op jit(solution)/shard_map/reduce_scatter | solution.py:272
  (225 shorter events, 73.5 us)
Async XLA Ops:
  7.2 64.5 %copy-start = (bf16[768,1536]{1,0:T(8,128)(2,1)S(1)}, bf16[768,1536]{1,0:T(8,128)(2,1)}, u32[]{:S(2)}) copy-start(bf16[768,1536]{1,0:T(8,128)(2,1)} %param.22) | copy-start | bytes 7077892
  7.2 157.2 %all-reduce.10.cloned.1.call-start = ((), (), s32[]{:S(2)}) async-start(), calls=%async_computation.11 | async-start | bytes 6291456 | tf_op jit(solution)/shard_map/psum | solution.py:145
  7.2 7.1 copy-start.1
  7.3 8.6 copy-start.38
  7.3 11.4 copy-start.56
  10.0 7.5 copy-start.46
  11.5 46.8 %copy-start.13 = (pred[1024,1024]{0,1:T(8,128)(4,1)}, pred[1024,1024]{0,1:T(8,128)(4,1)S(1)}, u32[]{:S(2)}) copy-start(pred[1024,1024]{0,1:T(8,128)(4,1)S(1)} %broadcast_compare_fusion) | copy-start | bytes 3145732
  15.8 7.4 copy-start.4
  20.5 15.1 copy-start.34
  35.6 11.2 copy-start.16
  35.6 11.2 copy-start.18
  46.8 11.4 copy-start.42
  58.2 12.2 copy-start.40
  75.7 499.0 %reduce-scatter.10.cloned.1.call-start = ((), (), s32[]{:S(2)}) async-start(), calls=%async_computation.12 | async-start | bytes 21233664 | tf_op jit(solution)/shard_map/reduce_scatter | solution.py:163
  143.7 24.8 copy-start.52
  148.3 21.9 copy-start.54
  204.4 312.5 %copy-start.29 = (bf16[1,1536,384]{2,1,0:T(8,128)(2,1)S(1)}, bf16[1,1536,384]{2,1,0:T(8,128)(2,1)}, u32[]{:S(2)}) copy-start(bf16[1,1536,384]{2,1,0:T(8,128)(2,1)} %param.24) | copy-start | bytes 3538948
  517.0 9.5 copy-start.15
  517.0 9.5 copy-start.31
  526.4 12.0 copy-start.59
  550.5 53.5 %all-gather.3.cloned.1.call-start = ((), (), s32[]{:S(2)}) async-start(), calls=%async_computation.13 | async-start | bytes 21233664 | tf_op jit(solution)/shard_map/all_gather | solution.py:169
  604.0 310.8 %all-to-all-start.1 = ((bf16[16,288,1536]{2,1,0:T(8,128)(2,1)}), bf16[16,288,1536]{2,1,0:T(8,128)(2,1)}, u32[]{:S(2)}, u32[]{:S(2)}) async-start(bf16[16,288,1536]{2,1,0:T(8,128)(2,1)} %all-gather.3.cloned.1.call-done), calls=%async_computation.2 | async-start | bytes 28311552 | tf_op jit(solution)/shard_map/all_to_all | solution.py:170
  610.6 807.2 %reduce-scatter.12.cloned.1.call-start = ((), (), s32[]{:S(2)}) async-start(), calls=%async_computation.14 | async-start | bytes 21233664 | tf_op jit(solution)/shard_map/reduce_scatter | solution.py:211
  614.4 31.7 %copy-start.48 = (bf16[1536,16]{0,1:T(8,128)(2,1)S(1)}, bf16[1536,16]{0,1:T(8,128)(2,1)}, u32[]{:S(2)}) copy-start(bf16[1536,16]{0,1:T(8,128)(2,1)} %param.23) | copy-start | bytes 147460
  1015.3 330.3 %copy-start.60 = (bf16[1,384,1536]{2,1,0:T(8,128)(2,1)S(1)}, bf16[1,384,1536]{2,1,0:T(8,128)(2,1)}, u32[]{:S(2)}) copy-start(bf16[1,384,1536]{2,1,0:T(8,128)(2,1)} %param.26) | copy-start | bytes 3538948
  1345.6 15.7 copy-start.30
  1361.4 12.9 copy-start.20
  1361.4 12.9 copy-start.24
  1361.4 12.9 copy-start.32
  1392.7 54.4 %all-gather.5.cloned.1.call-start = ((), (), s32[]{:S(2)}) async-start(), calls=%async_computation.15 | async-start | bytes 21233664 | tf_op jit(solution)/shard_map/all_gather | solution.py:214
  1447.0 314.8 %all-to-all-start.3 = ((bf16[16,288,1536]{2,1,0:T(8,128)(2,1)}), bf16[16,288,1536]{2,1,0:T(8,128)(2,1)}, u32[]{:S(2)}, u32[]{:S(2)}) async-start(bf16[16,288,1536]{2,1,0:T(8,128)(2,1)} %all-gather.5.cloned.1.call-done), calls=%async_computation.5 | async-start | bytes 28311552 | tf_op jit(solution)/shard_map/all_to_all | solution.py:215
  1453.4 518.4 %reduce-scatter.22.cloned.1.call-start = ((), (), s32[]{:S(2)}) async-start(), calls=%async_computation.21 | async-start | bytes 835584
  1457.8 549.6 %all-reduce.12.cloned.1.call-start = ((), (), s32[]{:S(2)}) async-start(), calls=%async_computation.16 | async-start | bytes 6291456 | tf_op jit(solution)/shard_map/psum | solution.py:265
  1817.2 14.2 copy-start.49
  1817.2 14.2 copy-start.51
  1817.2 14.2 copy-start.53
  1831.4 10.4 copy-start.3
  1831.4 10.4 copy-start.7
  1831.4 11.5 copy-start.8
  1831.4 12.3 copy-start.9
  1831.4 13.2 copy-start.10
  1831.5 14.1 copy-start.11
  1831.5 15.0 copy-start.12
  1856.0 6.7 copy-start.14
  1856.0 6.7 copy-start.41
  1891.9 22.6 copy-start.17
  1891.9 22.6 copy-start.19
  1914.4 9.1 copy-start.35
  1914.4 9.1 copy-start.37
  1923.5 8.2 copy-start.22
  1923.5 8.2 copy-start.23
  1947.3 169.8 %reduce-scatter.18.cloned.1.call-start = ((), (), s32[]{:S(2)}) async-start(), calls=%async_computation.19 | async-start | bytes 835584 | tf_op jit(solution)/shard_map/reduce_scatter | solution.py:274
  1951.2 292.4 %reduce-scatter.16.cloned.1.call-start = ((), (), s32[]{:S(2)}) async-start(), calls=%async_computation.18 | async-start | bytes 835584 | tf_op jit(solution)/shard_map/reduce_scatter | solution.py:273
  1955.1 429.5 %reduce-scatter.20.cloned.1.call-start = ((), (), s32[]{:S(2)}) async-start(), calls=%async_computation.20 | async-start | bytes 5013504 | tf_op jit(solution)/shard_map/reduce_scatter | solution.py:275
  1963.2 7.3 copy-start.62
  1963.2 563.8 %reduce-scatter.14.cloned.1.call-start = ((), (), s32[]{:S(2)}) async-start(), calls=%async_computation.17 | async-start | bytes 5013504 | tf_op jit(solution)/shard_map/reduce_scatter | solution.py:272
  1973.3 12.1 copy-start.25
  1973.3 25.1 slice-start
  1973.3 25.1 slice-start.1
  1973.3 25.1 slice-start.2
  1985.4 13.0 slice-start.3
  1985.4 13.0 copy-start.21
  1998.4 9.0 copy-start.45
  1998.5 9.0 copy-start.47
  (16 other events, 49.1 us)
Sparse Core Ops, SparseCore 0:
  75.9 25.0 all-reduce.9
  550.6 24.0 reduce-scatter.9
  576.4 27.5 all-gather.2
  1392.8 24.9 reduce-scatter.11
  1419.3 27.7 all-gather.4
  1459.4 363.5 reduce-scatter.21
  1947.4 43.3 all-reduce.11
  1996.1 120.9 reduce-scatter.17
  2122.3 121.2 reduce-scatter.15
  2249.2 135.3 reduce-scatter.19
  2391.2 135.7 reduce-scatter.13
where the time goes:
time: 2550 us; the launch traced here: 2530 us
  waiting for transfers between devices  1120 us (44%)
  blocking collectives  712 us (28%)
  local copies, waits for them, and re-layouts  327 us (13%)
  matrix products  248 us (10%)
  other arithmetic  101 us (4%)
    all_to_all x1, blocking collectives, on_device(): lax.all_to_all(grad_out, 'expert', split_axis=0, concat_axis=0, tiled=True)  330 us
    all_to_all x1, blocking collectives, on_device(): lax.all_to_all(outgoing, 'expert', split_axis=0, concat_axis=0, tiled=True)  313 us
    all_to_all x1, waiting for transfers between devices, on_device(): lax.all_to_all(row_whole, 'expert', split_axis=0, concat_axis=0, tiled=True)  304 us
    all_to_all x1, waiting for transfers between devices, on_device(): lax.all_to_all(summed_whole, 'expert', split_axis=0, concat_axis=0, tiled...  266 us
    reduce_scatter x1, waiting for transfers between devices, on_device(): lax.psum_scatter(query_grad, 'expert', scatter_dimension=0, tiled=True)  142 us
    reduce_scatter x1, waiting for transfers between devices, on_device(): lax.psum_scatter(out_grad, 'expert', scatter_dimension=1, tiled=True)  141 us
    reduce_scatter x1, waiting for transfers between devices, on_device(): lax.psum_scatter(key_grad, 'expert', scatter_dimension=0, tiled=True)  127 us
    dot_general x8, matrix products, times_transposed(): lax.dot_general(left, right, (((1,), (1,)), ((), ())), preferred_element_...  71.3 us
  transfers between devices with their start and end apart: 13, of which 10 were waited for; matrix products, arithmetic and copies ran while one was open for 15% of the time, Pallas kernels for 0%

commit v1 on v0

v1 whole, which is shorter than its diff:
```python
import math

import jax
import jax.numpy as jnp
from jax import lax
from jax.sharding import PartitionSpec as P

epsilon = 1e-06
rope_base = 1000000.0
masked_score = -1e30


def rope_tables(seq_length, head_width):
    half_width = head_width // 2
    exponent = jnp.arange(half_width, dtype=jnp.float32) * (2.0 / head_width)
    frequency = jnp.exp(-math.log(rope_base) * exponent)
    angle = jnp.arange(seq_length, dtype=jnp.float32)[:, None] * frequency[None, :]
    return (jnp.cos(angle), jnp.sin(angle))


def rotate(inputs, cosine_table, sine_table):
    half_width = inputs.shape[-1] // 2
    first_part = inputs[..., :half_width]
    second_part = inputs[..., half_width:]
    cosine_wide = cosine_table[:, None, :]
    sine_wide = sine_table[:, None, :]
    return jnp.concatenate(
        [
            first_part * cosine_wide - second_part * sine_wide,
            second_part * cosine_wide + first_part * sine_wide,
        ],
        axis=-1,
    )


def rotate_back(grads_in, cosine_table, sine_table):
    half_width = grads_in.shape[-1] // 2
    first_part = grads_in[..., :half_width]
    second_part = grads_in[..., half_width:]
    cosine_wide = cosine_table[:, None, :]
    sine_wide = sine_table[:, None, :]
    return jnp.concatenate(
        [
            first_part * cosine_wide + second_part * sine_wide,
            second_part * cosine_wide - first_part * sine_wide,
        ],
        axis=-1,
    )


def rms_scale(inputs):
    return lax.rsqrt(jnp.mean(inputs * inputs, axis=-1, keepdims=True) + epsilon)


def contract_rows(left, right):
    return lax.dot_general(
        left, right, (((0,), (0,)), ((), ())), preferred_element_type=jnp.float32
    )


def times_transposed(left, right):
    return lax.dot_general(
        left, right, (((1,), (1,)), ((), ())), preferred_element_type=jnp.float32
    )


def attention_scores(query, keys, allowed, score_scale):
    raw_scores = jnp.einsum("qhd,kd->hqk", query, keys, preferred_element_type=jnp.float32)
    return jnp.where(allowed[None], raw_scores * score_scale, masked_score)


def expert_front(expert_rows, gate_matrix, up_matrix):
    gate_pre = jnp.dot(expert_rows, gate_matrix, preferred_element_type=jnp.float32)
    up_pre = jnp.dot(expert_rows, up_matrix, preferred_element_type=jnp.float32)
    activation = (jax.nn.silu(gate_pre) * up_pre).astype(jnp.bfloat16)
    return (gate_pre, up_pre, activation)


def line_depth(count):
    depth = 1
    while depth * depth * 4 <= count:
        depth *= 2
    return depth


def place_table(routes, order, me, expert_count, capacity):
    relabeled = routes ^ me
    ranks = order.reshape(routes.shape)
    labels = jnp.arange(expert_count, dtype=jnp.int32)
    hit = relabeled[:, :, None] == labels[None, None, :]
    routed = jnp.any(hit, axis=1)
    rank = jnp.sum(jnp.where(hit, ranks[:, :, None], 0), axis=1)
    rank = jnp.where(routed, rank, order.size)
    earlier = rank.T[:, None, :] < rank.T[:, :, None]
    place = jnp.sum(earlier.astype(jnp.int32), axis=-1)
    return jnp.where(routed.T & (place < capacity), place, -1)


class Exchange:
    def __init__(self, count):
        self.count = count
        self.depth = line_depth(count)
        self.width = count // self.depth
        self.me = lax.axis_index("expert")
        self.line = self.me // self.width
        self.short = self.depth == 4

    def send(self, rows, pairs):
        width = self.width
        flat = [(a * width + s, b * width + s) for a, b in pairs for s in range(width)]
        return lax.ppermute(rows, "expert", flat)

    def flip(self, rows, mask):
        return lax.ppermute(rows, "expert", [(d, d ^ mask) for d in range(self.count)])

    def spread(self, rows):
        if not self.short:
            slots, bit = [rows], 1
            while bit < self.depth:
                slots = slots + [self.flip(s, bit * self.width) for s in slots]
                bit *= 2
            return slots
        middle = (self.line == 1) | (self.line == 2)
        beside = self.send(rows, [(0, 1), (1, 0), (2, 3), (3, 2)])
        across = self.send(rows, [(1, 2), (2, 1)])
        inner = self.send(beside, [(1, 2), (2, 1)])
        outer = self.send(across, [(1, 0), (2, 3)])
        second = jnp.where(middle, inner, outer)
        far = self.send(second, [(1, 0), (2, 3)])
        return [rows, beside, second, jnp.where(middle, across, far)]

    def collect(self, parts):
        def low(v):
            return v.astype(jnp.bfloat16)

        def wide(v):
            return v.astype(jnp.float32)

        if not self.short:
            bit = self.depth // 2
            while bit >= 1:
                sent = [self.flip(low(p), bit * self.width) for p in parts[bit : 2 * bit]]
                parts = [wide(p) + wide(s) for p, s in zip(parts[:bit], sent)]
                bit //= 2
            return parts[0]
        own, beside, second, third = parts
        second = low(wide(second) + wide(self.send(low(third), [(0, 1), (3, 2)])))
        inner = self.send(second, [(1, 2), (2, 1)])
        outer = self.send(second, [(0, 1), (3, 2)])
        beside = low(wide(beside) + wide(inner))
        third = low(wide(third) + wide(outer))
        first = self.send(beside, [(0, 1), (1, 0), (2, 3), (3, 2)])
        other = self.send(third, [(1, 2), (2, 1)])
        return wide(own) + wide(first) + wide(other)

    def plane(self, blocks):
        return [blocks[0]] + [self.flip(blocks[b], b) for b in range(1, self.width)]

    def scatter_sum(self, grads):
        rows = grads.shape[0] // self.count
        held = grads.reshape(self.count, rows, grads.shape[1])
        blocks, bit = self.count, 1
        while bit < self.width:
            parted = held.reshape(blocks // 2, 2, rows, -1)
            side = (self.me // bit) % 2
            kept = lax.dynamic_index_in_dim(parted, side, 1, keepdims=False)
            gone = lax.dynamic_index_in_dim(parted, 1 - side, 1, keepdims=False)
            came = self.flip(gone.astype(jnp.bfloat16), bit)
            held = kept.astype(jnp.float32) + came.astype(jnp.float32)
            blocks, bit = blocks // 2, bit * 2
        parts = [
            lax.dynamic_index_in_dim(held, self.line ^ g, 0, keepdims=False)
            for g in range(self.depth)
        ]
        return self.collect(parts)


def swap(rows):
    return lax.ppermute(rows, "tensor", [(0, 1), (1, 0)])


def half_of(array, side):
    width = array.shape[-1] // 2
    return lax.dynamic_slice_in_dim(array, side * width, width, array.ndim - 1)


def join_halves(mine, other, side):
    first = jnp.where(side == 0, mine, other)
    last = jnp.where(side == 0, other, mine)
    return jnp.concatenate([first, last], axis=-1)


def on_device(
    tokens,
    cotangent,
    norm_gain,
    ffn_gain,
    w_query,
    w_key,
    w_value,
    w_out,
    w_router,
    w_gate,
    w_up,
    w_down,
    routes,
    order,
    segments,
):
    seq_length, model_width = tokens.shape
    expert_count = w_router.shape[1]
    pick_count = routes.shape[1]
    capacity = 9 * seq_length * pick_count // (8 * expert_count)
    head_width = w_key.shape[1]
    local_heads = w_query.shape[1] // head_width
    score_scale = 1.0 / math.sqrt(head_width)
    link = Exchange(expert_count)
    depth, width = link.depth, link.width
    side = lax.axis_index("tensor")
    slot_ids = jnp.arange(capacity, dtype=jnp.float32)

    placed = place_table(routes, order[0], link.me, expert_count, capacity).astype(jnp.float32)
    routes_t = routes.T.astype(jnp.float32)
    tables = []
    for g in range(depth):
        table = jnp.concatenate([placed[g * width : (g + 1) * width], routes_t], axis=0)
        tables.append(table if g == 0 else link.flip(table, g * width))
    selectors = [
        (table[:width, None, :] == slot_ids[None, :, None]).astype(jnp.bfloat16)
        for table in tables
    ]

    def pick_rows(g, rows):
        return jnp.einsum(
            "bst,td->bsd", selectors[g], rows, preferred_element_type=jnp.float32
        ).astype(jnp.bfloat16)

    def spread_rows(rows_half):
        arrived = []
        for g, slot in enumerate(link.spread(rows_half)):
            picked = pick_rows(g, slot)
            came = link.plane([picked[b] for b in range(width)])
            mine = jnp.concatenate(came, axis=0)
            arrived.append((mine, swap(mine)))
        return arrived

    cot_rows = spread_rows(half_of(cotangent, side))
    route_rows = []
    for g in range(depth):
        slots = pick_rows(g, tables[g][width:].T.astype(jnp.bfloat16))
        route_rows.append(jnp.concatenate(link.plane([slots[b] for b in range(width)]), axis=0))

    cosine_table, sine_table = rope_tables(seq_length, head_width)
    allowed = segments[0][None, :] <= segments[0][:, None]
    source = tokens.astype(jnp.float32)
    inverse_first = rms_scale(source)
    normed_first = source * inverse_first
    first_in = (normed_first * norm_gain).astype(jnp.bfloat16)
    query_pre = jnp.dot(first_in, w_query, preferred_element_type=jnp.float32).reshape(
        seq_length, local_heads, head_width
    )
    query = rotate(query_pre, cosine_table, sine_table).astype(jnp.bfloat16)
    key_pre = jnp.dot(first_in, w_key, preferred_element_type=jnp.float32)[:, None, :]
    keys = rotate(key_pre, cosine_table, sine_table)[:, 0, :].astype(jnp.bfloat16)
    values = jnp.dot(first_in, w_value, preferred_element_type=jnp.float32).astype(jnp.bfloat16)
    scores = attention_scores(query, keys, allowed, score_scale)
    log_total = jax.nn.logsumexp(scores, axis=-1, keepdims=True)
    weights = jnp.exp(scores - log_total).astype(jnp.bfloat16)
    mixed = jnp.einsum("hqk,kd->qhd", weights, values, preferred_element_type=jnp.float32)
    mixed = mixed.astype(jnp.bfloat16).reshape(seq_length, local_heads * head_width)
    branch = jnp.dot(mixed, w_out, preferred_element_type=jnp.float32).astype(jnp.bfloat16)
    hidden = source + (branch.astype(jnp.float32) + swap(branch).astype(jnp.float32))
    inverse_second = rms_scale(hidden)
    normed_second = hidden * inverse_second
    second_in = (normed_second * ffn_gain).astype(jnp.bfloat16)
    logits = jnp.dot(second_in, w_router, preferred_element_type=jnp.float32)
    picked = routes[:, :, None] == jnp.arange(expert_count, dtype=jnp.int32)[None, None, :]
    chosen = jnp.sum(jnp.where(picked, logits[:, None, :], 0.0), axis=-1)
    gate_weights = jax.nn.softmax(chosen, axis=-1)

    in_rows = spread_rows(half_of(second_in, side))

    def fold(matrix, axis):
        half = matrix.shape[axis] // 2
        return (
            lax.dynamic_slice_in_dim(matrix, side * half, half, axis),
            lax.dynamic_slice_in_dim(matrix, (1 - side) * half, half, axis),
        )

    gate_up = jnp.concatenate([w_gate[0], w_up[0]], axis=-1)
    unit_count = w_down.shape[1]
    front_mine, front_other = fold(gate_up, 0)
    down_mine, down_other = fold(w_down[0], 1)
    router_mine, router_other = fold(w_router, 0)
    expert_ids = jnp.arange(expert_count, dtype=jnp.bfloat16)
    gate_up_grad = jnp.zeros((2, model_width // 2, 2 * unit_count), jnp.float32)
    down_grad = jnp.zeros((2, unit_count, model_width // 2), jnp.float32)
    out_rows, back_rows, term_rows = [], [], []
    for g in range(depth):
        x_mine, x_other = in_rows[g]
        c_mine, c_other = cot_rows[g]

        def both(a, b, wa, wb):
            return jnp.dot(a, wa, preferred_element_type=jnp.float32) + jnp.dot(
                b, wb, preferred_element_type=jnp.float32
            )

        pre = both(x_mine, x_other, front_mine, front_other)
        row_logits = both(x_mine, x_other, router_mine, router_other)
        raw = times_transposed(c_mine, down_mine) + times_transposed(c_other, down_other)
        mask = jnp.any(route_rows[g][:, :, None] == expert_ids[None, None, :], axis=1)
        masked = jnp.where(mask, row_logits, masked_score)
        spread_out = jnp.exp(masked - jnp.max(masked, axis=-1, keepdims=True))
        chance = spread_out / jnp.sum(spread_out, axis=-1, keepdims=True)
        own = jnp.arange(expert_count, dtype=jnp.int32) == link.me
        gate = jnp.sum(jnp.where(own[None, :], chance, 0.0), axis=-1, keepdims=True)
        gate_pre, up_pre = pre[:, :unit_count], pre[:, unit_count:]
        sig = jax.nn.sigmoid(gate_pre)
        silu = gate_pre * sig
        act = silu * up_pre
        term_rows.append(jnp.sum(act * raw, axis=-1).reshape(width, capacity))
        act_gated = (act * gate).astype(jnp.bfloat16)
        d_act = raw * gate
        d_pre = jnp.concatenate(
            [d_act * up_pre * sig * (1.0 + gate_pre * (1.0 - sig)), d_act * silu], axis=-1
        ).astype(jnp.bfloat16)
        back_mine = times_transposed(d_pre, front_mine)
        back_other = times_transposed(d_pre, front_other).astype(jnp.bfloat16)
        out_mine = jnp.dot(act_gated, down_mine, preferred_element_type=jnp.float32)
        out_other = jnp.dot(act_gated, down_other, preferred_element_type=jnp.float32)
        back_rows.append((back_mine + swap(back_other).astype(jnp.float32)).astype(jnp.bfloat16))
        out_rows.append(
            (out_mine + swap(out_other.astype(jnp.bfloat16)).astype(jnp.float32)).astype(
                jnp.bfloat16
            )
        )
        gate_up_grad += jnp.stack([contract_rows(x_mine, d_pre), contract_rows(x_other, d_pre)])
        down_grad += jnp.stack(
            [contract_rows(act_gated, c_mine), contract_rows(act_gated, c_other)]
        )
    gate_up_grad = jnp.where(side == 0, gate_up_grad, gate_up_grad[::-1])
    gate_up_grad = gate_up_grad.reshape(1, model_width, 2 * unit_count)
    gate_grad, up_grad = gate_up_grad[..., :unit_count], gate_up_grad[..., unit_count:]
    down_grad = join_halves(down_grad[0], down_grad[1], side)[None]

    def gather_back(rows):
        parts = [None] * depth
        for g in reversed(range(depth)):
            blocks = rows[g].reshape(width, capacity, model_width // 2)
            came = jnp.stack(link.plane([blocks[b] for b in range(width)]))
            parts[g] = jnp.einsum(
                "bst,bsd->td", selectors[g], came, preferred_element_type=jnp.float32
            )
        return link.collect(parts)

    terms = jnp.stack(link.plane([jnp.stack([t[b] for t in term_rows]) for b in range(width)]), 1)
    tables_back = []
    for g in range(depth):
        local = jnp.sum(
            jnp.where(selectors[g] > 0, terms[g][:, :, None], 0.0), axis=1
        )
        tables_back.append(local if g == 0 else link.flip(local, g * width))
    term_table = jnp.concatenate(tables_back, axis=0)
    term_table = term_table + swap(term_table)
    labels = jnp.arange(expert_count, dtype=jnp.int32)
    relabeled = (routes ^ link.me)[:, :, None] == labels[None, None, :]
    gate_total = jnp.sum(jnp.where(relabeled, term_table.T[:, None, :], 0.0), axis=-1)

    row_half = gather_back(back_rows).astype(jnp.bfloat16)
    row_total = join_halves(row_half, swap(row_half), side).astype(jnp.float32)
    combined = gather_back(out_rows)
    output_half = (half_of(hidden, side) + combined).astype(jnp.bfloat16)
    output = join_halves(output_half, swap(output_half), side)

    upstream = cotangent.astype(jnp.float32)
    d_chosen = gate_weights * (
        gate_total - jnp.sum(gate_weights * gate_total, axis=-1, keepdims=True)
    )
    d_logits = jnp.sum(jnp.where(picked, d_chosen[:, :, None], 0.0), axis=1).astype(jnp.bfloat16)
    router_grad = contract_rows(second_in, d_logits)
    d_second = row_total + times_transposed(d_logits, w_router)
    scaled_second = d_second * ffn_gain
    ffn_gain_grad = jnp.sum(d_second * normed_second, axis=0)
    d_hidden = upstream + inverse_second * (
        scaled_second
        - normed_second * jnp.mean(scaled_second * normed_second, axis=-1, keepdims=True)
    )
    d_branch = d_hidden.astype(jnp.bfloat16)
    small = jnp.concatenate([router_grad, ffn_gain_grad[:, None]], axis=1)
    small = lax.psum_scatter(small, "expert", scatter_dimension=0, tiled=True)
    out_grad = link.scatter_sum(contract_rows(d_branch, mixed)).T
    d_mixed = (
        times_transposed(d_branch, w_out)
        .astype(jnp.bfloat16)
        .reshape(seq_length, local_heads, head_width)
    )
    scores = attention_scores(query, keys, allowed, score_scale)
    probs = jnp.exp(scores - log_total)
    d_probs = jnp.einsum("qhd,kd->hqk", d_mixed, values, preferred_element_type=jnp.float32)
    row_dot = jnp.sum(probs * d_probs, axis=-1, keepdims=True)
    d_scores = (score_scale * probs * (d_probs - row_dot)).astype(jnp.bfloat16)
    d_query_turned = jnp.einsum("hqk,kd->qhd", d_scores, keys, preferred_element_type=jnp.float32)
    d_keys_turned = jnp.einsum("hqk,qhd->kd", d_scores, query, preferred_element_type=jnp.float32)
    d_values = jnp.einsum(
        "hqk,qhd->kd", probs.astype(jnp.bfloat16), d_mixed, preferred_element_type=jnp.float32
    ).astype(jnp.bfloat16)
    d_query = (
        rotate_back(d_query_turned, cosine_table, sine_table)
        .astype(jnp.bfloat16)
        .reshape(seq_length, local_heads * head_width)
    )
    d_keys = rotate_back(d_keys_turned[:, None, :], cosine_table, sine_table)[:, 0, :].astype(
        jnp.bfloat16
    )
    d_all = jnp.concatenate([d_query, d_keys, d_values], axis=1)
    w_all = jnp.concatenate([w_query, w_key, w_value], axis=1)
    d_first = times_transposed(d_all, w_all).astype(jnp.bfloat16)
    qkv_grad = link.scatter_sum(contract_rows(first_in, d_all))
    d_first = d_first.astype(jnp.float32) + swap(d_first).astype(jnp.float32)
    scaled_first = d_first * norm_gain
    input_grad = d_hidden + inverse_first * (
        scaled_first - normed_first * jnp.mean(scaled_first * normed_first, axis=-1, keepdims=True)
    )
    rows = model_width // expert_count
    w_mine = lax.dynamic_slice_in_dim(w_all, link.me * rows, rows, 0).astype(jnp.float32)
    gain_mine = lax.dynamic_slice_in_dim(norm_gain, link.me * rows, rows, 0)
    gain_part = jnp.sum(qkv_grad * w_mine, axis=1) / gain_mine
    norm_gain_grad = gain_part + swap(gain_part)
    span = local_heads * head_width
    return (
        output,
        input_grad,
        norm_gain_grad,
        small[:, expert_count],
        qkv_grad[:, :span],
        qkv_grad[:, span : span + head_width],
        qkv_grad[:, span + head_width :],
        out_grad,
        small[:, :expert_count],
        gate_grad,
        up_grad,
        down_grad,
    )


def solution(mesh):
    placed = (
        P("expert", None),
        P("expert", None),
        P(),
        P(),
        P(None, "tensor"),
        P(None, "tensor"),
        P(None, "tensor"),
        P("tensor", None),
        P(),
        P("expert", None, "tensor"),
        P("expert", None, "tensor"),
        P("expert", "tensor", None),
        P("expert", None),
        P("expert", None),
        P("expert", None),
    )
    return jax.shard_map(
        on_device,
        mesh=mesh,
        in_specs=placed,
        out_specs=(
            P("expert", None),
            P("expert", None),
            P("expert"),
            P("expert"),
            P("expert", "tensor"),
            P("expert", "tensor"),
            P("expert", "tensor"),
            P("tensor", "expert"),
            P("expert", None),
            P("expert", None, "tensor"),
            P("expert", None, "tensor"),
            P("expert", "tensor", None),
        ),
        check_vma=False,
    )
```

time: 2550 us -> 1040 us (0.41)
  waiting for transfers between devices: 1120 us -> 365 us
  blocking collectives: 712 us -> 0 us
  local copies, waits for them, and re-layouts: 327 us -> 49.8 us
  starting transfers between devices: 13.5 us -> 214 us
  matrix products: 248 us -> 277 us
    all_to_all x2 -> x0, blocking collectives: 643 us -> none  [the longest x1 330 us: on_device(): lax.all_to_all(grad_out, 'expert', split_axis=0, concat_axis=0, tiled=True)]
    all_to_all x2 -> x0, waiting for transfers between devices: 570 us -> none  [the longest x1 304 us: on_device(): lax.all_to_all(row_whole, 'expert', split_axis=0, concat_axis=0, tiled=True)]
    reduce_scatter x6 -> x0, waiting for transfers between devices: 487 us -> none  [the longest x1 142 us: on_device(): lax.psum_scatter(query_grad, 'expert', scatter_dimension=0, tiled=True)]
    ppermute x0 -> x125, waiting for transfers between devices: none -> 304 us  [the longest x73 205 us: flip(): lax.ppermute(rows, 'expert', [(d, d ^ mask) for d in range(self.count)])]
    gather x13 -> x0, local copies, waits for them, and re-layouts: 222 us -> none  [the longest x4 56.9 us: on_device(): returned_pad[pair_slot[:, pick_rank]]]
    ppermute x0 -> x125, starting transfers between devices: none -> 214 us  [the longest x22 84.9 us: swap(): return lax.ppermute(rows, 'tensor', [(0, 1), (1, 0)])]
    unnamed x1 -> x0, blocking collectives: 69.3 us -> none
    dot_general x4 -> x45, matrix products: 37.6 us -> 98.9 us  [the longest x8 25.2 us: gather_back(): jnp.einsum('bst,bsd->td', selectors[g], came, preferred_element_type=jnp....]
  transfers between devices with their start and end apart: 13 -> 126, of which waited for: 10 -> 45; matrix products, arithmetic and copies ran while one was open for 15% -> 28% of each run, Pallas kernels for 0% -> 0%
where the time goes in v1:
time: 1040 us
  waiting for transfers between devices  365 us (35%)
  matrix products  277 us (27%)
  starting transfers between devices  214 us (21%)
  other arithmetic  114 us (11%)
  local copies, waits for them, and re-layouts  49.8 us (5%)
  between operations  17.3 us (2%)
    ppermute x73, waiting for transfers between devices, flip(): lax.ppermute(rows, 'expert', [(d, d ^ mask) for d in range(self.count)])  205 us
    ppermute x30, waiting for transfers between devices, send(): return lax.ppermute(rows, 'expert', flat)  99 us
    ppermute x22, starting transfers between devices, swap(): return lax.ppermute(rows, 'tensor', [(0, 1), (1, 0)])  84.9 us
    ppermute x73, starting transfers between devices, flip(): lax.ppermute(rows, 'expert', [(d, d ^ mask) for d in range(self.count)])  65.7 us
    ppermute x30, starting transfers between devices, send(): return lax.ppermute(rows, 'expert', flat)  62.9 us
    unnamed x2, waiting for transfers between devices  61 us
    dot_general x19, matrix products, times_transposed(): lax.dot_general(left, right, (((1,), (1,)), ((), ())), preferred_element_...  54.3 us
    dot_general x19, matrix products, contract_rows(): lax.dot_general(left, right, (((0,), (0,)), ((), ())), preferred_element_...  39.4 us
  transfers between devices with their start and end apart: 126, of which 45 were waited for; matrix products, arithmetic and copies ran while one was open for 28% of the time, Pallas kernels for 0%

profile of v1, /device:TPU:9, one launch (start us, length us, event | category | flops | bytes accessed | tf_op | source)
XLA Modules:
  0.0 1037.4 jit_solution(16303913424085198631)
XLA Ops:
  10.2 4.6 fusion.320
  32.2 11.2 %fusion.4 = (f32[6,1024]{1,0:T(8,128)S(1)}, f32[1024,1024,6]{1,0,2:T(8,128)}) fusion(pred[1024,1024]{0,1:T(8,128)(4,1)S(1)} %broadcast_compare_fusion, bf16[1024,6,64]{2,0,1:T(8,128)(2,1)S(1)} %get-tuple-element.25, bf16[1024,6,64]{2,0,1:T(8,128)(2,1)S(1)} %get-tuple-element.24, bf16[1024,1,64]{0,2,1:T(8,128)(2,1)S(1)} %get-tuple-element.127, ...), kind=kOutput, calls=%fused_computation.10 | convolution fusion | flops 1633150976 | bytes 28073984 | tf_op jit(solution)/shard_map/qhd,kd->hqk/dot_general | solution.py:68
  43.4 11.5 %exponential_reduce_fusion = f32[6,1024]{1,0:T(8,128)S(1)} fusion(f32[1024,1024,6]{1,0,2:T(8,128)} %get-tuple-element.178, f32[6,1024]{1,0:T(8,128)S(1)} %is-finite_select_fusion, pred[1024,1024]{0,1:T(8,128)(4,1)S(1)} %broadcast_compare_fusion), kind=kLoop, calls=%fused_computation.8 | loop fusion | flops 25159680 | bytes 26263552 | tf_op jit(solution)/shard_map/reduce_sum | solution.py:267
  56.0 12.2 %convolution_convert_fusion.10 = bf16[128,6,1024]{2,0,1:T(8,128)(2,1)S(1)} fusion(bf16[1024,128,1]{1,0,2:T(8,128)(2,1)S(1)} %fusion.173, f32[1024,1024,6]{1,0,2:T(8,128)} %get-tuple-element.178, f32[6,1024]{1,0:T(8,128)S(1)} %log_add_fusion, pred[1024,1024]{0,1:T(8,128)(4,1)S(1)} %broadcast_compare_fusion), kind=kOutput, calls=%fused_computation.269 | convolution fusion | flops 1636564992 | bytes 28073984 | tf_op jit(solution)/shard_map/hqk,kd->qhd/dot_general | solution.py:269
  68.3 4.1 convolution_convert_fusion
  75.1 9.3 convert_reduce_fusion
  111.4 6.5 collective-permute-done.33
  121.8 4.1 collective-permute-start.77
  134.7 16.5 %collective-permute-done.60 = bf16[288,768]{1,0:T(8,128)(2,1)} collective-permute-done((bf16[288,768]{1,0:T(8,128)(2,1)}, bf16[288,768]{1,0:T(8,128)(2,1)}, u32[]{:S(2)}, u32[]{:S(2)}) %collective-permute-start.60) | collective-permute-done | bytes 442400 | tf_op jit(solution)/shard_map/ppermute | solution.py:114
  164.9 4.4 multiply_reduce_fusion.2
  172.1 26.2 %collective-permute-done.76 = bf16[1024,768]{1,0:T(8,128)(2,1)S(1)} collective-permute-done((bf16[1024,768]{1,0:T(8,128)(2,1)}, bf16[1024,768]{1,0:T(8,128)(2,1)S(1)}, u32[]{:S(2)}, u32[]{:S(2)}) %collective-permute-start.76) | collective-permute-done | bytes 1572896 | tf_op jit(solution)/shard_map/ppermute | solution.py:111
  211.8 7.0 collective-permute-done.1
  218.8 4.3 collective-permute-start.71
  229.7 8.1 collective-permute-done.79
  243.5 4.5 collective-permute-done.81
  255.9 8.0 collective-permute-done.87
  268.6 7.5 collective-permute-done.27
  280.7 5.9 collective-permute-done.16
  286.6 4.0 fusion.187
  290.6 5.7 collective-permute-done.88
  306.2 5.1 collective-permute-start.17
  323.2 5.1 collective-permute-done.26
  328.3 5.1 collective-permute-done.28
  335.7 5.6 collective-permute-start.29
  344.6 4.4 collective-permute-start.41
  351.1 5.7 collective-permute-start.91
  357.0 6.6 collective-permute-start.32
  366.6 11.1 %collective-permute-done.41 = bf16[1024,768]{1,0:T(8,128)(2,1)S(1)} collective-permute-done((bf16[1024,768]{1,0:T(8,128)(2,1)S(1)}, bf16[1024,768]{1,0:T(8,128)(2,1)S(1)}, u32[]{:S(2)}, u32[]{:S(2)}) %collective-permute-start.41) | collective-permute-done | bytes 1572896 | tf_op jit(solution)/shard_map/ppermute | solution.py:111
  387.1 4.4 collective-permute-done.43
  395.3 8.0 collective-permute-start.45
  418.9 4.2 convolution_bitcast_fusion.8
  442.7 4.0 convolution_add_fusion
  446.7 3.9 multiply_convert_fusion.2
  512.1 8.0 collective-permute-done.93
  521.3 9.6 collective-permute-start.63
  542.2 6.1 collective-permute-done.84
  551.3 10.8 %collective-permute-start.21 = (bf16[1152,768]{1,0:T(8,128)(2,1)S(1)}, bf16[1152,768]{1,0:T(8,128)(2,1)S(1)}, u32[]{:S(2)}, u32[]{:S(2)}) collective-permute-start(bf16[1152,768]{1,0:T(8,128)(2,1)S(1)} %copy-done.92), channel_id=1, source_target_pairs={{0,1},{1,0},{2,3},{3,2},{4,5},{5,4},{6,7},{7,6},{8,9},{9,8},{10,11... | collective-permute-start | bytes 5308424 | tf_op jit(solution)/shard_map/ppermute | solution.py:179
  562.0 11.0 %collective-permute-done.96 = bf16[1024,768]{1,0:T(8,128)(2,1)S(1)} collective-permute-done((bf16[1024,768]{1,0:T(8,128)(2,1)S(1)}, bf16[1024,768]{1,0:T(8,128)(2,1)S(1)}, u32[]{:S(2)}, u32[]{:S(2)}) %collective-permute-start.96) | collective-permute-done | bytes 1572896 | tf_op jit(solution)/shard_map/ppermute | solution.py:111
  585.7 14.1 %collective-permute-done.51 = bf16[288,768]{1,0:T(8,128)(2,1)S(1)} collective-permute-done((bf16[288,768]{1,0:T(8,128)(2,1)S(1)}, bf16[288,768]{1,0:T(8,128)(2,1)S(1)}, u32[]{:S(2)}, u32[]{:S(2)}) %collective-permute-start.51) | collective-permute-done | bytes 442400 | tf_op jit(solution)/shard_map/ppermute | solution.py:114
  603.6 16.3 %collective-permute-done.74 = bf16[288,768]{1,0:T(8,128)(2,1)S(1)} collective-permute-done((bf16[288,768]{1,0:T(8,128)(2,1)S(1)}, bf16[288,768]{1,0:T(8,128)(2,1)S(1)}, u32[]{:S(2)}, u32[]{:S(2)}) %collective-permute-start.74) | collective-permute-done | bytes 442400 | tf_op jit(solution)/shard_map/ppermute | solution.py:114
  628.0 3.9 collective-permute-start.100
  632.1 7.2 collective-permute-done.37
  642.1 12.1 %collective-permute-start.8 = (bf16[1152,768]{1,0:T(8,128)(2,1)S(1)}, bf16[1152,768]{1,0:T(8,128)(2,1)S(1)}, u32[]{:S(2)}, u32[]{:S(2)}) collective-permute-start(bf16[1152,768]{1,0:T(8,128)(2,1)S(1)} %copy-done.91), channel_id=1, source_target_pairs={{0,1},{1,0},{2,3},{3,2},{4,5},{5,4},{6,7},{7,6},{8,9},{9,8},{10,11... | collective-permute-start | bytes 5308424 | tf_op jit(solution)/shard_map/ppermute | solution.py:179
  661.0 14.7 %collective-permute-done.65 = bf16[288,768]{1,0:T(8,128)(2,1)S(1)} collective-permute-done((bf16[288,768]{1,0:T(8,128)(2,1)S(1)}, bf16[288,768]{1,0:T(8,128)(2,1)S(1)}, u32[]{:S(2)}, u32[]{:S(2)}) %collective-permute-start.65) | collective-permute-done | bytes 442400 | tf_op jit(solution)/shard_map/ppermute | solution.py:114
  677.6 13.0 %collective-permute-done.98 = bf16[1024,768]{1,0:T(8,128)(2,1)S(1)} collective-permute-done((bf16[1024,768]{1,0:T(8,128)(2,1)S(1)}, bf16[1024,768]{1,0:T(8,128)(2,1)S(1)}, u32[]{:S(2)}, u32[]{:S(2)}) %collective-permute-start.98) | collective-permute-done | bytes 1572896 | tf_op jit(solution)/shard_map/ppermute | solution.py:111
  702.5 17.3 %collective-permute-done.23 = bf16[288,768]{1,0:T(8,128)(2,1)S(1)} collective-permute-done((bf16[288,768]{1,0:T(8,128)(2,1)S(1)}, bf16[288,768]{1,0:T(8,128)(2,1)S(1)}, u32[]{:S(2)}, u32[]{:S(2)}) %collective-permute-start.23) | collective-permute-done | bytes 442400 | tf_op jit(solution)/shard_map/ppermute | solution.py:114
  730.1 4.3 collective-permute-start.57
  737.3 4.8 convert_bitcast_fusion
  745.9 17.6 %fusion = (f32[6,1024]{1,0:T(8,128)}, f32[1024,1024,6]{1,0,2:T(8,128)}) fusion(f32[1024,1024,6]{1,0,2:T(8,128)} %get-tuple-element.178, f32[6,1024]{1,0:T(8,128)S(1)} %copy-done.65, pred[1024,1024]{0,1:T(8,128)(4,1)S(1)} %copy-done.10, bf16[1024,128,1]{1,0,2:T(8,128)(2,1)} %copy-done.66, bf16[1024,6,128]{0,2,1:T(8,128)(2,1)} %bitcast.549), kind=kOutput, calls=%fused_computation.3 | convolution fusion | flops 1642063872 | bytes 53264384 | tf_op jit(solution)/shard_map/qhd,kd->hqk/dot_general | solution.py:399
  763.5 22.1 %fusion.2 = bf16[6,1024,1024]{1,2,0:T(8,128)(2,1)} fusion(f32[1024,1024,6]{1,0,2:T(8,128)} %get-tuple-element.193, f32[1024,1024,6]{1,0,2:T(8,128)} %get-tuple-element.178, f32[6,1024]{1,0:T(8,128)} %get-tuple-element.192, f32[6,1024]{1,0:T(8,128)S(1)} %copy-done.65, pred[1024,1024]{0,1:T(8,128)(4,1)S(1)} %copy-done.10), kind=kLoop, calls=%fused_computation.5 | loop fusion | flops 44040192 | bytes 64012288 | tf_op jit(solution)/shard_map/convert_element_type | solution.py:401
  785.7 11.6 %convolution_bitcast_fusion = f32[1024,6,128]{2,0,1:T(8,128)} fusion(bf16[6,1024,1024]{1,2,0:T(8,128)(2,1)} %fusion.2, bf16[1024,1,64]{0,2,1:T(8,128)(2,1)S(1)} %copy-done.43, bf16[1024,1,64]{0,2,1:T(8,128)(2,1)S(1)} %copy-done.41), kind=kOutput, calls=%fused_computation.160 | convolution fusion | flops 1611137024 | bytes 15990784 | tf_op jit(solution)/shard_map/hqk,kd->qhd/dot_general | solution.py:402
  797.2 9.9 convolution_bitcast_fusion.19
  807.2 12.3 %fusion.169 = bf16[1024,128]{0,1:T(8,128)(2,1)} fusion(bf16[1024,6,128]{0,2,1:T(8,128)(2,1)S(1)} %bitcast.550, f32[1024,1024,6]{1,0,2:T(8,128)} %get-tuple-element.178, f32[6,1024]{1,0:T(8,128)S(1)} %copy-done.65, pred[1024,1024]{0,1:T(8,128)(4,1)S(1)} %copy-done.10), kind=kOutput, calls=%fused_computation.312 | convolution fusion | flops 1635909632 | bytes 28073984 | tf_op jit(solution)/shard_map/hqk,qhd->kd/dot_general | solution.py:404
  819.5 4.7 copy.117
  824.2 4.0 add_convert_fusion.8
  834.4 6.3 fusion.180
  848.4 6.3 fusion.50
  858.8 7.9 convolution_convert_fusion.1
  866.7 6.1 collective-permute-done.118
  875.9 31.8 %collective-permute-done.110 = bf16[8,96,1024]{2,1,0:T(8,128)(2,1)} collective-permute-done((bf16[8,96,1024]{2,1,0:T(8,128)(2,1)}, bf16[8,96,1024]{2,1,0:T(8,128)(2,1)}, u32[]{:S(2)}, u32[]{:S(2)}) %collective-permute-start.110) | collective-permute-done | bytes 1572896 | tf_op jit(solution)/shard_map/ppermute | solution.py:114
  915.9 61.0 %reduce-scatter.4.cloned.1.call-done = f32[96,17]{1,0:T(8,128)} async-done(((f32[1536,17]{1,0:T(8,128)}), f32[96,17]{1,0:T(8,128)}) %reduce-scatter.4.cloned.1.call-update) | async-done | bytes 6544
  1013.2 4.5 collective-permute-start.117
  1019.7 4.6 fusion.9
  1024.3 6.0 fusion.12
  (771 shorter events, 411.5 us)
Async XLA Ops:
  7.2 969.7 %reduce-scatter.4.cloned.1.call-start = ((), (), s32[]{:S(2)}) async-start(), calls=%async_computation.1 | async-start | bytes 835584
  72.4 90.9 %collective-permute-start = (bf16[1024,1536]{1,0:T(8,128)(2,1)}, bf16[1024,1536]{1,0:T(8,128)(2,1)}, u32[]{:S(2)}, u32[]{:S(2)}) collective-permute-start(bf16[1024,1536]{1,0:T(8,128)(2,1)} %convolution_convert_fusion), channel_id=1, source_target_pairs={{0,1},{1,0},{2,3},{3,2},{4,5},{5,4},{6,7},{7,6},{8,9},{9,8},{10,11... | collective-permute-start | bytes 9437192 | tf_op jit(solution)/shard_map/ppermute | solution.py:179
  90.7 64.8 %collective-permute-start.67 = (bf16[1024,768]{1,0:T(8,128)(2,1)}, bf16[1024,768]{1,0:T(8,128)(2,1)}, u32[]{:S(2)}, u32[]{:S(2)}) collective-permute-start(bf16[1024,768]{1,0:T(8,128)(2,1)} %constant_dynamic-slice_fusion), channel_id=1, source_target_pairs={{0,8},{2,10},{4,12},{6,14},{8,0},{10,2},{12,4},{14,6},{16,24},{18,... | collective-permute-start | bytes 4718600 | tf_op jit(solution)/shard_map/ppermute | solution.py:111
  108.2 24.0 %collective-permute-start.59 = (bf16[288,768]{1,0:T(8,128)(2,1)}, bf16[288,768]{1,0:T(8,128)(2,1)S(1)}, u32[]{:S(2)}, u32[]{:S(2)}) collective-permute-start(bf16[288,768]{1,0:T(8,128)(2,1)} %get-tuple-element.75), channel_id=1, source_target_pairs={{0,2},{2,0},{4,6},{6,4},{8,10},{10,8},{12,14},{14,12},{16,18},{18,... | collective-permute-start | bytes 1327112 | tf_op jit(solution)/shard_map/ppermute | solution.py:114
  121.8 39.1 %collective-permute-start.77 = (bf16[1024,768]{1,0:T(8,128)(2,1)}, bf16[1024,768]{1,0:T(8,128)(2,1)}, u32[]{:S(2)}, u32[]{:S(2)}) collective-permute-start(bf16[1024,768]{1,0:T(8,128)(2,1)} %constant_dynamic-slice_fusion), channel_id=1, source_target_pairs={{8,16},{10,18},{12,20},{14,22},{16,8},{18,10},{20,12},{22,14},{9,1... | collective-permute-start | bytes 4718600 | tf_op jit(solution)/shard_map/ppermute | solution.py:111
  131.8 19.4 %collective-permute-start.60 = (bf16[288,768]{1,0:T(8,128)(2,1)}, bf16[288,768]{1,0:T(8,128)(2,1)}, u32[]{:S(2)}, u32[]{:S(2)}) collective-permute-start(bf16[288,768]{1,0:T(8,128)(2,1)} %get-tuple-element.74), channel_id=1, source_target_pairs={{0,4},{2,6},{4,0},{6,2},{8,12},{10,14},{12,8},{14,10},{16,20},{18,... | collective-permute-start | bytes 1327112 | tf_op jit(solution)/shard_map/ppermute | solution.py:114
  152.5 56.9 %collective-permute-start.62 = (bf16[1152,768]{1,0:T(8,128)(2,1)S(1)}, bf16[1152,768]{1,0:T(8,128)(2,1)S(1)}, u32[]{:S(2)}, u32[]{:S(2)}) collective-permute-start(bf16[1152,768]{1,0:T(8,128)(2,1)S(1)} %pad_maximum_fusion.6), channel_id=1, source_target_pairs={{0,1},{1,0},{2,3},{3,2},{4,5},{5,4},{6,7},{7,6},{8,9},{9,8},{10,11... | collective-permute-start | bytes 5308424 | tf_op jit(solution)/shard_map/ppermute | solution.py:179
  159.1 44.2 %collective-permute-start.68 = (bf16[288,768]{1,0:T(8,128)(2,1)S(1)}, bf16[288,768]{1,0:T(8,128)(2,1)S(1)}, u32[]{:S(2)}, u32[]{:S(2)}) collective-permute-start(bf16[288,768]{1,0:T(8,128)(2,1)S(1)} %get-tuple-element.79), channel_id=1, source_target_pairs={{0,2},{2,0},{4,6},{6,4},{8,10},{10,8},{12,14},{14,12},{16,18},{18,... | collective-permute-start | bytes 1327112 | tf_op jit(solution)/shard_map/ppermute | solution.py:114
  160.4 44.6 %collective-permute-start.69 = (bf16[288,768]{1,0:T(8,128)(2,1)S(1)}, bf16[288,768]{1,0:T(8,128)(2,1)S(1)}, u32[]{:S(2)}, u32[]{:S(2)}) collective-permute-start(bf16[288,768]{1,0:T(8,128)(2,1)S(1)} %get-tuple-element.78), channel_id=1, source_target_pairs={{0,4},{2,6},{4,0},{6,2},{8,12},{10,14},{12,8},{14,10},{16,20},{18,... | collective-permute-start | bytes 1327112 | tf_op jit(solution)/shard_map/ppermute | solution.py:114
  160.9 37.4 %collective-permute-start.76 = (bf16[1024,768]{1,0:T(8,128)(2,1)}, bf16[1024,768]{1,0:T(8,128)(2,1)S(1)}, u32[]{:S(2)}, u32[]{:S(2)}) collective-permute-start(bf16[1024,768]{1,0:T(8,128)(2,1)} %collective-permute-done.67), channel_id=1, source_target_pairs={{8,16},{10,18},{12,20},{14,22},{16,8},{18,10},{20,12},{22,14},{9,1... | collective-permute-start | bytes 4718600 | tf_op jit(solution)/shard_map/ppermute | solution.py:111
  163.2 35.5 %collective-permute-start.78 = (bf16[1024,768]{1,0:T(8,128)(2,1)}, bf16[1024,768]{1,0:T(8,128)(2,1)S(1)}, u32[]{:S(2)}, u32[]{:S(2)}) collective-permute-start(bf16[1024,768]{1,0:T(8,128)(2,1)} %collective-permute-done.77), channel_id=1, source_target_pairs={{8,0},{10,2},{12,4},{14,6},{16,24},{18,26},{20,28},{22,30},{9,1},{... | collective-permute-start | bytes 4718600 | tf_op jit(solution)/shard_map/ppermute | solution.py:111
  198.7 53.9 %collective-permute-start.13 = (bf16[1024,768]{1,0:T(8,128)(2,1)S(1)}, bf16[1024,768]{1,0:T(8,128)(2,1)S(1)}, u32[]{:S(2)}, u32[]{:S(2)}) collective-permute-start(bf16[1024,768]{1,0:T(8,128)(2,1)S(1)} %constant_dynamic-slice_fusion.1), channel_id=1, source_target_pairs={{0,8},{2,10},{4,12},{6,14},{8,0},{10,2},{12,4},{14,6},{16,24},{18,... | collective-permute-start | bytes 4718600 | tf_op jit(solution)/shard_map/ppermute | solution.py:111
  209.3 28.4 %collective-permute-start.79 = (bf16[288,768]{1,0:T(8,128)(2,1)S(1)}, bf16[288,768]{1,0:T(8,128)(2,1)S(1)}, u32[]{:S(2)}, u32[]{:S(2)}) collective-permute-start(bf16[288,768]{1,0:T(8,128)(2,1)S(1)} %get-tuple-element.83), channel_id=1, source_target_pairs={{0,2},{2,0},{4,6},{6,4},{8,10},{10,8},{12,14},{14,12},{16,18},{18,... | collective-permute-start | bytes 1327112 | tf_op jit(solution)/shard_map/ppermute | solution.py:114
  218.8 37.1 %collective-permute-start.71 = (bf16[1152,768]{1,0:T(8,128)(2,1)S(1)}, bf16[1152,768]{1,0:T(8,128)(2,1)S(1)}, u32[]{:S(2)}, u32[]{:S(2)}) collective-permute-start(bf16[1152,768]{1,0:T(8,128)(2,1)S(1)} %pad_maximum_fusion.8), channel_id=1, source_target_pairs={{0,1},{1,0},{2,3},{3,2},{4,5},{5,4},{6,7},{7,6},{8,9},{9,8},{10,11... | collective-permute-start | bytes 5308424 | tf_op jit(solution)/shard_map/ppermute | solution.py:179
  228.3 35.5 %collective-permute-start.87 = (bf16[1024,768]{1,0:T(8,128)(2,1)S(1)}, bf16[1024,768]{1,0:T(8,128)(2,1)S(1)}, u32[]{:S(2)}, u32[]{:S(2)}) collective-permute-start(bf16[1024,768]{1,0:T(8,128)(2,1)S(1)} %broadcast_select_fusion), channel_id=1, source_target_pairs={{8,0},{10,2},{12,4},{14,6},{16,24},{18,26},{20,28},{22,30},{9,1},{... | collective-permute-start | bytes 4718600 | tf_op jit(solution)/shard_map/ppermute | solution.py:111
  239.8 36.3 %collective-permute-start.27 = (bf16[1024,768]{1,0:T(8,128)(2,1)S(1)}, bf16[1024,768]{1,0:T(8,128)(2,1)S(1)}, u32[]{:S(2)}, u32[]{:S(2)}) collective-permute-start(bf16[1024,768]{1,0:T(8,128)(2,1)S(1)} %constant_dynamic-slice_fusion.1), channel_id=1, source_target_pairs={{8,16},{10,18},{12,20},{14,22},{16,8},{18,10},{20,12},{22,14},{9,1... | collective-permute-start | bytes 4718600 | tf_op jit(solution)/shard_map/ppermute | solution.py:111
  248.0 68.6 %collective-permute-start.4 = (bf16[1152,768]{1,0:T(8,128)(2,1)}, bf16[1152,768]{1,0:T(8,128)(2,1)}, u32[]{:S(2)}, u32[]{:S(2)}) collective-permute-start(bf16[1152,768]{1,0:T(8,128)(2,1)} %pad_maximum_fusion.2), channel_id=1, source_target_pairs={{0,1},{1,0},{2,3},{3,2},{4,5},{5,4},{6,7},{7,6},{8,9},{9,8},{10,11... | collective-permute-start | bytes 5308424 | tf_op jit(solution)/shard_map/ppermute | solution.py:179
  252.6 60.1 %collective-permute-start.82 = (bf16[1152,768]{1,0:T(8,128)(2,1)}, bf16[1152,768]{1,0:T(8,128)(2,1)}, u32[]{:S(2)}, u32[]{:S(2)}) collective-permute-start(bf16[1152,768]{1,0:T(8,128)(2,1)} %pad_maximum_fusion.10), channel_id=1, source_target_pairs={{0,1},{1,0},{2,3},{3,2},{4,5},{5,4},{6,7},{7,6},{8,9},{9,8},{10,11... | collective-permute-start | bytes 5308424 | tf_op jit(solution)/shard_map/ppermute | solution.py:179
  255.9 21.9 %collective-permute-start.14 = (bf16[288,768]{1,0:T(8,128)(2,1)S(1)}, bf16[288,768]{1,0:T(8,128)(2,1)}, u32[]{:S(2)}, u32[]{:S(2)}) collective-permute-start(bf16[288,768]{1,0:T(8,128)(2,1)S(1)} %get-tuple-element.115), channel_id=1, source_target_pairs={{0,2},{2,0},{4,6},{6,4},{8,10},{10,8},{12,14},{14,12},{16,18},{18,... | collective-permute-start | bytes 1327112 | tf_op jit(solution)/shard_map/ppermute | solution.py:114
  279.8 21.8 %collective-permute-start.89 = (bf16[288,768]{1,0:T(8,128)(2,1)}, bf16[288,768]{1,0:T(8,128)(2,1)}, u32[]{:S(2)}, u32[]{:S(2)}) collective-permute-start(bf16[288,768]{1,0:T(8,128)(2,1)} %get-tuple-element.86), channel_id=1, source_target_pairs={{0,4},{2,6},{4,0},{6,2},{8,12},{10,14},{12,8},{14,10},{16,20},{18,... | collective-permute-start | bytes 1327112 | tf_op jit(solution)/shard_map/ppermute | solution.py:114
  286.6 19.6 %collective-permute-start.90 = (bf16[288,768]{1,0:T(8,128)(2,1)}, bf16[288,768]{1,0:T(8,128)(2,1)S(1)}, u32[]{:S(2)}, u32[]{:S(2)}) collective-permute-start(bf16[288,768]{1,0:T(8,128)(2,1)} %get-tuple-element.85), channel_id=1, source_target_pairs={{0,6},{2,4},{4,2},{6,0},{8,14},{10,12},{12,10},{14,8},{16,22},{18,... | collective-permute-start | bytes 1327112 | tf_op jit(solution)/shard_map/ppermute | solution.py:114
  296.3 31.9 %collective-permute-start.26 = (bf16[1024,768]{1,0:T(8,128)(2,1)S(1)}, bf16[1024,768]{1,0:T(8,128)(2,1)S(1)}, u32[]{:S(2)}, u32[]{:S(2)}) collective-permute-start(bf16[1024,768]{1,0:T(8,128)(2,1)S(1)} %copy-done.104), channel_id=1, source_target_pairs={{8,16},{10,18},{12,20},{14,22},{16,8},{18,10},{20,12},{22,14},{9,1... | collective-permute-start | bytes 4718600 | tf_op jit(solution)/shard_map/ppermute | solution.py:111
  301.6 31.7 %collective-permute-start.28 = (bf16[1024,768]{1,0:T(8,128)(2,1)S(1)}, bf16[1024,768]{1,0:T(8,128)(2,1)S(1)}, u32[]{:S(2)}, u32[]{:S(2)}) collective-permute-start(bf16[1024,768]{1,0:T(8,128)(2,1)S(1)} %copy-done.106), channel_id=1, source_target_pairs={{8,0},{10,2},{12,4},{14,6},{16,24},{18,26},{20,28},{22,30},{9,1},{... | collective-permute-start | bytes 4718600 | tf_op jit(solution)/shard_map/ppermute | solution.py:111
  306.2 57.3 %collective-permute-start.17 = (bf16[1152,768]{1,0:T(8,128)(2,1)S(1)}, bf16[1152,768]{1,0:T(8,128)(2,1)S(1)}, u32[]{:S(2)}, u32[]{:S(2)}) collective-permute-start(bf16[1152,768]{1,0:T(8,128)(2,1)S(1)} %pad_maximum_fusion.3), channel_id=1, source_target_pairs={{0,1},{1,0},{2,3},{3,2},{4,5},{5,4},{6,7},{7,6},{8,9},{9,8},{10,11... | collective-permute-start | bytes 5308424 | tf_op jit(solution)/shard_map/ppermute | solution.py:179
  344.6 33.1 %collective-permute-start.41 = (bf16[1024,768]{1,0:T(8,128)(2,1)S(1)}, bf16[1024,768]{1,0:T(8,128)(2,1)S(1)}, u32[]{:S(2)}, u32[]{:S(2)}) collective-permute-start(bf16[1024,768]{1,0:T(8,128)(2,1)S(1)} %broadcast_select_fusion.1), channel_id=1, source_target_pairs={{8,0},{10,2},{12,4},{14,6},{16,24},{18,26},{20,28},{22,30},{9,1},{... | collective-permute-start | bytes 4718600 | tf_op jit(solution)/shard_map/ppermute | solution.py:111
  351.1 52.2 %collective-permute-start.91 = (bf16[1152,768]{1,0:T(8,128)(2,1)S(1)}, bf16[1152,768]{1,0:T(8,128)(2,1)S(1)}, u32[]{:S(2)}, u32[]{:S(2)}) collective-permute-start(bf16[1152,768]{1,0:T(8,128)(2,1)S(1)} %pad_maximum_fusion.12), channel_id=1, source_target_pairs={{0,1},{1,0},{2,3},{3,2},{4,5},{5,4},{6,7},{7,6},{8,9},{9,8},{10,11... | collective-permute-start | bytes 5308424 | tf_op jit(solution)/shard_map/ppermute | solution.py:179
  357.0 48.6 %collective-permute-start.32 = (bf16[1152,768]{1,0:T(8,128)(2,1)S(1)}, bf16[1152,768]{1,0:T(8,128)(2,1)S(1)}, u32[]{:S(2)}, u32[]{:S(2)}) collective-permute-start(bf16[1152,768]{1,0:T(8,128)(2,1)S(1)} %pad_maximum_fusion.4), channel_id=1, source_target_pairs={{0,1},{1,0},{2,3},{3,2},{4,5},{5,4},{6,7},{7,6},{8,9},{9,8},{10,11... | collective-permute-start | bytes 5308424 | tf_op jit(solution)/shard_map/ppermute | solution.py:179
  495.4 41.5 %collective-permute-start.72 = (bf16[1152,768]{1,0:T(8,128)(2,1)S(1)}, bf16[1152,768]{1,0:T(8,128)(2,1)S(1)}, u32[]{:S(2)}, u32[]{:S(2)}) collective-permute-start(bf16[1152,768]{1,0:T(8,128)(2,1)S(1)} %copy-done.98), channel_id=1, source_target_pairs={{0,1},{1,0},{2,3},{3,2},{4,5},{5,4},{6,7},{7,6},{8,9},{9,8},{10,11... | collective-permute-start | bytes 5308424 | tf_op jit(solution)/shard_map/ppermute | solution.py:179
  503.0 30.8 %collective-permute-start.83 = (bf16[1152,768]{1,0:T(8,128)(2,1)S(1)}, bf16[1152,768]{1,0:T(8,128)(2,1)S(1)}, u32[]{:S(2)}, u32[]{:S(2)}) collective-permute-start(bf16[1152,768]{1,0:T(8,128)(2,1)S(1)} %copy-done.99), channel_id=1, source_target_pairs={{0,1},{1,0},{2,3},{3,2},{4,5},{5,4},{6,7},{7,6},{8,9},{9,8},{10,11... | collective-permute-start | bytes 5308424 | tf_op jit(solution)/shard_map/ppermute | solution.py:179
  510.0 20.9 %collective-permute-start.95 = (bf16[288,768]{1,0:T(8,128)(2,1)S(1)}, bf16[288,768]{1,0:T(8,128)(2,1)S(1)}, u32[]{:S(2)}, u32[]{:S(2)}) collective-permute-start(bf16[288,768]{1,0:T(8,128)(2,1)S(1)} %get-tuple-element.69), channel_id=1, source_target_pairs={{0,6},{2,4},{4,2},{6,0},{8,14},{10,12},{12,10},{14,8},{16,22},{18,... | collective-permute-start | bytes 1327112 | tf_op jit(solution)/shard_map/ppermute | solution.py:114
  520.0 19.9 %collective-permute-start.49 = (bf16[1152,768]{1,0:T(8,128)(2,1)S(1)}, bf16[1152,768]{1,0:T(8,128)(2,1)S(1)}, u32[]{:S(2)}, u32[]{:S(2)}) collective-permute-start(bf16[1152,768]{1,0:T(8,128)(2,1)S(1)} %convolution_convert_fusion.2), channel_id=1, source_target_pairs={{0,1},{1,0},{2,3},{3,2},{4,5},{5,4},{6,7},{7,6},{8,9},{9,8},{10,11... | collective-permute-start | bytes 5308424 | tf_op jit(solution)/shard_map/ppermute | solution.py:179
  521.3 58.6 %collective-permute-start.63 = (bf16[1152,768]{1,0:T(8,128)(2,1)S(1)}, bf16[1152,768]{1,0:T(8,128)(2,1)S(1)}, u32[]{:S(2)}, u32[]{:S(2)}) collective-permute-start(bf16[1152,768]{1,0:T(8,128)(2,1)S(1)} %copy-done.95), channel_id=1, source_target_pairs={{0,1},{1,0},{2,3},{3,2},{4,5},{5,4},{6,7},{7,6},{8,9},{9,8},{10,11... | collective-permute-start | bytes 5308424 | tf_op jit(solution)/shard_map/ppermute | solution.py:179
  530.9 45.8 %collective-permute-start.36 = (bf16[1152,768]{1,0:T(8,128)(2,1)S(1)}, bf16[1152,768]{1,0:T(8,128)(2,1)S(1)}, u32[]{:S(2)}, u32[]{:S(2)}) collective-permute-start(bf16[1152,768]{1,0:T(8,128)(2,1)S(1)} %convolution_convert_fusion.3), channel_id=1, source_target_pairs={{0,1},{1,0},{2,3},{3,2},{4,5},{5,4},{6,7},{7,6},{8,9},{9,8},{10,11... | collective-permute-start | bytes 5308424 | tf_op jit(solution)/shard_map/ppermute | solution.py:179
  533.8 39.2 %collective-permute-start.96 = (bf16[1024,768]{1,0:T(8,128)(2,1)S(1)}, bf16[1024,768]{1,0:T(8,128)(2,1)S(1)}, u32[]{:S(2)}, u32[]{:S(2)}) collective-permute-start(bf16[1024,768]{1,0:T(8,128)(2,1)S(1)} %get-tuple-element.189), channel_id=1, source_target_pairs={{0,8},{2,10},{4,12},{6,14},{24,16},{26,18},{28,20},{30,22},{1,9},{... | collective-permute-start | bytes 4718600 | tf_op jit(solution)/shard_map/ppermute | solution.py:111
  551.3 76.7 %collective-permute-start.21 = (bf16[1152,768]{1,0:T(8,128)(2,1)S(1)}, bf16[1152,768]{1,0:T(8,128)(2,1)S(1)}, u32[]{:S(2)}, u32[]{:S(2)}) collective-permute-start(bf16[1152,768]{1,0:T(8,128)(2,1)S(1)} %copy-done.92), channel_id=1, source_target_pairs={{0,1},{1,0},{2,3},{3,2},{4,5},{5,4},{6,7},{7,6},{8,9},{9,8},{10,11... | collective-permute-start | bytes 5308424 | tf_op jit(solution)/shard_map/ppermute | solution.py:179
  562.0 19.9 %collective-permute-start.73 = (bf16[288,768]{1,0:T(8,128)(2,1)S(1)}, bf16[288,768]{1,0:T(8,128)(2,1)S(1)}, u32[]{:S(2)}, u32[]{:S(2)}) collective-permute-start(bf16[288,768]{1,0:T(8,128)(2,1)S(1)} %get-tuple-element.63), channel_id=1, source_target_pairs={{0,2},{2,0},{4,6},{6,4},{8,10},{10,8},{12,14},{14,12},{16,18},{18,... | collective-permute-start | bytes 1327112 | tf_op jit(solution)/shard_map/ppermute | solution.py:114
  576.7 44.8 %collective-permute-start.97 = (bf16[1024,768]{1,0:T(8,128)(2,1)S(1)}, bf16[1024,768]{1,0:T(8,128)(2,1)S(1)}, u32[]{:S(2)}, u32[]{:S(2)}) collective-permute-start(bf16[1024,768]{1,0:T(8,128)(2,1)S(1)} %fusion.41), channel_id=1, source_target_pairs={{8,16},{10,18},{12,20},{14,22},{16,8},{18,10},{20,12},{22,14},{9,1... | collective-permute-start | bytes 4718600 | tf_op jit(solution)/shard_map/ppermute | solution.py:111
  579.9 19.8 %collective-permute-start.51 = (bf16[288,768]{1,0:T(8,128)(2,1)S(1)}, bf16[288,768]{1,0:T(8,128)(2,1)S(1)}, u32[]{:S(2)}, u32[]{:S(2)}) collective-permute-start(bf16[288,768]{1,0:T(8,128)(2,1)S(1)} %get-tuple-element.102), channel_id=1, source_target_pairs={{0,4},{2,6},{4,0},{6,2},{8,12},{10,14},{12,8},{14,10},{16,20},{18,... | collective-permute-start | bytes 1327112 | tf_op jit(solution)/shard_map/ppermute | solution.py:114
  583.7 41.5 %collective-permute-start.99 = (bf16[1024,768]{1,0:T(8,128)(2,1)S(1)}, bf16[1024,768]{1,0:T(8,128)(2,1)S(1)}, u32[]{:S(2)}, u32[]{:S(2)}) collective-permute-start(bf16[1024,768]{1,0:T(8,128)(2,1)S(1)} %fusion.41), channel_id=1, source_target_pairs={{0,8},{2,10},{4,12},{6,14},{24,16},{26,18},{28,20},{30,22},{1,9},{... | collective-permute-start | bytes 4718600 | tf_op jit(solution)/shard_map/ppermute | solution.py:111
  599.7 20.2 %collective-permute-start.74 = (bf16[288,768]{1,0:T(8,128)(2,1)S(1)}, bf16[288,768]{1,0:T(8,128)(2,1)S(1)}, u32[]{:S(2)}, u32[]{:S(2)}) collective-permute-start(bf16[288,768]{1,0:T(8,128)(2,1)S(1)} %get-tuple-element.62), channel_id=1, source_target_pairs={{0,4},{2,6},{4,0},{6,2},{8,12},{10,14},{12,8},{14,10},{16,20},{18,... | collective-permute-start | bytes 1327112 | tf_op jit(solution)/shard_map/ppermute | solution.py:114
  600.1 19.9 %collective-permute-start.75 = (bf16[288,768]{1,0:T(8,128)(2,1)S(1)}, bf16[288,768]{1,0:T(8,128)(2,1)S(1)}, u32[]{:S(2)}, u32[]{:S(2)}) collective-permute-start(bf16[288,768]{1,0:T(8,128)(2,1)S(1)} %get-tuple-element.61), channel_id=1, source_target_pairs={{0,6},{2,4},{4,2},{6,0},{8,14},{10,12},{12,10},{14,8},{16,22},{18,... | collective-permute-start | bytes 1327112 | tf_op jit(solution)/shard_map/ppermute | solution.py:114
  620.0 19.3 %collective-permute-start.37 = (bf16[288,768]{1,0:T(8,128)(2,1)S(1)}, bf16[288,768]{1,0:T(8,128)(2,1)S(1)}, u32[]{:S(2)}, u32[]{:S(2)}) collective-permute-start(bf16[288,768]{1,0:T(8,128)(2,1)S(1)} %get-tuple-element.99), channel_id=1, source_target_pairs={{0,2},{2,0},{4,6},{6,4},{8,10},{10,8},{12,14},{14,12},{16,18},{18,... | collective-permute-start | bytes 1327112 | tf_op jit(solution)/shard_map/ppermute | solution.py:114
  621.5 35.4 %collective-permute-start.53 = (bf16[1024,768]{1,0:T(8,128)(2,1)S(1)}, bf16[1024,768]{1,0:T(8,128)(2,1)S(1)}, u32[]{:S(2)}, u32[]{:S(2)}) collective-permute-start(bf16[1024,768]{1,0:T(8,128)(2,1)S(1)} %get-tuple-element.187), channel_id=1, source_target_pairs={{0,8},{2,10},{4,12},{6,14},{24,16},{26,18},{28,20},{30,22},{1,9},{... | collective-permute-start | bytes 4718600 | tf_op jit(solution)/shard_map/ppermute | solution.py:111
  625.2 65.3 %collective-permute-start.98 = (bf16[1024,768]{1,0:T(8,128)(2,1)S(1)}, bf16[1024,768]{1,0:T(8,128)(2,1)S(1)}, u32[]{:S(2)}, u32[]{:S(2)}) collective-permute-start(bf16[1024,768]{1,0:T(8,128)(2,1)S(1)} %fusion.42), channel_id=1, source_target_pairs={{0,8},{2,10},{4,12},{6,14},{8,0},{10,2},{12,4},{14,6},{16,24},{18,... | collective-permute-start | bytes 4718600 | tf_op jit(solution)/shard_map/ppermute | solution.py:111
  628.0 64.1 %collective-permute-start.100 = (bf16[1024,768]{1,0:T(8,128)(2,1)S(1)}, bf16[1024,768]{1,0:T(8,128)(2,1)S(1)}, u32[]{:S(2)}, u32[]{:S(2)}) collective-permute-start(bf16[1024,768]{1,0:T(8,128)(2,1)S(1)} %fusion.40), channel_id=1, source_target_pairs={{8,16},{10,18},{12,20},{14,22},{16,8},{18,10},{20,12},{22,14},{9,1... | collective-permute-start | bytes 4718600 | tf_op jit(solution)/shard_map/ppermute | solution.py:111
  642.1 56.5 %collective-permute-start.8 = (bf16[1152,768]{1,0:T(8,128)(2,1)S(1)}, bf16[1152,768]{1,0:T(8,128)(2,1)S(1)}, u32[]{:S(2)}, u32[]{:S(2)}) collective-permute-start(bf16[1152,768]{1,0:T(8,128)(2,1)S(1)} %copy-done.91), channel_id=1, source_target_pairs={{0,1},{1,0},{2,3},{3,2},{4,5},{5,4},{6,7},{7,6},{8,9},{9,8},{10,11... | collective-permute-start | bytes 5308424 | tf_op jit(solution)/shard_map/ppermute | solution.py:179
  654.3 21.3 %collective-permute-start.65 = (bf16[288,768]{1,0:T(8,128)(2,1)S(1)}, bf16[288,768]{1,0:T(8,128)(2,1)S(1)}, u32[]{:S(2)}, u32[]{:S(2)}) collective-permute-start(bf16[288,768]{1,0:T(8,128)(2,1)S(1)} %get-tuple-element.58), channel_id=1, source_target_pairs={{0,4},{2,6},{4,0},{6,2},{8,12},{10,14},{12,8},{14,10},{16,20},{18,... | collective-permute-start | bytes 1327112 | tf_op jit(solution)/shard_map/ppermute | solution.py:114
  675.6 23.2 %collective-permute-start.22 = (bf16[288,768]{1,0:T(8,128)(2,1)S(1)}, bf16[288,768]{1,0:T(8,128)(2,1)S(1)}, u32[]{:S(2)}, u32[]{:S(2)}) collective-permute-start(bf16[288,768]{1,0:T(8,128)(2,1)S(1)} %get-tuple-element.95), channel_id=1, source_target_pairs={{0,2},{2,0},{4,6},{6,4},{8,10},{10,8},{12,14},{14,12},{16,18},{18,... | collective-permute-start | bytes 1327112 | tf_op jit(solution)/shard_map/ppermute | solution.py:114
  675.7 45.9 %collective-permute-start.54 = (bf16[1024,768]{1,0:T(8,128)(2,1)S(1)}, bf16[1024,768]{1,0:T(8,128)(2,1)S(1)}, u32[]{:S(2)}, u32[]{:S(2)}) collective-permute-start(bf16[1024,768]{1,0:T(8,128)(2,1)S(1)} %fusion.46), channel_id=1, source_target_pairs={{8,16},{10,18},{12,20},{14,22},{16,8},{18,10},{20,12},{22,14},{9,1... | collective-permute-start | bytes 4718600 | tf_op jit(solution)/shard_map/ppermute | solution.py:111
  690.6 35.5 %collective-permute-start.56 = (bf16[1024,768]{1,0:T(8,128)(2,1)S(1)}, bf16[1024,768]{1,0:T(8,128)(2,1)S(1)}, u32[]{:S(2)}, u32[]{:S(2)}) collective-permute-start(bf16[1024,768]{1,0:T(8,128)(2,1)S(1)} %fusion.46), channel_id=1, source_target_pairs={{0,8},{2,10},{4,12},{6,14},{24,16},{26,18},{28,20},{30,22},{1,9},{... | collective-permute-start | bytes 4718600 | tf_op jit(solution)/shard_map/ppermute | solution.py:111
  694.7 35.4 %collective-permute-start.101 = (bf16[1024,768]{1,0:T(8,128)(2,1)S(1)}, bf16[1024,768]{1,0:T(8,128)(2,1)S(1)}, u32[]{:S(2)}, u32[]{:S(2)}) collective-permute-start(bf16[1024,768]{1,0:T(8,128)(2,1)S(1)} %fusion.44), channel_id=1, source_target_pairs={{0,1},{1,0},{2,3},{3,2},{4,5},{5,4},{6,7},{7,6},{8,9},{9,8},{10,11... | collective-permute-start | bytes 4718600 | tf_op jit(solution)/shard_map/ppermute | solution.py:179
  698.5 21.3 %collective-permute-start.23 = (bf16[288,768]{1,0:T(8,128)(2,1)S(1)}, bf16[288,768]{1,0:T(8,128)(2,1)S(1)}, u32[]{:S(2)}, u32[]{:S(2)}) collective-permute-start(bf16[288,768]{1,0:T(8,128)(2,1)S(1)} %get-tuple-element.94), channel_id=1, source_target_pairs={{0,4},{2,6},{4,0},{6,2},{8,12},{10,14},{12,8},{14,10},{16,20},{18,... | collective-permute-start | bytes 1327112 | tf_op jit(solution)/shard_map/ppermute | solution.py:114
  698.8 21.4 %collective-permute-start.24 = (bf16[288,768]{1,0:T(8,128)(2,1)S(1)}, bf16[288,768]{1,0:T(8,128)(2,1)S(1)}, u32[]{:S(2)}, u32[]{:S(2)}) collective-permute-start(bf16[288,768]{1,0:T(8,128)(2,1)S(1)} %get-tuple-element.93), channel_id=1, source_target_pairs={{0,6},{2,4},{4,2},{6,0},{8,14},{10,12},{12,10},{14,8},{16,22},{18,... | collective-permute-start | bytes 1327112 | tf_op jit(solution)/shard_map/ppermute | solution.py:114
  719.8 127.1 %collective-permute-start.9 = (bf16[288,768]{1,0:T(8,128)(2,1)}, bf16[288,768]{1,0:T(8,128)(2,1)}, u32[]{:S(2)}, u32[]{:S(2)}) collective-permute-start(bf16[288,768]{1,0:T(8,128)(2,1)} %get-tuple-element.91), channel_id=1, source_target_pairs={{0,2},{2,0},{4,6},{6,4},{8,10},{10,8},{12,14},{14,12},{16,18},{18,... | collective-permute-start | bytes 1327112 | tf_op jit(solution)/shard_map/ppermute | solution.py:114
  720.2 126.7 %collective-permute-start.10 = (bf16[288,768]{1,0:T(8,128)(2,1)}, bf16[288,768]{1,0:T(8,128)(2,1)}, u32[]{:S(2)}, u32[]{:S(2)}) collective-permute-start(bf16[288,768]{1,0:T(8,128)(2,1)} %get-tuple-element.90), channel_id=1, source_target_pairs={{0,4},{2,6},{4,0},{6,2},{8,12},{10,14},{12,8},{14,10},{16,20},{18,... | collective-permute-start | bytes 1327112 | tf_op jit(solution)/shard_map/ppermute | solution.py:114
  721.5 126.8 %collective-permute-start.11 = (bf16[288,768]{1,0:T(8,128)(2,1)}, bf16[288,768]{1,0:T(8,128)(2,1)}, u32[]{:S(2)}, u32[]{:S(2)}) collective-permute-start(bf16[288,768]{1,0:T(8,128)(2,1)} %get-tuple-element.89), channel_id=1, source_target_pairs={{0,6},{2,4},{4,2},{6,0},{8,14},{10,12},{12,10},{14,8},{16,22},{18,... | collective-permute-start | bytes 1327112 | tf_op jit(solution)/shard_map/ppermute | solution.py:114
  726.1 122.3 %collective-permute-start.55 = (bf16[1024,768]{1,0:T(8,128)(2,1)}, bf16[1024,768]{1,0:T(8,128)(2,1)}, u32[]{:S(2)}, u32[]{:S(2)}) collective-permute-start(bf16[1024,768]{1,0:T(8,128)(2,1)} %fusion.47), channel_id=1, source_target_pairs={{0,8},{2,10},{4,12},{6,14},{8,0},{10,2},{12,4},{14,6},{16,24},{18,... | collective-permute-start | bytes 4718600 | tf_op jit(solution)/shard_map/ppermute | solution.py:111
  730.1 118.3 %collective-permute-start.57 = (bf16[1024,768]{1,0:T(8,128)(2,1)}, bf16[1024,768]{1,0:T(8,128)(2,1)}, u32[]{:S(2)}, u32[]{:S(2)}) collective-permute-start(bf16[1024,768]{1,0:T(8,128)(2,1)} %fusion.45), channel_id=1, source_target_pairs={{8,16},{10,18},{12,20},{14,22},{16,8},{18,10},{20,12},{22,14},{9,1... | collective-permute-start | bytes 4718600 | tf_op jit(solution)/shard_map/ppermute | solution.py:111
  846.9 25.9 %collective-permute-start.118 = (bf16[8,96,768]{2,1,0:T(8,128)(2,1)}, bf16[8,96,768]{2,1,0:T(8,128)(2,1)}, u32[]{:S(2)}, u32[]{:S(2)}) collective-permute-start(bf16[8,96,768]{2,1,0:T(8,128)(2,1)} %fusion.170), channel_id=1, source_target_pairs={{0,2},{2,0},{4,6},{6,4},{8,10},{10,8},{12,14},{14,12},{16,18},{18,... | collective-permute-start | bytes 3538952 | tf_op jit(solution)/shard_map/ppermute | solution.py:114
  846.9 60.8 %collective-permute-start.110 = (bf16[8,96,1024]{2,1,0:T(8,128)(2,1)}, bf16[8,96,1024]{2,1,0:T(8,128)(2,1)}, u32[]{:S(2)}, u32[]{:S(2)}) collective-permute-start(bf16[8,96,1024]{2,1,0:T(8,128)(2,1)} %fusion.145), channel_id=1, source_target_pairs={{0,2},{2,0},{4,6},{6,4},{8,10},{10,8},{12,14},{14,12},{16,18},{18,... | collective-permute-start | bytes 4718600 | tf_op jit(solution)/shard_map/ppermute | solution.py:114
  854.7 56.7 %collective-permute-start.58 = (bf16[1024,768]{1,0:T(8,128)(2,1)}, bf16[1024,768]{1,0:T(8,128)(2,1)}, u32[]{:S(2)}, u32[]{:S(2)}) collective-permute-start(bf16[1024,768]{1,0:T(8,128)(2,1)} %fusion.50), channel_id=1, source_target_pairs={{0,1},{1,0},{2,3},{3,2},{4,5},{5,4},{6,7},{7,6},{8,9},{9,8},{10,11... | collective-permute-start | bytes 4718600 | tf_op jit(solution)/shard_map/ppermute | solution.py:179
  866.7 152.9 %collective-permute-start.109 = (bf16[1024,1536]{1,0:T(8,128)(2,1)}, bf16[1024,1536]{1,0:T(8,128)(2,1)}, u32[]{:S(2)}, u32[]{:S(2)}) collective-permute-start(bf16[1024,1536]{1,0:T(8,128)(2,1)} %convolution_convert_fusion.1), channel_id=1, source_target_pairs={{0,1},{1,0},{2,3},{3,2},{4,5},{5,4},{6,7},{7,6},{8,9},{9,8},{10,11... | collective-permute-start | bytes 9437192 | tf_op jit(solution)/shard_map/ppermute | solution.py:179
  875.3 104.5 %collective-permute-start.119 = (bf16[4,96,768]{2,1,0:T(8,128)(2,1)}, bf16[4,96,768]{2,1,0:T(8,128)(2,1)}, u32[]{:S(2)}, u32[]{:S(2)}) collective-permute-start(bf16[4,96,768]{2,1,0:T(8,128)(2,1)} %fusion.182), channel_id=1, source_target_pairs={{0,4},{2,6},{4,0},{6,2},{8,12},{10,14},{12,8},{14,10},{16,20},{18,... | collective-permute-start | bytes 1769480 | tf_op jit(solution)/shard_map/ppermute | solution.py:114
  910.9 72.0 %collective-permute-start.111 = (bf16[4,96,1024]{2,1,0:T(8,128)(2,1)S(1)}, bf16[4,96,1024]{2,1,0:T(8,128)(2,1)}, u32[]{:S(2)}, u32[]{:S(2)}) collective-permute-start(bf16[4,96,1024]{2,1,0:T(8,128)(2,1)S(1)} %fusion.181), channel_id=1, source_target_pairs={{0,4},{2,6},{4,0},{6,2},{8,12},{10,14},{12,8},{14,10},{16,20},{18,... | collective-permute-start | bytes 2359304 | tf_op jit(solution)/shard_map/ppermute | solution.py:114
  (219 other events, 2247.9 us)
Sparse Core Ops, SparseCore 0:
  858.9 117.8 reduce-scatter.3

commit v2 on v0

v2 whole, which is shorter than its diff:
```python
import functools
import math

import jax
import jax.numpy as jnp
import numpy as np
from jax import lax
from jax.experimental import pallas as pl
from jax.experimental.pallas import tpu as pltpu
from jax.sharding import PartitionSpec as P

epsilon = 1e-06
rope_base = 1000000.0
masked_score = -1e30


def contract_rows(left, right):
    return lax.dot_general(
        left, right, (((0,), (0,)), ((), ())), preferred_element_type=jnp.float32
    )


def times_transposed(left, right):
    return lax.dot_general(
        left, right, (((1,), (1,)), ((), ())), preferred_element_type=jnp.float32
    )


def line_depth(count):
    depth = 1
    while depth * depth * 4 <= count:
        depth *= 2
    return depth


VMEM_LIMIT = 56 * 1024 * 1024


def kernel_params(*semantics):
    return pltpu.CompilerParams(vmem_limit_bytes=VMEM_LIMIT)


def lasting(microseconds):
    return pl.CostEstimate(
        flops=int(microseconds * 1.0e9), bytes_accessed=1024, transcendentals=0
    )


def whole(array):
    return pl.BlockSpec(array.shape, lambda *_: (0,) * array.ndim)


def anywhere(arrays):
    return [pl.BlockSpec(memory_space=pl.ANY)] * len(arrays)


SCALAR = pl.BlockSpec(memory_space=pltpu.SMEM)


def dot(left, right, left_axis=1, right_axis=0):
    return lax.dot_general(
        left,
        right,
        (((left_axis,), (right_axis,)), ((), ())),
        preferred_element_type=jnp.float32,
    )


def rope_constants(seq_length, head_width):
    half = head_width // 2
    frequency = np.exp(-math.log(rope_base) * np.arange(half) * (2.0 / head_width))
    angle = np.arange(seq_length)[:, None] * frequency[None, :]
    cosine, sine = np.cos(angle), np.sin(angle)
    return (
        np.concatenate([cosine, cosine], axis=1).astype(np.float32),
        np.concatenate([-sine, sine], axis=1).astype(np.float32),
    )


def place_kernel(seq_length, capacity, keys_ref, out_ref):
    block = keys_ref[...]
    columns = block.T
    limit = seq_length * 1024
    for row in range(block.shape[0]):
        mine = block[row : row + 1, :]
        total = jnp.zeros((1, seq_length), jnp.float32)
        for start in range(0, seq_length, 256):
            less = columns[start : start + 256, row : row + 1] < mine
            total = total + jnp.sum(jnp.where(less, 1.0, 0.0), axis=0, keepdims=True)
        kept = (mine < limit) & (total < capacity)
        out_ref[row : row + 1, :] = jnp.where(kept, total, -1.0).astype(jnp.int32)


def place_table(routes, order, me, expert_count, capacity):
    seq_length = routes.shape[0]
    relabeled = (routes ^ me).T
    ranks = order.reshape(routes.shape).T
    labels = jnp.arange(expert_count, dtype=jnp.int32)
    hit = relabeled[:, None, :] == labels[None, :, None]
    rank = jnp.sum(jnp.where(hit, ranks[:, None, :] + 1, 0), axis=0)
    rank = jnp.where(rank > 0, rank, seq_length * 1024)
    spec = pl.BlockSpec((8, seq_length), lambda e: (e, 0))
    return pl.pallas_call(
        functools.partial(place_kernel, seq_length, capacity),
        grid=(expert_count // 8,),
        out_shape=jax.ShapeDtypeStruct(rank.shape, jnp.int32),
        in_specs=[spec],
        out_specs=spec,
        compiler_params=kernel_params(),
        cost_estimate=lasting(9.0 * expert_count / 16),
    )(rank)


def turn(values, cosine, sine):
    return values * cosine + pltpu.roll(values, values.shape[1] // 2, 1) * sine


def project_kernel(
    heads, x_ref, gain_ref, wq_ref, wk_ref, wv_ref, cos_ref, sin_ref, in_ref, q_ref, k_ref, v_ref, inv_ref
):
    source = x_ref[...].astype(jnp.float32)
    inverse = lax.rsqrt(jnp.mean(source * source, axis=1, keepdims=True) + epsilon)
    first = (source * inverse * gain_ref[...]).astype(jnp.bfloat16)
    in_ref[...] = first
    inv_ref[...] = inverse
    cosine, sine = cos_ref[...], sin_ref[...]
    size = cosine.shape[1]
    query = dot(first, wq_ref[...])
    for head in range(heads):
        span = slice(head * size, (head + 1) * size)
        q_ref[:, span] = turn(query[:, span], cosine, sine).astype(jnp.bfloat16)
    k_ref[...] = turn(dot(first, wk_ref[...]), cosine, sine).astype(jnp.bfloat16)
    v_ref[...] = dot(first, wv_ref[...]).astype(jnp.bfloat16)


def project(tokens, gain, w_query, w_key, w_value, cosine, sine, tile):
    length, model = tokens.shape
    size = w_key.shape[1]
    span = w_query.shape[1]

    def rows(columns):
        return pl.BlockSpec((tile, columns), lambda i: (i, 0))

    def shape(columns, kind=jnp.bfloat16):
        return jax.ShapeDtypeStruct((length, columns), kind)

    return pl.pallas_call(
        functools.partial(project_kernel, span // size),
        grid=(length // tile,),
        in_specs=[
            rows(model),
            whole(gain),
            whole(w_query),
            whole(w_key),
            whole(w_value),
            rows(size),
            rows(size),
        ],
        out_specs=[rows(model), rows(span), rows(size), rows(size), rows(1)],
        out_shape=[shape(model), shape(span), shape(size), shape(size), shape(1, jnp.float32)],
        compiler_params=kernel_params(),
        cost_estimate=lasting(9.0),
    )(tokens, gain, w_query, w_key, w_value, cosine, sine)


def attend_kernel(
    heads, scale, q_ref, k_ref, v_ref, segq_ref, segk_ref, wo_ref, mix_ref, lse_ref, branch_ref
):
    allowed = segk_ref[...] <= segq_ref[...]
    keys = k_ref[...]
    values = v_ref[...].T
    size = keys.shape[1]
    for head in range(heads):
        span = slice(head * size, (head + 1) * size)
        scores = dot(keys, q_ref[:, span], 1, 1)
        scores = jnp.where(allowed, scores * scale, masked_score)
        top = jnp.max(scores, axis=0, keepdims=True)
        spread = jnp.exp(scores - top)
        total = jnp.sum(spread, axis=0, keepdims=True)
        mixed = dot(values, spread.astype(jnp.bfloat16)) / total
        mix_ref[:, span] = mixed.T.astype(jnp.bfloat16)
        lse_ref[head : head + 1, :] = top + jnp.log(total)
    branch_ref[...] = dot(mix_ref[...], wo_ref[...]).astype(jnp.bfloat16)


def attend(query, keys, values, seg_row, seg_col, w_out, scale, tile):
    length, span = query.shape
    size = keys.shape[1]
    heads = span // size
    model = w_out.shape[1]
    rows = pl.BlockSpec((tile, span), lambda i: (i, 0))
    return pl.pallas_call(
        functools.partial(attend_kernel, heads, scale),
        grid=(length // tile,),
        in_specs=[
            rows,
            whole(keys),
            whole(values),
            pl.BlockSpec((1, tile), lambda i: (0, i)),
            whole(seg_col),
            whole(w_out),
        ],
        out_specs=[
            rows,
            pl.BlockSpec((heads, tile), lambda i: (0, i)),
            pl.BlockSpec((tile, model), lambda i: (i, 0)),
        ],
        out_shape=[
            jax.ShapeDtypeStruct((length, span), jnp.bfloat16),
            jax.ShapeDtypeStruct((heads, length), jnp.float32),
            jax.ShapeDtypeStruct((length, model), jnp.bfloat16),
        ],
        compiler_params=kernel_params(),
        cost_estimate=lasting(20.0),
    )(query, keys, values, seg_row, seg_col, w_out)


def second_kernel(
    side_ref, x_ref, a_ref, b_ref, gain_ref, router_ref, routes_ref, *refs
):
    hidden_ref, in_ref, half_ref, inv_ref, gate_ref = refs[-5:]
    hidden = x_ref[...].astype(jnp.float32) + (
        a_ref[...].astype(jnp.float32) + b_ref[...].astype(jnp.float32)
    )
    inverse = lax.rsqrt(jnp.mean(hidden * hidden, axis=1, keepdims=True) + epsilon)
    second = (hidden * inverse * gain_ref[...]).astype(jnp.bfloat16)
    hidden_ref[...] = hidden
    in_ref[...] = second
    inv_ref[...] = inverse
    half = half_ref.shape[1]
    half_ref[...] = jnp.where(side_ref[0] == 0, second[:, :half], second[:, half:])
    logits = dot(second, router_ref[...])
    gate_ref[...] = routed_softmax(logits, routes_ref[...])


def routed_softmax(logits, routes):
    labels = lax.broadcasted_iota(jnp.int32, logits.shape, 1)
    picked = routes[:, 0:1] == labels
    for k in range(1, routes.shape[1]):
        picked = picked | (routes[:, k : k + 1] == labels)
    masked = jnp.where(picked, logits, masked_score)
    spread = jnp.exp(masked - jnp.max(masked, axis=1, keepdims=True))
    return spread / jnp.sum(spread, axis=1, keepdims=True)


def second_norm(side, tokens, mine, other, gain, router, routes, tile, earlier):
    length, model = tokens.shape
    count = router.shape[1]

    def rows(columns):
        return pl.BlockSpec((tile, columns), lambda i: (i, 0))

    def shape(columns, kind=jnp.float32):
        return jax.ShapeDtypeStruct((length, columns), kind)

    return pl.pallas_call(
        second_kernel,
        grid=(length // tile,),
        in_specs=[
            SCALAR,
            rows(model),
            rows(model),
            rows(model),
            whole(gain),
            whole(router),
            rows(routes.shape[1]),
        ]
        + anywhere(earlier),
        out_specs=[rows(model), rows(model), rows(model // 2), rows(1), rows(count)],
        out_shape=[
            shape(model),
            shape(model, jnp.bfloat16),
            shape(model // 2, jnp.bfloat16),
            shape(1),
            shape(count),
        ],
        compiler_params=kernel_params(),
        cost_estimate=lasting(9.0),
    )(side, tokens, mine, other, gain, router, routes, *earlier)


def chosen_slots(place_row, capacity):
    slot = lax.broadcasted_iota(jnp.int32, (capacity, place_row.shape[1]), 0)
    return jnp.where(place_row == slot, 1.0, 0.0).astype(jnp.bfloat16)


def pick_kernel(width, capacity, outputs, line_ref, tab_ref, slot_ref, *refs):
    outs = refs[len(refs) - outputs :]
    chosen = jnp.concatenate([chosen_slots(tab_ref[0, b], capacity) for b in range(width)])

    def give(rows, targets):
        for b in range(width):
            targets[b][0] = rows[b * capacity : (b + 1) * capacity].astype(jnp.bfloat16)

    give(dot(chosen, slot_ref[0]), outs[:width])
    if len(outs) > width:
        give(dot(chosen, refs[0][0]), outs[width:])


def pick_rows(line, tables, slots, capacity, small=None, earlier=()):
    count, width, _, length = tables.shape
    columns = slots.shape[2]
    if capacity % 16:
        slot = jnp.arange(capacity, dtype=jnp.int32)
        chosen = low(tables == slot[None, None, :, None])

        def taken(rows):
            picked = jnp.einsum("gbst,gtd->bgsd", chosen, rows, preferred_element_type=jnp.float32)
            return [low(picked[b]) for b in range(width)]

        near = slots[jnp.arange(count, dtype=jnp.int32) ^ line[0]]
        return taken(near) + ([] if small is None else taken(small))
    in_specs = [
        pl.BlockSpec((1, width, 1, length), lambda g, line: (g, 0, 0, 0)),
        pl.BlockSpec((1, length, columns), lambda g, line: (g ^ line[0], 0, 0)),
    ]
    out_specs = [pl.BlockSpec((1, capacity, columns), lambda g, line: (g, 0, 0))] * width
    out_shape = [jax.ShapeDtypeStruct((count, capacity, columns), jnp.bfloat16)] * width
    operands = [tables, slots]
    if small is not None:
        picks = small.shape[2]
        in_specs.append(pl.BlockSpec((1, length, picks), lambda g, line: (g, 0, 0)))
        out_specs += [pl.BlockSpec((1, capacity, picks), lambda g, line: (g, 0, 0))] * width
        out_shape += [jax.ShapeDtypeStruct((count, capacity, picks), jnp.bfloat16)] * width
        operands.append(small)
    return pl.pallas_call(
        functools.partial(pick_kernel, width, capacity, len(out_shape)),
        grid_spec=pltpu.PrefetchScalarGridSpec(
            num_scalar_prefetch=1,
            grid=(count,),
            in_specs=in_specs + anywhere(earlier),
            out_specs=out_specs,
        ),
        out_shape=out_shape,
        compiler_params=kernel_params(),
        cost_estimate=lasting(3.0 * count * columns / 768),
    )(line, *operands, *earlier)


def combine_kernel(width, capacity, line_ref, tab_ref, *refs):
    out_ref = refs[-1]
    places = tab_ref[0]
    slot = lax.broadcasted_iota(jnp.int32, (places.shape[0], capacity), 1)
    total = None
    for b in range(width):
        chosen = jnp.where(places[:, b : b + 1] == slot, 1.0, 0.0).astype(jnp.bfloat16)
        part = dot(chosen, refs[b][0])
        total = part if total is None else total + part
    out_ref[0] = total.astype(out_ref.dtype)


def combine(line, table_columns, came, earlier=()):
    count, length, width = table_columns.shape
    _, capacity, columns = came[0].shape
    if capacity % 16:
        slot = jnp.arange(capacity, dtype=jnp.int32)
        chosen = low(table_columns[:, :, :, None] == slot)
        rows = jnp.stack(came)
        total = jnp.einsum("gtbs,bgsd->gtd", chosen, rows, preferred_element_type=jnp.float32)
        return low(total[jnp.arange(count, dtype=jnp.int32) ^ line[0]])
    return pl.pallas_call(
        functools.partial(combine_kernel, width, capacity),
        grid_spec=pltpu.PrefetchScalarGridSpec(
            num_scalar_prefetch=1,
            grid=(count,),
            in_specs=[pl.BlockSpec((1, length, width), lambda g, line: (g, 0, 0))]
            + [pl.BlockSpec((1, capacity, columns), lambda g, line: (g, 0, 0))] * width
            + anywhere(earlier),
            out_specs=pl.BlockSpec((1, length, columns), lambda g, line: (g ^ line[0], 0, 0)),
        ),
        out_shape=jax.ShapeDtypeStruct((count, length, columns), jnp.bfloat16),
        compiler_params=kernel_params(),
        cost_estimate=lasting(4.0 * count * columns / 768),
    )(line, table_columns, *came, *earlier)


def expert_kernel(chunks, width, me_ref, *refs):
    x_refs = refs[: 2 * chunks]
    cm_ref, co_ref, route_ref, wg_ref, wu_ref, wd_ref, wr_ref, *outs = refs[2 * chunks :]
    pre_ref, act_ref, term_ref = outs[:3]
    aways = outs[3 : 3 + chunks]
    homes = outs[3 + chunks :]
    side = me_ref[1]
    batch, _, capacity, half = cm_ref.shape
    chunk = half // chunks

    def flat(ref):
        return ref[...].reshape(batch * capacity, ref.shape[3])

    def keep(ref, rows):
        ref[...] = rows.reshape(ref.shape).astype(ref.dtype)

    def columns(which, part, size):
        start = which * half + part * size
        return pl.ds(pl.multiple_of(start, size), size)

    mine, other = columns(side, 0, half), columns(1 - side, 0, half)
    spans = [columns(side, c, chunk) for c in range(chunks)]
    spans += [columns(1 - side, c, chunk) for c in range(chunks)]
    pieces = [flat(ref) for ref in x_refs]

    def through(weight_ref):
        total = None
        for piece, at in zip(pieces, spans):
            part = dot(piece, weight_ref[at, :])
            total = part if total is None else total + part
        return total

    gate_pre, up_pre, logits = through(wg_ref), through(wu_ref), through(wr_ref)
    raw = dot(flat(cm_ref), wd_ref[:, mine], 1, 1) + dot(flat(co_ref), wd_ref[:, other], 1, 1)
    chance = routed_softmax(logits, flat(route_ref).astype(jnp.float32).astype(jnp.int32))
    label = lax.broadcasted_iota(jnp.int32, chance.shape, 1)
    gate = jnp.sum(jnp.where(label == me_ref[0], chance, 0.0), axis=1, keepdims=True)
    sig = jax.nn.sigmoid(gate_pre)
    silu = gate_pre * sig
    act = silu * up_pre
    keep(term_ref, jnp.sum(act * raw, axis=1, keepdims=True))
    keep(act_ref, act * gate)
    d_act = raw * gate
    units = act.shape[1]
    d_gate = (d_act * up_pre * sig * (1.0 + gate_pre * (1.0 - sig))).astype(jnp.bfloat16)
    d_up = (d_act * silu).astype(jnp.bfloat16)
    pre_ref[:, :, :, :units] = d_gate.reshape(batch, 1, capacity, units)
    pre_ref[:, :, :, units:] = d_up.reshape(batch, 1, capacity, units)
    for c in range(chunks):
        at = spans[chunks + c]
        keep(aways[c], dot(d_gate, wg_ref[at, :], 1, 1) + dot(d_up, wu_ref[at, :], 1, 1))
        at = spans[c]
        home = dot(d_gate, wg_ref[at, :], 1, 1) + dot(d_up, wu_ref[at, :], 1, 1)
        home = home.astype(jnp.bfloat16).reshape(batch, capacity, chunk)
        give_homes(home, homes[c * width : (c + 1) * width])


def give_homes(rows, homes):
    batch = rows.shape[0]
    for b in range(len(homes)):

        @pl.when(pl.program_id(0) == b // batch)
        def _(b=b):
            homes[b][0] = rows[b % batch]


def block_batch(width, capacity):
    return 1 if capacity % 16 else min(2, width)


def home_specs(width, batch, count, capacity, columns):
    return [
        pl.BlockSpec((1, capacity, columns), functools.partial(home_block, k // batch, count))
        for k in range(width)
    ]


def expert_rows(me, pieces, c_mine, c_other, routes, w_gate, w_up, w_down, router):
    chunks = len(pieces) // 2
    width, count, capacity, chunk = pieces[0].shape
    half = c_mine.shape[3]
    units = w_gate.shape[1]
    batch = block_batch(width, capacity)

    def rows(columns):
        return pl.BlockSpec((batch, 1, capacity, columns), lambda b, g: (b, g, 0, 0))

    def shape(columns, kind=jnp.bfloat16):
        return jax.ShapeDtypeStruct((width, count, capacity, columns), kind)

    outs = pl.pallas_call(
        functools.partial(expert_kernel, chunks, width),
        grid=(width // batch, count),
        in_specs=[SCALAR]
        + [rows(chunk)] * (2 * chunks)
        + [
            rows(half),
            rows(half),
            rows(routes.shape[3]),
            whole(w_gate),
            whole(w_up),
            whole(w_down),
            whole(router),
        ],
        out_specs=[rows(2 * units), rows(units), rows(1)]
        + [rows(chunk)] * chunks
        + home_specs(width, batch, count, capacity, chunk) * chunks,
        out_shape=[shape(2 * units), shape(units), shape(1, jnp.float32)]
        + [shape(chunk)] * chunks
        + [jax.ShapeDtypeStruct((count, capacity, chunk), jnp.bfloat16)] * (width * chunks),
        compiler_params=kernel_params(),
        cost_estimate=lasting(10.0 * count),
    )(me, *pieces, c_mine, c_other, routes, w_gate, w_up, w_down, router)
    aways, homes = outs[3 : 3 + chunks], outs[3 + chunks :]
    return (
        *outs[:3],
        [(aways[c], homes[c * width : (c + 1) * width]) for c in range(chunks)],
    )


def home_block(k, count, b, g):
    return (jnp.where(b < k, 0, jnp.where(b > k, count - 1, g)), 0, 0)


def down_kernel(width, me_ref, act_ref, wd_ref, *refs):
    outs = refs[-1 - width :]
    away_ref, homes = outs[0], outs[1:]
    side = me_ref[1]
    batch, _, capacity, half = away_ref.shape
    mine = pl.ds(pl.multiple_of(side * half, half), half)
    other = pl.ds(pl.multiple_of((1 - side) * half, half), half)
    act = act_ref[...].reshape(batch * capacity, act_ref.shape[3])
    away_ref[...] = low(dot(act, wd_ref[:, other])).reshape(away_ref.shape)
    give_homes(low(dot(act, wd_ref[:, mine])).reshape(batch, capacity, half), homes)


def down_rows(me, act, w_down, earlier):
    width, count, capacity, units = act.shape
    half = w_down.shape[1] // 2
    batch = block_batch(width, capacity)

    def rows(columns):
        return pl.BlockSpec((batch, 1, capacity, columns), lambda b, g: (b, g, 0, 0))

    return pl.pallas_call(
        functools.partial(down_kernel, width),
        grid=(width // batch, count),
        in_specs=[SCALAR, rows(units), whole(w_down)] + anywhere(earlier),
        out_specs=[rows(half)] + home_specs(width, batch, count, capacity, half),
        out_shape=[jax.ShapeDtypeStruct((width, count, capacity, half), jnp.bfloat16)]
        + [jax.ShapeDtypeStruct((count, capacity, half), jnp.bfloat16)] * width,
        compiler_params=kernel_params(),
        cost_estimate=lasting(3.0 * count),
    )(me, act, w_down, *earlier)


def attend_back_kernel(
    heads,
    scale,
    tile,
    q_ref,
    k_ref,
    v_ref,
    segq_ref,
    segk_ref,
    lse_ref,
    db_ref,
    wo_ref,
    cos_ref,
    sin_ref,
    *refs,
):
    out_ref, dk_ref, dv_ref = refs[-3:]
    step = pl.program_id(0)
    allowed = segk_ref[...] <= segq_ref[...]
    keys = k_ref[...]
    values = v_ref[...]
    size = keys.shape[1]
    here = pl.ds(pl.multiple_of(step * tile, tile), tile)
    cosine, sine = cos_ref[here, :], sin_ref[here, :]
    keys_t = keys.T
    d_mixed = dot(db_ref[...], wo_ref[...], 1, 1).astype(jnp.bfloat16)
    dk_total = jnp.zeros(keys.shape, jnp.float32)
    dv_total = jnp.zeros(keys.shape, jnp.float32)
    for head in range(heads):
        span = slice(head * size, (head + 1) * size)
        query = q_ref[:, span]
        d_head = d_mixed[:, span]
        scores = dot(keys, query, 1, 1) * scale - lse_ref[head : head + 1, :]
        probs = jnp.where(allowed, jnp.exp(scores), 0.0)
        d_probs = dot(values, d_head, 1, 1)
        scaled = probs * d_probs
        row_dot = jnp.sum(scaled, axis=0, keepdims=True)
        d_scores = (scale * (scaled - probs * row_dot)).astype(jnp.bfloat16)
        dv_total = dv_total + dot(probs.astype(jnp.bfloat16), d_head)
        dk_total = dk_total + dot(d_scores, query)
        d_query = dot(keys_t, d_scores).T
        out_ref[here, span] = turn(d_query, cosine, -sine).astype(jnp.bfloat16)

    @pl.when(step == 0)
    def _():
        dk_ref[...] = dk_total
        dv_ref[...] = dv_total

    @pl.when(step > 0)
    def _():
        dk_ref[...] += dk_total
        dv_ref[...] += dv_total

    @pl.when(step == pl.num_programs(0) - 1)
    def _():
        base = heads * size
        turned = turn(dk_ref[...], cos_ref[...], -sin_ref[...])
        out_ref[:, base : base + size] = turned.astype(jnp.bfloat16)
        out_ref[:, base + size : base + 2 * size] = dv_ref[...].astype(jnp.bfloat16)


def attend_back(
    query, keys, values, seg_row, seg_col, lse, d_branch, w_out, cosine, sine, scale, tile, earlier
):
    length, span = query.shape
    size = keys.shape[1]
    heads = span // size
    model = w_out.shape[1]
    out = jax.ShapeDtypeStruct((length, span + 2 * size), jnp.bfloat16)
    return pl.pallas_call(
        functools.partial(attend_back_kernel, heads, scale, tile),
        grid=(length // tile,),
        in_specs=[
            pl.BlockSpec((tile, span), lambda i: (i, 0)),
            whole(keys),
            whole(values),
            pl.BlockSpec((1, tile), lambda i: (0, i)),
            whole(seg_col),
            pl.BlockSpec((heads, tile), lambda i: (0, i)),
            pl.BlockSpec((tile, model), lambda i: (i, 0)),
            whole(w_out),
            whole(cosine),
            whole(sine),
        ]
        + anywhere(earlier),
        out_specs=whole(out),
        out_shape=out,
        scratch_shapes=[pltpu.VMEM((length, size), jnp.float32)] * 2,
        compiler_params=kernel_params(),
        cost_estimate=lasting(28.0),
    )(query, keys, values, seg_row, seg_col, lse, d_branch, w_out, cosine, sine, *earlier)


def first_grad_kernel(d_ref, wq_ref, wk_ref, wv_ref, *refs):
    out_ref = refs[-1]
    span, size = wq_ref.shape[1], wk_ref.shape[1]
    total = dot(d_ref[:, :span], wq_ref[...], 1, 1)
    total = total + dot(d_ref[:, span : span + size], wk_ref[...], 1, 1)
    total = total + dot(d_ref[:, span + size :], wv_ref[...], 1, 1)
    out_ref[...] = total.astype(jnp.bfloat16)


def first_grad(d_all, w_query, w_key, w_value, tile, earlier):
    length, columns = d_all.shape
    model = w_query.shape[0]
    return pl.pallas_call(
        first_grad_kernel,
        grid=(length // tile,),
        in_specs=[
            pl.BlockSpec((tile, columns), lambda i: (i, 0)),
            whole(w_query),
            whole(w_key),
            whole(w_value),
        ]
        + anywhere(earlier),
        out_specs=pl.BlockSpec((tile, model), lambda i: (i, 0)),
        out_shape=jax.ShapeDtypeStruct((length, model), jnp.bfloat16),
        compiler_params=kernel_params(),
        cost_estimate=lasting(8.0),
    )(d_all, w_query, w_key, w_value, *earlier)


class Exchange:
    def __init__(self, count):
        self.count = count
        self.depth = line_depth(count)
        self.width = count // self.depth
        self.me = lax.axis_index("expert")
        self.line = self.me // self.width
        self.lines = [[l * self.width + s for l in range(self.depth)] for s in range(self.width)]

    def flip(self, rows, mask):
        return lax.ppermute(rows, "expert", [(d, d ^ mask) for d in range(self.count)])

    def spread(self, rows):
        return lax.all_gather(rows, "expert", axis_index_groups=self.lines)

    def collect(self, parts):
        flat = parts.reshape(-1, parts.shape[-1])
        return lax.psum_scatter(
            flat, "expert", scatter_dimension=0, axis_index_groups=self.lines, tiled=True
        )

    def plane(self, blocks):
        return [blocks[0]] + [self.flip(blocks[b], b) for b in range(1, self.width)]

    def scatter_sum(self, grads):
        rows = grads.shape[0] // self.count
        held = grads.reshape(self.count, rows, grads.shape[1])
        blocks, bit = self.count, 1
        while bit < self.width:
            parted = held.reshape(blocks // 2, 2, rows, -1)
            side = (self.me // bit) % 2
            kept = lax.dynamic_index_in_dim(parted, side, 1, keepdims=False)
            gone = lax.dynamic_index_in_dim(parted, 1 - side, 1, keepdims=False)
            came = self.flip(gone.astype(jnp.bfloat16), bit)
            held = kept.astype(jnp.float32) + came.astype(jnp.float32)
            blocks, bit = blocks // 2, bit * 2
        total = lax.dynamic_index_in_dim(held, self.line, 0, keepdims=False)
        for g in range(1, self.depth):
            part = lax.dynamic_index_in_dim(held, self.line ^ g, 0, keepdims=False)
            total = total + wide(self.flip(low(part), g * self.width))
        return total


def low(array):
    return array.astype(jnp.bfloat16)


def wide(array):
    return array.astype(jnp.float32)


def swap(rows):
    return lax.ppermute(rows, "tensor", [(0, 1), (1, 0)])


def half_of(array, side):
    width = array.shape[-1] // 2
    return lax.dynamic_slice_in_dim(array, side * width, width, array.ndim - 1)


def join_halves(mine, other, side):
    first = jnp.where(side == 0, mine, other)
    last = jnp.where(side == 0, other, mine)
    return jnp.concatenate([first, last], axis=-1)


def on_device(
    tokens,
    cotangent,
    norm_gain,
    ffn_gain,
    w_query,
    w_key,
    w_value,
    w_out,
    w_router,
    w_gate,
    w_up,
    w_down,
    routes,
    order,
    segments,
):
    seq_length, model_width = tokens.shape
    half_width = model_width // 2
    expert_count = w_router.shape[1]
    pick_count = routes.shape[1]
    capacity = 9 * seq_length * pick_count // (8 * expert_count)
    head_width = w_key.shape[1]
    span = w_query.shape[1]
    unit_count = w_down.shape[1]
    score_scale = 1.0 / math.sqrt(head_width)
    tile = 256
    link = Exchange(expert_count)
    depth, width = link.depth, link.width
    chunks = 2
    chunk_width = half_width // chunks
    side = lax.axis_index("tensor")
    side_ref = side.astype(jnp.int32)[None]
    me_ref = jnp.stack([link.me, side]).astype(jnp.int32)
    line_ref = link.line.astype(jnp.int32)[None]

    cot_slots = link.spread(half_of(cotangent, side))
    placed = place_table(routes, order[0], link.me, expert_count, capacity)
    tables = []
    for g in range(depth):
        table = jnp.concatenate([placed[g * width : (g + 1) * width], routes.T], axis=0)
        tables.append(table if g == 0 else link.flip(table, g * width))
    places = jnp.stack([table[:width] for table in tables])
    place_rows = places[:, :, None, :]
    place_columns = jnp.stack([table[:width].T for table in tables])
    route_columns = jnp.stack([low(table[width:].T) for table in tables])

    cosine, sine = (jnp.asarray(t) for t in rope_constants(seq_length, head_width))
    first_in, query, keys, values, inverse_first = project(
        tokens, norm_gain[None], w_query, w_key, w_value, cosine, sine, tile
    )
    seg_row, seg_col = segments, segments[0][:, None]
    mixed, lse, branch = attend(
        query, keys, values, seg_row, seg_col, w_out, score_scale, tile
    )
    hidden, second_in, in_half, inverse_second, gates = second_norm(
        side_ref,
        tokens,
        branch,
        swap(branch),
        ffn_gain[None],
        w_router,
        routes,
        tile,
        (),
    )

    def to_expert(blocks):
        mine = jnp.stack(link.plane(blocks))
        return mine, swap(mine)

    in_slots = [
        link.spread(in_half[:, c * chunk_width : (c + 1) * chunk_width]) for c in range(chunks)
    ]
    picked = pick_rows(line_ref, place_rows, cot_slots, capacity, route_columns, (in_half,))
    cot_mine, cot_other = to_expert(picked[:width])
    route_rows = jnp.stack(link.plane(picked[width:]))
    in_rows = [
        to_expert(pick_rows(line_ref, place_rows, slots, capacity)) for slots in in_slots
    ]
    pieces = [rows[0] for rows in in_rows] + [rows[1] for rows in in_rows]

    pre, acts, terms, backs = expert_rows(
        me_ref, pieces, cot_mine, cot_other, route_rows, w_gate[0], w_up[0], w_down[0], w_router
    )
    terms = terms[..., 0]

    def to_token(away, homes):
        swapped = swap(away)
        return link.plane([low(wide(homes[b]) + wide(swapped[b])) for b in range(width)])

    came_back = [to_token(away, homes) for away, homes in backs]

    terms = jnp.stack(link.plane([terms[b] for b in range(width)]), axis=1)
    slot_ids = jnp.arange(capacity, dtype=jnp.int32)
    local = jnp.sum(
        jnp.where(
            places[:, :, None, :] == slot_ids[None, None, :, None], terms[:, :, :, None], 0.0
        ),
        axis=2,
    )
    term_table = jnp.concatenate(
        [local[g] if g == 0 else link.flip(local[g], g * width) for g in range(depth)]
    )
    term_table = term_table + swap(term_table)
    term_table = term_table[jnp.arange(expert_count, dtype=jnp.int32) ^ link.me].T

    row_half = jnp.concatenate(
        [link.collect(combine(line_ref, place_columns, came)) for came in came_back], axis=1
    )
    row_total = wide(join_halves(row_half, swap(row_half), side))

    arrived = [block for came in came_back for block in came]
    away, *homes = down_rows(me_ref, acts, w_down[0], arrived)
    out_came = to_token(away, homes)
    out_parts = combine(line_ref, place_columns, out_came, (row_half,))
    combined = wide(link.collect(out_parts))
    output_half = low(half_of(hidden, side) + combined)
    output = join_halves(output_half, swap(output_half), side)

    pre = pre.reshape(-1, 2 * unit_count)
    grads = [contract_rows(piece.reshape(-1, chunk_width), pre) for piece in pieces]
    first, second = grads[:chunks], grads[chunks:]
    joined = [jnp.where(side == 0, a, b) for a, b in zip(first + second, second + first)]
    gate_grad = jnp.concatenate([part[:, :unit_count] for part in joined])[None]
    up_grad = jnp.concatenate([part[:, unit_count:] for part in joined])[None]
    act_rows = acts.reshape(-1, unit_count)
    down_grad = join_halves(
        contract_rows(act_rows, cot_mine.reshape(-1, half_width)),
        contract_rows(act_rows, cot_other.reshape(-1, half_width)),
        side,
    )[None]

    upstream = wide(cotangent)
    normed_second = hidden * inverse_second
    d_logits = low(
        gates * (term_table - jnp.sum(gates * term_table, axis=-1, keepdims=True))
    )
    router_grad = contract_rows(second_in, d_logits)
    d_second = row_total + times_transposed(d_logits, w_router)
    scaled_second = d_second * ffn_gain
    ffn_gain_grad = jnp.sum(d_second * normed_second, axis=0)
    d_hidden = upstream + inverse_second * (
        scaled_second
        - normed_second * jnp.mean(scaled_second * normed_second, axis=-1, keepdims=True)
    )
    d_branch = low(d_hidden)
    pad = jnp.zeros((model_width, -(expert_count + 1) % 128), jnp.float32)
    early = jnp.concatenate(
        [contract_rows(d_branch, mixed), router_grad, ffn_gain_grad[:, None], pad], axis=1
    )
    early = link.scatter_sum(early)
    out_grad, small = early[:, :span].T, early[:, span:]

    d_all = attend_back(
        query,
        keys,
        values,
        seg_row,
        seg_col,
        lse,
        d_branch,
        w_out,
        cosine,
        sine,
        score_scale,
        tile,
        (out_parts,),
    )
    d_first = first_grad(d_all, w_query, w_key, w_value, tile, ())
    qkv_grad = link.scatter_sum(contract_rows(first_in, d_all))
    d_first = wide(d_first) + wide(swap(d_first))
    normed_first = wide(tokens) * inverse_first
    scaled_first = d_first * norm_gain
    input_grad = d_hidden + inverse_first * (
        scaled_first - normed_first * jnp.mean(scaled_first * normed_first, axis=-1, keepdims=True)
    )
    rows = model_width // expert_count
    gain_part = jnp.zeros((rows,), jnp.float32)
    start = 0
    for weight in (w_query, w_key, w_value):
        mine = lax.dynamic_slice_in_dim(weight, link.me * rows, rows, 0)
        grads = qkv_grad[:, start : start + weight.shape[1]]
        gain_part = gain_part + jnp.sum(grads * wide(mine), axis=1)
        start += weight.shape[1]
    gain_part = gain_part / lax.dynamic_slice_in_dim(norm_gain, link.me * rows, rows, 0)
    norm_gain_grad = gain_part + swap(gain_part)
    return (
        output,
        input_grad,
        norm_gain_grad,
        small[:, expert_count],
        qkv_grad[:, :span],
        qkv_grad[:, span : span + head_width],
        qkv_grad[:, span + head_width :],
        out_grad,
        small[:, :expert_count],
        gate_grad,
        up_grad,
        down_grad,
    )


def solution(mesh):
    placed = (
        P("expert", None),
        P("expert", None),
        P(),
        P(),
        P(None, "tensor"),
        P(None, "tensor"),
        P(None, "tensor"),
        P("tensor", None),
        P(),
        P("expert", None, "tensor"),
        P("expert", None, "tensor"),
        P("expert", "tensor", None),
        P("expert", None),
        P("expert", None),
        P("expert", None),
    )
    return jax.shard_map(
        on_device,
        mesh=mesh,
        in_specs=placed,
        out_specs=(
            P("expert", None),
            P("expert", None),
            P("expert"),
            P("expert"),
            P("expert", "tensor"),
            P("expert", "tensor"),
            P("expert", "tensor"),
            P("tensor", "expert"),
            P("expert", None),
            P("expert", None, "tensor"),
            P("expert", None, "tensor"),
            P("expert", "tensor", None),
        ),
        check_vma=False,
    )
```

time: 2550 us -> 853 us (0.33)
  waiting for transfers between devices: 1120 us -> 365 us
  blocking collectives: 712 us -> 0 us
  local copies, waits for them, and re-layouts: 327 us -> 42.4 us
  Pallas kernels: 0 us -> 227 us
  matrix products: 248 us -> 52.4 us
  starting transfers between devices: 13.5 us -> 64.9 us
    all_to_all x2 -> x0, blocking collectives: 643 us -> none  [the longest x1 330 us: on_device(): lax.all_to_all(grad_out, 'expert', split_axis=0, concat_axis=0, tiled=True)]
    all_to_all x2 -> x0, waiting for transfers between devices: 570 us -> none  [the longest x1 304 us: on_device(): lax.all_to_all(row_whole, 'expert', split_axis=0, concat_axis=0, tiled=True)]
    reduce_scatter x6 -> x3, waiting for transfers between devices: 487 us -> 4.54 us  [collect(): lax.psum_scatter(flat, 'expert', scatter_dimension=0, axis_index_groups=s...]
    ppermute x0 -> x52, waiting for transfers between devices: none -> 302 us  [the longest x40 293 us: flip(): lax.ppermute(rows, 'expert', [(d, d ^ mask) for d in range(self.count)])]
    pallas_call x0 -> x14, Pallas kernels: none -> 227 us  [the longest x1 57.6 us: expert_rows(): pl.pallas_call(functools.partial(expert_kernel, chunks, width), grid=(wid...]
    gather x13 -> x2, local copies, waits for them, and re-layouts: 222 us -> 0.9 us  [on_device(): term_table[jnp.arange(expert_count, dtype=jnp.int32) ^ link.me]]
    dot_general x14 -> x0, matrix products: 116 us -> none  [the longest x1 17.5 us: on_device(): jnp.einsum('qhd,kd->hqk', d_mixed, values, preferred_element_type=jnp.flo...]
    unnamed x1 -> x0, blocking collectives: 69.3 us -> none
  transfers between devices with their start and end apart: 13 -> 58, of which waited for: 10 -> 34; matrix products, arithmetic and copies ran while one was open for 15% -> 19% of each run, Pallas kernels for 0% -> 20%
where the time goes in v2:
time: 853 us; the launch traced here: 845 us
  waiting for transfers between devices  365 us (43%)
  Pallas kernels  227 us (27%)
  other arithmetic  77.1 us (9%)
  starting transfers between devices  64.9 us (8%)
  matrix products  52.4 us (6%)
  local copies, waits for them, and re-layouts  42.4 us (5%)
  between operations  15.7 us (2%)
    ppermute x40, waiting for transfers between devices, flip(): lax.ppermute(rows, 'expert', [(d, d ^ mask) for d in range(self.count)])  293 us
    all_gather x3, waiting for transfers between devices, spread(): return lax.all_gather(rows, 'expert', axis_index_groups=self.lines)  58 us
    pallas_call x1, Pallas kernels, expert_rows(): pl.pallas_call(functools.partial(expert_kernel, chunks, width), grid=(wid...  57.6 us
    dot_general x9, matrix products, contract_rows(): lax.dot_general(left, right, (((0,), (0,)), ((), ())), preferred_element_...  46.2 us
    ppermute x40, starting transfers between devices, flip(): lax.ppermute(rows, 'expert', [(d, d ^ mask) for d in range(self.count)])  42.1 us
    pallas_call x3, Pallas kernels, combine(): pl.pallas_call(functools.partial(combine_kernel, width, capacity), grid_s...  38.7 us
    pallas_call x1, Pallas kernels, attend_back(): pl.pallas_call(functools.partial(attend_back_kernel, heads, scale, tile),...  29.5 us
    pallas_call x3, Pallas kernels, pick_rows(): pl.pallas_call(functools.partial(pick_kernel, width, capacity, len(out_sh...  28.5 us
  transfers between devices with their start and end apart: 58, of which 34 were waited for; matrix products, arithmetic and copies ran while one was open for 19% of the time, Pallas kernels for 20%

profile of v2, /device:TPU:9, one launch (start us, length us, event | category | flops | bytes accessed | tf_op | source)
XLA Modules:
  0.0 844.7 jit_solution(12122609763088952923)
XLA Ops:
  11.7 9.0 %shard_map.256 = (bf16[1024,1536]{1,0:T(8,128)(2,1)}, bf16[1024,768]{1,0:T(8,128)(2,1)}, bf16[1024,128]{1,0:T(8,128)(2,1)}, bf16[1024,128]{1,0:T(8,128)(2,1)}, f32[1024,1]{1,0:T(8,128)}) custom-call(bf16[1024,1536]{1,0:T(8,128)(2,1)} %x_ref.3, f32[1,1536]{1,0:T(1,128)} %broadcast_in_dim.69.gain_ref, bf16[1536,768]{1,0:T(8,128)(2,1)} %wq_ref.3, ...), custom_call_target="tpu_custom_call" | custom-call | flops 8999999488 | bytes 1024 | tf_op jit(solution)/shard_map/pallas_call | solution.py:147
  20.7 24.1 %shard_map.257 = (bf16[1024,768]{1,0:T(8,128)(2,1)}, f32[6,1024]{1,0:T(8,128)}, bf16[1024,1536]{1,0:T(8,128)(2,1)}) custom-call(bf16[1024,768]{1,0:T(8,128)(2,1)} %get-tuple-element.59.q_ref, bf16[1024,128]{1,0:T(8,128)(2,1)} %get-tuple-element.60.k_ref, bf16[1024,128]{1,0:T(8,128)(2,1)} %get-tuple-element.61.v_ref, s32[1,1024]{1,0:T(1,128)} %segq_ref.3, ...), custom_call_target="tpu_custom_call" | custom-call | flops 20000000000 | bytes 1024 | tf_op jit(solution)/shard_map/pallas_call | solution.py:192
  48.1 3.1 collective-permute-done.b_ref
  51.2 9.8 %shard_map.258 = (f32[1024,1536]{1,0:T(8,128)}, bf16[1024,1536]{1,0:T(8,128)(2,1)}, bf16[1024,768]{1,0:T(8,128)(2,1)}, f32[1024,1]{1,0:T(8,128)}, f32[1024,16]{1,0:T(8,128)}) custom-call(s32[1]{0:T(128)} %bitcast.side_ref, bf16[1024,1536]{1,0:T(8,128)(2,1)} %x_ref.3, bf16[1024,1536]{1,0:T(8,128)(2,1)} %get-tuple-element.62.a_ref, ...), custom_call_target="tpu_custom_call" | custom-call | flops 8999999488 | bytes 1024 | tf_op jit(solution)/shard_map/pallas_call | solution.py:256
  65.5 8.9 %shard_map.259 = s32[16,1024]{1,0:T(8,128)} custom-call(s32[16,1024]{1,0:T(8,128)} %compare_select_fusion.keys_ref), custom_call_target="tpu_custom_call" | custom-call | flops 8999999488 | bytes 1024 | tf_op jit(solution)/shard_map/pallas_call | solution.py:103
  86.6 39.3 %all-gather.11.cloned.1.call-done = bf16[4096,768]{1,0:T(8,128)(2,1)} async-done(((bf16[1024,768]{1,0:T(8,128)(2,1)}), bf16[4096,768]{1,0:T(8,128)(2,1)}) %all-gather.11.cloned.1.call-update) | async-done | bytes 6291472 | tf_op jit(solution)/shard_map/all_gather | solution.py:668
  126.0 13.2 %shard_map.262 = (bf16[4,288,768]{2,1,0:T(8,128)(2,1)}, bf16[4,288,768]{2,1,0:T(8,128)(2,1)}, bf16[4,288,768]{2,1,0:T(8,128)(2,1)}, bf16[4,288,768]{2,1,0:T(8,12...) custom-call(s32[1]{0:T(128)} %bitcast.2.line_ref, ...), custom_call_target="tpu_custom_call" | custom-call | flops 12000000000 | bytes 1024 | tf_op jit(solution)/shard_map/pallas_call | solution.py:326
  141.9 37.2 %collective-permute-done.12 = bf16[4,288,768]{2,1,0:T(8,128)(2,1)S(1)} collective-permute-done((bf16[4,288,768]{2,1,0:T(8,128)(2,1)}, bf16[4,288,768]{2,1,0:T(8,128)(2,1)S(1)}, u32[]{:S(2)}, u32[]{:S(2)}) %collective-permute-start.12) | collective-permute-done | bytes 1769504 | tf_op jit(solution)/shard_map/ppermute | solution.py:665
  180.0 37.9 %collective-permute-done.14 = bf16[4,288,768]{2,1,0:T(8,128)(2,1)S(1)} collective-permute-done((bf16[4,288,768]{2,1,0:T(8,128)(2,1)}, bf16[4,288,768]{2,1,0:T(8,128)(2,1)S(1)}, u32[]{:S(2)}, u32[]{:S(2)}) %collective-permute-start.14) | collective-permute-done | bytes 1769504 | tf_op jit(solution)/shard_map/ppermute | solution.py:665
  217.9 5.4 pad_maximum_fusion.refs_4_
  225.1 7.7 shard_map.261
  235.4 18.6 %all-gather.7.cloned.1.call-done = bf16[4096,384]{1,0:T(8,128)(2,1)} async-done(((bf16[1024,384]{1,0:T(8,128)(2,1)}), bf16[4096,384]{1,0:T(8,128)(2,1)}) %all-gather.7.cloned.1.call-update) | async-done | bytes 3145744 | tf_op jit(solution)/shard_map/all_gather | solution.py:668
  254.1 7.6 shard_map.260
  264.4 9.8 %collective-permute-done.9 = bf16[4,288,384]{2,1,0:T(8,128)(2,1)S(1)} collective-permute-done((bf16[4,288,384]{2,1,0:T(8,128)(2,1)}, bf16[4,288,384]{2,1,0:T(8,128)(2,1)S(1)}, u32[]{:S(2)}, u32[]{:S(2)}) %collective-permute-start.9) | collective-permute-done | bytes 884768 | tf_op jit(solution)/shard_map/ppermute | solution.py:665
  275.1 2.9 collective-permute-start.11
  277.9 14.2 %collective-permute-done.4 = bf16[4,288,384]{2,1,0:T(8,128)(2,1)S(1)} collective-permute-done((bf16[4,288,384]{2,1,0:T(8,128)(2,1)}, bf16[4,288,384]{2,1,0:T(8,128)(2,1)S(1)}, u32[]{:S(2)}, u32[]{:S(2)}) %collective-permute-start.4) | collective-permute-done | bytes 884768 | tf_op jit(solution)/shard_map/ppermute | solution.py:665
  293.9 18.1 %collective-permute-done.6 = bf16[4,288,384]{2,1,0:T(8,128)(2,1)S(1)} collective-permute-done((bf16[4,288,384]{2,1,0:T(8,128)(2,1)}, bf16[4,288,384]{2,1,0:T(8,128)(2,1)S(1)}, u32[]{:S(2)}, u32[]{:S(2)}) %collective-permute-start.6) | collective-permute-done | bytes 884768 | tf_op jit(solution)/shard_map/ppermute | solution.py:665
  315.8 6.4 collective-permute-done.16
  324.8 5.8 collective-permute-done.18
  334.7 57.6 %shard_map.263 = (bf16[4,4,288,768]{3,2,1,0:T(8,128)(2,1)}, bf16[4,4,288,384]{3,2,1,0:T(8,128)(2,1)}, f32[4,4,288,1]{3,2,1,0:T(8,128)}, bf16[4,4,288,384]{3,2,1,...) custom-call(s32[2]{0:T(128)} %pad_add_fusion.5.me_ref, ...), custom_call_target="tpu_custom_call" | custom-call | flops 40000000000 | bytes 1024 | tf_op jit(solution)/shard_map/pallas_call | solution.py:467
  394.5 6.0 collective-permute-done.19
  400.5 4.3 fusion.8
  408.1 2.8 copy.175.tab_ref
  410.9 15.1 %collective-permute-done.20.refs_1_ = bf16[4,288,384]{2,1,0:T(8,128)(2,1)} collective-permute-done((bf16[4,288,384]{2,1,0:T(8,128)(2,1)}, bf16[4,288,384]{2,1,0:T(8,128)(2,1)}, u32[]{:S(2)}, u32[]{:S(2)}) %collective-permute-start.20) | collective-permute-done | bytes 884768 | tf_op jit(solution)/shard_map/ppermute | solution.py:665
  426.6 19.1 %collective-permute-done.22.refs_3_ = bf16[4,288,384]{2,1,0:T(8,128)(2,1)} collective-permute-done((bf16[4,288,384]{2,1,0:T(8,128)(2,1)}, bf16[4,288,384]{2,1,0:T(8,128)(2,1)}, u32[]{:S(2)}, u32[]{:S(2)}) %collective-permute-start.22) | collective-permute-done | bytes 884768 | tf_op jit(solution)/shard_map/ppermute | solution.py:665
  445.7 10.9 %shard_map.265 = bf16[4,1024,384]{2,1,0:T(8,128)(2,1)} custom-call(s32[1]{0:T(128)} %bitcast.2.line_ref, s32[4,1024,4]{2,1,0:T(8,128)} %copy.175.tab_ref, bf16[4,288,384]{2,1,0:T(8,128)(2,1)} %get-tuple-element.215.refs_0_, bf16[4,288,384]{2,1,0:T(8,128)(2,1)} %collective-permute-done.20.refs_1_, bf16[4,288,384]{2,1,0:T(8,128)(2,1)} %collective-permute-done.21.refs_2_, ...), custom_call_target="tpu_custom_call" | custom-call | flops 8000000000 | bytes 1024 | tf_op jit(solution)/shard_map/pallas_call | solution.py:361
  456.9 4.4 fusion.4
  467.8 3.2 slice_reduce_fusion.3
  472.4 8.9 %collective-permute-done.24.refs_5_.refs_1_ = bf16[4,288,384]{2,1,0:T(8,128)(2,1)S(1)} collective-permute-done((bf16[4,288,384]{2,1,0:T(8,128)(2,1)}, bf16[4,288,384]{2,1,0:T(8,128)(2,1)S(1)}, u32[]{:S(2)}, u32[]{:S(2)}) %collective-permute-start.24) | collective-permute-done | bytes 884768 | tf_op jit(solution)/shard_map/ppermute | solution.py:665
  484.1 15.6 %collective-permute-done.26.refs_7_.refs_3_ = bf16[4,288,384]{2,1,0:T(8,128)(2,1)} collective-permute-done((bf16[4,288,384]{2,1,0:T(8,128)(2,1)}, bf16[4,288,384]{2,1,0:T(8,128)(2,1)}, u32[]{:S(2)}, u32[]{:S(2)}) %collective-permute-start.26) | collective-permute-done | bytes 884768 | tf_op jit(solution)/shard_map/ppermute | solution.py:665
  499.7 13.4 %shard_map.264 = (bf16[4,4,288,768]{3,2,1,0:T(8,128)(2,1)}, bf16[4,288,768]{2,1,0:T(8,128)(2,1)}, bf16[4,288,768]{2,1,0:T(8,128)(2,1)}, bf16[4,288,768]{2,1,0:T(8,128)(2,1)}, bf16[4,288,768]{2,1,0:T(8,128)(2,1)}) custom-call(s32[2]{0:T(128)} %pad_add_fusion.5.me_ref, bf16[4,4,288,384]{3,2,1,0:T(8,128)(2,1)} %get-tuple-element.81.act_ref, ...), custom_call_target="tpu_custom_call" | custom-call | flops 12000000000 | bytes 1024 | tf_op jit(solution)/shard_map/pallas_call | solution.py:521
  513.1 4.3 collective-permute-start.27
  517.4 8.1 convolution_bitcast_fusion
  525.6 4.0 convolution_bitcast_fusion.4
  529.6 10.9 %shard_map.266 = bf16[4,1024,384]{2,1,0:T(8,128)(2,1)} custom-call(s32[1]{0:T(128)} %bitcast.2.line_ref, s32[4,1024,4]{2,1,0:T(8,128)} %copy.175.tab_ref, bf16[4,288,384]{2,1,0:T(8,128)(2,1)} %get-tuple-element.211.refs_4_.refs_0_, bf16[4,288,384]{2,1,0:T(8,128)(2,1)} %copy-done.64, bf16[4,288,384]{2,1,0:T(8,128)(2,1)} %collective-permute-done.25.refs_6_.refs_2_, ...), custom_call_target="tpu_custom_call" | custom-call | flops 8000000000 | bytes 1024 | tf_op jit(solution)/shard_map/pallas_call | solution.py:361
  541.0 9.1 %broadcast_select_fusion.5 = (f32[384,768]{1,0:T(8,128)}, f32[384,768]{1,0:T(8,128)}) fusion(f32[384,768]{1,0:T(8,128)} %convolution_bitcast_fusion, pred[]{:T(512)S(6)} %eq.18, bf16[4,4,288,384]{3,2,1,0:T(8,128)(2,1)} %get-tuple-element.81.act_ref, bf16[1,4,288,768]{3,2,1,0:T(8,128)(2,1)} %bitcast.277, bf16[1,4,288,768]{3,2,1,0:T(8,128)(2,1)} %bitcast.275, ...), kind=kOutput, calls=%fused_computation.84 | convolution fusion | flops 2729115648 | bytes 14155777 | tf_op jit(solution)/shard_map/dot_general | solution.py:18
  550.2 6.1 convolution_bitcast_fusion.2
  556.4 6.3 broadcast_select_fusion.9
  563.5 4.4 select_reduce_fusion
  568.0 4.6 collective-permute-start.36
  572.6 5.6 fusion
  580.9 3.1 broadcast_select_fusion.8
  588.1 4.4 collective-permute-start.39
  597.5 4.5 reduce-scatter.6.cloned.1.call-done
  604.7 13.6 %collective-permute-done.28.refs_1_ = bf16[4,288,768]{2,1,0:T(8,128)(2,1)} collective-permute-done((bf16[4,288,768]{2,1,0:T(8,128)(2,1)}, bf16[4,288,768]{2,1,0:T(8,128)(2,1)}, u32[]{:S(2)}, u32[]{:S(2)}) %collective-permute-start.28) | collective-permute-done | bytes 1769504 | tf_op jit(solution)/shard_map/ppermute | solution.py:665
  618.4 37.7 %collective-permute-done.30.refs_3_ = bf16[4,288,768]{2,1,0:T(8,128)(2,1)} collective-permute-done((bf16[4,288,768]{2,1,0:T(8,128)(2,1)S(1)}, bf16[4,288,768]{2,1,0:T(8,128)(2,1)}, u32[]{:S(2)}, u32[]{:S(2)}) %collective-permute-start.30) | collective-permute-done | bytes 1769504 | tf_op jit(solution)/shard_map/ppermute | solution.py:665
  656.1 16.9 %shard_map.267.refs_0_ = bf16[4,1024,768]{2,1,0:T(8,128)(2,1)} custom-call(s32[1]{0:T(128)} %bitcast.2.line_ref, s32[4,1024,4]{2,1,0:T(8,128)} %copy.175.tab_ref, bf16[4,288,768]{2,1,0:T(8,128)(2,1)} %get-tuple-element.207.refs_0_, bf16[4,288,768]{2,1,0:T(8,128)(2,1)} %collective-permute-done.28.refs_1_, ...), custom_call_target="tpu_custom_call" | custom-call | flops 16000000000 | bytes 1024 | tf_op jit(solution)/shard_map/pallas_call | solution.py:361
  678.9 6.2 multiply_reduce_fusion
  686.4 9.5 %fusion.34 = (bf16[1024,1536]{1,0:T(8,128)(2,1)S(1)}, f32[1024,1536]{1,0:T(8,128)}) fusion(f32[1024]{0:T(1024)S(1)} %broadcast_multiply_fusion.1, f32[1024,1536]{1,0:T(8,128)} %get-tuple-element.63, f32[1536]{0:T(1024)S(1)} %copy-done.57, f32[1024,1536]{1,0:T(8,128)} %get-tuple-element.267, bf16[1024,768]{1,0:T(8,128)(2,1)S(1)} %get-tuple-element.217, ...), kind=kLoop, calls=%fused_computation.160 | loop fusion | flops 20447232 | bytes 28325888 | tf_op jit(solution)/shard_map/convert_element_type | solution.py:699
  695.9 2.8 fusion.41
  700.4 29.5 %shard_map.268.d_ref = bf16[1024,1024]{1,0:T(8,128)(2,1)} custom-call(bf16[1024,768]{1,0:T(8,128)(2,1)} %get-tuple-element.59.q_ref, bf16[1024,128]{1,0:T(8,128)(2,1)} %get-tuple-element.60.k_ref, bf16[1024,128]{1,0:T(8,128)(2,1)} %get-tuple-element.61.v_ref, s32[1,1024]{1,0:T(1,128)} %segq_ref.3, s32[1024,1]{1,0:T(8,128)} %copy.167.segk_ref, ...), custom_call_target="tpu_custom_call" | custom-call | flops 28000000000 | bytes 1024 | tf_op jit(solution)/shard_map/pallas_call | solution.py:602
  729.9 6.1 fusion.40
  746.4 7.8 shard_map.269
  755.7 15.5 %collective-permute-done.41 = bf16[8,96,1024]{2,1,0:T(8,128)(2,1)} collective-permute-done((bf16[8,96,1024]{2,1,0:T(8,128)(2,1)}, bf16[8,96,1024]{2,1,0:T(8,128)(2,1)}, u32[]{:S(2)}, u32[]{:S(2)}) %collective-permute-start.41) | collective-permute-done | bytes 1572896 | tf_op jit(solution)/shard_map/ppermute | solution.py:665
  771.2 2.8 bitcast_add_fusion
  781.4 3.1 collective-permute-done.49
  784.5 4.8 collective-permute-done.50
  789.3 4.9 collective-permute-done.51
  794.7 2.9 collective-permute-start.44
  799.2 10.5 %collective-permute-done.44 = bf16[96,1024]{1,0:T(8,128)(2,1)S(1)} collective-permute-done((bf16[96,1024]{1,0:T(8,128)(2,1)S(1)}, bf16[96,1024]{1,0:T(8,128)(2,1)S(1)}, u32[]{:S(2)}, u32[]{:S(2)}) %collective-permute-start.44) | collective-permute-done | bytes 196640 | tf_op jit(solution)/shard_map/ppermute | solution.py:665
  809.7 4.4 collective-permute-done.45
  821.2 2.9 add_convert_fusion
  824.5 5.3 multiply_reduce_fusion.1
  829.9 5.4 multiply_add_fusion
  (325 shorter events, 120.7 us)
Async XLA Ops:
  7.2 118.8 %all-gather.11.cloned.1.call-start = ((), (), s32[]{:S(2)}) async-start(), calls=%async_computation.8 | async-start | bytes 7864320 | tf_op jit(solution)/shard_map/all_gather | solution.py:668
  9.9 215.1 %all-gather.9.cloned.1.call-start = ((), (), s32[]{:S(2)}) async-start(), calls=%async_computation.7 | async-start | bytes 3932160 | tf_op jit(solution)/shard_map/all_gather | solution.py:668
  20.7 26.8 %copy-start.56 = (f32[1536]{0:T(1024)S(1)}, f32[1536]{0:T(1024)}, u32[]{:S(2)}) copy-start(f32[1536]{0:T(1024)} %param.20) | copy-start | bytes 18436
  44.8 6.4 collective-permute-start
  63.7 190.3 %all-gather.7.cloned.1.call-start = ((), (), s32[]{:S(2)}) async-start(), calls=%async_computation.6 | async-start | bytes 3932160 | tf_op jit(solution)/shard_map/all_gather | solution.py:668
  75.3 4.0 collective-permute-start.1
  75.4 6.2 collective-permute-start.2
  77.9 4.8 collective-permute-start.3
  86.0 509.3 %reduce-scatter.4.cloned.1.call-start = ((), (), s32[]{:S(2)}) async-start(), calls=%async_computation.3 | async-start | bytes 3932160 | tf_op jit(solution)/shard_map/reduce_scatter | solution.py:672
  139.1 39.9 %collective-permute-start.12 = (bf16[4,288,768]{2,1,0:T(8,128)(2,1)}, bf16[4,288,768]{2,1,0:T(8,128)(2,1)S(1)}, u32[]{:S(2)}, u32[]{:S(2)}) collective-permute-start(bf16[4,288,768]{2,1,0:T(8,128)(2,1)} %get-tuple-element.74), channel_id=1, source_target_pairs={{0,2},{2,0},{4,6},{6,4},{8,10},{10,8},{12,14},{14,12},{16,18},{18,... | collective-permute-start | bytes 5308424 | tf_op jit(solution)/shard_map/ppermute | solution.py:665
  140.5 39.5 %collective-permute-start.13 = (bf16[4,288,768]{2,1,0:T(8,128)(2,1)}, bf16[4,288,768]{2,1,0:T(8,128)(2,1)S(1)}, u32[]{:S(2)}, u32[]{:S(2)}) collective-permute-start(bf16[4,288,768]{2,1,0:T(8,128)(2,1)} %get-tuple-element.75), channel_id=1, source_target_pairs={{0,4},{2,6},{4,0},{6,2},{8,12},{10,14},{12,8},{14,10},{16,20},{18,... | collective-permute-start | bytes 5308424 | tf_op jit(solution)/shard_map/ppermute | solution.py:665
  141.7 76.2 %collective-permute-start.14 = (bf16[4,288,768]{2,1,0:T(8,128)(2,1)}, bf16[4,288,768]{2,1,0:T(8,128)(2,1)S(1)}, u32[]{:S(2)}, u32[]{:S(2)}) collective-permute-start(bf16[4,288,768]{2,1,0:T(8,128)(2,1)} %get-tuple-element.76), channel_id=1, source_target_pairs={{0,6},{2,4},{4,2},{6,0},{8,14},{10,12},{12,10},{14,8},{16,22},{18,... | collective-permute-start | bytes 5308424 | tf_op jit(solution)/shard_map/ppermute | solution.py:665
  179.1 44.2 %copy-start.22 = (bf16[4,288,768]{2,1,0:T(8,128)(2,1)}, bf16[4,288,768]{2,1,0:T(8,128)(2,1)S(1)}, u32[]{:S(2)}) copy-start(bf16[4,288,768]{2,1,0:T(8,128)(2,1)S(1)} %collective-permute-done.12) | copy-start | bytes 5308420
  180.0 43.3 %copy-start.23 = (bf16[4,288,768]{2,1,0:T(8,128)(2,1)}, bf16[4,288,768]{2,1,0:T(8,128)(2,1)S(1)}, u32[]{:S(2)}) copy-start(bf16[4,288,768]{2,1,0:T(8,128)(2,1)S(1)} %collective-permute-done.13) | copy-start | bytes 5308420
  223.3 108.6 %collective-permute-start.15 = (bf16[4,4,288,768]{3,2,1,0:T(8,128)(2,1)}, bf16[4,4,288,768]{3,2,1,0:T(8,128)(2,1)}, u32[]{:S(2)}, u32[]{:S(2)}) collective-permute-start(bf16[4,4,288,768]{3,2,1,0:T(8,128)(2,1)} %pad_maximum_fusion.refs_4_), channel_id=1, source_target_pairs={{0,1},{1,0},{2,3},{3,2},{4,5},{5,4},{6,7},{7,6},{8,9},{9,8},{10,11... | collective-permute-start | bytes 21233672 | tf_op jit(solution)/shard_map/ppermute | solution.py:707
  232.8 30.2 %collective-permute-start.7 = (bf16[4,288,384]{2,1,0:T(8,128)(2,1)}, bf16[4,288,384]{2,1,0:T(8,128)(2,1)S(1)}, u32[]{:S(2)}, u32[]{:S(2)}) collective-permute-start(bf16[4,288,384]{2,1,0:T(8,128)(2,1)} %get-tuple-element.70), channel_id=1, source_target_pairs={{0,2},{2,0},{4,6},{6,4},{8,10},{10,8},{12,14},{14,12},{16,18},{18,... | collective-permute-start | bytes 2654216 | tf_op jit(solution)/shard_map/ppermute | solution.py:665
  233.7 30.4 %collective-permute-start.8 = (bf16[4,288,384]{2,1,0:T(8,128)(2,1)}, bf16[4,288,384]{2,1,0:T(8,128)(2,1)S(1)}, u32[]{:S(2)}, u32[]{:S(2)}) collective-permute-start(bf16[4,288,384]{2,1,0:T(8,128)(2,1)} %get-tuple-element.71), channel_id=1, source_target_pairs={{0,4},{2,6},{4,0},{6,2},{8,12},{10,14},{12,8},{14,10},{16,20},{18,... | collective-permute-start | bytes 2654216 | tf_op jit(solution)/shard_map/ppermute | solution.py:665
  234.2 39.9 %collective-permute-start.9 = (bf16[4,288,384]{2,1,0:T(8,128)(2,1)}, bf16[4,288,384]{2,1,0:T(8,128)(2,1)S(1)}, u32[]{:S(2)}, u32[]{:S(2)}) collective-permute-start(bf16[4,288,384]{2,1,0:T(8,128)(2,1)} %get-tuple-element.72), channel_id=1, source_target_pairs={{0,6},{2,4},{4,2},{6,0},{8,14},{10,12},{12,10},{14,8},{16,22},{18,... | collective-permute-start | bytes 2654216 | tf_op jit(solution)/shard_map/ppermute | solution.py:665
  261.7 30.4 %collective-permute-start.4 = (bf16[4,288,384]{2,1,0:T(8,128)(2,1)}, bf16[4,288,384]{2,1,0:T(8,128)(2,1)S(1)}, u32[]{:S(2)}, u32[]{:S(2)}) collective-permute-start(bf16[4,288,384]{2,1,0:T(8,128)(2,1)} %get-tuple-element.66), channel_id=1, source_target_pairs={{0,2},{2,0},{4,6},{6,4},{8,10},{10,8},{12,14},{14,12},{16,18},{18,... | collective-permute-start | bytes 2654216 | tf_op jit(solution)/shard_map/ppermute | solution.py:665
  263.0 30.9 %collective-permute-start.5 = (bf16[4,288,384]{2,1,0:T(8,128)(2,1)}, bf16[4,288,384]{2,1,0:T(8,128)(2,1)S(1)}, u32[]{:S(2)}, u32[]{:S(2)}) collective-permute-start(bf16[4,288,384]{2,1,0:T(8,128)(2,1)} %get-tuple-element.67), channel_id=1, source_target_pairs={{0,4},{2,6},{4,0},{6,2},{8,12},{10,14},{12,8},{14,10},{16,20},{18,... | collective-permute-start | bytes 2654216 | tf_op jit(solution)/shard_map/ppermute | solution.py:665
  264.2 47.9 %collective-permute-start.6 = (bf16[4,288,384]{2,1,0:T(8,128)(2,1)}, bf16[4,288,384]{2,1,0:T(8,128)(2,1)S(1)}, u32[]{:S(2)}, u32[]{:S(2)}) collective-permute-start(bf16[4,288,384]{2,1,0:T(8,128)(2,1)} %get-tuple-element.68), channel_id=1, source_target_pairs={{0,6},{2,4},{4,2},{6,0},{8,14},{10,12},{12,10},{14,8},{16,22},{18,... | collective-permute-start | bytes 2654216 | tf_op jit(solution)/shard_map/ppermute | solution.py:665
  274.1 37.9 %copy-start.40 = (bf16[4,288,384]{2,1,0:T(8,128)(2,1)S(1)}, bf16[4,288,384]{2,1,0:T(8,128)(2,1)}, u32[]{:S(2)}) copy-start(bf16[4,288,384]{2,1,0:T(8,128)(2,1)} %get-tuple-element.65) | copy-start | bytes 2654212
  275.0 37.6 %copy-start.7 = (bf16[4,4,288,384]{3,2,1,0:T(8,128)(2,1)}, bf16[4,4,288,384]{3,2,1,0:T(8,128)(2,1)S(1)}, u32[]{:S(2)}) copy-start(bf16[4,4,288,384]{3,2,1,0:T(8,128)(2,1)S(1)} %pad_maximum_fusion.2.refs_1_) | copy-start | bytes 10616836
  275.1 56.8 %collective-permute-start.11 = (bf16[4,4,288,384]{3,2,1,0:T(8,128)(2,1)S(1)}, bf16[4,4,288,384]{3,2,1,0:T(8,128)(2,1)S(1)}, u32[]{:S(2)}, u32[]{:S(2)}) collective-permute-start(bf16[4,4,288,384]{3,2,1,0:T(8,128)(2,1)S(1)} %pad_maximum_fusion.2.refs_1_), channel_id=1, source_target_pairs={{0,1},{1,0},{2,3},{3,2},{4,5},{5,4},{6,7},{7,6},{8,9},{9,8},{10,11... | collective-permute-start | bytes 10616840 | tf_op jit(solution)/shard_map/ppermute | solution.py:707
  313.0 18.9 %collective-permute-start.10 = (bf16[4,4,288,384]{3,2,1,0:T(8,128)(2,1)S(1)}, bf16[4,4,288,384]{3,2,1,0:T(8,128)(2,1)S(1)}, u32[]{:S(2)}, u32[]{:S(2)}) collective-permute-start(bf16[4,4,288,384]{3,2,1,0:T(8,128)(2,1)S(1)} %pad_maximum_fusion.1.refs_0_), channel_id=1, source_target_pairs={{0,1},{1,0},{2,3},{3,2},{4,5},{5,4},{6,7},{7,6},{8,9},{9,8},{10,11... | collective-permute-start | bytes 10616840 | tf_op jit(solution)/shard_map/ppermute | solution.py:707
  313.8 8.4 collective-permute-start.16
  314.6 10.2 %collective-permute-start.17 = (bf16[4,288,4]{2,1,0:T(8,128)(2,1)S(1)}, bf16[4,288,4]{2,1,0:T(8,128)(2,1)S(1)}, u32[]{:S(2)}, u32[]{:S(2)}) collective-permute-start(bf16[4,288,4]{2,1,0:T(8,128)(2,1)S(1)} %copy-done.66), channel_id=1, source_target_pairs={{0,4},{2,6},{4,0},{6,2},{8,12},{10,14},{12,8},{14,10},{16,20},{18,... | collective-permute-start | bytes 27656 | tf_op jit(solution)/shard_map/ppermute | solution.py:665
  322.2 8.3 collective-permute-start.18
  392.3 8.2 collective-permute-start.19
  394.4 62.5 %collective-permute-start.23 = (bf16[4,4,288,384]{3,2,1,0:T(8,128)(2,1)}, bf16[4,4,288,384]{3,2,1,0:T(8,128)(2,1)S(1)}, u32[]{:S(2)}, u32[]{:S(2)}) collective-permute-start(bf16[4,4,288,384]{3,2,1,0:T(8,128)(2,1)} %get-tuple-element.88), channel_id=1, source_target_pairs={{0,1},{1,0},{2,3},{3,2},{4,5},{5,4},{6,7},{7,6},{8,9},{9,8},{10,11... | collective-permute-start | bytes 10616840 | tf_op jit(solution)/shard_map/ppermute | solution.py:707
  404.8 21.2 %collective-permute-start.20 = (bf16[4,288,384]{2,1,0:T(8,128)(2,1)}, bf16[4,288,384]{2,1,0:T(8,128)(2,1)}, u32[]{:S(2)}, u32[]{:S(2)}) collective-permute-start(bf16[4,288,384]{2,1,0:T(8,128)(2,1)} %get-tuple-element.214), channel_id=1, source_target_pairs={{0,2},{2,0},{4,6},{6,4},{8,10},{10,8},{12,14},{14,12},{16,18},{18,... | collective-permute-start | bytes 2654216 | tf_op jit(solution)/shard_map/ppermute | solution.py:665
  405.8 20.9 %collective-permute-start.21 = (bf16[4,288,384]{2,1,0:T(8,128)(2,1)}, bf16[4,288,384]{2,1,0:T(8,128)(2,1)}, u32[]{:S(2)}, u32[]{:S(2)}) collective-permute-start(bf16[4,288,384]{2,1,0:T(8,128)(2,1)} %get-tuple-element.213), channel_id=1, source_target_pairs={{0,4},{2,6},{4,0},{6,2},{8,12},{10,14},{12,8},{14,10},{16,20},{18,... | collective-permute-start | bytes 2654216 | tf_op jit(solution)/shard_map/ppermute | solution.py:665
  407.0 38.7 %collective-permute-start.22 = (bf16[4,288,384]{2,1,0:T(8,128)(2,1)}, bf16[4,288,384]{2,1,0:T(8,128)(2,1)}, u32[]{:S(2)}, u32[]{:S(2)}) collective-permute-start(bf16[4,288,384]{2,1,0:T(8,128)(2,1)} %get-tuple-element.212), channel_id=1, source_target_pairs={{0,6},{2,4},{4,2},{6,0},{8,14},{10,12},{12,10},{14,8},{16,22},{18,... | collective-permute-start | bytes 2654216 | tf_op jit(solution)/shard_map/ppermute | solution.py:665
  456.7 145.3 %reduce-scatter.6.cloned.1.call-start = ((), (), s32[]{:S(2)}) async-start(), calls=%async_computation.4 | async-start | bytes 3932160 | tf_op jit(solution)/shard_map/reduce_scatter | solution.py:672
  461.3 20.0 %collective-permute-start.24 = (bf16[4,288,384]{2,1,0:T(8,128)(2,1)}, bf16[4,288,384]{2,1,0:T(8,128)(2,1)S(1)}, u32[]{:S(2)}, u32[]{:S(2)}) collective-permute-start(bf16[4,288,384]{2,1,0:T(8,128)(2,1)} %get-tuple-element.210), channel_id=1, source_target_pairs={{0,2},{2,0},{4,6},{6,4},{8,10},{10,8},{12,14},{14,12},{16,18},{18,... | collective-permute-start | bytes 2654216 | tf_op jit(solution)/shard_map/ppermute | solution.py:665
  462.5 21.7 %collective-permute-start.25 = (bf16[4,288,384]{2,1,0:T(8,128)(2,1)}, bf16[4,288,384]{2,1,0:T(8,128)(2,1)}, u32[]{:S(2)}, u32[]{:S(2)}) collective-permute-start(bf16[4,288,384]{2,1,0:T(8,128)(2,1)} %get-tuple-element.209), channel_id=1, source_target_pairs={{0,4},{2,6},{4,0},{6,2},{8,12},{10,14},{12,8},{14,10},{16,20},{18,... | collective-permute-start | bytes 2654216 | tf_op jit(solution)/shard_map/ppermute | solution.py:665
  462.8 37.0 %collective-permute-start.26 = (bf16[4,288,384]{2,1,0:T(8,128)(2,1)}, bf16[4,288,384]{2,1,0:T(8,128)(2,1)}, u32[]{:S(2)}, u32[]{:S(2)}) collective-permute-start(bf16[4,288,384]{2,1,0:T(8,128)(2,1)} %get-tuple-element.208), channel_id=1, source_target_pairs={{0,6},{2,4},{4,2},{6,0},{8,14},{10,12},{12,10},{14,8},{16,22},{18,... | collective-permute-start | bytes 2654216 | tf_op jit(solution)/shard_map/ppermute | solution.py:665
  467.8 57.8 %slice-start = ((s8[7077888]{0:T(1024)(128)(4,1)}), s8[4194304]{0:T(1024)(128)(4,1)S(1)}, s32[]{:S(2)}) async-start(s8[7077888]{0:T(1024)(128)(4,1)} %bitcast.253), calls=%async_computation.9 | async-start | bytes 8388608
  471.0 91.7 %collective-permute-start.33 = (f32[4,288]{1,0:T(4,128)}, f32[4,288]{1,0:T(4,128)}, u32[]{:S(2)}, u32[]{:S(2)}) collective-permute-start(f32[4,288]{1,0:T(4,128)} %get-tuple-element.195), channel_id=1, source_target_pairs={{0,2},{2,0},{4,6},{6,4},{8,10},{10,8},{12,14},{14,12},{16,18},{18,... | collective-permute-start | bytes 13832 | tf_op jit(solution)/shard_map/ppermute | solution.py:665
  472.1 90.6 %collective-permute-start.34 = (f32[4,288]{1,0:T(4,128)}, f32[4,288]{1,0:T(4,128)}, u32[]{:S(2)}, u32[]{:S(2)}) collective-permute-start(f32[4,288]{1,0:T(4,128)} %get-tuple-element.194), channel_id=1, source_target_pairs={{0,4},{2,6},{4,0},{6,2},{8,12},{10,14},{12,8},{14,10},{16,20},{18,... | collective-permute-start | bytes 13832 | tf_op jit(solution)/shard_map/ppermute | solution.py:665
  481.4 81.4 %collective-permute-start.35 = (f32[4,288]{1,0:T(4,128)}, f32[4,288]{1,0:T(4,128)}, u32[]{:S(2)}, u32[]{:S(2)}) collective-permute-start(f32[4,288]{1,0:T(4,128)} %get-tuple-element.193), channel_id=1, source_target_pairs={{0,6},{2,4},{4,2},{6,0},{8,14},{10,12},{12,10},{14,8},{16,22},{18,... | collective-permute-start | bytes 13832 | tf_op jit(solution)/shard_map/ppermute | solution.py:665
  513.1 59.4 %collective-permute-start.27 = (bf16[4,4,288,768]{3,2,1,0:T(8,128)(2,1)}, bf16[4,4,288,768]{3,2,1,0:T(8,128)(2,1)}, u32[]{:S(2)}, u32[]{:S(2)}) collective-permute-start(bf16[4,4,288,768]{3,2,1,0:T(8,128)(2,1)} %get-tuple-element.93), channel_id=1, source_target_pairs={{0,1},{1,0},{2,3},{3,2},{4,5},{5,4},{6,7},{7,6},{8,9},{9,8},{10,11... | collective-permute-start | bytes 21233672 | tf_op jit(solution)/shard_map/ppermute | solution.py:707
  540.6 280.7 %reduce-scatter.8.cloned.1.call-start = ((), (), s32[]{:S(2)}) async-start(), calls=%async_computation.5 | async-start | bytes 7864320 | tf_op jit(solution)/shard_map/reduce_scatter | solution.py:672
  568.0 16.1 %collective-permute-start.36 = (f32[4,1024]{1,0:T(4,128)S(1)}, f32[4,1024]{1,0:T(4,128)S(1)}, u32[]{:S(2)}, u32[]{:S(2)}) collective-permute-start(f32[4,1024]{1,0:T(4,128)S(1)} %get-tuple-element.247), channel_id=1, source_target_pairs={{0,8},{2,10},{4,12},{6,14},{8,0},{10,2},{12,4},{14,6},{16,24},{18,... | collective-permute-start | bytes 49160 | tf_op jit(solution)/shard_map/ppermute | solution.py:665
  578.2 40.1 %collective-permute-start.28 = (bf16[4,288,768]{2,1,0:T(8,128)(2,1)}, bf16[4,288,768]{2,1,0:T(8,128)(2,1)}, u32[]{:S(2)}, u32[]{:S(2)}) collective-permute-start(bf16[4,288,768]{2,1,0:T(8,128)(2,1)} %get-tuple-element.206), channel_id=1, source_target_pairs={{0,2},{2,0},{4,6},{6,4},{8,10},{10,8},{12,14},{14,12},{16,18},{18,... | collective-permute-start | bytes 5308424 | tf_op jit(solution)/shard_map/ppermute | solution.py:665
  578.2 40.2 %collective-permute-start.29 = (bf16[4,288,768]{2,1,0:T(8,128)(2,1)}, bf16[4,288,768]{2,1,0:T(8,128)(2,1)}, u32[]{:S(2)}, u32[]{:S(2)}) collective-permute-start(bf16[4,288,768]{2,1,0:T(8,128)(2,1)} %get-tuple-element.205), channel_id=1, source_target_pairs={{0,4},{2,6},{4,0},{6,2},{8,12},{10,14},{12,8},{14,10},{16,20},{18,... | collective-permute-start | bytes 5308424 | tf_op jit(solution)/shard_map/ppermute | solution.py:665
  578.7 77.4 %collective-permute-start.30 = (bf16[4,288,768]{2,1,0:T(8,128)(2,1)S(1)}, bf16[4,288,768]{2,1,0:T(8,128)(2,1)}, u32[]{:S(2)}, u32[]{:S(2)}) collective-permute-start(bf16[4,288,768]{2,1,0:T(8,128)(2,1)S(1)} %get-tuple-element.204), channel_id=1, source_target_pairs={{0,6},{2,4},{4,2},{6,0},{8,14},{10,12},{12,10},{14,8},{16,22},{18,... | collective-permute-start | bytes 5308424 | tf_op jit(solution)/shard_map/ppermute | solution.py:665
  584.0 4.1 collective-permute-start.37
  584.1 4.0 collective-permute-start.38
  588.1 5.8 collective-permute-start.39
  604.1 72.7 %collective-permute-start.32 = (bf16[1024,768]{1,0:T(8,128)(2,1)}, bf16[1024,768]{1,0:T(8,128)(2,1)}, u32[]{:S(2)}, u32[]{:S(2)}) collective-permute-start(bf16[1024,768]{1,0:T(8,128)(2,1)} %constant_dynamic-update-slice_fusion.refs_4_), channel_id=1, source_target_pairs={{0,1},{1,0},{2,3},{3,2},{4,5},{5,4},{6,7},{7,6},{8,9},{9,8},{10,11... | collective-permute-start | bytes 4718600 | tf_op jit(solution)/shard_map/ppermute | solution.py:707
  699.7 43.8 %collective-permute-start.47 = (bf16[8,96,896]{2,1,0:T(8,128)(2,1)S(1)}, bf16[8,96,896]{2,1,0:T(8,128)(2,1)}, u32[]{:S(2)}, u32[]{:S(2)}) collective-permute-start(bf16[8,96,896]{2,1,0:T(8,128)(2,1)S(1)} %fusion.13), channel_id=1, source_target_pairs={{0,2},{2,0},{4,6},{6,4},{8,10},{10,8},{12,14},{14,12},{16,18},{18,... | collective-permute-start | bytes 4128776 | tf_op jit(solution)/shard_map/ppermute | solution.py:665
  737.5 33.7 %collective-permute-start.41 = (bf16[8,96,1024]{2,1,0:T(8,128)(2,1)}, bf16[8,96,1024]{2,1,0:T(8,128)(2,1)}, u32[]{:S(2)}, u32[]{:S(2)}) collective-permute-start(bf16[8,96,1024]{2,1,0:T(8,128)(2,1)} %fusion.12), channel_id=1, source_target_pairs={{0,2},{2,0},{4,6},{6,4},{8,10},{10,8},{12,14},{14,12},{16,18},{18,... | collective-permute-start | bytes 4718600 | tf_op jit(solution)/shard_map/ppermute | solution.py:665
  745.2 31.7 %collective-permute-start.48 = (bf16[4,96,896]{2,1,0:T(8,128)(2,1)S(1)}, bf16[4,96,896]{2,1,0:T(8,128)(2,1)S(1)}, u32[]{:S(2)}, u32[]{:S(2)}) collective-permute-start(bf16[4,96,896]{2,1,0:T(8,128)(2,1)S(1)} %fusion.15), channel_id=1, source_target_pairs={{0,4},{2,6},{4,0},{6,2},{8,12},{10,14},{12,8},{14,10},{16,20},{18,... | collective-permute-start | bytes 2064392 | tf_op jit(solution)/shard_map/ppermute | solution.py:665
  754.3 69.9 %collective-permute-start.40 = (bf16[1024,1536]{1,0:T(8,128)(2,1)}, bf16[1024,1536]{1,0:T(8,128)(2,1)}, u32[]{:S(2)}, u32[]{:S(2)}) collective-permute-start(bf16[1024,1536]{1,0:T(8,128)(2,1)} %shard_map.269), channel_id=1, source_target_pairs={{0,1},{1,0},{2,3},{3,2},{4,5},{5,4},{6,7},{7,6},{8,9},{9,8},{10,11... | collective-permute-start | bytes 9437192 | tf_op jit(solution)/shard_map/ppermute | solution.py:707
  774.3 20.0 %collective-permute-start.42 = (bf16[4,96,1024]{2,1,0:T(8,128)(2,1)S(1)}, bf16[4,96,1024]{2,1,0:T(8,128)(2,1)S(1)}, u32[]{:S(2)}, u32[]{:S(2)}) collective-permute-start(bf16[4,96,1024]{2,1,0:T(8,128)(2,1)S(1)} %fusion.14), channel_id=1, source_target_pairs={{0,4},{2,6},{4,0},{6,2},{8,12},{10,14},{12,8},{14,10},{16,20},{18,... | collective-permute-start | bytes 2359304 | tf_op jit(solution)/shard_map/ppermute | solution.py:665
  777.1 7.4 collective-permute-start.49
  778.0 11.3 %collective-permute-start.50 = (bf16[96,896]{1,0:T(8,128)(2,1)S(1)}, bf16[96,896]{1,0:T(8,128)(2,1)S(1)}, u32[]{:S(2)}, u32[]{:S(2)}) collective-permute-start(bf16[96,896]{1,0:T(8,128)(2,1)S(1)} %get-tuple-element.233), channel_id=1, source_target_pairs={{0,16},{2,18},{4,20},{6,22},{8,24},{10,26},{12,28},{14,30},{16,0},... | collective-permute-start | bytes 516104 | tf_op jit(solution)/shard_map/ppermute | solution.py:665
  778.0 16.2 %collective-permute-start.51 = (bf16[96,896]{1,0:T(8,128)(2,1)S(1)}, bf16[96,896]{1,0:T(8,128)(2,1)S(1)}, u32[]{:S(2)}, u32[]{:S(2)}) collective-permute-start(bf16[96,896]{1,0:T(8,128)(2,1)S(1)} %get-tuple-element.232), channel_id=1, source_target_pairs={{0,24},{2,26},{4,28},{6,30},{8,16},{10,18},{12,20},{14,22},{16,8},... | collective-permute-start | bytes 516104 | tf_op jit(solution)/shard_map/ppermute | solution.py:665
  794.6 4.6 collective-permute-start.43
  794.7 15.0 %collective-permute-start.44 = (bf16[96,1024]{1,0:T(8,128)(2,1)S(1)}, bf16[96,1024]{1,0:T(8,128)(2,1)S(1)}, u32[]{:S(2)}, u32[]{:S(2)}) collective-permute-start(bf16[96,1024]{1,0:T(8,128)(2,1)S(1)} %get-tuple-element.228), channel_id=1, source_target_pairs={{0,16},{2,18},{4,20},{6,22},{8,24},{10,26},{12,28},{14,30},{16,0},... | collective-permute-start | bytes 589832 | tf_op jit(solution)/shard_map/ppermute | solution.py:665
  797.6 16.5 %collective-permute-start.45 = (bf16[96,1024]{1,0:T(8,128)(2,1)S(1)}, bf16[96,1024]{1,0:T(8,128)(2,1)S(1)}, u32[]{:S(2)}, u32[]{:S(2)}) collective-permute-start(bf16[96,1024]{1,0:T(8,128)(2,1)S(1)} %get-tuple-element.227), channel_id=1, source_target_pairs={{0,24},{2,26},{4,28},{6,30},{8,16},{10,18},{12,20},{14,22},{16,8},... | collective-permute-start | bytes 589832 | tf_op jit(solution)/shard_map/ppermute | solution.py:665
  817.5 3.2 collective-permute-start.46
  824.1 11.2 %collective-permute-start.31 = (bf16[1024,768]{1,0:T(8,128)(2,1)S(1)}, bf16[1024,768]{1,0:T(8,128)(2,1)S(1)}, u32[]{:S(2)}, u32[]{:S(2)}) collective-permute-start(bf16[1024,768]{1,0:T(8,128)(2,1)S(1)} %add_convert_fusion), channel_id=1, source_target_pairs={{0,1},{1,0},{2,3},{3,2},{4,5},{5,4},{6,7},{7,6},{8,9},{9,8},{10,11... | collective-permute-start | bytes 4718600 | tf_op jit(solution)/shard_map/ppermute | solution.py:707
  (69 other events, 602.0 us)
Sparse Core Ops, SparseCore 0:
  10.2 115.7 all-gather.10
  127.5 62.7 all-gather.8
  191.9 62.1 all-gather.6
  456.8 61.5 reduce-scatter.3
  540.7 61.2 reduce-scatter.5
  673.1 110.0 reduce-scatter.7

commit v3 on v2

--- a/solution.py
+++ b/solution.py
@@ -42,8 +42,22 @@
 
 def lasting(microseconds):
     return pl.CostEstimate(
-        flops=int(microseconds * 1.0e9), bytes_accessed=1024, transcendentals=0
-    )
+        flops=int(microseconds * 1.0e6), bytes_accessed=1024, transcendentals=0
+    )
+
+
+def hold_kernel(*refs):
+    del refs
+
+
+def hold(array, *earlier):
+    return pl.pallas_call(
+        hold_kernel,
+        in_specs=anywhere((array, *earlier)),
+        out_specs=pl.BlockSpec(memory_space=pl.ANY),
+        out_shape=jax.ShapeDtypeStruct(array.shape, array.dtype),
+        input_output_aliases={0: 0},
+    )(array, *earlier)
 
 
 def whole(array):
@@ -216,9 +230,10 @@
 
 
 def second_kernel(
-    side_ref, x_ref, a_ref, b_ref, gain_ref, router_ref, routes_ref, *refs
+    outputs, side_ref, x_ref, a_ref, b_ref, gain_ref, router_ref, routes_ref, *refs
 ):
-    hidden_ref, in_ref, half_ref, inv_ref, gate_ref = refs[-5:]
+    refs = refs[len(refs) - outputs :]
+    hidden_ref, in_ref, inv_ref, gate_ref, *parts = refs
     hidden = x_ref[...].astype(jnp.float32) + (
         a_ref[...].astype(jnp.float32) + b_ref[...].astype(jnp.float32)
     )
@@ -227,8 +242,12 @@
     hidden_ref[...] = hidden
     in_ref[...] = second
     inv_ref[...] = inverse
-    half = half_ref.shape[1]
-    half_ref[...] = jnp.where(side_ref[0] == 0, second[:, :half], second[:, half:])
+    half = second.shape[1] // 2
+    sent = jnp.where(side_ref[0] == 0, second[:, :half], second[:, half:])
+    start = 0
+    for part in parts:
+        part[...] = sent[:, start : start + part.shape[1]]
+        start += part.shape[1]
     logits = dot(second, router_ref[...])
     gate_ref[...] = routed_softmax(logits, routes_ref[...])
 
@@ -243,7 +262,7 @@
     return spread / jnp.sum(spread, axis=1, keepdims=True)
 
 
-def second_norm(side, tokens, mine, other, gain, router, routes, tile, earlier):
+def second_norm(side, tokens, mine, other, gain, router, routes, tile, widths, earlier):
     length, model = tokens.shape
     count = router.shape[1]
 
@@ -254,7 +273,7 @@
         return jax.ShapeDtypeStruct((length, columns), kind)
 
     return pl.pallas_call(
-        second_kernel,
+        functools.partial(second_kernel, 4 + len(widths)),
         grid=(length // tile,),
         in_specs=[
             SCALAR,
@@ -266,14 +285,9 @@
             rows(routes.shape[1]),
         ]
         + anywhere(earlier),
-        out_specs=[rows(model), rows(model), rows(model // 2), rows(1), rows(count)],
-        out_shape=[
-            shape(model),
-            shape(model, jnp.bfloat16),
-            shape(model // 2, jnp.bfloat16),
-            shape(1),
-            shape(count),
-        ],
+        out_specs=[rows(model), rows(model), rows(1), rows(count)] + [rows(w) for w in widths],
+        out_shape=[shape(model), shape(model, jnp.bfloat16), shape(1), shape(count)]
+        + [shape(w, jnp.bfloat16) for w in widths],
         compiler_params=kernel_params(),
         cost_estimate=lasting(9.0),
     )(side, tokens, mine, other, gain, router, routes, *earlier)
@@ -339,21 +353,26 @@
 
 def combine_kernel(width, capacity, line_ref, tab_ref, *refs):
     out_ref = refs[-1]
-    places = tab_ref[0]
-    slot = lax.broadcasted_iota(jnp.int32, (places.shape[0], capacity), 1)
-    total = None
-    for b in range(width):
-        chosen = jnp.where(places[:, b : b + 1] == slot, 1.0, 0.0).astype(jnp.bfloat16)
-        part = dot(chosen, refs[b][0])
-        total = part if total is None else total + part
-    out_ref[0] = total.astype(out_ref.dtype)
+    codes = tab_ref[0]
+    total = width * capacity
+    chosen = []
+    for start in range(0, total, 128):
+        size = min(128, total - start)
+        slot = lax.broadcasted_iota(jnp.int32, (codes.shape[0], size), 1) + start
+        hit = None
+        for b in range(start // capacity, (start + size - 1) // capacity + 1):
+            same = codes[:, b : b + 1] == slot
+            hit = same if hit is None else hit | same
+        chosen.append(jnp.where(hit, 1.0, 0.0).astype(jnp.bfloat16))
+    rows = jnp.concatenate([refs[b][0] for b in range(width)])
+    out_ref[0] = dot(jnp.concatenate(chosen, axis=1), rows).astype(out_ref.dtype)
 
 
 def combine(line, table_columns, came, earlier=()):
     count, length, width = table_columns.shape
     _, capacity, columns = came[0].shape
     if capacity % 16:
-        slot = jnp.arange(capacity, dtype=jnp.int32)
+        slot = jnp.arange(width * capacity, dtype=jnp.int32).reshape(width, capacity)
         chosen = low(table_columns[:, :, :, None] == slot)
         rows = jnp.stack(came)
         total = jnp.einsum("gtbs,bgsd->gtd", chosen, rows, preferred_element_type=jnp.float32)
@@ -370,19 +389,20 @@
         ),
         out_shape=jax.ShapeDtypeStruct((count, length, columns), jnp.bfloat16),
         compiler_params=kernel_params(),
-        cost_estimate=lasting(4.0 * count * columns / 768),
+        cost_estimate=lasting(3.0 * count * columns / 768),
     )(line, table_columns, *came, *earlier)
 
 
-def expert_kernel(chunks, width, me_ref, *refs):
-    x_refs = refs[: 2 * chunks]
-    cm_ref, co_ref, route_ref, wg_ref, wu_ref, wd_ref, wr_ref, *outs = refs[2 * chunks :]
+def expert_kernel(count_in, count_cot, widths, width, me_ref, *refs):
+    x_refs, refs = refs[: 2 * count_in], refs[2 * count_in :]
+    c_refs, refs = refs[: 2 * count_cot], refs[2 * count_cot :]
+    route_ref, wgu_ref, wd_ref, wr_ref, *outs = refs
     pre_ref, act_ref, term_ref = outs[:3]
-    aways = outs[3 : 3 + chunks]
-    homes = outs[3 + chunks :]
+    aways = outs[3 : 3 + len(widths)]
+    homes = outs[3 + len(widths) :]
     side = me_ref[1]
-    batch, _, capacity, half = cm_ref.shape
-    chunk = half // chunks
+    batch, _, capacity, _ = x_refs[0].shape
+    half = sum(ref.shape[3] for ref in x_refs[:count_in])
 
     def flat(ref):
         return ref[...].reshape(batch * capacity, ref.shape[3])
@@ -390,24 +410,30 @@
     def keep(ref, rows):
         ref[...] = rows.reshape(ref.shape).astype(ref.dtype)
 
-    def columns(which, part, size):
-        start = which * half + part * size
-        return pl.ds(pl.multiple_of(start, size), size)
-
-    mine, other = columns(side, 0, half), columns(1 - side, 0, half)
-    spans = [columns(side, c, chunk) for c in range(chunks)]
-    spans += [columns(1 - side, c, chunk) for c in range(chunks)]
-    pieces = [flat(ref) for ref in x_refs]
+    def columns(which, start, size):
+        return pl.ds(pl.multiple_of(which * half + start, 128), size)
+
+    def spans(array_refs):
+        count = len(array_refs) // 2
+        for index, ref in enumerate(array_refs):
+            which = side if index < count else 1 - side
+            start = sum(r.shape[3] for r in array_refs[: index % count])
+            yield flat(ref), columns(which, start, ref.shape[3])
 
     def through(weight_ref):
         total = None
-        for piece, at in zip(pieces, spans):
-            part = dot(piece, weight_ref[at, :])
+        for rows, at in spans(x_refs):
+            part = dot(rows, weight_ref[at, :])
             total = part if total is None else total + part
         return total
 
-    gate_pre, up_pre, logits = through(wg_ref), through(wu_ref), through(wr_ref)
-    raw = dot(flat(cm_ref), wd_ref[:, mine], 1, 1) + dot(flat(co_ref), wd_ref[:, other], 1, 1)
+    both, logits = through(wgu_ref), through(wr_ref)
+    units = both.shape[1] // 2
+    gate_pre, up_pre = both[:, :units], both[:, units:]
+    raw = None
+    for rows, at in spans(c_refs):
+        part = dot(rows, wd_ref[:, at], 1, 1)
+        raw = part if raw is None else raw + part
     chance = routed_softmax(logits, flat(route_ref).astype(jnp.float32).astype(jnp.int32))
     label = lax.broadcasted_iota(jnp.int32, chance.shape, 1)
     gate = jnp.sum(jnp.where(label == me_ref[0], chance, 0.0), axis=1, keepdims=True)
@@ -417,18 +443,17 @@
     keep(term_ref, jnp.sum(act * raw, axis=1, keepdims=True))
     keep(act_ref, act * gate)
     d_act = raw * gate
-    units = act.shape[1]
     d_gate = (d_act * up_pre * sig * (1.0 + gate_pre * (1.0 - sig))).astype(jnp.bfloat16)
     d_up = (d_act * silu).astype(jnp.bfloat16)
-    pre_ref[:, :, :, :units] = d_gate.reshape(batch, 1, capacity, units)
-    pre_ref[:, :, :, units:] = d_up.reshape(batch, 1, capacity, units)
-    for c in range(chunks):
-        at = spans[chunks + c]
-        keep(aways[c], dot(d_gate, wg_ref[at, :], 1, 1) + dot(d_up, wu_ref[at, :], 1, 1))
-        at = spans[c]
-        home = dot(d_gate, wg_ref[at, :], 1, 1) + dot(d_up, wu_ref[at, :], 1, 1)
-        home = home.astype(jnp.bfloat16).reshape(batch, capacity, chunk)
+    d_both = jnp.concatenate([d_gate, d_up], axis=1)
+    keep(pre_ref, d_both)
+    start = 0
+    for c, size in enumerate(widths):
+        keep(aways[c], dot(d_both, wgu_ref[columns(1 - side, start, size), :], 1, 1))
+        home = dot(d_both, wgu_ref[columns(side, start, size), :], 1, 1)
+        home = home.astype(jnp.bfloat16).reshape(batch, capacity, size)
         give_homes(home, homes[c * width : (c + 1) * width])
+        start += size
 
 
 def give_homes(rows, homes):
@@ -451,11 +476,9 @@
     ]
 
 
-def expert_rows(me, pieces, c_mine, c_other, routes, w_gate, w_up, w_down, router):
-    chunks = len(pieces) // 2
-    width, count, capacity, chunk = pieces[0].shape
-    half = c_mine.shape[3]
-    units = w_gate.shape[1]
+def expert_rows(me, pieces, c_pieces, widths, routes, w_both, w_down, router):
+    width, count, capacity, _ = pieces[0].shape
+    units = w_down.shape[0]
     batch = block_batch(width, capacity)
 
     def rows(columns):
@@ -464,34 +487,169 @@
     def shape(columns, kind=jnp.bfloat16):
         return jax.ShapeDtypeStruct((width, count, capacity, columns), kind)
 
+    out_specs = [rows(2 * units), rows(units), rows(1)] + [rows(size) for size in widths]
+    out_shape = [shape(2 * units), shape(units), shape(1, jnp.float32)]
+    out_shape += [shape(size) for size in widths]
+    for size in widths:
+        out_specs += home_specs(width, batch, count, capacity, size)
+        out_shape += [jax.ShapeDtypeStruct((count, capacity, size), jnp.bfloat16)] * width
     outs = pl.pallas_call(
-        functools.partial(expert_kernel, chunks, width),
+        functools.partial(expert_kernel, len(pieces) // 2, len(c_pieces) // 2, widths, width),
         grid=(width // batch, count),
         in_specs=[SCALAR]
-        + [rows(chunk)] * (2 * chunks)
+        + [rows(piece.shape[3]) for piece in (*pieces, *c_pieces)]
         + [
-            rows(half),
-            rows(half),
             rows(routes.shape[3]),
-            whole(w_gate),
-            whole(w_up),
+            whole(w_both),
             whole(w_down),
             whole(router),
         ],
-        out_specs=[rows(2 * units), rows(units), rows(1)]
-        + [rows(chunk)] * chunks
-        + home_specs(width, batch, count, capacity, chunk) * chunks,
-        out_shape=[shape(2 * units), shape(units), shape(1, jnp.float32)]
-        + [shape(chunk)] * chunks
-        + [jax.ShapeDtypeStruct((count, capacity, chunk), jnp.bfloat16)] * (width * chunks),
+        out_specs=out_specs,
+        out_shape=out_shape,
         compiler_params=kernel_params(),
         cost_estimate=lasting(10.0 * count),
-    )(me, *pieces, c_mine, c_other, routes, w_gate, w_up, w_down, router)
-    aways, homes = outs[3 : 3 + chunks], outs[3 + chunks :]
+    )(me, *pieces, *c_pieces, routes, w_both, w_down, router)
+    aways, homes = outs[3 : 3 + len(widths)], outs[3 + len(widths) :]
     return (
         *outs[:3],
-        [(aways[c], homes[c * width : (c + 1) * width]) for c in range(chunks)],
-    )
+        [(aways[c], homes[c * width : (c + 1) * width]) for c in range(len(widths))],
+    )
+
+
+def pile_kernel(count, *refs):
+    blocks, out_ref = refs[:count], refs[-1]
+    for b in range(count):
+        out_ref[b] = blocks[b][...]
+
+
+def pile(blocks, earlier):
+    slots, capacity, columns = blocks[0].shape
+    count = len(blocks)
+    return pl.pallas_call(
+        functools.partial(pile_kernel, count),
+        grid=(slots,),
+        in_specs=[pl.BlockSpec((1, capacity, columns), lambda g: (g, 0, 0))] * count
+        + anywhere(earlier),
+        out_specs=pl.BlockSpec((count, 1, capacity, columns), lambda g: (0, g, 0, 0)),
+        out_shape=jax.ShapeDtypeStruct((count, slots, capacity, columns), blocks[0].dtype),
+        compiler_params=kernel_params(),
+        cost_estimate=lasting(5.0),
+    )(*blocks, *earlier)
+
+
+def join_kernel(count, *refs):
+    homes, swapped_ref, outs = refs[:count], refs[count], refs[len(refs) - count :]
+    for b in range(count):
+        total = homes[b][...].astype(jnp.float32) + swapped_ref[b].astype(jnp.float32)
+        outs[b][...] = total.astype(jnp.bfloat16)
+
+
+def join_cores(homes, swapped, earlier):
+    slots, capacity, columns = homes[0].shape
+    count = len(homes)
+    block = pl.BlockSpec((1, capacity, columns), lambda g: (g, 0, 0))
+    return pl.pallas_call(
+        functools.partial(join_kernel, count),
+        grid=(slots,),
+        in_specs=[block] * count
+        + [pl.BlockSpec((count, 1, capacity, columns), lambda g: (0, g, 0, 0))]
+        + anywhere(earlier),
+        out_specs=[block] * count,
+        out_shape=[jax.ShapeDtypeStruct(homes[0].shape, jnp.bfloat16)] * count,
+        compiler_params=kernel_params(),
+        cost_estimate=lasting(7.0),
+    )(*homes, swapped, *earlier)
+
+
+def settle_kernel(pieces, side_ref, *refs):
+    halves, refs = refs[: 2 * pieces], refs[2 * pieces :]
+    hid_ref, inv_ref, cot_ref, gate_ref, term_ref, router_ref, gain_ref = refs[:7]
+    dh_ref, db_ref, dl_ref, gg_ref = refs[-4:]
+    gates, terms = gate_ref[...], term_ref[...]
+    d_logits = gates * (terms - jnp.sum(gates * terms, axis=1, keepdims=True))
+    d_logits = d_logits.astype(jnp.bfloat16)
+    dl_ref[...] = jnp.zeros_like(dl_ref)
+    dl_ref[:, : d_logits.shape[1]] = d_logits
+    mine = jnp.concatenate([ref[...] for ref in halves[:pieces]], axis=1)
+    other = jnp.concatenate([ref[...] for ref in halves[pieces:]], axis=1)
+    first = side_ref[0] == 0
+    rows = jnp.concatenate([jnp.where(first, mine, other), jnp.where(first, other, mine)], axis=1)
+    d_second = rows.astype(jnp.float32) + dot(d_logits, router_ref[...], 1, 1)
+    inverse = inv_ref[...]
+    normed = hid_ref[...] * inverse
+    scaled = d_second * gain_ref[...]
+    gain_grad = jnp.sum(d_second * normed, axis=0, keepdims=True)
+
+    @pl.when(pl.program_id(0) == 0)
+    def _():
+        gg_ref[...] = gain_grad
+
+    @pl.when(pl.program_id(0) > 0)
+    def _():
+        gg_ref[...] += gain_grad
+
+    center = jnp.mean(scaled * normed, axis=1, keepdims=True)
+    d_hidden = cot_ref[...].astype(jnp.float32) + inverse * (scaled - normed * center)
+    dh_ref[...] = d_hidden
+    db_ref[...] = d_hidden.astype(jnp.bfloat16)
+
+
+def settle(
+    side, mine, other, hidden, inverse, cotangent, gates, terms, router, gain, tile, earlier
+):
+    length, model = hidden.shape
+    count = router.shape[1]
+    padded = count + 128 - count % 128
+
+    def rows(columns):
+        return pl.BlockSpec((tile, columns), lambda i: (i, 0))
+
+    def shape(columns, kind=jnp.float32):
+        return jax.ShapeDtypeStruct((length, columns), kind)
+
+    return pl.pallas_call(
+        functools.partial(settle_kernel, len(mine)),
+        grid=(length // tile,),
+        in_specs=[SCALAR]
+        + [rows(piece.shape[1]) for piece in (*mine, *other)]
+        + [rows(model), rows(1), rows(model), rows(count), rows(count), whole(router), whole(gain)]
+        + anywhere(earlier),
+        out_specs=[rows(model), rows(model), rows(padded), whole(gain)],
+        out_shape=[
+            shape(model),
+            shape(model, jnp.bfloat16),
+            shape(padded, jnp.bfloat16),
+            jax.ShapeDtypeStruct(gain.shape, jnp.float32),
+        ],
+        compiler_params=kernel_params(),
+        cost_estimate=lasting(10.0),
+    )(side, *mine, *other, hidden, inverse, cotangent, gates, terms, router, gain, *earlier)
+
+
+def finish_kernel(a_ref, b_ref, x_ref, inv_ref, dh_ref, gain_ref, out_ref):
+    d_first = a_ref[...].astype(jnp.float32) + b_ref[...].astype(jnp.float32)
+    inverse = inv_ref[...]
+    normed = x_ref[...].astype(jnp.float32) * inverse
+    scaled = d_first * gain_ref[...]
+    center = jnp.mean(scaled * normed, axis=1, keepdims=True)
+    out_ref[...] = dh_ref[...] + inverse * (scaled - normed * center)
+
+
+def finish(mine, other, tokens, inverse, d_hidden, gain, tile):
+    length, model = tokens.shape
+
+    def rows(columns):
+        return pl.BlockSpec((tile, columns), lambda i: (i, 0))
+
+    return pl.pallas_call(
+        finish_kernel,
+        grid=(length // tile,),
+        in_specs=[rows(model), rows(model), rows(model), rows(1), rows(model), whole(gain)],
+        out_specs=rows(model),
+        out_shape=jax.ShapeDtypeStruct((length, model), jnp.float32),
+        compiler_params=kernel_params(),
+        cost_estimate=lasting(8.0),
+    )(mine, other, tokens, inverse, d_hidden, gain)
 
 
 def home_block(k, count, b, g):
@@ -555,6 +713,10 @@
     here = pl.ds(pl.multiple_of(step * tile, tile), tile)
     cosine, sine = cos_ref[here, :], sin_ref[here, :]
     keys_t = keys.T
+
+    def put(rows, start, array):
+        out_ref[rows, start : start + size] = array.astype(jnp.bfloat16)
+
     d_mixed = dot(db_ref[...], wo_ref[...], 1, 1).astype(jnp.bfloat16)
     dk_total = jnp.zeros(keys.shape, jnp.float32)
     dv_total = jnp.zeros(keys.shape, jnp.float32)
@@ -571,7 +733,7 @@
         dv_total = dv_total + dot(probs.astype(jnp.bfloat16), d_head)
         dk_total = dk_total + dot(d_scores, query)
         d_query = dot(keys_t, d_scores).T
-        out_ref[here, span] = turn(d_query, cosine, -sine).astype(jnp.bfloat16)
+        put(here, head * size, turn(d_query, cosine, -sine))
 
     @pl.when(step == 0)
     def _():
@@ -586,9 +748,8 @@
     @pl.when(step == pl.num_programs(0) - 1)
     def _():
         base = heads * size
-        turned = turn(dk_ref[...], cos_ref[...], -sin_ref[...])
-        out_ref[:, base : base + size] = turned.astype(jnp.bfloat16)
-        out_ref[:, base + size : base + 2 * size] = dv_ref[...].astype(jnp.bfloat16)
+        put(slice(None), base, turn(dk_ref[...], cos_ref[...], -sin_ref[...]))
+        put(slice(None), base + size, dv_ref[...])
 
 
 def attend_back(
@@ -652,6 +813,58 @@
     )(d_all, w_query, w_key, w_value, *earlier)
 
 
+def share_kernel(width, rows, extra, spot_ref, left_ref, right_ref, *refs):
+    kept_ref, *gone = refs[3 * extra : 3 * extra + width]
+    hold_ref = refs[3 * extra + width]
+    products = [(0, dot(left_ref[...], right_ref[...], 0, 0))]
+    if extra:
+        also_ref, picks_ref, row_ref = refs[:3]
+        column = jnp.broadcast_to(row_ref[...], (8, row_ref.shape[1])).T[:, :1]
+        more = dot(also_ref[...], picks_ref[...], 0, 0)
+        lane = lax.broadcasted_iota(jnp.int32, more.shape, 1)
+        last = more.shape[1] - 1
+        products.append((right_ref.shape[1], jnp.where(lane == last, column, more)))
+    for start, product in products:
+        for s in range(width):
+            part = product[s * rows : (s + 1) * rows]
+            hold_ref[s, :, start : start + product.shape[1]] = part
+    kept_ref[0] = hold_ref[spot_ref[0]]
+    for b in range(1, width):
+        gone[b - 1][0] = hold_ref[spot_ref[0] ^ b].astype(jnp.bfloat16)
+
+
+def share_grads(spot, left, right, depth, width, extra=()):
+    length, model = left.shape
+    columns = right.shape[1] + (extra[1].shape[1] if extra else 0)
+    rows = model // (depth * width)
+    if (width * rows) % 128:
+        product = dot(left, right, 0, 0)
+        if extra:
+            more = jnp.concatenate([dot(extra[0], extra[1], 0, 0)[:, :-1], extra[2].T], axis=1)
+            product = jnp.concatenate([product, more], axis=1)
+        parted = product.reshape(depth, width, rows, columns)
+        blocks = [
+            lax.dynamic_index_in_dim(parted, spot[0] ^ b, 1, keepdims=False) for b in range(width)
+        ]
+        return [blocks[0]] + [low(block) for block in blocks[1:]]
+    block = pl.BlockSpec((1, rows, columns), lambda l: (l, 0, 0))
+    stripe = pl.BlockSpec((length, width * rows), lambda l: (0, l))
+    more_specs = []
+    if extra:
+        more_specs = [stripe, whole(extra[1]), pl.BlockSpec((1, width * rows), lambda l: (0, l))]
+    return pl.pallas_call(
+        functools.partial(share_kernel, width, rows, int(bool(extra))),
+        grid=(depth,),
+        in_specs=[SCALAR, stripe, whole(right)] + more_specs,
+        out_specs=[block] * width,
+        out_shape=[jax.ShapeDtypeStruct((depth, rows, columns), jnp.float32)]
+        + [jax.ShapeDtypeStruct((depth, rows, columns), jnp.bfloat16)] * (width - 1),
+        scratch_shapes=[pltpu.VMEM((width, rows, columns), jnp.float32)],
+        compiler_params=kernel_params(),
+        cost_estimate=lasting(6.0),
+    )(spot, left, right, *extra)
+
+
 class Exchange:
     def __init__(self, count):
         self.count = count
@@ -676,18 +889,13 @@
     def plane(self, blocks):
         return [blocks[0]] + [self.flip(blocks[b], b) for b in range(1, self.width)]
 
-    def scatter_sum(self, grads):
-        rows = grads.shape[0] // self.count
-        held = grads.reshape(self.count, rows, grads.shape[1])
-        blocks, bit = self.count, 1
-        while bit < self.width:
-            parted = held.reshape(blocks // 2, 2, rows, -1)
-            side = (self.me // bit) % 2
-            kept = lax.dynamic_index_in_dim(parted, side, 1, keepdims=False)
-            gone = lax.dynamic_index_in_dim(parted, 1 - side, 1, keepdims=False)
-            came = self.flip(gone.astype(jnp.bfloat16), bit)
-            held = kept.astype(jnp.float32) + came.astype(jnp.float32)
-            blocks, bit = blocks // 2, bit * 2
+    def sum_plane(self, blocks):
+        held = wide(blocks[0])
+        for b in range(1, self.width):
+            held = held + wide(self.flip(blocks[b], b))
+        return held
+
+    def sum_line(self, held):
         total = lax.dynamic_index_in_dim(held, self.line, 0, keepdims=False)
         for g in range(1, self.depth):
             part = lax.dynamic_index_in_dim(held, self.line ^ g, 0, keepdims=False)
@@ -747,13 +955,13 @@
     tile = 256
     link = Exchange(expert_count)
     depth, width = link.depth, link.width
-    chunks = 2
-    chunk_width = half_width // chunks
     side = lax.axis_index("tensor")
     side_ref = side.astype(jnp.int32)[None]
     me_ref = jnp.stack([link.me, side]).astype(jnp.int32)
     line_ref = link.line.astype(jnp.int32)[None]
 
+    third = half_width // 3
+    widths = (2 * third, third)
     cot_slots = link.spread(half_of(cotangent, side))
     placed = place_table(routes, order[0], link.me, expert_count, capacity)
     tables = []
@@ -762,8 +970,15 @@
         tables.append(table if g == 0 else link.flip(table, g * width))
     places = jnp.stack([table[:width] for table in tables])
     place_rows = places[:, :, None, :]
-    place_columns = jnp.stack([table[:width].T for table in tables])
+    starts = capacity * jnp.arange(width, dtype=jnp.int32)
+    place_columns = jnp.where(places >= 0, places + starts[None, :, None], -1)
+    place_columns = jnp.swapaxes(place_columns, 1, 2)
     route_columns = jnp.stack([low(table[width:].T) for table in tables])
+
+    route_blocks = link.plane(
+        pick_rows(jnp.zeros_like(line_ref), place_rows, route_columns, capacity)
+    )
+    route_rows = jnp.stack(route_blocks)
 
     cosine, sine = (jnp.asarray(t) for t in rope_constants(seq_length, head_width))
     first_in, query, keys, values, inverse_first = project(
@@ -773,7 +988,7 @@
     mixed, lse, branch = attend(
         query, keys, values, seg_row, seg_col, w_out, score_scale, tile
     )
-    hidden, second_in, in_half, inverse_second, gates = second_norm(
+    hidden, second_in, inverse_second, gates, *in_parts = second_norm(
         side_ref,
         tokens,
         branch,
@@ -782,36 +997,57 @@
         w_router,
         routes,
         tile,
-        (),
-    )
-
-    def to_expert(blocks):
-        mine = jnp.stack(link.plane(blocks))
-        return mine, swap(mine)
-
-    in_slots = [
-        link.spread(in_half[:, c * chunk_width : (c + 1) * chunk_width]) for c in range(chunks)
-    ]
-    picked = pick_rows(line_ref, place_rows, cot_slots, capacity, route_columns, (in_half,))
-    cot_mine, cot_other = to_expert(picked[:width])
-    route_rows = jnp.stack(link.plane(picked[width:]))
-    in_rows = [
-        to_expert(pick_rows(line_ref, place_rows, slots, capacity)) for slots in in_slots
-    ]
-    pieces = [rows[0] for rows in in_rows] + [rows[1] for rows in in_rows]
+        widths,
+        (place_rows, *route_blocks[1:]),
+    )
+    w_both = jnp.concatenate([w_gate[0], w_up[0]], axis=1)
+    in_slots = [link.spread(hold(in_parts[0], cot_slots))]
+    cot_blocks = pick_rows(line_ref, place_rows, cot_slots, capacity, None, (second_in, w_both))
+    cot_came = link.plane(cot_blocks)
+    in_slots.append(link.spread(hold(in_parts[1], in_slots[0], *cot_came[1:])))
+    in_first = pick_rows(line_ref, place_rows, in_slots[0], capacity)
+    in_came = [link.plane(in_first)]
+    in_last = pick_rows(line_ref, place_rows, in_slots[1], capacity, None, in_came[0][1:])
+    in_came.append(link.plane(in_last))
+    cot_mine = pile(cot_came, in_last[1:])
+    cot_other = swap(cot_mine)
+    in_mine = [pile(in_came[0], (cot_mine,))]
+    in_other = [swap(in_mine[0])]
+    in_mine.append(pile(in_came[1], (in_other[0], cot_other)))
+    in_other.append(swap(in_mine[1]))
+    pieces, c_pieces = in_mine + in_other, [cot_mine, cot_other]
 
     pre, acts, terms, backs = expert_rows(
-        me_ref, pieces, cot_mine, cot_other, route_rows, w_gate[0], w_up[0], w_down[0], w_router
-    )
-    terms = terms[..., 0]
-
-    def to_token(away, homes):
-        swapped = swap(away)
-        return link.plane([low(wide(homes[b]) + wide(swapped[b])) for b in range(width)])
-
-    came_back = [to_token(away, homes) for away, homes in backs]
-
+        me_ref, pieces, c_pieces, widths, route_rows, w_both, w_down[0], w_router
+    )
+    swapped = [swap(away) for away, _ in backs]
+    first_came = link.plane(join_cores(backs[0][1], swapped[0], ()))
+    out_away, *out_homes = down_rows(me_ref, acts, w_down[0], ())
+    terms = hold(terms, out_away)[..., 0]
     terms = jnp.stack(link.plane([terms[b] for b in range(width)]), axis=1)
+    blocks = join_cores(backs[1][1], swapped[1], (*first_came[1:], out_away))
+    row_parts = [combine(line_ref, place_columns, first_came, blocks[1:])]
+    came = link.plane(blocks)
+    row_parts.append(combine(line_ref, place_columns, came, (row_parts[0],)))
+    out_blocks = join_cores(out_homes, swap(out_away), (row_parts[1], terms))
+    out_came = link.plane(out_blocks)
+    row_mine = [hold(link.collect(row_parts[0]), *out_blocks[1:])]
+    row_mine.append(link.collect(hold(row_parts[1], row_mine[0])))
+    row_other = [swap(part) for part in row_mine]
+
+    act_rows = hold(acts, *out_blocks[1:]).reshape(-1, unit_count)
+    grads = [contract_rows(act_rows, piece.reshape(-1, piece.shape[3])) for piece in c_pieces]
+    down_grad = join_halves(
+        *grads, side
+    )[None]
+    pre = hold(pre, *out_blocks[1:]).reshape(-1, 2 * unit_count)
+    grads = [contract_rows(piece.reshape(-1, piece.shape[3]), pre) for piece in pieces]
+    first, last = jnp.concatenate(grads[:2]), jnp.concatenate(grads[2:])
+    upper, lower = jnp.where(side == 0, first, last), jnp.where(side == 0, last, first)
+    gate_grad = jnp.concatenate([upper[:, :unit_count], lower[:, :unit_count]])[None]
+    up_grad = jnp.concatenate([upper[:, unit_count:], lower[:, unit_count:]])[None]
+
+    terms = hold(terms, *out_blocks[1:])
     slot_ids = jnp.arange(capacity, dtype=jnp.int32)
     local = jnp.sum(
         jnp.where(
@@ -825,52 +1061,28 @@
     term_table = term_table + swap(term_table)
     term_table = term_table[jnp.arange(expert_count, dtype=jnp.int32) ^ link.me].T
 
-    row_half = jnp.concatenate(
-        [link.collect(combine(line_ref, place_columns, came)) for came in came_back], axis=1
-    )
-    row_total = wide(join_halves(row_half, swap(row_half), side))
-
-    arrived = [block for came in came_back for block in came]
-    away, *homes = down_rows(me_ref, acts, w_down[0], arrived)
-    out_came = to_token(away, homes)
-    out_parts = combine(line_ref, place_columns, out_came, (row_half,))
-    combined = wide(link.collect(out_parts))
-    output_half = low(half_of(hidden, side) + combined)
-    output = join_halves(output_half, swap(output_half), side)
-
-    pre = pre.reshape(-1, 2 * unit_count)
-    grads = [contract_rows(piece.reshape(-1, chunk_width), pre) for piece in pieces]
-    first, second = grads[:chunks], grads[chunks:]
-    joined = [jnp.where(side == 0, a, b) for a, b in zip(first + second, second + first)]
-    gate_grad = jnp.concatenate([part[:, :unit_count] for part in joined])[None]
-    up_grad = jnp.concatenate([part[:, unit_count:] for part in joined])[None]
-    act_rows = acts.reshape(-1, unit_count)
-    down_grad = join_halves(
-        contract_rows(act_rows, cot_mine.reshape(-1, half_width)),
-        contract_rows(act_rows, cot_other.reshape(-1, half_width)),
-        side,
-    )[None]
-
-    upstream = wide(cotangent)
-    normed_second = hidden * inverse_second
-    d_logits = low(
-        gates * (term_table - jnp.sum(gates * term_table, axis=-1, keepdims=True))
-    )
-    router_grad = contract_rows(second_in, d_logits)
-    d_second = row_total + times_transposed(d_logits, w_router)
-    scaled_second = d_second * ffn_gain
-    ffn_gain_grad = jnp.sum(d_second * normed_second, axis=0)
-    d_hidden = upstream + inverse_second * (
-        scaled_second
-        - normed_second * jnp.mean(scaled_second * normed_second, axis=-1, keepdims=True)
-    )
-    d_branch = low(d_hidden)
-    pad = jnp.zeros((model_width, -(expert_count + 1) % 128), jnp.float32)
-    early = jnp.concatenate(
-        [contract_rows(d_branch, mixed), router_grad, ffn_gain_grad[:, None], pad], axis=1
-    )
-    early = link.scatter_sum(early)
-    out_grad, small = early[:, :span].T, early[:, span:]
+    d_hidden, d_branch, d_logits, ffn_gain_grad = settle(
+        side_ref,
+        row_mine,
+        row_other,
+        hidden,
+        inverse_second,
+        cotangent,
+        gates,
+        term_table,
+        w_router,
+        ffn_gain[None],
+        tile,
+        (down_grad, gate_grad, up_grad),
+    )
+
+    out_parts = combine(line_ref, place_columns, out_came, (d_branch,))
+    out_held = hold(out_parts, row_mine[1])
+    spot_ref = (link.me % width).astype(jnp.int32)[None]
+    shared_early = share_grads(
+        spot_ref, d_branch, mixed, depth, width, (second_in, d_logits, ffn_gain_grad)
+    )
+    early_held = link.sum_plane(shared_early)
 
     d_all = attend_back(
         query,
@@ -885,16 +1097,22 @@
         sine,
         score_scale,
         tile,
-        (out_parts,),
-    )
-    d_first = first_grad(d_all, w_query, w_key, w_value, tile, ())
-    qkv_grad = link.scatter_sum(contract_rows(first_in, d_all))
-    d_first = wide(d_first) + wide(swap(d_first))
-    normed_first = wide(tokens) * inverse_first
-    scaled_first = d_first * norm_gain
-    input_grad = d_hidden + inverse_first * (
-        scaled_first - normed_first * jnp.mean(scaled_first * normed_first, axis=-1, keepdims=True)
-    )
+        (*shared_early[1:], out_held),
+    )
+    d_first = first_grad(d_all, w_query, w_key, w_value, tile, (early_held,))
+    input_grad = finish(
+        d_first, swap(d_first), tokens, inverse_first, d_hidden, norm_gain[None], tile
+    )
+    shared = share_grads(spot_ref, first_in, hold(d_all, d_first), depth, width)
+    shared = [hold(shared[0], input_grad), *shared[1:]]
+    summed = link.sum_line(jnp.concatenate([link.sum_plane(shared), early_held], axis=2))
+    columns = span + 2 * head_width
+    qkv_grad, early_sum = summed[:, :columns], summed[:, columns:]
+    out_grad = early_sum[:, :span].T
+    router_grad, ffn_gain_grad = early_sum[:, span : span + expert_count], early_sum[:, -1]
+    combined = wide(hold(link.collect(out_held), qkv_grad))
+    output_half = low(half_of(hidden, side) + combined)
+    output = join_halves(output_half, swap(output_half), side)
     rows = model_width // expert_count
     gain_part = jnp.zeros((rows,), jnp.float32)
     start = 0
@@ -909,12 +1127,12 @@
         output,
         input_grad,
         norm_gain_grad,
-        small[:, expert_count],
+        ffn_gain_grad,
         qkv_grad[:, :span],
         qkv_grad[:, span : span + head_width],
         qkv_grad[:, span + head_width :],
         out_grad,
-        small[:, :expert_count],
+        router_grad,
         gate_grad,
         up_grad,
         down_grad,

time: 853 us -> 816 us (0.957)
  Pallas kernels: 227 us -> 277 us
  other arithmetic: 77.1 us -> 35.2 us
  waiting for transfers between devices: 365 us -> 330 us
  matrix products: 52.4 us -> 37.8 us
    pallas_call x2 -> x24, Pallas kernels: 67.4 us -> 126 us  [the longest x1 44.7 us: expert_rows(): pl.pallas_call(functools.partial(expert_kernel, len(pieces) // 2, len(c_p...]
    all_gather x3, waiting for transfers between devices: 58 us -> 28.2 us  [spread(): return lax.all_gather(rows, 'expert', axis_index_groups=self.lines)]
    convert_element_type x6 -> x2, other arithmetic: 26.9 us -> 3.8 us  [low(): return array.astype(jnp.bfloat16)]
    unnamed x154 -> x101, local copies, waits for them, and re-layouts: 13 us -> 23.7 us
    pallas_call x3, Pallas kernels: 38.7 us -> 29.4 us  [combine(): pl.pallas_call(functools.partial(combine_kernel, width, capacity), grid_s...]
    dot_general x9 -> x6, matrix products: 46.2 us -> 37.8 us  [contract_rows(): lax.dot_general(left, right, (((0,), (0,)), ((), ())), preferred_element_...]
    ppermute x40 -> x39, waiting for transfers between devices: 293 us -> 287 us  [flip(): lax.ppermute(rows, 'expert', [(d, d ^ mask) for d in range(self.count)])]
    ppermute x40 -> x39, starting transfers between devices: 42.1 us -> 43.7 us  [flip(): lax.ppermute(rows, 'expert', [(d, d ^ mask) for d in range(self.count)])]
  transfers between devices with their start and end apart: 58 -> 58, of which waited for: 34 -> 32; matrix products, arithmetic and copies ran while one was open for 19% -> 11% of each run, Pallas kernels for 20% -> 25%
where the time goes in v3:
time: 816 us; the launch traced here: 805 us
  waiting for transfers between devices  330 us (40%)
  Pallas kernels  277 us (34%)
  starting transfers between devices  66.1 us (8%)
  local copies, waits for them, and re-layouts  43.5 us (5%)
  matrix products  37.8 us (5%)
  other arithmetic  35.2 us (4%)
  between operations  14.9 us (2%)
    ppermute x39, waiting for transfers between devices, flip(): lax.ppermute(rows, 'expert', [(d, d ^ mask) for d in range(self.count)])  287 us
    pallas_call x1, Pallas kernels, expert_rows(): pl.pallas_call(functools.partial(expert_kernel, len(pieces) // 2, len(c_p...  44.7 us
    ppermute x39, starting transfers between devices, flip(): lax.ppermute(rows, 'expert', [(d, d ^ mask) for d in range(self.count)])  43.7 us
    dot_general x6, matrix products, contract_rows(): lax.dot_general(left, right, (((0,), (0,)), ((), ())), preferred_element_...  37.8 us
    pallas_call x3, Pallas kernels, combine(): pl.pallas_call(functools.partial(combine_kernel, width, capacity), grid_s...  29.4 us
    pallas_call x1, Pallas kernels, attend_back(): pl.pallas_call(functools.partial(attend_back_kernel, heads, scale, tile),...  29.4 us
    pallas_call x4, Pallas kernels, pick_rows(): pl.pallas_call(functools.partial(pick_kernel, width, capacity, len(out_sh...  29.2 us
    all_gather x3, waiting for transfers between devices, spread(): return lax.all_gather(rows, 'expert', axis_index_groups=self.lines)  28.2 us
  transfers between devices with their start and end apart: 58, of which 32 were waited for; matrix products, arithmetic and copies ran while one was open for 11% of the time, Pallas kernels for 25%

profile of v3, /device:TPU:9, one launch (start us, length us, event | category | flops | bytes accessed | tf_op | source)
XLA Modules:
  0.0 804.9 jit_solution(243737072161190777)
XLA Ops:
  7.3 2.7 constant_dynamic-slice_fusion
  11.7 9.0 %shard_map.256 = (bf16[1024,1536]{1,0:T(8,128)(2,1)}, bf16[1024,768]{1,0:T(8,128)(2,1)}, bf16[1024,128]{1,0:T(8,128)(2,1)}, bf16[1024,128]{1,0:T(8,128)(2,1)}, f32[1024,1]{1,0:T(8,128)}) custom-call(bf16[1024,1536]{1,0:T(8,128)(2,1)} %x_ref.5, f32[1,1536]{1,0:T(1,128)} %broadcast_in_dim.70.gain_ref, bf16[1536,768]{1,0:T(8,128)(2,1)} %wq_ref.3, ...), custom_call_target="tpu_custom_call" | custom-call | flops 9000000 | bytes 1024 | tf_op jit(solution)/shard_map/pallas_call | solution.py:161
  20.7 24.1 %shard_map.257 = (bf16[1024,768]{1,0:T(8,128)(2,1)}, f32[6,1024]{1,0:T(8,128)}, bf16[1024,1536]{1,0:T(8,128)(2,1)}) custom-call(bf16[1024,768]{1,0:T(8,128)(2,1)} %get-tuple-element.84.q_ref, bf16[1024,128]{1,0:T(8,128)(2,1)} %get-tuple-element.85.k_ref, bf16[1024,128]{1,0:T(8,128)(2,1)} %get-tuple-element.86.v_ref, s32[1,1024]{1,0:T(1,128)} %segq_ref.3, ...), custom_call_target="tpu_custom_call" | custom-call | flops 20000000 | bytes 1024 | tf_op jit(solution)/shard_map/pallas_call | solution.py:206
  48.9 8.9 %shard_map.258 = s32[16,1024]{1,0:T(8,128)} custom-call(s32[16,1024]{1,0:T(8,128)} %compare_select_fusion.keys_ref), custom_call_target="tpu_custom_call" | custom-call | flops 9000000 | bytes 1024 | tf_op jit(solution)/shard_map/pallas_call | solution.py:117
  58.7 2.5 collective-permute-start.2
  69.5 5.4 shard_map.259
  81.2 3.7 collective-permute-done.5.refs_2_
  87.9 9.9 %shard_map.260 = (f32[1024,1536]{1,0:T(8,128)}, bf16[1024,1536]{1,0:T(8,128)(2,1)}, f32[1024,1]{1,0:T(8,128)}, f32[1024,16]{1,0:T(8,128)}, bf16[1024,512]{1,0:T(8,128)(2,1)}, /*index=5*/bf16[1024,256]{1,0:T(8,128)(2,1)}) custom-call(s32[1]{0:T(128)} %bitcast.side_ref, bf16[1024,1536]{1,0:T(8,128)(2,1)} %x_ref.5, bf16[1024,1536]{1,0:T(8,128)(2,1)} %get-tuple-element.87.a_ref, ...), custom_call_target="tpu_custom_call" | custom-call | flops 9000000 | bytes 1024 | tf_op jit(solution)/shard_map/pallas_call | solution.py:275
  97.8 28.1 %all-gather.7.cloned.1.call-done = bf16[4096,768]{1,0:T(8,128)(2,1)} async-done(((bf16[1024,768]{1,0:T(8,128)(2,1)}), bf16[4096,768]{1,0:T(8,128)(2,1)}) %all-gather.7.cloned.1.call-update) | async-done | bytes 6291472 | tf_op jit(solution)/shard_map/all_gather | solution.py:881
  129.2 10.6 %shard_map.263 = (bf16[4,288,768]{2,1,0:T(8,128)(2,1)}, bf16[4,288,768]{2,1,0:T(8,128)(2,1)}, bf16[4,288,768]{2,1,0:T(8,128)(2,1)}, bf16[4,288,768]{2,1,0:T(8,128)(2,1)}) custom-call(s32[1]{0:T(128)} %bitcast.16.line_ref, s32[4,4,1,1024]{3,2,1,0:T(1,128)} %broadcast_in_dim.75.tab_ref.refs_0_, bf16[4,1024,768]{2,1,0:T(8,128)(2,1)} %bitcast.125, ...), custom_call_target="tpu_custom_call" | custom-call | flops 12000000 | bytes 1024 | tf_op jit(solution)/shard_map/pallas_call | solution.py:340
  142.4 37.2 %collective-permute-done.10.refs_2_.refs_1_ = bf16[4,288,768]{2,1,0:T(8,128)(2,1)S(1)} collective-permute-done((bf16[4,288,768]{2,1,0:T(8,128)(2,1)}, bf16[4,288,768]{2,1,0:T(8,128)(2,1)S(1)}, u32[]{:S(2)}, u32[]{:S(2)}) %collective-permute-start.10) | collective-permute-done | bytes 1769504 | tf_op jit(solution)/shard_map/ppermute | solution.py:878
  180.4 38.1 %collective-permute-done.12.refs_4_.refs_3_ = bf16[4,288,768]{2,1,0:T(8,128)(2,1)} collective-permute-done((bf16[4,288,768]{2,1,0:T(8,128)(2,1)}, bf16[4,288,768]{2,1,0:T(8,128)(2,1)}, u32[]{:S(2)}, u32[]{:S(2)}) %collective-permute-start.12) | collective-permute-done | bytes 1769504 | tf_op jit(solution)/shard_map/ppermute | solution.py:878
  218.6 7.9 shard_map.262
  229.2 22.5 %collective-permute-done.7.refs_0_.refs_1_ = bf16[4,288,512]{2,1,0:T(8,128)(2,1)S(1)} collective-permute-done((bf16[4,288,512]{2,1,0:T(8,128)(2,1)}, bf16[4,288,512]{2,1,0:T(8,128)(2,1)S(1)}, u32[]{:S(2)}, u32[]{:S(2)}) %collective-permute-start.7) | collective-permute-done | bytes 1179680 | tf_op jit(solution)/shard_map/ppermute | solution.py:878
  251.7 4.8 collective-permute-done.8.refs_1_.refs_2_
  256.5 20.4 %collective-permute-done.9.refs_2_.refs_3_ = bf16[4,288,512]{2,1,0:T(8,128)(2,1)} collective-permute-done((bf16[4,288,512]{2,1,0:T(8,128)(2,1)}, bf16[4,288,512]{2,1,0:T(8,128)(2,1)}, u32[]{:S(2)}, u32[]{:S(2)}) %collective-permute-start.9) | collective-permute-done | bytes 1179680 | tf_op jit(solution)/shard_map/ppermute | solution.py:878
  277.0 5.3 shard_map.265
  282.3 6.3 shard_map.266.refs_4_
  288.6 5.6 collective-permute-start.17
  294.2 5.0 shard_map.267.refs_0_
  301.9 12.0 %collective-permute-done.13.refs_1_ = bf16[4,288,256]{2,1,0:T(8,128)(2,1)S(1)} collective-permute-done((bf16[4,288,256]{2,1,0:T(8,128)(2,1)}, bf16[4,288,256]{2,1,0:T(8,128)(2,1)S(1)}, u32[]{:S(2)}, u32[]{:S(2)}) %collective-permute-start.13) | collective-permute-done | bytes 589856 | tf_op jit(solution)/shard_map/ppermute | solution.py:878
  313.9 12.7 %collective-permute-done.15.refs_3_ = bf16[4,288,256]{2,1,0:T(8,128)(2,1)S(1)} collective-permute-done((bf16[4,288,256]{2,1,0:T(8,128)(2,1)S(1)}, bf16[4,288,256]{2,1,0:T(8,128)(2,1)S(1)}, u32[]{:S(2)}, u32[]{:S(2)}) %collective-permute-start.15) | collective-permute-done | bytes 589856 | tf_op jit(solution)/shard_map/ppermute | solution.py:878
  329.0 2.9 copy-done.1
  331.9 4.0 shard_map.268.refs_1_
  343.0 44.7 %shard_map.269 = (bf16[4,4,288,768]{3,2,1,0:T(8,128)(2,1)}, bf16[4,4,288,384]{3,2,1,0:T(8,128)(2,1)}, f32[4,4,288,1]{3,2,1,0:T(8,128)}, bf16[4,4,288,512]{3,2,1,...) custom-call(s32[2]{0:T(128)} %pad_add_fusion.4.me_ref, ...), custom_call_target="tpu_custom_call" | custom-call | flops 40000000 | bytes 1024 | tf_op jit(solution)/shard_map/pallas_call | solution.py:496
  388.2 13.2 %shard_map.270 = (bf16[4,4,288,768]{3,2,1,0:T(8,128)(2,1)}, bf16[4,288,768]{2,1,0:T(8,128)(2,1)}, bf16[4,288,768]{2,1,0:T(8,128)(2,1)}, bf16[4,288,768]{2,1,0:T(8,128)(2,1)}, bf16[4,288,768]{2,1,0:T(8,128)(2,1)}) custom-call(s32[2]{0:T(128)} %pad_add_fusion.4.me_ref, bf16[4,4,288,384]{3,2,1,0:T(8,128)(2,1)} %get-tuple-element.108.act_ref.refs_0_, ...), custom_call_target="tpu_custom_call" | custom-call | flops 12000000 | bytes 1024 | tf_op jit(solution)/shard_map/pallas_call | solution.py:679
  404.0 6.4 shard_map.271
  413.1 2.9 copy.135
  416.4 21.7 %collective-permute-done.22.refs_5_.refs_1_ = bf16[4,288,512]{2,1,0:T(8,128)(2,1)S(1)} collective-permute-done((bf16[4,288,512]{2,1,0:T(8,128)(2,1)}, bf16[4,288,512]{2,1,0:T(8,128)(2,1)S(1)}, u32[]{:S(2)}, u32[]{:S(2)}) %collective-permute-start.22) | collective-permute-done | bytes 1179680 | tf_op jit(solution)/shard_map/ppermute | solution.py:878
  439.4 24.9 %collective-permute-done.24.refs_7_.refs_3_ = bf16[4,288,512]{2,1,0:T(8,128)(2,1)S(1)} collective-permute-done((bf16[4,288,512]{2,1,0:T(8,128)(2,1)}, bf16[4,288,512]{2,1,0:T(8,128)(2,1)S(1)}, u32[]{:S(2)}, u32[]{:S(2)}) %collective-permute-start.24) | collective-permute-done | bytes 1179680 | tf_op jit(solution)/shard_map/ppermute | solution.py:878
  465.3 4.5 shard_map.272
  469.8 9.1 %shard_map.273.refs_4_ = bf16[4,1024,512]{2,1,0:T(8,128)(2,1)} custom-call(s32[1]{0:T(128)} %bitcast.16.line_ref, s32[4,1024,4]{2,1,0:T(8,128)} %bitcast.121, bf16[4,288,512]{2,1,0:T(8,128)(2,1)} %get-tuple-element.131.refs_0_, bf16[4,288,512]{2,1,0:T(8,128)(2,1)} %copy-done.15, bf16[4,288,512]{2,1,0:T(8,128)(2,1)} %copy-done.16, ...), custom_call_target="tpu_custom_call" | custom-call | flops 8000000 | bytes 1024 | tf_op jit(solution)/shard_map/pallas_call | solution.py:380
  485.3 8.6 %collective-permute-done.29 = f32[4,288]{1,0:T(4,128)S(1)} collective-permute-done((f32[4,288]{1,0:T(4,128)S(1)}, f32[4,288]{1,0:T(4,128)S(1)}, u32[]{:S(2)}, u32[]{:S(2)}) %collective-permute-start.29) | collective-permute-done | bytes 4640 | tf_op jit(solution)/shard_map/ppermute | solution.py:878
  493.9 3.3 collective-permute-start.30
  497.5 8.2 %collective-permute-done.30 = f32[4,288]{1,0:T(4,128)S(1)} collective-permute-done((f32[4,288]{1,0:T(4,128)S(1)}, f32[4,288]{1,0:T(4,128)S(1)}, u32[]{:S(2)}, u32[]{:S(2)}) %collective-permute-start.30) | collective-permute-done | bytes 4640 | tf_op jit(solution)/shard_map/ppermute | solution.py:878
  509.6 7.0 shard_map.274.refs_5_.refs_0_
  516.7 8.7 %shard_map.276 = (bf16[4,288,768]{2,1,0:T(8,128)(2,1)}, bf16[4,288,768]{2,1,0:T(8,128)(2,1)}, bf16[4,288,768]{2,1,0:T(8,128)(2,1)}, bf16[4,288,768]{2,1,0:T(8,128)(2,1)}) custom-call(bf16[4,288,768]{2,1,0:T(8,128)(2,1)} %get-tuple-element.109.refs_0_, bf16[4,288,768]{2,1,0:T(8,128)(2,1)} %get-tuple-element.110.refs_1_, ...), custom_call_target="tpu_custom_call" | custom-call | flops 7000000 | bytes 1024 | tf_op jit(solution)/shard_map/pallas_call | solution.py:551
  530.5 4.3 select_reduce_fusion
  537.0 4.2 collective-permute-start.37
  541.2 6.0 convolution_bitcast_fusion.5
  547.2 7.5 convolution_bitcast_fusion.1
  554.7 5.2 convolution_bitcast_fusion
  560.6 5.8 convolution_bitcast_fusion.4
  566.4 7.2 convolution_bitcast_fusion.2
  573.6 6.2 broadcast_select_fusion.3
  581.9 8.5 %collective-permute-start.34 = (bf16[1024,512]{1,0:T(8,128)(2,1)S(1)}, bf16[1024,512]{1,0:T(8,128)(2,1)}, u32[]{:S(2)}, u32[]{:S(2)}) collective-permute-start(bf16[1024,512]{1,0:T(8,128)(2,1)S(1)} %copy-done.7), channel_id=1, source_target_pairs={{0,1},{1,0},{2,3},{3,2},{4,5},{5,4},{6,7},{7,6},{8,9},{9,8},{10,11... | collective-permute-start | bytes 3145736 | tf_op jit(solution)/shard_map/ppermute | solution.py:915
  592.2 2.5 collective-permute-start.39
  596.3 12.0 %reduce-scatter.6.cloned.1.call-done.refs_1_ = bf16[1024,256]{1,0:T(8,128)(2,1)} async-done(((bf16[4096,256]{1,0:T(8,128)(2,1)}), bf16[1024,256]{1,0:T(8,128)(2,1)}) %reduce-scatter.6.cloned.1.call-update) | async-done | bytes 524304 | tf_op jit(solution)/shard_map/reduce_scatter | solution.py:885
  609.0 3.2 maximum_bitcast_fusion.1.refs_12_
  614.6 11.2 %shard_map.282 = (f32[1024,1536]{1,0:T(8,128)}, bf16[1024,1536]{1,0:T(8,128)(2,1)}, bf16[1024,128]{1,0:T(8,128)(2,1)}, f32[1,1536]{1,0:T(1,128)}) custom-call(s32[1]{0:T(128)} %bitcast.side_ref, bf16[1024,512]{1,0:T(8,128)(2,1)} %shard_map.277.refs_1_.refs_0_, bf16[1024,256]{1,0:T(8,128)(2,1)} %reduce-scatter.6.cloned.1.call-done.refs_1_, ...), custom_call_target="tpu_custom_call" | custom-call | flops 10000000 | bytes 1024 | tf_op jit(solution)/shard_map/pallas_call | solution.py:610
  625.7 13.3 %shard_map.283.refs_0_ = bf16[4,1024,768]{2,1,0:T(8,128)(2,1)} custom-call(s32[1]{0:T(128)} %bitcast.16.line_ref, s32[4,1024,4]{2,1,0:T(8,128)} %bitcast.123, bf16[4,288,768]{2,1,0:T(8,128)(2,1)} %get-tuple-element.133.refs_0_, bf16[4,288,768]{2,1,0:T(8,128)(2,1)} %collective-permute-done.31.refs_1_, bf16[4,288,768]{2,1,0:T(8,128)(2,1)} %collective-permute-done.32.refs_2_, ...), custom_call_target="tpu_custom_call" | custom-call | flops 12000000 | bytes 1024 | tf_op jit(solution)/shard_map/pallas_call | solution.py:380
  639.1 8.3 %shard_map.285 = (f32[4,96,896]{2,1,0:T(8,128)}, bf16[4,96,896]{2,1,0:T(8,128)(2,1)}, bf16[4,96,896]{2,1,0:T(8,128)(2,1)}, bf16[4,96,896]{2,1,0:T(8,128)(2,1)}) custom-call(s32[1]{0:T(128)} %bitcast.59.spot_ref, bf16[1024,1536]{1,0:T(8,128)(2,1)} %get-tuple-element.140.refs_4_.left_ref.db_ref, bf16[1024,768]{1,0:T(8,128)(2,1)} %get-tuple-element.143.right_ref, ...), custom_call_target="tpu_custom_call" | custom-call | flops 6000000 | bytes 1024 | tf_op jit(solution)/shard_map/pallas_call | solution.py:855
  650.1 29.4 %shard_map.286.d_ref.refs_0_ = bf16[1024,1024]{1,0:T(8,128)(2,1)} custom-call(bf16[1024,768]{1,0:T(8,128)(2,1)} %get-tuple-element.84.q_ref, bf16[1024,128]{1,0:T(8,128)(2,1)} %get-tuple-element.85.k_ref, bf16[1024,128]{1,0:T(8,128)(2,1)} %get-tuple-element.86.v_ref, s32[1,1024]{1,0:T(1,128)} %segq_ref.3, s32[1024,1]{1,0:T(8,128)} %copy.130.segk_ref, ...), custom_call_target="tpu_custom_call" | custom-call | flops 28000000 | bytes 1024 | tf_op jit(solution)/shard_map/pallas_call | solution.py:763
  681.9 7.8 shard_map.287.refs_1_.a_ref
  690.8 7.7 shard_map.289
  702.8 9.7 %shard_map.290.refs_1_ = f32[1024,1536]{1,0:T(8,128)} custom-call(bf16[1024,1536]{1,0:T(8,128)(2,1)} %shard_map.287.refs_1_.a_ref, bf16[1024,1536]{1,0:T(8,128)(2,1)} %copy-done.18, bf16[1024,1536]{1,0:T(8,128)(2,1)} %x_ref.5, f32[1024,1]{1,0:T(8,128)} %get-tuple-element.151.inv_ref, f32[1024,1536]{1,0:T(8,128)} %get-tuple-element.152.dh_ref, ...), custom_call_target="tpu_custom_call" | custom-call | flops 8000000 | bytes 1024 | tf_op jit(solution)/shard_map/pallas_call | solution.py:644
  712.5 5.4 collective-permute-done.44
  718.5 17.2 %collective-permute-done.46 = bf16[4,96,1024]{2,1,0:T(8,128)(2,1)} collective-permute-done((bf16[4,96,1024]{2,1,0:T(8,128)(2,1)}, bf16[4,96,1024]{2,1,0:T(8,128)(2,1)}, u32[]{:S(2)}, u32[]{:S(2)}) %collective-permute-start.46) | collective-permute-done | bytes 786464 | tf_op jit(solution)/shard_map/ppermute | solution.py:878
  735.7 2.6 convert_add_fusion
  739.3 3.5 collective-permute-start.47
  744.0 20.2 %collective-permute-done.47 = bf16[96,1920]{1,0:T(8,128)(2,1)} collective-permute-done((bf16[96,1920]{1,0:T(8,128)(2,1)}, bf16[96,1920]{1,0:T(8,128)(2,1)}, u32[]{:S(2)}, u32[]{:S(2)}) %collective-permute-start.47) | collective-permute-done | bytes 368672 | tf_op jit(solution)/shard_map/ppermute | solution.py:878
  764.2 3.0 collective-permute-done.48
  767.2 14.6 %collective-permute-done.49 = bf16[96,1920]{1,0:T(8,128)(2,1)} collective-permute-done((bf16[96,1920]{1,0:T(8,128)(2,1)S(1)}, bf16[96,1920]{1,0:T(8,128)(2,1)}, u32[]{:S(2)}, u32[]{:S(2)}) %collective-permute-start.49) | collective-permute-done | bytes 368672 | tf_op jit(solution)/shard_map/ppermute | solution.py:878
  784.9 2.8 add_convert_fusion
  (260 shorter events, 107.7 us)
Async XLA Ops:
  7.2 118.8 %all-gather.7.cloned.1.call-start = ((), (), s32[]{:S(2)}) async-start(), calls=%async_computation.6 | async-start | bytes 7864320 | tf_op jit(solution)/shard_map/all_gather | solution.py:881
  9.9 208.6 %all-gather.9.cloned.1.call-start = ((), (), s32[]{:S(2)}) async-start(), calls=%async_computation.7 | async-start | bytes 5242880 | tf_op jit(solution)/shard_map/all_gather | solution.py:881
  20.7 27.5 %copy-start.39 = (s32[1024,4]{0,1:T(4,128)S(1)}, s32[1024,4]{0,1:T(4,128)}, u32[]{:S(2)}) copy-start(s32[1024,4]{0,1:T(4,128)} %param.29) | copy-start | bytes 49156
  44.8 41.4 %collective-permute-start = (bf16[1024,1536]{1,0:T(8,128)(2,1)}, bf16[1024,1536]{1,0:T(8,128)(2,1)S(1)}, u32[]{:S(2)}, u32[]{:S(2)}) collective-permute-start(bf16[1024,1536]{1,0:T(8,128)(2,1)} %get-tuple-element.87.a_ref), channel_id=1, source_target_pairs={{0,1},{1,0},{2,3},{3,2},{4,5},{5,4},{6,7},{7,6},{8,9},{9,8},{10,11... | collective-permute-start | bytes 9437192 | tf_op jit(solution)/shard_map/ppermute | solution.py:915
  48.2 30.5 %copy-start.44 = (f32[1536]{0:T(1024)S(1)}, f32[1536]{0:T(1024)}, u32[]{:S(2)}) copy-start(f32[1536]{0:T(1024)} %param.20) | copy-start | bytes 18436
  48.2 31.1 %copy-start.40 = (bf16[1536,16]{0,1:T(8,128)(2,1)S(1)}, bf16[1536,16]{0,1:T(8,128)(2,1)}, u32[]{:S(2)}) copy-start(bf16[1536,16]{0,1:T(8,128)(2,1)} %param.25) | copy-start | bytes 147460
  58.7 4.1 collective-permute-start.1
  58.7 6.3 collective-permute-start.2
  61.2 4.8 collective-permute-start.3
  74.9 6.2 collective-permute-start.4
  76.2 8.6 %collective-permute-start.5 = (bf16[4,288,4]{2,1,0:T(8,128)(2,1)}, bf16[4,288,4]{2,1,0:T(8,128)(2,1)}, u32[]{:S(2)}, u32[]{:S(2)}) collective-permute-start(bf16[4,288,4]{2,1,0:T(8,128)(2,1)} %get-tuple-element.89), channel_id=1, source_target_pairs={{0,4},{2,6},{4,0},{6,2},{8,12},{10,14},{12,8},{14,10},{16,20},{18,... | collective-permute-start | bytes 27656 | tf_op jit(solution)/shard_map/ppermute | solution.py:878
  77.4 8.8 %collective-permute-start.6 = (bf16[4,288,4]{2,1,0:T(8,128)(2,1)}, bf16[4,288,4]{2,1,0:T(8,128)(2,1)}, u32[]{:S(2)}, u32[]{:S(2)}) collective-permute-start(bf16[4,288,4]{2,1,0:T(8,128)(2,1)} %get-tuple-element.90), channel_id=1, source_target_pairs={{0,6},{2,4},{4,2},{6,0},{8,14},{10,12},{12,10},{14,8},{16,22},{18,... | collective-permute-start | bytes 27656 | tf_op jit(solution)/shard_map/ppermute | solution.py:878
  126.0 151.0 %all-gather.11.cloned.1.call-start = ((), (), s32[]{:S(2)}) async-start(), calls=%async_computation.8 | async-start | bytes 2621440 | tf_op jit(solution)/shard_map/all_gather | solution.py:881
  139.8 39.9 %collective-permute-start.10 = (bf16[4,288,768]{2,1,0:T(8,128)(2,1)}, bf16[4,288,768]{2,1,0:T(8,128)(2,1)S(1)}, u32[]{:S(2)}, u32[]{:S(2)}) collective-permute-start(bf16[4,288,768]{2,1,0:T(8,128)(2,1)} %get-tuple-element.99), channel_id=1, source_target_pairs={{0,2},{2,0},{4,6},{6,4},{8,10},{10,8},{12,14},{14,12},{16,18},{18,... | collective-permute-start | bytes 5308424 | tf_op jit(solution)/shard_map/ppermute | solution.py:878
  141.0 39.4 %collective-permute-start.11 = (bf16[4,288,768]{2,1,0:T(8,128)(2,1)}, bf16[4,288,768]{2,1,0:T(8,128)(2,1)S(1)}, u32[]{:S(2)}, u32[]{:S(2)}) collective-permute-start(bf16[4,288,768]{2,1,0:T(8,128)(2,1)} %get-tuple-element.100), channel_id=1, source_target_pairs={{0,4},{2,6},{4,0},{6,2},{8,12},{10,14},{12,8},{14,10},{16,20},{18,... | collective-permute-start | bytes 5308424 | tf_op jit(solution)/shard_map/ppermute | solution.py:878
  142.2 76.3 %collective-permute-start.12 = (bf16[4,288,768]{2,1,0:T(8,128)(2,1)}, bf16[4,288,768]{2,1,0:T(8,128)(2,1)}, u32[]{:S(2)}, u32[]{:S(2)}) collective-permute-start(bf16[4,288,768]{2,1,0:T(8,128)(2,1)} %get-tuple-element.101), channel_id=1, source_target_pairs={{0,6},{2,4},{4,2},{6,0},{8,14},{10,12},{12,10},{14,8},{16,22},{18,... | collective-permute-start | bytes 5308424 | tf_op jit(solution)/shard_map/ppermute | solution.py:878
  179.6 38.9 %copy-start.8 = (bf16[4,288,768]{2,1,0:T(8,128)(2,1)}, bf16[4,288,768]{2,1,0:T(8,128)(2,1)S(1)}, u32[]{:S(2)}) copy-start(bf16[4,288,768]{2,1,0:T(8,128)(2,1)S(1)} %collective-permute-done.10.refs_2_.refs_1_) | copy-start | bytes 5308420
  180.4 38.1 %copy-start.9 = (bf16[4,288,768]{2,1,0:T(8,128)(2,1)}, bf16[4,288,768]{2,1,0:T(8,128)(2,1)S(1)}, u32[]{:S(2)}) copy-start(bf16[4,288,768]{2,1,0:T(8,128)(2,1)S(1)} %collective-permute-done.11.refs_3_.refs_2_) | copy-start | bytes 5308420
  218.6 342.0 %reduce-scatter.4.cloned.1.call-start = ((), (), s32[]{:S(2)}) async-start(), calls=%async_computation.3 | async-start | bytes 5242880 | tf_op jit(solution)/shard_map/reduce_scatter | solution.py:885
  226.5 25.2 %collective-permute-start.7 = (bf16[4,288,512]{2,1,0:T(8,128)(2,1)}, bf16[4,288,512]{2,1,0:T(8,128)(2,1)S(1)}, u32[]{:S(2)}, u32[]{:S(2)}) collective-permute-start(bf16[4,288,512]{2,1,0:T(8,128)(2,1)} %get-tuple-element.94), channel_id=1, source_target_pairs={{0,2},{2,0},{4,6},{6,4},{8,10},{10,8},{12,14},{14,12},{16,18},{18,... | collective-permute-start | bytes 3538952 | tf_op jit(solution)/shard_map/ppermute | solution.py:878
  227.7 28.9 %collective-permute-start.8 = (bf16[4,288,512]{2,1,0:T(8,128)(2,1)}, bf16[4,288,512]{2,1,0:T(8,128)(2,1)S(1)}, u32[]{:S(2)}, u32[]{:S(2)}) collective-permute-start(bf16[4,288,512]{2,1,0:T(8,128)(2,1)} %get-tuple-element.95), channel_id=1, source_target_pairs={{0,4},{2,6},{4,0},{6,2},{8,12},{10,14},{12,8},{14,10},{16,20},{18,... | collective-permute-start | bytes 3538952 | tf_op jit(solution)/shard_map/ppermute | solution.py:878
  228.0 49.0 %collective-permute-start.9 = (bf16[4,288,512]{2,1,0:T(8,128)(2,1)}, bf16[4,288,512]{2,1,0:T(8,128)(2,1)}, u32[]{:S(2)}, u32[]{:S(2)}) collective-permute-start(bf16[4,288,512]{2,1,0:T(8,128)(2,1)} %get-tuple-element.96), channel_id=1, source_target_pairs={{0,6},{2,4},{4,2},{6,0},{8,14},{10,12},{12,10},{14,8},{16,22},{18,... | collective-permute-start | bytes 3538952 | tf_op jit(solution)/shard_map/ppermute | solution.py:878
  288.6 38.0 %collective-permute-start.17 = (bf16[4,4,288,768]{3,2,1,0:T(8,128)(2,1)}, bf16[4,4,288,768]{3,2,1,0:T(8,128)(2,1)S(1)}, u32[]{:S(2)}, u32[]{:S(2)}) collective-permute-start(bf16[4,4,288,768]{3,2,1,0:T(8,128)(2,1)} %shard_map.266.refs_4_), channel_id=1, source_target_pairs={{0,1},{1,0},{2,3},{3,2},{4,5},{5,4},{6,7},{7,6},{8,9},{9,8},{10,11... | collective-permute-start | bytes 21233672 | tf_op jit(solution)/shard_map/ppermute | solution.py:915
  299.2 27.3 %collective-permute-start.16 = (bf16[4,4,288,512]{3,2,1,0:T(8,128)(2,1)}, bf16[4,4,288,512]{3,2,1,0:T(8,128)(2,1)S(1)}, u32[]{:S(2)}, u32[]{:S(2)}) collective-permute-start(bf16[4,4,288,512]{3,2,1,0:T(8,128)(2,1)} %shard_map.267.refs_0_), channel_id=1, source_target_pairs={{0,1},{1,0},{2,3},{3,2},{4,5},{5,4},{6,7},{7,6},{8,9},{9,8},{10,11... | collective-permute-start | bytes 14155784 | tf_op jit(solution)/shard_map/ppermute | solution.py:915
  299.2 14.6 %collective-permute-start.13 = (bf16[4,288,256]{2,1,0:T(8,128)(2,1)}, bf16[4,288,256]{2,1,0:T(8,128)(2,1)S(1)}, u32[]{:S(2)}, u32[]{:S(2)}) collective-permute-start(bf16[4,288,256]{2,1,0:T(8,128)(2,1)} %get-tuple-element.103.refs_4_), channel_id=1, source_target_pairs={{0,2},{2,0},{4,6},{6,4},{8,10},{10,8},{12,14},{14,12},{16,18},{18,... | collective-permute-start | bytes 1769480 | tf_op jit(solution)/shard_map/ppermute | solution.py:878
  299.6 14.3 %collective-permute-start.14 = (bf16[4,288,256]{2,1,0:T(8,128)(2,1)S(1)}, bf16[4,288,256]{2,1,0:T(8,128)(2,1)S(1)}, u32[]{:S(2)}, u32[]{:S(2)}) collective-permute-start(bf16[4,288,256]{2,1,0:T(8,128)(2,1)S(1)} %copy-done.30), channel_id=1, source_target_pairs={{0,4},{2,6},{4,0},{6,2},{8,12},{10,14},{12,8},{14,10},{16,20},{18,... | collective-permute-start | bytes 1769480 | tf_op jit(solution)/shard_map/ppermute | solution.py:878
  299.6 26.9 %collective-permute-start.15 = (bf16[4,288,256]{2,1,0:T(8,128)(2,1)S(1)}, bf16[4,288,256]{2,1,0:T(8,128)(2,1)S(1)}, u32[]{:S(2)}, u32[]{:S(2)}) collective-permute-start(bf16[4,288,256]{2,1,0:T(8,128)(2,1)S(1)} %copy-done.29), channel_id=1, source_target_pairs={{0,6},{2,4},{4,2},{6,0},{8,14},{10,12},{12,10},{14,8},{16,22},{18,... | collective-permute-start | bytes 1769480 | tf_op jit(solution)/shard_map/ppermute | solution.py:878
  335.8 5.8 collective-permute-start.18
  387.7 14.3 %collective-permute-start.21 = (bf16[4,4,288,512]{3,2,1,0:T(8,128)(2,1)}, bf16[4,4,288,512]{3,2,1,0:T(8,128)(2,1)S(1)}, u32[]{:S(2)}, u32[]{:S(2)}) collective-permute-start(bf16[4,4,288,512]{3,2,1,0:T(8,128)(2,1)} %get-tuple-element.123), channel_id=1, source_target_pairs={{0,1},{1,0},{2,3},{3,2},{4,5},{5,4},{6,7},{7,6},{8,9},{9,8},{10,11... | collective-permute-start | bytes 14155784 | tf_op jit(solution)/shard_map/ppermute | solution.py:915
  401.4 115.2 %collective-permute-start.19 = (bf16[4,4,288,768]{3,2,1,0:T(8,128)(2,1)}, bf16[4,4,288,768]{3,2,1,0:T(8,128)(2,1)}, u32[]{:S(2)}, u32[]{:S(2)}) collective-permute-start(bf16[4,4,288,768]{3,2,1,0:T(8,128)(2,1)} %get-tuple-element.113.refs_8_.refs_1_), channel_id=1, source_target_pairs={{0,1},{1,0},{2,3},{3,2},{4,5},{5,4},{6,7},{7,6},{8,9},{9,8},{10,11... | collective-permute-start | bytes 21233672 | tf_op jit(solution)/shard_map/ppermute | solution.py:915
  401.5 14.9 %collective-permute-start.20 = (bf16[4,4,288,256]{3,2,1,0:T(8,128)(2,1)}, bf16[4,4,288,256]{3,2,1,0:T(8,128)(2,1)}, u32[]{:S(2)}, u32[]{:S(2)}) collective-permute-start(bf16[4,4,288,256]{3,2,1,0:T(8,128)(2,1)} %get-tuple-element.118), channel_id=1, source_target_pairs={{0,1},{1,0},{2,3},{3,2},{4,5},{5,4},{6,7},{7,6},{8,9},{9,8},{10,11... | collective-permute-start | bytes 7077896 | tf_op jit(solution)/shard_map/ppermute | solution.py:915
  410.4 27.7 %collective-permute-start.22 = (bf16[4,288,512]{2,1,0:T(8,128)(2,1)}, bf16[4,288,512]{2,1,0:T(8,128)(2,1)S(1)}, u32[]{:S(2)}, u32[]{:S(2)}) collective-permute-start(bf16[4,288,512]{2,1,0:T(8,128)(2,1)} %get-tuple-element.124), channel_id=1, source_target_pairs={{0,2},{2,0},{4,6},{6,4},{8,10},{10,8},{12,14},{14,12},{16,18},{18,... | collective-permute-start | bytes 3538952 | tf_op jit(solution)/shard_map/ppermute | solution.py:878
  411.8 27.6 %collective-permute-start.23 = (bf16[4,288,512]{2,1,0:T(8,128)(2,1)}, bf16[4,288,512]{2,1,0:T(8,128)(2,1)S(1)}, u32[]{:S(2)}, u32[]{:S(2)}) collective-permute-start(bf16[4,288,512]{2,1,0:T(8,128)(2,1)} %get-tuple-element.125), channel_id=1, source_target_pairs={{0,4},{2,6},{4,0},{6,2},{8,12},{10,14},{12,8},{14,10},{16,20},{18,... | collective-permute-start | bytes 3538952 | tf_op jit(solution)/shard_map/ppermute | solution.py:878
  411.9 52.4 %collective-permute-start.24 = (bf16[4,288,512]{2,1,0:T(8,128)(2,1)}, bf16[4,288,512]{2,1,0:T(8,128)(2,1)S(1)}, u32[]{:S(2)}, u32[]{:S(2)}) collective-permute-start(bf16[4,288,512]{2,1,0:T(8,128)(2,1)} %get-tuple-element.126), channel_id=1, source_target_pairs={{0,6},{2,4},{4,2},{6,0},{8,14},{10,12},{12,10},{14,8},{16,22},{18,... | collective-permute-start | bytes 3538952 | tf_op jit(solution)/shard_map/ppermute | solution.py:878
  478.9 129.4 %reduce-scatter.6.cloned.1.call-start = ((), (), s32[]{:S(2)}) async-start(), calls=%async_computation.4 | async-start | bytes 2621440 | tf_op jit(solution)/shard_map/reduce_scatter | solution.py:885
  479.0 30.6 %collective-permute-start.25 = (bf16[4,288,256]{2,1,0:T(8,128)(2,1)}, bf16[4,288,256]{2,1,0:T(8,128)(2,1)}, u32[]{:S(2)}, u32[]{:S(2)}) collective-permute-start(bf16[4,288,256]{2,1,0:T(8,128)(2,1)} %get-tuple-element.128.refs_4_), channel_id=1, source_target_pairs={{0,2},{2,0},{4,6},{6,4},{8,10},{10,8},{12,14},{14,12},{16,18},{18,... | collective-permute-start | bytes 1769480 | tf_op jit(solution)/shard_map/ppermute | solution.py:878
  480.1 29.6 %collective-permute-start.26 = (bf16[4,288,256]{2,1,0:T(8,128)(2,1)S(1)}, bf16[4,288,256]{2,1,0:T(8,128)(2,1)}, u32[]{:S(2)}, u32[]{:S(2)}) collective-permute-start(bf16[4,288,256]{2,1,0:T(8,128)(2,1)S(1)} %copy-done.28), channel_id=1, source_target_pairs={{0,4},{2,6},{4,0},{6,2},{8,12},{10,14},{12,8},{14,10},{16,20},{18,... | collective-permute-start | bytes 1769480 | tf_op jit(solution)/shard_map/ppermute | solution.py:878
  480.8 28.8 %collective-permute-start.27 = (bf16[4,288,256]{2,1,0:T(8,128)(2,1)S(1)}, bf16[4,288,256]{2,1,0:T(8,128)(2,1)}, u32[]{:S(2)}, u32[]{:S(2)}) collective-permute-start(bf16[4,288,256]{2,1,0:T(8,128)(2,1)S(1)} %copy-done.27), channel_id=1, source_target_pairs={{0,6},{2,4},{4,2},{6,0},{8,14},{10,12},{12,10},{14,8},{16,22},{18,... | collective-permute-start | bytes 1769480 | tf_op jit(solution)/shard_map/ppermute | solution.py:878
  483.8 10.1 %collective-permute-start.29 = (f32[4,288]{1,0:T(4,128)S(1)}, f32[4,288]{1,0:T(4,128)S(1)}, u32[]{:S(2)}, u32[]{:S(2)}) collective-permute-start(f32[4,288]{1,0:T(4,128)S(1)} %bitcast.144), channel_id=1, source_target_pairs={{0,4},{2,6},{4,0},{6,2},{8,12},{10,14},{12,8},{14,10},{16,20},{18,... | collective-permute-start | bytes 13832 | tf_op jit(solution)/shard_map/ppermute | solution.py:878
  493.9 11.8 %collective-permute-start.30 = (f32[4,288]{1,0:T(4,128)S(1)}, f32[4,288]{1,0:T(4,128)S(1)}, u32[]{:S(2)}, u32[]{:S(2)}) collective-permute-start(f32[4,288]{1,0:T(4,128)S(1)} %bitcast.143), channel_id=1, source_target_pairs={{0,6},{2,4},{4,2},{6,0},{8,14},{10,12},{12,10},{14,8},{16,22},{18,... | collective-permute-start | bytes 13832 | tf_op jit(solution)/shard_map/ppermute | solution.py:878
  505.7 3.3 collective-permute-start.28
  525.3 100.4 %collective-permute-start.31 = (bf16[4,288,768]{2,1,0:T(8,128)(2,1)}, bf16[4,288,768]{2,1,0:T(8,128)(2,1)}, u32[]{:S(2)}, u32[]{:S(2)}) collective-permute-start(bf16[4,288,768]{2,1,0:T(8,128)(2,1)} %get-tuple-element.134.refs_1_), channel_id=1, source_target_pairs={{0,2},{2,0},{4,6},{6,4},{8,10},{10,8},{12,14},{14,12},{16,18},{18,... | collective-permute-start | bytes 5308424 | tf_op jit(solution)/shard_map/ppermute | solution.py:878
  526.9 98.9 %collective-permute-start.32 = (bf16[4,288,768]{2,1,0:T(8,128)(2,1)}, bf16[4,288,768]{2,1,0:T(8,128)(2,1)}, u32[]{:S(2)}, u32[]{:S(2)}) collective-permute-start(bf16[4,288,768]{2,1,0:T(8,128)(2,1)} %get-tuple-element.135.refs_2_), channel_id=1, source_target_pairs={{0,4},{2,6},{4,0},{6,2},{8,12},{10,14},{12,8},{14,10},{16,20},{18,... | collective-permute-start | bytes 5308424 | tf_op jit(solution)/shard_map/ppermute | solution.py:878
  528.4 97.4 %collective-permute-start.33 = (bf16[4,288,768]{2,1,0:T(8,128)(2,1)S(1)}, bf16[4,288,768]{2,1,0:T(8,128)(2,1)}, u32[]{:S(2)}, u32[]{:S(2)}) collective-permute-start(bf16[4,288,768]{2,1,0:T(8,128)(2,1)S(1)} %copy-done.3), channel_id=1, source_target_pairs={{0,6},{2,4},{4,2},{6,0},{8,14},{10,12},{12,10},{14,8},{16,22},{18,... | collective-permute-start | bytes 5308424 | tf_op jit(solution)/shard_map/ppermute | solution.py:878
  534.8 47.1 %collective-permute-start.38 = (f32[4,1024]{1,0:T(4,128)S(1)}, f32[4,1024]{1,0:T(4,128)S(1)}, u32[]{:S(2)}, u32[]{:S(2)}) collective-permute-start(f32[4,1024]{1,0:T(4,128)S(1)} %get-tuple-element.243), channel_id=1, source_target_pairs={{0,24},{2,26},{4,28},{6,30},{8,16},{10,18},{12,20},{14,22},{16,8},... | collective-permute-start | bytes 49160 | tf_op jit(solution)/shard_map/ppermute | solution.py:878
  537.0 44.9 %collective-permute-start.37 = (f32[4,1024]{1,0:T(4,128)S(1)}, f32[4,1024]{1,0:T(4,128)S(1)}, u32[]{:S(2)}, u32[]{:S(2)}) collective-permute-start(f32[4,1024]{1,0:T(4,128)S(1)} %get-tuple-element.244), channel_id=1, source_target_pairs={{0,16},{2,18},{4,20},{6,22},{8,24},{10,26},{12,28},{14,30},{16,0},... | collective-permute-start | bytes 49160 | tf_op jit(solution)/shard_map/ppermute | solution.py:878
  560.6 224.3 %reduce-scatter.8.cloned.1.call-start = ((), (), s32[]{:S(2)}) async-start(), calls=%async_computation.5 | async-start | bytes 7864320 | tf_op jit(solution)/shard_map/reduce_scatter | solution.py:885
  581.9 10.3 %collective-permute-start.36 = (f32[4,1024]{1,0:T(4,128)S(1)}, f32[4,1024]{1,0:T(4,128)S(1)}, u32[]{:S(2)}, u32[]{:S(2)}) collective-permute-start(f32[4,1024]{1,0:T(4,128)S(1)} %get-tuple-element.245), channel_id=1, source_target_pairs={{0,8},{2,10},{4,12},{6,14},{8,0},{10,2},{12,4},{14,6},{16,24},{18,... | collective-permute-start | bytes 49160 | tf_op jit(solution)/shard_map/ppermute | solution.py:878
  581.9 31.8 %collective-permute-start.34 = (bf16[1024,512]{1,0:T(8,128)(2,1)S(1)}, bf16[1024,512]{1,0:T(8,128)(2,1)}, u32[]{:S(2)}, u32[]{:S(2)}) collective-permute-start(bf16[1024,512]{1,0:T(8,128)(2,1)S(1)} %copy-done.7), channel_id=1, source_target_pairs={{0,1},{1,0},{2,3},{3,2},{4,5},{5,4},{6,7},{7,6},{8,9},{9,8},{10,11... | collective-permute-start | bytes 3145736 | tf_op jit(solution)/shard_map/ppermute | solution.py:915
  592.2 4.1 collective-permute-start.39
  608.3 5.4 collective-permute-start.35
  647.5 32.0 %collective-permute-start.40 = (bf16[4,96,896]{2,1,0:T(8,128)(2,1)}, bf16[4,96,896]{2,1,0:T(8,128)(2,1)S(1)}, u32[]{:S(2)}, u32[]{:S(2)}) collective-permute-start(bf16[4,96,896]{2,1,0:T(8,128)(2,1)} %get-tuple-element.146.refs_0_), channel_id=1, source_target_pairs={{0,2},{2,0},{4,6},{6,4},{8,10},{10,8},{12,14},{14,12},{16,18},{18,... | collective-permute-start | bytes 2064392 | tf_op jit(solution)/shard_map/ppermute | solution.py:878
  648.8 30.7 %collective-permute-start.41 = (bf16[4,96,896]{2,1,0:T(8,128)(2,1)}, bf16[4,96,896]{2,1,0:T(8,128)(2,1)S(1)}, u32[]{:S(2)}, u32[]{:S(2)}) collective-permute-start(bf16[4,96,896]{2,1,0:T(8,128)(2,1)} %get-tuple-element.147.refs_1_), channel_id=1, source_target_pairs={{0,4},{2,6},{4,0},{6,2},{8,12},{10,14},{12,8},{14,10},{16,20},{18,... | collective-permute-start | bytes 2064392 | tf_op jit(solution)/shard_map/ppermute | solution.py:878
  649.9 30.6 %collective-permute-start.42 = (bf16[4,96,896]{2,1,0:T(8,128)(2,1)}, bf16[4,96,896]{2,1,0:T(8,128)(2,1)S(1)}, u32[]{:S(2)}, u32[]{:S(2)}) collective-permute-start(bf16[4,96,896]{2,1,0:T(8,128)(2,1)} %get-tuple-element.148.refs_2_), channel_id=1, source_target_pairs={{0,6},{2,4},{4,2},{6,0},{8,14},{10,12},{12,10},{14,8},{16,22},{18,... | collective-permute-start | bytes 2064392 | tf_op jit(solution)/shard_map/ppermute | solution.py:878
  650.1 30.4 %copy-start.22 = (f32[4,96,896]{2,1,0:T(8,128)S(1)}, f32[4,96,896]{2,1,0:T(8,128)}, u32[]{:S(2)}) copy-start(f32[4,96,896]{2,1,0:T(8,128)} %get-tuple-element.149) | copy-start | bytes 4128772
  689.7 11.5 %collective-permute-start.43 = (bf16[1024,1536]{1,0:T(8,128)(2,1)}, bf16[1024,1536]{1,0:T(8,128)(2,1)S(1)}, u32[]{:S(2)}, u32[]{:S(2)}) collective-permute-start(bf16[1024,1536]{1,0:T(8,128)(2,1)} %shard_map.287.refs_1_.a_ref), channel_id=1, source_target_pairs={{0,1},{1,0},{2,3},{3,2},{4,5},{5,4},{6,7},{7,6},{8,9},{9,8},{10,11... | collective-permute-start | bytes 9437192 | tf_op jit(solution)/shard_map/ppermute | solution.py:915
  698.5 19.5 %collective-permute-start.44 = (bf16[4,96,1024]{2,1,0:T(8,128)(2,1)}, bf16[4,96,1024]{2,1,0:T(8,128)(2,1)}, u32[]{:S(2)}, u32[]{:S(2)}) collective-permute-start(bf16[4,96,1024]{2,1,0:T(8,128)(2,1)} %get-tuple-element.153), channel_id=1, source_target_pairs={{0,2},{2,0},{4,6},{6,4},{8,10},{10,8},{12,14},{14,12},{16,18},{18,... | collective-permute-start | bytes 2359304 | tf_op jit(solution)/shard_map/ppermute | solution.py:878
  699.4 19.1 %collective-permute-start.45 = (bf16[4,96,1024]{2,1,0:T(8,128)(2,1)}, bf16[4,96,1024]{2,1,0:T(8,128)(2,1)}, u32[]{:S(2)}, u32[]{:S(2)}) collective-permute-start(bf16[4,96,1024]{2,1,0:T(8,128)(2,1)} %get-tuple-element.154), channel_id=1, source_target_pairs={{0,4},{2,6},{4,0},{6,2},{8,12},{10,14},{12,8},{14,10},{16,20},{18,... | collective-permute-start | bytes 2359304 | tf_op jit(solution)/shard_map/ppermute | solution.py:878
  700.0 35.7 %collective-permute-start.46 = (bf16[4,96,1024]{2,1,0:T(8,128)(2,1)}, bf16[4,96,1024]{2,1,0:T(8,128)(2,1)}, u32[]{:S(2)}, u32[]{:S(2)}) collective-permute-start(bf16[4,96,1024]{2,1,0:T(8,128)(2,1)} %get-tuple-element.155), channel_id=1, source_target_pairs={{0,6},{2,4},{4,2},{6,0},{8,14},{10,12},{12,10},{14,8},{16,22},{18,... | collective-permute-start | bytes 2359304 | tf_op jit(solution)/shard_map/ppermute | solution.py:878
  739.3 24.9 %collective-permute-start.47 = (bf16[96,1920]{1,0:T(8,128)(2,1)}, bf16[96,1920]{1,0:T(8,128)(2,1)}, u32[]{:S(2)}, u32[]{:S(2)}) collective-permute-start(bf16[96,1920]{1,0:T(8,128)(2,1)} %get-tuple-element.226), channel_id=1, source_target_pairs={{0,8},{2,10},{4,12},{6,14},{8,0},{10,2},{12,4},{14,6},{16,24},{18,... | collective-permute-start | bytes 1105928 | tf_op jit(solution)/shard_map/ppermute | solution.py:878
  742.8 24.5 %collective-permute-start.48 = (bf16[96,1920]{1,0:T(8,128)(2,1)}, bf16[96,1920]{1,0:T(8,128)(2,1)}, u32[]{:S(2)}, u32[]{:S(2)}) collective-permute-start(bf16[96,1920]{1,0:T(8,128)(2,1)} %get-tuple-element.227), channel_id=1, source_target_pairs={{0,16},{2,18},{4,20},{6,22},{8,24},{10,26},{12,28},{14,30},{16,0},... | collective-permute-start | bytes 1105928 | tf_op jit(solution)/shard_map/ppermute | solution.py:878
  743.9 38.0 %collective-permute-start.49 = (bf16[96,1920]{1,0:T(8,128)(2,1)S(1)}, bf16[96,1920]{1,0:T(8,128)(2,1)}, u32[]{:S(2)}, u32[]{:S(2)}) collective-permute-start(bf16[96,1920]{1,0:T(8,128)(2,1)S(1)} %get-tuple-element.228), channel_id=1, source_target_pairs={{0,24},{2,26},{4,28},{6,30},{8,16},{10,18},{12,20},{14,22},{16,8},... | collective-permute-start | bytes 1105928 | tf_op jit(solution)/shard_map/ppermute | solution.py:878
  787.7 6.6 collective-permute-start.50
  792.4 1.4 collective-permute-start.51
  (42 other events, 296.0 us)
Sparse Core Ops, SparseCore 0:
  10.2 115.7 all-gather.6
  127.5 79.9 all-gather.8
  218.7 47.2 all-gather.10
  479.1 81.4 reduce-scatter.3
  562.8 45.4 reduce-scatter.5
  639.2 114.6 reduce-scatter.7

commit v4 on v3

--- a/solution.py
+++ b/solution.py
@@ -33,6 +33,7 @@
     return depth
 
 
+longest_block = 256
 VMEM_LIMIT = 56 * 1024 * 1024
 
 
@@ -352,7 +353,8 @@
 
 
 def combine_kernel(width, capacity, line_ref, tab_ref, *refs):
-    out_ref = refs[-1]
+    out_ref, token_ref = refs[-2:]
+    token_ref[...] = jnp.zeros_like(token_ref)
     codes = tab_ref[0]
     total = width * capacity
     chosen = []
@@ -376,7 +378,8 @@
         chosen = low(table_columns[:, :, :, None] == slot)
         rows = jnp.stack(came)
         total = jnp.einsum("gtbs,bgsd->gtd", chosen, rows, preferred_element_type=jnp.float32)
-        return low(total[jnp.arange(count, dtype=jnp.int32) ^ line[0]])
+        total = low(total[jnp.arange(count, dtype=jnp.int32) ^ line[0]])
+        return total, total[:1, :8, :128]
     return pl.pallas_call(
         functools.partial(combine_kernel, width, capacity),
         grid_spec=pltpu.PrefetchScalarGridSpec(
@@ -385,9 +388,15 @@
             in_specs=[pl.BlockSpec((1, length, width), lambda g, line: (g, 0, 0))]
             + [pl.BlockSpec((1, capacity, columns), lambda g, line: (g, 0, 0))] * width
             + anywhere(earlier),
-            out_specs=pl.BlockSpec((1, length, columns), lambda g, line: (g ^ line[0], 0, 0)),
+            out_specs=[
+                pl.BlockSpec((1, length, columns), lambda g, line: (g ^ line[0], 0, 0)),
+                pl.BlockSpec((1, 8, 128), lambda g, line: (0, 0, 0)),
+            ],
         ),
-        out_shape=jax.ShapeDtypeStruct((count, length, columns), jnp.bfloat16),
+        out_shape=[
+            jax.ShapeDtypeStruct((count, length, columns), jnp.bfloat16),
+            jax.ShapeDtypeStruct((1, 8, 128), jnp.float32),
+        ],
         compiler_params=kernel_params(),
         cost_estimate=lasting(3.0 * count * columns / 768),
     )(line, table_columns, *came, *earlier)
@@ -692,6 +701,7 @@
     heads,
     scale,
     tile,
+    block,
     q_ref,
     k_ref,
     v_ref,
@@ -706,44 +716,48 @@
 ):
     out_ref, dk_ref, dv_ref = refs[-3:]
     step = pl.program_id(0)
-    allowed = segk_ref[...] <= segq_ref[...]
-    keys = k_ref[...]
-    values = v_ref[...]
-    size = keys.shape[1]
+    length, size = k_ref.shape
     here = pl.ds(pl.multiple_of(step * tile, tile), tile)
     cosine, sine = cos_ref[here, :], sin_ref[here, :]
-    keys_t = keys.T
 
     def put(rows, start, array):
         out_ref[rows, start : start + size] = array.astype(jnp.bfloat16)
 
-    d_mixed = dot(db_ref[...], wo_ref[...], 1, 1).astype(jnp.bfloat16)
-    dk_total = jnp.zeros(keys.shape, jnp.float32)
-    dv_total = jnp.zeros(keys.shape, jnp.float32)
-    for head in range(heads):
-        span = slice(head * size, (head + 1) * size)
-        query = q_ref[:, span]
-        d_head = d_mixed[:, span]
-        scores = dot(keys, query, 1, 1) * scale - lse_ref[head : head + 1, :]
-        probs = jnp.where(allowed, jnp.exp(scores), 0.0)
-        d_probs = dot(values, d_head, 1, 1)
-        scaled = probs * d_probs
-        row_dot = jnp.sum(scaled, axis=0, keepdims=True)
-        d_scores = (scale * (scaled - probs * row_dot)).astype(jnp.bfloat16)
-        dv_total = dv_total + dot(probs.astype(jnp.bfloat16), d_head)
-        dk_total = dk_total + dot(d_scores, query)
-        d_query = dot(keys_t, d_scores).T
-        put(here, head * size, turn(d_query, cosine, -sine))
-
     @pl.when(step == 0)
     def _():
-        dk_ref[...] = dk_total
-        dv_ref[...] = dv_total
-
-    @pl.when(step > 0)
-    def _():
-        dk_ref[...] += dk_total
-        dv_ref[...] += dv_total
+        dk_ref[...] = jnp.zeros_like(dk_ref)
+        dv_ref[...] = jnp.zeros_like(dv_ref)
+
+    d_mixed = dot(db_ref[...], wo_ref[...], 1, 1).astype(jnp.bfloat16)
+
+    def work(seen):
+        allowed = segk_ref[:seen] <= segq_ref[...]
+        keys, values = k_ref[:seen], v_ref[:seen]
+        keys_t = keys.T
+        dk_total = jnp.zeros(keys.shape, jnp.float32)
+        dv_total = jnp.zeros(keys.shape, jnp.float32)
+        for head in range(heads):
+            span = slice(head * size, (head + 1) * size)
+            query = q_ref[:, span]
+            d_head = d_mixed[:, span]
+            scores = dot(keys, query, 1, 1) * scale - lse_ref[head : head + 1, :]
+            probs = jnp.where(allowed, jnp.exp(scores), 0.0)
+            d_probs = dot(values, d_head, 1, 1)
+            scaled = probs * d_probs
+            row_dot = jnp.sum(scaled, axis=0, keepdims=True)
+            d_scores = (scale * (scaled - probs * row_dot)).astype(jnp.bfloat16)
+            dv_total = dv_total + dot(probs.astype(jnp.bfloat16), d_head)
+            dk_total = dk_total + dot(d_scores, query)
+            d_query = dot(keys_t, d_scores).T
+            put(here, head * size, turn(d_query, cosine, -sine))
+        dk_ref[:seen] += dk_total
+        dv_ref[:seen] += dv_total
+
+    for at in range(length // tile):
+
+        @pl.when(step == at)
+        def _(at=at):
+            work(min((at + 1) * tile + block, length))
 
     @pl.when(step == pl.num_programs(0) - 1)
     def _():
@@ -761,7 +775,7 @@
     model = w_out.shape[1]
     out = jax.ShapeDtypeStruct((length, span + 2 * size), jnp.bfloat16)
     return pl.pallas_call(
-        functools.partial(attend_back_kernel, heads, scale, tile),
+        functools.partial(attend_back_kernel, heads, scale, tile, longest_block),
         grid=(length // tile,),
         in_specs=[
             pl.BlockSpec((tile, span), lambda i: (i, 0)),
@@ -998,7 +1012,7 @@
         routes,
         tile,
         widths,
-        (place_rows, *route_blocks[1:]),
+        (place_rows, route_rows),
     )
     w_both = jnp.concatenate([w_gate[0], w_up[0]], axis=1)
     in_slots = [link.spread(hold(in_parts[0], cot_slots))]
@@ -1018,7 +1032,7 @@
     pieces, c_pieces = in_mine + in_other, [cot_mine, cot_other]
 
     pre, acts, terms, backs = expert_rows(
-        me_ref, pieces, c_pieces, widths, route_rows, w_both, w_down[0], w_router
+        me_ref, pieces, c_pieces, widths[::-1], route_rows, w_both, w_down[0], w_router
     )
     swapped = [swap(away) for away, _ in backs]
     first_came = link.plane(join_cores(backs[0][1], swapped[0], ()))
@@ -1026,26 +1040,16 @@
     terms = hold(terms, out_away)[..., 0]
     terms = jnp.stack(link.plane([terms[b] for b in range(width)]), axis=1)
     blocks = join_cores(backs[1][1], swapped[1], (*first_came[1:], out_away))
-    row_parts = [combine(line_ref, place_columns, first_came, blocks[1:])]
+    first_part, first_token = combine(line_ref, place_columns, first_came, blocks[1:])
+    row_parts = [first_part]
     came = link.plane(blocks)
-    row_parts.append(combine(line_ref, place_columns, came, (row_parts[0],)))
-    out_blocks = join_cores(out_homes, swap(out_away), (row_parts[1], terms))
+    last_part, last_token = combine(line_ref, place_columns, came, (first_token,))
+    row_parts.append(last_part)
+    out_blocks = join_cores(out_homes, swap(out_away), (last_token, terms))
     out_came = link.plane(out_blocks)
-    row_mine = [hold(link.collect(row_parts[0]), *out_blocks[1:])]
+    row_mine = [link.collect(row_parts[0])]
     row_mine.append(link.collect(hold(row_parts[1], row_mine[0])))
     row_other = [swap(part) for part in row_mine]
-
-    act_rows = hold(acts, *out_blocks[1:]).reshape(-1, unit_count)
-    grads = [contract_rows(act_rows, piece.reshape(-1, piece.shape[3])) for piece in c_pieces]
-    down_grad = join_halves(
-        *grads, side
-    )[None]
-    pre = hold(pre, *out_blocks[1:]).reshape(-1, 2 * unit_count)
-    grads = [contract_rows(piece.reshape(-1, piece.shape[3]), pre) for piece in pieces]
-    first, last = jnp.concatenate(grads[:2]), jnp.concatenate(grads[2:])
-    upper, lower = jnp.where(side == 0, first, last), jnp.where(side == 0, last, first)
-    gate_grad = jnp.concatenate([upper[:, :unit_count], lower[:, :unit_count]])[None]
-    up_grad = jnp.concatenate([upper[:, unit_count:], lower[:, unit_count:]])[None]
 
     terms = hold(terms, *out_blocks[1:])
     slot_ids = jnp.arange(capacity, dtype=jnp.int32)
@@ -1060,6 +1064,18 @@
     )
     term_table = term_table + swap(term_table)
     term_table = term_table[jnp.arange(expert_count, dtype=jnp.int32) ^ link.me].T
+
+    act_rows = hold(acts, *out_blocks[1:]).reshape(-1, unit_count)
+    grads = [contract_rows(act_rows, piece.reshape(-1, piece.shape[3])) for piece in c_pieces]
+    down_grad = join_halves(
+        *grads, side
+    )[None]
+    pre = hold(pre, term_table, down_grad).reshape(-1, 2 * unit_count)
+    grads = [contract_rows(piece.reshape(-1, piece.shape[3]), pre) for piece in pieces]
+    first, last = jnp.concatenate(grads[:2]), jnp.concatenate(grads[2:])
+    upper, lower = jnp.where(side == 0, first, last), jnp.where(side == 0, last, first)
+    gate_grad = jnp.concatenate([upper[:, :unit_count], lower[:, :unit_count]])[None]
+    up_grad = jnp.concatenate([upper[:, unit_count:], lower[:, unit_count:]])[None]
 
     d_hidden, d_branch, d_logits, ffn_gain_grad = settle(
         side_ref,
@@ -1076,7 +1092,7 @@
         (down_grad, gate_grad, up_grad),
     )
 
-    out_parts = combine(line_ref, place_columns, out_came, (d_branch,))
+    out_parts, _ = combine(line_ref, place_columns, out_came, (d_branch,))
     out_held = hold(out_parts, row_mine[1])
     spot_ref = (link.me % width).astype(jnp.int32)[None]
     shared_early = share_grads(

time: 816 us -> 802 us (0.983)
  starting transfers between devices: 66.1 us -> 55.7 us
  waiting for transfers between devices: 330 us -> 340 us
  matrix products: 37.8 us -> 28.5 us
    ppermute x39, waiting for transfers between devices: 287 us -> 301 us  [flip(): lax.ppermute(rows, 'expert', [(d, d ^ mask) for d in range(self.count)])]
    dot_general x6, matrix products: 37.8 us -> 28.5 us  [contract_rows(): lax.dot_general(left, right, (((0,), (0,)), ((), ())), preferred_element_...]
    unnamed x101 -> x103, local copies, waits for them, and re-layouts: 23.7 us -> 26.2 us
  transfers between devices with their start and end apart: 58 -> 58, of which waited for: 32 -> 32; matrix products, arithmetic and copies ran while one was open for 11% -> 10% of each run, Pallas kernels for 25% -> 25%
where the time goes in v4:
time: 802 us; the launch traced here: 792 us
  waiting for transfers between devices  340 us (42%)
  Pallas kernels  274 us (34%)
  starting transfers between devices  55.7 us (7%)
  local copies, waits for them, and re-layouts  43.2 us (5%)
  other arithmetic  35.8 us (4%)
  matrix products  28.5 us (4%)
  between operations  15.1 us (2%)
    ppermute x39, waiting for transfers between devices, flip(): lax.ppermute(rows, 'expert', [(d, d ^ mask) for d in range(self.count)])  301 us
    pallas_call x1, Pallas kernels, expert_rows(): pl.pallas_call(functools.partial(expert_kernel, len(pieces) // 2, len(c_p...  44.9 us
    ppermute x39, starting transfers between devices, flip(): lax.ppermute(rows, 'expert', [(d, d ^ mask) for d in range(self.count)])  38.6 us
    pallas_call x3, Pallas kernels, combine(): pl.pallas_call(functools.partial(combine_kernel, width, capacity), grid_s...  29.5 us
    pallas_call x4, Pallas kernels, pick_rows(): pl.pallas_call(functools.partial(pick_kernel, width, capacity, len(out_sh...  29.1 us
    dot_general x6, matrix products, contract_rows(): lax.dot_general(left, right, (((0,), (0,)), ((), ())), preferred_element_...  28.5 us
    pallas_call x1, Pallas kernels, attend_back(): pl.pallas_call(functools.partial(attend_back_kernel, heads, scale, tile,...  26.3 us
    unnamed x103, local copies, waits for them, and re-layouts  26.2 us
  transfers between devices with their start and end apart: 58, of which 32 were waited for; matrix products, arithmetic and copies ran while one was open for 10% of the time, Pallas kernels for 25%

profile of v4, /device:TPU:9, one launch (start us, length us, event | category | flops | bytes accessed | tf_op | source)
XLA Modules:
  0.0 791.7 jit_solution(3552313337378481382)
XLA Ops:
  7.3 2.7 constant_dynamic-slice_fusion
  11.7 9.0 %shard_map.256 = (bf16[1024,1536]{1,0:T(8,128)(2,1)}, bf16[1024,768]{1,0:T(8,128)(2,1)}, bf16[1024,128]{1,0:T(8,128)(2,1)}, bf16[1024,128]{1,0:T(8,128)(2,1)}, f32[1024,1]{1,0:T(8,128)}) custom-call(bf16[1024,1536]{1,0:T(8,128)(2,1)} %x_ref.5, f32[1,1536]{1,0:T(1,128)} %broadcast_in_dim.70.gain_ref, bf16[1536,768]{1,0:T(8,128)(2,1)} %wq_ref.3, ...), custom_call_target="tpu_custom_call" | custom-call | flops 9000000 | bytes 1024 | tf_op jit(solution)/shard_map/pallas_call | solution.py:162
  20.7 24.1 %shard_map.257 = (bf16[1024,768]{1,0:T(8,128)(2,1)}, f32[6,1024]{1,0:T(8,128)}, bf16[1024,1536]{1,0:T(8,128)(2,1)}) custom-call(bf16[1024,768]{1,0:T(8,128)(2,1)} %get-tuple-element.89.q_ref, bf16[1024,128]{1,0:T(8,128)(2,1)} %get-tuple-element.90.k_ref, bf16[1024,128]{1,0:T(8,128)(2,1)} %get-tuple-element.91.v_ref, s32[1,1024]{1,0:T(1,128)} %segq_ref.3, ...), custom_call_target="tpu_custom_call" | custom-call | flops 20000000 | bytes 1024 | tf_op jit(solution)/shard_map/pallas_call | solution.py:207
  48.9 8.9 %shard_map.258 = s32[16,1024]{1,0:T(8,128)} custom-call(s32[16,1024]{1,0:T(8,128)} %compare_select_fusion.keys_ref), custom_call_target="tpu_custom_call" | custom-call | flops 9000000 | bytes 1024 | tf_op jit(solution)/shard_map/pallas_call | solution.py:118
  58.8 2.5 collective-permute-start.2
  62.8 2.3 collective-permute-done.2
  69.5 5.3 shard_map.259
  81.1 3.7 collective-permute-done.5
  86.2 2.5 pad_maximum_fusion.4.refs_1_.refs_6_
  90.4 9.8 %shard_map.260 = (f32[1024,1536]{1,0:T(8,128)}, bf16[1024,1536]{1,0:T(8,128)(2,1)}, f32[1024,1]{1,0:T(8,128)}, f32[1024,16]{1,0:T(8,128)}, bf16[1024,512]{1,0:T(8,128)(2,1)}, /*index=5*/bf16[1024,256]{1,0:T(8,128)(2,1)}) custom-call(s32[1]{0:T(128)} %bitcast.side_ref, bf16[1024,1536]{1,0:T(8,128)(2,1)} %x_ref.5, bf16[1024,1536]{1,0:T(8,128)(2,1)} %get-tuple-element.92.a_ref, ...), custom_call_target="tpu_custom_call" | custom-call | flops 9000000 | bytes 1024 | tf_op jit(solution)/shard_map/pallas_call | solution.py:276
  100.2 25.8 %all-gather.7.cloned.1.call-done = bf16[4096,768]{1,0:T(8,128)(2,1)} async-done(((bf16[1024,768]{1,0:T(8,128)(2,1)}), bf16[4096,768]{1,0:T(8,128)(2,1)}) %all-gather.7.cloned.1.call-update) | async-done | bytes 6291472 | tf_op jit(solution)/shard_map/all_gather | solution.py:895
  129.2 10.6 %shard_map.263 = (bf16[4,288,768]{2,1,0:T(8,128)(2,1)}, bf16[4,288,768]{2,1,0:T(8,128)(2,1)}, bf16[4,288,768]{2,1,0:T(8,128)(2,1)}, bf16[4,288,768]{2,1,0:T(8,128)(2,1)}) custom-call(s32[1]{0:T(128)} %bitcast.20.line_ref, s32[4,4,1,1024]{3,2,1,0:T(1,128)} %broadcast_in_dim.75.tab_ref.refs_0_, bf16[4,1024,768]{2,1,0:T(8,128)(2,1)} %bitcast.125, ...), custom_call_target="tpu_custom_call" | custom-call | flops 12000000 | bytes 1024 | tf_op jit(solution)/shard_map/pallas_call | solution.py:341
  142.4 37.2 %collective-permute-done.10.refs_2_.refs_1_ = bf16[4,288,768]{2,1,0:T(8,128)(2,1)S(1)} collective-permute-done((bf16[4,288,768]{2,1,0:T(8,128)(2,1)}, bf16[4,288,768]{2,1,0:T(8,128)(2,1)S(1)}, u32[]{:S(2)}, u32[]{:S(2)}) %collective-permute-start.10) | collective-permute-done | bytes 1769504 | tf_op jit(solution)/shard_map/ppermute | solution.py:892
  180.4 38.1 %collective-permute-done.12.refs_4_.refs_3_ = bf16[4,288,768]{2,1,0:T(8,128)(2,1)} collective-permute-done((bf16[4,288,768]{2,1,0:T(8,128)(2,1)}, bf16[4,288,768]{2,1,0:T(8,128)(2,1)}, u32[]{:S(2)}, u32[]{:S(2)}) %collective-permute-start.12) | collective-permute-done | bytes 1769504 | tf_op jit(solution)/shard_map/ppermute | solution.py:892
  218.6 7.9 %shard_map.262 = (bf16[4,288,512]{2,1,0:T(8,128)(2,1)}, bf16[4,288,512]{2,1,0:T(8,128)(2,1)}, bf16[4,288,512]{2,1,0:T(8,128)(2,1)}, bf16[4,288,512]{2,1,0:T(8,128)(2,1)}) custom-call(s32[1]{0:T(128)} %bitcast.20.line_ref, s32[4,4,1,1024]{3,2,1,0:T(1,128)} %broadcast_in_dim.75.tab_ref.refs_0_, bf16[4,1024,512]{2,1,0:T(8,128)(2,1)} %bitcast.129), custom_call_target="tpu_custom_call" | custom-call | flops 8000000 | bytes 1024 | tf_op jit(solution)/shard_map/pallas_call | solution.py:341
  229.2 22.5 %collective-permute-done.7.refs_0_.refs_1_ = bf16[4,288,512]{2,1,0:T(8,128)(2,1)S(1)} collective-permute-done((bf16[4,288,512]{2,1,0:T(8,128)(2,1)}, bf16[4,288,512]{2,1,0:T(8,128)(2,1)S(1)}, u32[]{:S(2)}, u32[]{:S(2)}) %collective-permute-start.7) | collective-permute-done | bytes 1179680 | tf_op jit(solution)/shard_map/ppermute | solution.py:892
  251.7 4.8 collective-permute-done.8.refs_1_.refs_2_
  256.5 20.4 %collective-permute-done.9.refs_2_.refs_3_ = bf16[4,288,512]{2,1,0:T(8,128)(2,1)} collective-permute-done((bf16[4,288,512]{2,1,0:T(8,128)(2,1)}, bf16[4,288,512]{2,1,0:T(8,128)(2,1)}, u32[]{:S(2)}, u32[]{:S(2)}) %collective-permute-start.9) | collective-permute-done | bytes 1179680 | tf_op jit(solution)/shard_map/ppermute | solution.py:892
  277.0 5.3 shard_map.265
  282.3 6.2 shard_map.266.refs_4_
  288.5 5.6 collective-permute-start.17
  294.1 5.0 shard_map.267.refs_0_
  299.6 2.3 collective-permute-start.15
  301.8 12.0 %collective-permute-done.13.refs_1_ = bf16[4,288,256]{2,1,0:T(8,128)(2,1)S(1)} collective-permute-done((bf16[4,288,256]{2,1,0:T(8,128)(2,1)}, bf16[4,288,256]{2,1,0:T(8,128)(2,1)S(1)}, u32[]{:S(2)}, u32[]{:S(2)}) %collective-permute-start.13) | collective-permute-done | bytes 589856 | tf_op jit(solution)/shard_map/ppermute | solution.py:892
  313.8 12.7 %collective-permute-done.15.refs_3_ = bf16[4,288,256]{2,1,0:T(8,128)(2,1)S(1)} collective-permute-done((bf16[4,288,256]{2,1,0:T(8,128)(2,1)S(1)}, bf16[4,288,256]{2,1,0:T(8,128)(2,1)S(1)}, u32[]{:S(2)}, u32[]{:S(2)}) %collective-permute-start.15) | collective-permute-done | bytes 589856 | tf_op jit(solution)/shard_map/ppermute | solution.py:892
  328.8 3.0 copy-done.1
  331.8 3.9 shard_map.268.refs_1_
  337.7 3.8 collective-permute-done.18.refs_3_
  342.8 44.9 %shard_map.269 = (bf16[4,4,288,768]{3,2,1,0:T(8,128)(2,1)}, bf16[4,4,288,384]{3,2,1,0:T(8,128)(2,1)}, f32[4,4,288,1]{3,2,1,0:T(8,128)}, bf16[4,4,288,256]{3,2,1,...) custom-call(s32[2]{0:T(128)} %pad_add_fusion.4.me_ref, ...), custom_call_target="tpu_custom_call" | custom-call | flops 40000000 | bytes 1024 | tf_op jit(solution)/shard_map/pallas_call | solution.py:505
  388.3 13.3 %shard_map.270 = (bf16[4,4,288,768]{3,2,1,0:T(8,128)(2,1)}, bf16[4,288,768]{2,1,0:T(8,128)(2,1)}, bf16[4,288,768]{2,1,0:T(8,128)(2,1)}, bf16[4,288,768]{2,1,0:T(8,128)(2,1)}, bf16[4,288,768]{2,1,0:T(8,128)(2,1)}) custom-call(s32[2]{0:T(128)} %pad_add_fusion.4.me_ref, bf16[4,4,288,384]{3,2,1,0:T(8,128)(2,1)} %get-tuple-element.113.act_ref.refs_0_, ...), custom_call_target="tpu_custom_call" | custom-call | flops 12000000 | bytes 1024 | tf_op jit(solution)/shard_map/pallas_call | solution.py:688
  403.4 4.5 shard_map.271
  412.6 10.5 %collective-permute-done.22.refs_5_.refs_1_ = bf16[4,288,256]{2,1,0:T(8,128)(2,1)S(1)} collective-permute-done((bf16[4,288,256]{2,1,0:T(8,128)(2,1)}, bf16[4,288,256]{2,1,0:T(8,128)(2,1)S(1)}, u32[]{:S(2)}, u32[]{:S(2)}) %collective-permute-start.22) | collective-permute-done | bytes 589856 | tf_op jit(solution)/shard_map/ppermute | solution.py:892
  424.3 12.3 %collective-permute-done.24.refs_7_.refs_3_ = bf16[4,288,256]{2,1,0:T(8,128)(2,1)S(1)} collective-permute-done((bf16[4,288,256]{2,1,0:T(8,128)(2,1)}, bf16[4,288,256]{2,1,0:T(8,128)(2,1)S(1)}, u32[]{:S(2)}, u32[]{:S(2)}) %collective-permute-start.24) | collective-permute-done | bytes 589856 | tf_op jit(solution)/shard_map/ppermute | solution.py:892
  437.3 6.3 shard_map.272
  443.7 7.2 shard_map.273
  453.7 23.3 %collective-permute-done.25.refs_1_ = bf16[4,288,512]{2,1,0:T(8,128)(2,1)} collective-permute-done((bf16[4,288,512]{2,1,0:T(8,128)(2,1)S(1)}, bf16[4,288,512]{2,1,0:T(8,128)(2,1)}, u32[]{:S(2)}, u32[]{:S(2)}) %collective-permute-start.25) | collective-permute-done | bytes 1179680 | tf_op jit(solution)/shard_map/ppermute | solution.py:892
  477.4 25.3 %collective-permute-done.27.refs_3_ = bf16[4,288,512]{2,1,0:T(8,128)(2,1)} collective-permute-done((bf16[4,288,512]{2,1,0:T(8,128)(2,1)S(1)}, bf16[4,288,512]{2,1,0:T(8,128)(2,1)}, u32[]{:S(2)}, u32[]{:S(2)}) %collective-permute-start.27) | collective-permute-done | bytes 1179680 | tf_op jit(solution)/shard_map/ppermute | solution.py:892
  502.7 9.1 %shard_map.274 = (bf16[4,1024,512]{2,1,0:T(8,128)(2,1)}, f32[1,8,128]{2,1,0:T(8,128)}) custom-call(s32[1]{0:T(128)} %bitcast.20.line_ref, s32[4,1024,4]{2,1,0:T(8,128)} %bitcast.122, bf16[4,288,512]{2,1,0:T(8,128)(2,1)} %get-tuple-element.132.refs_0_, bf16[4,288,512]{2,1,0:T(8,128)(2,1)} %collective-permute-done.25.refs_1_, ...), custom_call_target="tpu_custom_call" | custom-call | flops 8000000 | bytes 1024 | tf_op jit(solution)/shard_map/pallas_call | solution.py:383
  523.4 8.6 %shard_map.276 = (bf16[4,288,768]{2,1,0:T(8,128)(2,1)}, bf16[4,288,768]{2,1,0:T(8,128)(2,1)}, bf16[4,288,768]{2,1,0:T(8,128)(2,1)}, bf16[4,288,768]{2,1,0:T(8,128)(2,1)}) custom-call(bf16[4,288,768]{2,1,0:T(8,128)(2,1)} %get-tuple-element.114.refs_0_, bf16[4,288,768]{2,1,0:T(8,128)(2,1)} %get-tuple-element.115.refs_1_, ...), custom_call_target="tpu_custom_call" | custom-call | flops 7000000 | bytes 1024 | tf_op jit(solution)/shard_map/pallas_call | solution.py:560
  533.9 5.1 select_reduce_fusion
  539.0 4.6 collective-permute-start.36
  544.8 7.2 convolution_bitcast_fusion.2
  552.1 3.0 broadcast_select_fusion.3
  556.2 5.3 collective-permute-start.39
  566.5 5.2 convolution_bitcast_fusion.5
  571.7 6.2 convolution_bitcast_fusion.1
  577.9 5.0 convolution_bitcast_fusion
  585.0 9.3 %reduce-scatter.6.cloned.1.call-done.refs_1_ = bf16[1024,512]{1,0:T(8,128)(2,1)} async-done(((bf16[4096,512]{1,0:T(8,128)(2,1)}), bf16[1024,512]{1,0:T(8,128)(2,1)}) %reduce-scatter.6.cloned.1.call-update) | async-done | bytes 1048592 | tf_op jit(solution)/shard_map/reduce_scatter | solution.py:899
  601.9 10.6 %shard_map.281 = (f32[1024,1536]{1,0:T(8,128)}, bf16[1024,1536]{1,0:T(8,128)(2,1)}, bf16[1024,128]{1,0:T(8,128)(2,1)}, f32[1,1536]{1,0:T(1,128)}) custom-call(s32[1]{0:T(128)} %bitcast.side_ref, bf16[1024,256]{1,0:T(8,128)(2,1)} %reduce-scatter.4.cloned.1.call-done.refs_1_.refs_0_, bf16[1024,512]{1,0:T(8,128)(2,1)} %reduce-scatter.6.cloned.1.call-done.refs_1_, ...), custom_call_target="tpu_custom_call" | custom-call | flops 10000000 | bytes 1024 | tf_op jit(solution)/shard_map/pallas_call | solution.py:619
  612.6 13.3 %shard_map.282 = (bf16[4,1024,768]{2,1,0:T(8,128)(2,1)}, f32[1,8,128]{2,1,0:T(8,128)}) custom-call(s32[1]{0:T(128)} %bitcast.20.line_ref, s32[4,1024,4]{2,1,0:T(8,128)} %bitcast.123, bf16[4,288,768]{2,1,0:T(8,128)(2,1)} %get-tuple-element.140.refs_0_, bf16[4,288,768]{2,1,0:T(8,128)(2,1)} %collective-permute-done.31.refs_1_, ...), custom_call_target="tpu_custom_call" | custom-call | flops 12000000 | bytes 1024 | tf_op jit(solution)/shard_map/pallas_call | solution.py:383
  626.0 8.4 %shard_map.284 = (f32[4,96,896]{2,1,0:T(8,128)}, bf16[4,96,896]{2,1,0:T(8,128)(2,1)}, bf16[4,96,896]{2,1,0:T(8,128)(2,1)}, bf16[4,96,896]{2,1,0:T(8,128)(2,1)}) custom-call(s32[1]{0:T(128)} %bitcast.59.spot_ref, bf16[1024,1536]{1,0:T(8,128)(2,1)} %get-tuple-element.149.refs_4_.left_ref.db_ref, bf16[1024,768]{1,0:T(8,128)(2,1)} %get-tuple-element.153.right_ref, ...), custom_call_target="tpu_custom_call" | custom-call | flops 6000000 | bytes 1024 | tf_op jit(solution)/shard_map/pallas_call | solution.py:869
  637.0 26.3 %shard_map.285.d_ref.refs_0_ = bf16[1024,1024]{1,0:T(8,128)(2,1)} custom-call(bf16[1024,768]{1,0:T(8,128)(2,1)} %get-tuple-element.89.q_ref, bf16[1024,128]{1,0:T(8,128)(2,1)} %get-tuple-element.90.k_ref, bf16[1024,128]{1,0:T(8,128)(2,1)} %get-tuple-element.91.v_ref, s32[1,1024]{1,0:T(1,128)} %segq_ref.3, s32[1024,1]{1,0:T(8,128)} %copy.130.segk_ref, ...), custom_call_target="tpu_custom_call" | custom-call | flops 28000000 | bytes 1024 | tf_op jit(solution)/shard_map/pallas_call | solution.py:777
  663.3 3.4 collective-permute-done.42
  668.2 7.8 shard_map.286.refs_1_.a_ref
  677.6 7.5 shard_map.288
  689.4 9.6 %shard_map.289.refs_1_ = f32[1024,1536]{1,0:T(8,128)} custom-call(bf16[1024,1536]{1,0:T(8,128)(2,1)} %shard_map.286.refs_1_.a_ref, bf16[1024,1536]{1,0:T(8,128)(2,1)} %copy-done.15, bf16[1024,1536]{1,0:T(8,128)(2,1)} %x_ref.5, f32[1024,1]{1,0:T(8,128)} %get-tuple-element.161.inv_ref, f32[1024,1536]{1,0:T(8,128)} %get-tuple-element.162.dh_ref, ...), custom_call_target="tpu_custom_call" | custom-call | flops 8000000 | bytes 1024 | tf_op jit(solution)/shard_map/pallas_call | solution.py:653
  699.0 5.6 collective-permute-done.44
  705.1 17.2 %collective-permute-done.46 = bf16[4,96,1024]{2,1,0:T(8,128)(2,1)} collective-permute-done((bf16[4,96,1024]{2,1,0:T(8,128)(2,1)}, bf16[4,96,1024]{2,1,0:T(8,128)(2,1)}, u32[]{:S(2)}, u32[]{:S(2)}) %collective-permute-start.46) | collective-permute-done | bytes 786464 | tf_op jit(solution)/shard_map/ppermute | solution.py:892
  722.4 2.6 convert_add_fusion
  726.2 2.4 collective-permute-start.48
  728.6 21.8 %collective-permute-done.47 = bf16[96,1920]{1,0:T(8,128)(2,1)} collective-permute-done((bf16[96,1920]{1,0:T(8,128)(2,1)}, bf16[96,1920]{1,0:T(8,128)(2,1)}, u32[]{:S(2)}, u32[]{:S(2)}) %collective-permute-start.47) | collective-permute-done | bytes 368672 | tf_op jit(solution)/shard_map/ppermute | solution.py:892
  750.4 3.5 collective-permute-done.48
  753.8 14.6 %collective-permute-done.49 = bf16[96,1920]{1,0:T(8,128)(2,1)} collective-permute-done((bf16[96,1920]{1,0:T(8,128)(2,1)S(1)}, bf16[96,1920]{1,0:T(8,128)(2,1)}, u32[]{:S(2)}, u32[]{:S(2)}) %collective-permute-start.49) | collective-permute-done | bytes 368672 | tf_op jit(solution)/shard_map/ppermute | solution.py:892
  771.5 2.8 add_convert_fusion
  (262 shorter events, 105.4 us)
Async XLA Ops:
  7.2 118.8 %all-gather.7.cloned.1.call-start = ((), (), s32[]{:S(2)}) async-start(), calls=%async_computation.6 | async-start | bytes 7864320 | tf_op jit(solution)/shard_map/all_gather | solution.py:895
  9.9 208.6 %all-gather.9.cloned.1.call-start = ((), (), s32[]{:S(2)}) async-start(), calls=%async_computation.7 | async-start | bytes 5242880 | tf_op jit(solution)/shard_map/all_gather | solution.py:895
  20.7 27.5 %copy-start.38 = (s32[1024,4]{0,1:T(4,128)S(1)}, s32[1024,4]{0,1:T(4,128)}, u32[]{:S(2)}) copy-start(s32[1024,4]{0,1:T(4,128)} %param.29) | copy-start | bytes 49156
  44.8 43.9 %collective-permute-start = (bf16[1024,1536]{1,0:T(8,128)(2,1)}, bf16[1024,1536]{1,0:T(8,128)(2,1)S(1)}, u32[]{:S(2)}, u32[]{:S(2)}) collective-permute-start(bf16[1024,1536]{1,0:T(8,128)(2,1)} %get-tuple-element.92.a_ref), channel_id=1, source_target_pairs={{0,1},{1,0},{2,3},{3,2},{4,5},{5,4},{6,7},{7,6},{8,9},{9,8},{10,11... | collective-permute-start | bytes 9437192 | tf_op jit(solution)/shard_map/ppermute | solution.py:929
  48.2 30.4 %copy-start.39 = (bf16[1536,16]{0,1:T(8,128)(2,1)S(1)}, bf16[1536,16]{0,1:T(8,128)(2,1)}, u32[]{:S(2)}) copy-start(bf16[1536,16]{0,1:T(8,128)(2,1)} %param.25) | copy-start | bytes 147460
  48.9 30.6 %copy-start.43 = (f32[1536]{0:T(1024)S(1)}, f32[1536]{0:T(1024)}, u32[]{:S(2)}) copy-start(f32[1536]{0:T(1024)} %param.20) | copy-start | bytes 18436
  58.7 4.1 collective-permute-start.1
  58.8 6.3 collective-permute-start.2
  61.2 4.8 collective-permute-start.3
  74.8 6.2 collective-permute-start.4
  76.1 8.6 %collective-permute-start.5 = (bf16[4,288,4]{2,1,0:T(8,128)(2,1)}, bf16[4,288,4]{2,1,0:T(8,128)(2,1)}, u32[]{:S(2)}, u32[]{:S(2)}) collective-permute-start(bf16[4,288,4]{2,1,0:T(8,128)(2,1)} %get-tuple-element.95), channel_id=1, source_target_pairs={{0,4},{2,6},{4,0},{6,2},{8,12},{10,14},{12,8},{14,10},{16,20},{18,... | collective-permute-start | bytes 27656 | tf_op jit(solution)/shard_map/ppermute | solution.py:892
  77.3 8.9 %collective-permute-start.6 = (bf16[4,288,4]{2,1,0:T(8,128)(2,1)}, bf16[4,288,4]{2,1,0:T(8,128)(2,1)}, u32[]{:S(2)}, u32[]{:S(2)}) collective-permute-start(bf16[4,288,4]{2,1,0:T(8,128)(2,1)} %get-tuple-element.96), channel_id=1, source_target_pairs={{0,6},{2,4},{4,2},{6,0},{8,14},{10,12},{12,10},{14,8},{16,22},{18,... | collective-permute-start | bytes 27656 | tf_op jit(solution)/shard_map/ppermute | solution.py:892
  126.0 151.0 %all-gather.11.cloned.1.call-start = ((), (), s32[]{:S(2)}) async-start(), calls=%async_computation.8 | async-start | bytes 2621440 | tf_op jit(solution)/shard_map/all_gather | solution.py:895
  139.8 39.9 %collective-permute-start.10 = (bf16[4,288,768]{2,1,0:T(8,128)(2,1)}, bf16[4,288,768]{2,1,0:T(8,128)(2,1)S(1)}, u32[]{:S(2)}, u32[]{:S(2)}) collective-permute-start(bf16[4,288,768]{2,1,0:T(8,128)(2,1)} %get-tuple-element.105), channel_id=1, source_target_pairs={{0,2},{2,0},{4,6},{6,4},{8,10},{10,8},{12,14},{14,12},{16,18},{18,... | collective-permute-start | bytes 5308424 | tf_op jit(solution)/shard_map/ppermute | solution.py:892
  141.0 39.4 %collective-permute-start.11 = (bf16[4,288,768]{2,1,0:T(8,128)(2,1)}, bf16[4,288,768]{2,1,0:T(8,128)(2,1)S(1)}, u32[]{:S(2)}, u32[]{:S(2)}) collective-permute-start(bf16[4,288,768]{2,1,0:T(8,128)(2,1)} %get-tuple-element.106), channel_id=1, source_target_pairs={{0,4},{2,6},{4,0},{6,2},{8,12},{10,14},{12,8},{14,10},{16,20},{18,... | collective-permute-start | bytes 5308424 | tf_op jit(solution)/shard_map/ppermute | solution.py:892
  142.2 76.3 %collective-permute-start.12 = (bf16[4,288,768]{2,1,0:T(8,128)(2,1)}, bf16[4,288,768]{2,1,0:T(8,128)(2,1)}, u32[]{:S(2)}, u32[]{:S(2)}) collective-permute-start(bf16[4,288,768]{2,1,0:T(8,128)(2,1)} %get-tuple-element.107), channel_id=1, source_target_pairs={{0,6},{2,4},{4,2},{6,0},{8,14},{10,12},{12,10},{14,8},{16,22},{18,... | collective-permute-start | bytes 5308424 | tf_op jit(solution)/shard_map/ppermute | solution.py:892
  179.6 38.9 %copy-start.9 = (bf16[4,288,768]{2,1,0:T(8,128)(2,1)}, bf16[4,288,768]{2,1,0:T(8,128)(2,1)S(1)}, u32[]{:S(2)}) copy-start(bf16[4,288,768]{2,1,0:T(8,128)(2,1)S(1)} %collective-permute-done.10.refs_2_.refs_1_) | copy-start | bytes 5308420
  180.4 38.1 %copy-start.10 = (bf16[4,288,768]{2,1,0:T(8,128)(2,1)}, bf16[4,288,768]{2,1,0:T(8,128)(2,1)S(1)}, u32[]{:S(2)}) copy-start(bf16[4,288,768]{2,1,0:T(8,128)(2,1)S(1)} %collective-permute-done.11.refs_3_.refs_2_) | copy-start | bytes 5308420
  218.6 293.2 %reduce-scatter.4.cloned.1.call-start = ((), (), s32[]{:S(2)}) async-start(), calls=%async_computation.3 | async-start | bytes 2621440 | tf_op jit(solution)/shard_map/reduce_scatter | solution.py:899
  226.5 25.2 %collective-permute-start.7 = (bf16[4,288,512]{2,1,0:T(8,128)(2,1)}, bf16[4,288,512]{2,1,0:T(8,128)(2,1)S(1)}, u32[]{:S(2)}, u32[]{:S(2)}) collective-permute-start(bf16[4,288,512]{2,1,0:T(8,128)(2,1)} %get-tuple-element.100), channel_id=1, source_target_pairs={{0,2},{2,0},{4,6},{6,4},{8,10},{10,8},{12,14},{14,12},{16,18},{18,... | collective-permute-start | bytes 3538952 | tf_op jit(solution)/shard_map/ppermute | solution.py:892
  227.7 28.9 %collective-permute-start.8 = (bf16[4,288,512]{2,1,0:T(8,128)(2,1)}, bf16[4,288,512]{2,1,0:T(8,128)(2,1)S(1)}, u32[]{:S(2)}, u32[]{:S(2)}) collective-permute-start(bf16[4,288,512]{2,1,0:T(8,128)(2,1)} %get-tuple-element.101), channel_id=1, source_target_pairs={{0,4},{2,6},{4,0},{6,2},{8,12},{10,14},{12,8},{14,10},{16,20},{18,... | collective-permute-start | bytes 3538952 | tf_op jit(solution)/shard_map/ppermute | solution.py:892
  228.0 49.0 %collective-permute-start.9 = (bf16[4,288,512]{2,1,0:T(8,128)(2,1)}, bf16[4,288,512]{2,1,0:T(8,128)(2,1)}, u32[]{:S(2)}, u32[]{:S(2)}) collective-permute-start(bf16[4,288,512]{2,1,0:T(8,128)(2,1)} %get-tuple-element.102), channel_id=1, source_target_pairs={{0,6},{2,4},{4,2},{6,0},{8,14},{10,12},{12,10},{14,8},{16,22},{18,... | collective-permute-start | bytes 3538952 | tf_op jit(solution)/shard_map/ppermute | solution.py:892
  288.5 38.0 %collective-permute-start.17 = (bf16[4,4,288,768]{3,2,1,0:T(8,128)(2,1)}, bf16[4,4,288,768]{3,2,1,0:T(8,128)(2,1)S(1)}, u32[]{:S(2)}, u32[]{:S(2)}) collective-permute-start(bf16[4,4,288,768]{3,2,1,0:T(8,128)(2,1)} %shard_map.266.refs_4_), channel_id=1, source_target_pairs={{0,1},{1,0},{2,3},{3,2},{4,5},{5,4},{6,7},{7,6},{8,9},{9,8},{10,11... | collective-permute-start | bytes 21233672 | tf_op jit(solution)/shard_map/ppermute | solution.py:929
  299.2 27.3 %collective-permute-start.16 = (bf16[4,4,288,512]{3,2,1,0:T(8,128)(2,1)}, bf16[4,4,288,512]{3,2,1,0:T(8,128)(2,1)S(1)}, u32[]{:S(2)}, u32[]{:S(2)}) collective-permute-start(bf16[4,4,288,512]{3,2,1,0:T(8,128)(2,1)} %shard_map.267.refs_0_), channel_id=1, source_target_pairs={{0,1},{1,0},{2,3},{3,2},{4,5},{5,4},{6,7},{7,6},{8,9},{9,8},{10,11... | collective-permute-start | bytes 14155784 | tf_op jit(solution)/shard_map/ppermute | solution.py:929
  299.2 14.6 %collective-permute-start.13 = (bf16[4,288,256]{2,1,0:T(8,128)(2,1)}, bf16[4,288,256]{2,1,0:T(8,128)(2,1)S(1)}, u32[]{:S(2)}, u32[]{:S(2)}) collective-permute-start(bf16[4,288,256]{2,1,0:T(8,128)(2,1)} %get-tuple-element.109.refs_4_), channel_id=1, source_target_pairs={{0,2},{2,0},{4,6},{6,4},{8,10},{10,8},{12,14},{14,12},{16,18},{18,... | collective-permute-start | bytes 1769480 | tf_op jit(solution)/shard_map/ppermute | solution.py:892
  299.5 14.3 %collective-permute-start.14 = (bf16[4,288,256]{2,1,0:T(8,128)(2,1)S(1)}, bf16[4,288,256]{2,1,0:T(8,128)(2,1)S(1)}, u32[]{:S(2)}, u32[]{:S(2)}) collective-permute-start(bf16[4,288,256]{2,1,0:T(8,128)(2,1)S(1)} %copy-done.30), channel_id=1, source_target_pairs={{0,4},{2,6},{4,0},{6,2},{8,12},{10,14},{12,8},{14,10},{16,20},{18,... | collective-permute-start | bytes 1769480 | tf_op jit(solution)/shard_map/ppermute | solution.py:892
  299.6 26.9 %collective-permute-start.15 = (bf16[4,288,256]{2,1,0:T(8,128)(2,1)S(1)}, bf16[4,288,256]{2,1,0:T(8,128)(2,1)S(1)}, u32[]{:S(2)}, u32[]{:S(2)}) collective-permute-start(bf16[4,288,256]{2,1,0:T(8,128)(2,1)S(1)} %copy-done.29), channel_id=1, source_target_pairs={{0,6},{2,4},{4,2},{6,0},{8,14},{10,12},{12,10},{14,8},{16,22},{18,... | collective-permute-start | bytes 1769480 | tf_op jit(solution)/shard_map/ppermute | solution.py:892
  335.7 5.8 collective-permute-start.18
  387.7 48.8 %collective-permute-start.20 = (bf16[4,4,288,512]{3,2,1,0:T(8,128)(2,1)}, bf16[4,4,288,512]{3,2,1,0:T(8,128)(2,1)}, u32[]{:S(2)}, u32[]{:S(2)}) collective-permute-start(bf16[4,4,288,512]{3,2,1,0:T(8,128)(2,1)} %get-tuple-element.123), channel_id=1, source_target_pairs={{0,1},{1,0},{2,3},{3,2},{4,5},{5,4},{6,7},{7,6},{8,9},{9,8},{10,11... | collective-permute-start | bytes 14155784 | tf_op jit(solution)/shard_map/ppermute | solution.py:929
  388.2 13.8 %collective-permute-start.21 = (bf16[4,4,288,256]{3,2,1,0:T(8,128)(2,1)}, bf16[4,4,288,256]{3,2,1,0:T(8,128)(2,1)S(1)}, u32[]{:S(2)}, u32[]{:S(2)}) collective-permute-start(bf16[4,4,288,256]{3,2,1,0:T(8,128)(2,1)} %get-tuple-element.128), channel_id=1, source_target_pairs={{0,1},{1,0},{2,3},{3,2},{4,5},{5,4},{6,7},{7,6},{8,9},{9,8},{10,11... | collective-permute-start | bytes 7077896 | tf_op jit(solution)/shard_map/ppermute | solution.py:929
  401.6 121.8 %collective-permute-start.19 = (bf16[4,4,288,768]{3,2,1,0:T(8,128)(2,1)}, bf16[4,4,288,768]{3,2,1,0:T(8,128)(2,1)}, u32[]{:S(2)}, u32[]{:S(2)}) collective-permute-start(bf16[4,4,288,768]{3,2,1,0:T(8,128)(2,1)} %get-tuple-element.118.refs_8_.refs_1_), channel_id=1, source_target_pairs={{0,1},{1,0},{2,3},{3,2},{4,5},{5,4},{6,7},{7,6},{8,9},{9,8},{10,11... | collective-permute-start | bytes 21233672 | tf_op jit(solution)/shard_map/ppermute | solution.py:929
  408.0 15.1 %collective-permute-start.22 = (bf16[4,288,256]{2,1,0:T(8,128)(2,1)}, bf16[4,288,256]{2,1,0:T(8,128)(2,1)S(1)}, u32[]{:S(2)}, u32[]{:S(2)}) collective-permute-start(bf16[4,288,256]{2,1,0:T(8,128)(2,1)} %get-tuple-element.129), channel_id=1, source_target_pairs={{0,2},{2,0},{4,6},{6,4},{8,10},{10,8},{12,14},{14,12},{16,18},{18,... | collective-permute-start | bytes 1769480 | tf_op jit(solution)/shard_map/ppermute | solution.py:892
  409.3 15.0 %collective-permute-start.23 = (bf16[4,288,256]{2,1,0:T(8,128)(2,1)}, bf16[4,288,256]{2,1,0:T(8,128)(2,1)S(1)}, u32[]{:S(2)}, u32[]{:S(2)}) collective-permute-start(bf16[4,288,256]{2,1,0:T(8,128)(2,1)} %get-tuple-element.130), channel_id=1, source_target_pairs={{0,4},{2,6},{4,0},{6,2},{8,12},{10,14},{12,8},{14,10},{16,20},{18,... | collective-permute-start | bytes 1769480 | tf_op jit(solution)/shard_map/ppermute | solution.py:892
  409.4 27.1 %collective-permute-start.24 = (bf16[4,288,256]{2,1,0:T(8,128)(2,1)}, bf16[4,288,256]{2,1,0:T(8,128)(2,1)S(1)}, u32[]{:S(2)}, u32[]{:S(2)}) collective-permute-start(bf16[4,288,256]{2,1,0:T(8,128)(2,1)} %get-tuple-element.131), channel_id=1, source_target_pairs={{0,6},{2,4},{4,2},{6,0},{8,14},{10,12},{12,10},{14,8},{16,22},{18,... | collective-permute-start | bytes 1769480 | tf_op jit(solution)/shard_map/ppermute | solution.py:892
  450.9 143.4 %reduce-scatter.6.cloned.1.call-start = ((), (), s32[]{:S(2)}) async-start(), calls=%async_computation.4 | async-start | bytes 5242880 | tf_op jit(solution)/shard_map/reduce_scatter | solution.py:899
  450.9 26.1 %collective-permute-start.25 = (bf16[4,288,512]{2,1,0:T(8,128)(2,1)S(1)}, bf16[4,288,512]{2,1,0:T(8,128)(2,1)}, u32[]{:S(2)}, u32[]{:S(2)}) collective-permute-start(bf16[4,288,512]{2,1,0:T(8,128)(2,1)S(1)} %copy-done.27), channel_id=1, source_target_pairs={{0,2},{2,0},{4,6},{6,4},{8,10},{10,8},{12,14},{14,12},{16,18},{18,... | collective-permute-start | bytes 3538952 | tf_op jit(solution)/shard_map/ppermute | solution.py:892
  451.4 26.0 %collective-permute-start.26 = (bf16[4,288,512]{2,1,0:T(8,128)(2,1)S(1)}, bf16[4,288,512]{2,1,0:T(8,128)(2,1)}, u32[]{:S(2)}, u32[]{:S(2)}) collective-permute-start(bf16[4,288,512]{2,1,0:T(8,128)(2,1)S(1)} %copy-done.26), channel_id=1, source_target_pairs={{0,4},{2,6},{4,0},{6,2},{8,12},{10,14},{12,8},{14,10},{16,20},{18,... | collective-permute-start | bytes 3538952 | tf_op jit(solution)/shard_map/ppermute | solution.py:892
  452.7 50.0 %collective-permute-start.27 = (bf16[4,288,512]{2,1,0:T(8,128)(2,1)S(1)}, bf16[4,288,512]{2,1,0:T(8,128)(2,1)}, u32[]{:S(2)}, u32[]{:S(2)}) collective-permute-start(bf16[4,288,512]{2,1,0:T(8,128)(2,1)S(1)} %copy-done.25), channel_id=1, source_target_pairs={{0,6},{2,4},{4,2},{6,0},{8,14},{10,12},{12,10},{14,8},{16,22},{18,... | collective-permute-start | bytes 3538952 | tf_op jit(solution)/shard_map/ppermute | solution.py:892
  511.8 259.7 %reduce-scatter.8.cloned.1.call-start = ((), (), s32[]{:S(2)}) async-start(), calls=%async_computation.5 | async-start | bytes 7864320 | tf_op jit(solution)/shard_map/reduce_scatter | solution.py:899
  516.0 4.8 collective-permute-start.28
  519.0 2.7 collective-permute-start.29
  519.3 3.4 collective-permute-start.30
  532.0 80.6 %collective-permute-start.31 = (bf16[4,288,768]{2,1,0:T(8,128)(2,1)}, bf16[4,288,768]{2,1,0:T(8,128)(2,1)}, u32[]{:S(2)}, u32[]{:S(2)}) collective-permute-start(bf16[4,288,768]{2,1,0:T(8,128)(2,1)} %get-tuple-element.141.refs_1_), channel_id=1, source_target_pairs={{0,2},{2,0},{4,6},{6,4},{8,10},{10,8},{12,14},{14,12},{16,18},{18,... | collective-permute-start | bytes 5308424 | tf_op jit(solution)/shard_map/ppermute | solution.py:892
  532.9 79.7 %collective-permute-start.32 = (bf16[4,288,768]{2,1,0:T(8,128)(2,1)}, bf16[4,288,768]{2,1,0:T(8,128)(2,1)}, u32[]{:S(2)}, u32[]{:S(2)}) collective-permute-start(bf16[4,288,768]{2,1,0:T(8,128)(2,1)} %get-tuple-element.142.refs_2_), channel_id=1, source_target_pairs={{0,4},{2,6},{4,0},{6,2},{8,12},{10,14},{12,8},{14,10},{16,20},{18,... | collective-permute-start | bytes 5308424 | tf_op jit(solution)/shard_map/ppermute | solution.py:892
  539.0 16.0 %collective-permute-start.36 = (f32[4,1024]{1,0:T(4,128)S(1)}, f32[4,1024]{1,0:T(4,128)S(1)}, u32[]{:S(2)}, u32[]{:S(2)}) collective-permute-start(f32[4,1024]{1,0:T(4,128)S(1)} %get-tuple-element.255), channel_id=1, source_target_pairs={{0,8},{2,10},{4,12},{6,14},{8,0},{10,2},{12,4},{14,6},{16,24},{18,... | collective-permute-start | bytes 49160 | tf_op jit(solution)/shard_map/ppermute | solution.py:892
  543.6 12.6 %collective-permute-start.37 = (f32[4,1024]{1,0:T(4,128)S(1)}, f32[4,1024]{1,0:T(4,128)S(1)}, u32[]{:S(2)}, u32[]{:S(2)}) collective-permute-start(f32[4,1024]{1,0:T(4,128)S(1)} %get-tuple-element.254), channel_id=1, source_target_pairs={{0,16},{2,18},{4,20},{6,22},{8,24},{10,26},{12,28},{14,30},{16,0},... | collective-permute-start | bytes 49160 | tf_op jit(solution)/shard_map/ppermute | solution.py:892
  543.6 12.6 %collective-permute-start.38 = (f32[4,1024]{1,0:T(4,128)S(1)}, f32[4,1024]{1,0:T(4,128)S(1)}, u32[]{:S(2)}, u32[]{:S(2)}) collective-permute-start(f32[4,1024]{1,0:T(4,128)S(1)} %get-tuple-element.253), channel_id=1, source_target_pairs={{0,24},{2,26},{4,28},{6,30},{8,16},{10,18},{12,20},{14,22},{16,8},... | collective-permute-start | bytes 49160 | tf_op jit(solution)/shard_map/ppermute | solution.py:892
  555.0 57.6 %collective-permute-start.33 = (bf16[4,288,768]{2,1,0:T(8,128)(2,1)}, bf16[4,288,768]{2,1,0:T(8,128)(2,1)}, u32[]{:S(2)}, u32[]{:S(2)}) collective-permute-start(bf16[4,288,768]{2,1,0:T(8,128)(2,1)} %get-tuple-element.143.refs_3_), channel_id=1, source_target_pairs={{0,6},{2,4},{4,2},{6,0},{8,14},{10,12},{12,10},{14,8},{16,22},{18,... | collective-permute-start | bytes 5308424 | tf_op jit(solution)/shard_map/ppermute | solution.py:892
  556.2 7.0 collective-permute-start.39
  594.3 6.5 collective-permute-start.35
  597.7 3.1 collective-permute-start.34
  634.3 29.0 %collective-permute-start.40 = (bf16[4,96,896]{2,1,0:T(8,128)(2,1)}, bf16[4,96,896]{2,1,0:T(8,128)(2,1)S(1)}, u32[]{:S(2)}, u32[]{:S(2)}) collective-permute-start(bf16[4,96,896]{2,1,0:T(8,128)(2,1)} %get-tuple-element.156.refs_0_), channel_id=1, source_target_pairs={{0,2},{2,0},{4,6},{6,4},{8,10},{10,8},{12,14},{14,12},{16,18},{18,... | collective-permute-start | bytes 2064392 | tf_op jit(solution)/shard_map/ppermute | solution.py:892
  635.5 27.8 %collective-permute-start.41 = (bf16[4,96,896]{2,1,0:T(8,128)(2,1)}, bf16[4,96,896]{2,1,0:T(8,128)(2,1)S(1)}, u32[]{:S(2)}, u32[]{:S(2)}) collective-permute-start(bf16[4,96,896]{2,1,0:T(8,128)(2,1)} %get-tuple-element.157.refs_1_), channel_id=1, source_target_pairs={{0,4},{2,6},{4,0},{6,2},{8,12},{10,14},{12,8},{14,10},{16,20},{18,... | collective-permute-start | bytes 2064392 | tf_op jit(solution)/shard_map/ppermute | solution.py:892
  636.7 30.0 %collective-permute-start.42 = (bf16[4,96,896]{2,1,0:T(8,128)(2,1)}, bf16[4,96,896]{2,1,0:T(8,128)(2,1)S(1)}, u32[]{:S(2)}, u32[]{:S(2)}) collective-permute-start(bf16[4,96,896]{2,1,0:T(8,128)(2,1)} %get-tuple-element.158.refs_2_), channel_id=1, source_target_pairs={{0,6},{2,4},{4,2},{6,0},{8,14},{10,12},{12,10},{14,8},{16,22},{18,... | collective-permute-start | bytes 2064392 | tf_op jit(solution)/shard_map/ppermute | solution.py:892
  637.0 29.8 %copy-start.22 = (f32[4,96,896]{2,1,0:T(8,128)S(1)}, f32[4,96,896]{2,1,0:T(8,128)}, u32[]{:S(2)}) copy-start(f32[4,96,896]{2,1,0:T(8,128)} %get-tuple-element.159) | copy-start | bytes 4128772
  676.0 11.8 %collective-permute-start.43 = (bf16[1024,1536]{1,0:T(8,128)(2,1)}, bf16[1024,1536]{1,0:T(8,128)(2,1)S(1)}, u32[]{:S(2)}, u32[]{:S(2)}) collective-permute-start(bf16[1024,1536]{1,0:T(8,128)(2,1)} %shard_map.286.refs_1_.a_ref), channel_id=1, source_target_pairs={{0,1},{1,0},{2,3},{3,2},{4,5},{5,4},{6,7},{7,6},{8,9},{9,8},{10,11... | collective-permute-start | bytes 9437192 | tf_op jit(solution)/shard_map/ppermute | solution.py:929
  685.1 19.5 %collective-permute-start.44 = (bf16[4,96,1024]{2,1,0:T(8,128)(2,1)}, bf16[4,96,1024]{2,1,0:T(8,128)(2,1)}, u32[]{:S(2)}, u32[]{:S(2)}) collective-permute-start(bf16[4,96,1024]{2,1,0:T(8,128)(2,1)} %get-tuple-element.163), channel_id=1, source_target_pairs={{0,2},{2,0},{4,6},{6,4},{8,10},{10,8},{12,14},{14,12},{16,18},{18,... | collective-permute-start | bytes 2359304 | tf_op jit(solution)/shard_map/ppermute | solution.py:892
  686.0 19.1 %collective-permute-start.45 = (bf16[4,96,1024]{2,1,0:T(8,128)(2,1)}, bf16[4,96,1024]{2,1,0:T(8,128)(2,1)}, u32[]{:S(2)}, u32[]{:S(2)}) collective-permute-start(bf16[4,96,1024]{2,1,0:T(8,128)(2,1)} %get-tuple-element.164), channel_id=1, source_target_pairs={{0,4},{2,6},{4,0},{6,2},{8,12},{10,14},{12,8},{14,10},{16,20},{18,... | collective-permute-start | bytes 2359304 | tf_op jit(solution)/shard_map/ppermute | solution.py:892
  686.6 35.7 %collective-permute-start.46 = (bf16[4,96,1024]{2,1,0:T(8,128)(2,1)}, bf16[4,96,1024]{2,1,0:T(8,128)(2,1)}, u32[]{:S(2)}, u32[]{:S(2)}) collective-permute-start(bf16[4,96,1024]{2,1,0:T(8,128)(2,1)} %get-tuple-element.165), channel_id=1, source_target_pairs={{0,6},{2,4},{4,2},{6,0},{8,14},{10,12},{12,10},{14,8},{16,22},{18,... | collective-permute-start | bytes 2359304 | tf_op jit(solution)/shard_map/ppermute | solution.py:892
  726.0 24.4 %collective-permute-start.47 = (bf16[96,1920]{1,0:T(8,128)(2,1)}, bf16[96,1920]{1,0:T(8,128)(2,1)}, u32[]{:S(2)}, u32[]{:S(2)}) collective-permute-start(bf16[96,1920]{1,0:T(8,128)(2,1)} %get-tuple-element.236), channel_id=1, source_target_pairs={{0,8},{2,10},{4,12},{6,14},{8,0},{10,2},{12,4},{14,6},{16,24},{18,... | collective-permute-start | bytes 1105928 | tf_op jit(solution)/shard_map/ppermute | solution.py:892
  726.2 27.7 %collective-permute-start.48 = (bf16[96,1920]{1,0:T(8,128)(2,1)}, bf16[96,1920]{1,0:T(8,128)(2,1)}, u32[]{:S(2)}, u32[]{:S(2)}) collective-permute-start(bf16[96,1920]{1,0:T(8,128)(2,1)} %get-tuple-element.237), channel_id=1, source_target_pairs={{0,16},{2,18},{4,20},{6,22},{8,24},{10,26},{12,28},{14,30},{16,0},... | collective-permute-start | bytes 1105928 | tf_op jit(solution)/shard_map/ppermute | solution.py:892
  728.6 39.9 %collective-permute-start.49 = (bf16[96,1920]{1,0:T(8,128)(2,1)S(1)}, bf16[96,1920]{1,0:T(8,128)(2,1)}, u32[]{:S(2)}, u32[]{:S(2)}) collective-permute-start(bf16[96,1920]{1,0:T(8,128)(2,1)S(1)} %get-tuple-element.238), channel_id=1, source_target_pairs={{0,24},{2,26},{4,28},{6,30},{8,16},{10,18},{12,20},{14,22},{16,8},... | collective-permute-start | bytes 1105928 | tf_op jit(solution)/shard_map/ppermute | solution.py:892
  774.3 6.7 collective-permute-start.50
  779.0 1.4 collective-permute-start.51
  (43 other events, 289.5 us)
Sparse Core Ops, SparseCore 0:
  10.2 115.7 all-gather.6
  127.5 79.9 all-gather.8
  218.7 47.2 all-gather.10
  451.0 44.5 reduce-scatter.3
  511.9 82.3 reduce-scatter.5
  626.1 121.2 reduce-scatter.7

commit v5 on v4

--- a/solution.py
+++ b/solution.py
@@ -1121,12 +1121,13 @@
     )
     shared = share_grads(spot_ref, first_in, hold(d_all, d_first), depth, width)
     shared = [hold(shared[0], input_grad), *shared[1:]]
-    summed = link.sum_line(jnp.concatenate([link.sum_plane(shared), early_held], axis=2))
+    qkv_held = link.sum_plane(shared)
+    summed = link.sum_line(jnp.concatenate([qkv_held, early_held], axis=2))
     columns = span + 2 * head_width
     qkv_grad, early_sum = summed[:, :columns], summed[:, columns:]
     out_grad = early_sum[:, :span].T
     router_grad, ffn_gain_grad = early_sum[:, span : span + expert_count], early_sum[:, -1]
-    combined = wide(hold(link.collect(out_held), qkv_grad))
+    combined = wide(hold(link.collect(out_held), qkv_held))
     output_half = low(half_of(hidden, side) + combined)
     output = join_halves(output_half, swap(output_half), side)
     rows = model_width // expert_count

time: 802 us -> 798 us (level)
    ppermute x39, waiting for transfers between devices: 301 us -> 277 us  [flip(): lax.ppermute(rows, 'expert', [(d, d ^ mask) for d in range(self.count)])]
    reduce_scatter x3, waiting for transfers between devices: 9.3 us -> 28 us  [collect(): lax.psum_scatter(flat, 'expert', scatter_dimension=0, axis_index_groups=s...]
where the time goes in v5:
time: 798 us; the launch traced here: 788 us
  waiting for transfers between devices  335 us (42%)
  Pallas kernels  274 us (34%)
  starting transfers between devices  56.5 us (7%)
  local copies, waits for them, and re-layouts  41.5 us (5%)
  other arithmetic  37.6 us (5%)
  matrix products  28.5 us (4%)
  between operations  15.1 us (2%)
    ppermute x39, waiting for transfers between devices, flip(): lax.ppermute(rows, 'expert', [(d, d ^ mask) for d in range(self.count)])  277 us
    pallas_call x1, Pallas kernels, expert_rows(): pl.pallas_call(functools.partial(expert_kernel, len(pieces) // 2, len(c_p...  44.9 us
    ppermute x39, starting transfers between devices, flip(): lax.ppermute(rows, 'expert', [(d, d ^ mask) for d in range(self.count)])  38.6 us
    pallas_call x3, Pallas kernels, combine(): pl.pallas_call(functools.partial(combine_kernel, width, capacity), grid_s...  29.5 us
    pallas_call x4, Pallas kernels, pick_rows(): pl.pallas_call(functools.partial(pick_kernel, width, capacity, len(out_sh...  29.1 us
    dot_general x6, matrix products, contract_rows(): lax.dot_general(left, right, (((0,), (0,)), ((), ())), preferred_element_...  28.5 us
    reduce_scatter x3, waiting for transfers between devices, collect(): lax.psum_scatter(flat, 'expert', scatter_dimension=0, axis_index_groups=s...  28 us
    pallas_call x1, Pallas kernels, attend_back(): pl.pallas_call(functools.partial(attend_back_kernel, heads, scale, tile,...  26.3 us
  transfers between devices with their start and end apart: 58, of which 32 were waited for; matrix products, arithmetic and copies ran while one was open for 10% of the time, Pallas kernels for 25%

profile of v5, /device:TPU:9, one launch (start us, length us, event | category | flops | bytes accessed | tf_op | source)
XLA Modules:
  0.0 787.7 jit_solution(16596259422434063013)
XLA Ops:
  7.3 2.7 constant_dynamic-slice_fusion
  11.7 9.0 %shard_map.256 = (bf16[1024,1536]{1,0:T(8,128)(2,1)}, bf16[1024,768]{1,0:T(8,128)(2,1)}, bf16[1024,128]{1,0:T(8,128)(2,1)}, bf16[1024,128]{1,0:T(8,128)(2,1)}, f32[1024,1]{1,0:T(8,128)}) custom-call(bf16[1024,1536]{1,0:T(8,128)(2,1)} %x_ref.5, f32[1,1536]{1,0:T(1,128)} %broadcast_in_dim.70.gain_ref, bf16[1536,768]{1,0:T(8,128)(2,1)} %wq_ref.3, ...), custom_call_target="tpu_custom_call" | custom-call | flops 9000000 | bytes 1024 | tf_op jit(solution)/shard_map/pallas_call | solution.py:162
  20.7 24.1 %shard_map.257 = (bf16[1024,768]{1,0:T(8,128)(2,1)}, f32[6,1024]{1,0:T(8,128)}, bf16[1024,1536]{1,0:T(8,128)(2,1)}) custom-call(bf16[1024,768]{1,0:T(8,128)(2,1)} %get-tuple-element.89.q_ref, bf16[1024,128]{1,0:T(8,128)(2,1)} %get-tuple-element.90.k_ref, bf16[1024,128]{1,0:T(8,128)(2,1)} %get-tuple-element.91.v_ref, s32[1,1024]{1,0:T(1,128)} %segq_ref.3, ...), custom_call_target="tpu_custom_call" | custom-call | flops 20000000 | bytes 1024 | tf_op jit(solution)/shard_map/pallas_call | solution.py:207
  48.9 8.9 %shard_map.258 = s32[16,1024]{1,0:T(8,128)} custom-call(s32[16,1024]{1,0:T(8,128)} %compare_select_fusion.keys_ref), custom_call_target="tpu_custom_call" | custom-call | flops 9000000 | bytes 1024 | tf_op jit(solution)/shard_map/pallas_call | solution.py:118
  58.7 2.5 collective-permute-start.2
  62.8 2.3 collective-permute-done.2
  69.5 5.3 shard_map.259
  81.0 3.9 collective-permute-done.5
  86.1 2.5 pad_maximum_fusion.4.refs_1_.refs_6_
  90.3 10.0 %shard_map.260 = (f32[1024,1536]{1,0:T(8,128)}, bf16[1024,1536]{1,0:T(8,128)(2,1)}, f32[1024,1]{1,0:T(8,128)}, f32[1024,16]{1,0:T(8,128)}, bf16[1024,512]{1,0:T(8,128)(2,1)}, /*index=5*/bf16[1024,256]{1,0:T(8,128)(2,1)}) custom-call(s32[1]{0:T(128)} %bitcast.side_ref, bf16[1024,1536]{1,0:T(8,128)(2,1)} %x_ref.5, bf16[1024,1536]{1,0:T(8,128)(2,1)} %get-tuple-element.92.a_ref, ...), custom_call_target="tpu_custom_call" | custom-call | flops 9000000 | bytes 1024 | tf_op jit(solution)/shard_map/pallas_call | solution.py:276
  100.3 25.7 %all-gather.7.cloned.1.call-done = bf16[4096,768]{1,0:T(8,128)(2,1)} async-done(((bf16[1024,768]{1,0:T(8,128)(2,1)}), bf16[4096,768]{1,0:T(8,128)(2,1)}) %all-gather.7.cloned.1.call-update) | async-done | bytes 6291472 | tf_op jit(solution)/shard_map/all_gather | solution.py:895
  129.2 10.6 %shard_map.263 = (bf16[4,288,768]{2,1,0:T(8,128)(2,1)}, bf16[4,288,768]{2,1,0:T(8,128)(2,1)}, bf16[4,288,768]{2,1,0:T(8,128)(2,1)}, bf16[4,288,768]{2,1,0:T(8,128)(2,1)}) custom-call(s32[1]{0:T(128)} %bitcast.20.line_ref, s32[4,4,1,1024]{3,2,1,0:T(1,128)} %broadcast_in_dim.75.tab_ref.refs_0_, bf16[4,1024,768]{2,1,0:T(8,128)(2,1)} %bitcast.125, ...), custom_call_target="tpu_custom_call" | custom-call | flops 12000000 | bytes 1024 | tf_op jit(solution)/shard_map/pallas_call | solution.py:341
  142.4 37.2 %collective-permute-done.10.refs_2_.refs_1_ = bf16[4,288,768]{2,1,0:T(8,128)(2,1)S(1)} collective-permute-done((bf16[4,288,768]{2,1,0:T(8,128)(2,1)}, bf16[4,288,768]{2,1,0:T(8,128)(2,1)S(1)}, u32[]{:S(2)}, u32[]{:S(2)}) %collective-permute-start.10) | collective-permute-done | bytes 1769504 | tf_op jit(solution)/shard_map/ppermute | solution.py:892
  180.4 38.1 %collective-permute-done.12.refs_4_.refs_3_ = bf16[4,288,768]{2,1,0:T(8,128)(2,1)} collective-permute-done((bf16[4,288,768]{2,1,0:T(8,128)(2,1)}, bf16[4,288,768]{2,1,0:T(8,128)(2,1)}, u32[]{:S(2)}, u32[]{:S(2)}) %collective-permute-start.12) | collective-permute-done | bytes 1769504 | tf_op jit(solution)/shard_map/ppermute | solution.py:892
  218.6 7.9 %shard_map.262 = (bf16[4,288,512]{2,1,0:T(8,128)(2,1)}, bf16[4,288,512]{2,1,0:T(8,128)(2,1)}, bf16[4,288,512]{2,1,0:T(8,128)(2,1)}, bf16[4,288,512]{2,1,0:T(8,128)(2,1)}) custom-call(s32[1]{0:T(128)} %bitcast.20.line_ref, s32[4,4,1,1024]{3,2,1,0:T(1,128)} %broadcast_in_dim.75.tab_ref.refs_0_, bf16[4,1024,512]{2,1,0:T(8,128)(2,1)} %bitcast.129), custom_call_target="tpu_custom_call" | custom-call | flops 8000000 | bytes 1024 | tf_op jit(solution)/shard_map/pallas_call | solution.py:341
  229.2 22.5 %collective-permute-done.7.refs_0_.refs_1_ = bf16[4,288,512]{2,1,0:T(8,128)(2,1)S(1)} collective-permute-done((bf16[4,288,512]{2,1,0:T(8,128)(2,1)}, bf16[4,288,512]{2,1,0:T(8,128)(2,1)S(1)}, u32[]{:S(2)}, u32[]{:S(2)}) %collective-permute-start.7) | collective-permute-done | bytes 1179680 | tf_op jit(solution)/shard_map/ppermute | solution.py:892
  251.7 4.8 collective-permute-done.8.refs_1_.refs_2_
  256.5 20.5 %collective-permute-done.9.refs_2_.refs_3_ = bf16[4,288,512]{2,1,0:T(8,128)(2,1)} collective-permute-done((bf16[4,288,512]{2,1,0:T(8,128)(2,1)}, bf16[4,288,512]{2,1,0:T(8,128)(2,1)}, u32[]{:S(2)}, u32[]{:S(2)}) %collective-permute-start.9) | collective-permute-done | bytes 1179680 | tf_op jit(solution)/shard_map/ppermute | solution.py:892
  277.0 5.3 shard_map.265
  282.2 6.3 shard_map.266.refs_4_
  288.5 5.6 collective-permute-start.17
  294.1 5.0 shard_map.267.refs_0_
  299.6 2.3 collective-permute-start.15
  301.9 12.0 %collective-permute-done.13.refs_1_ = bf16[4,288,256]{2,1,0:T(8,128)(2,1)S(1)} collective-permute-done((bf16[4,288,256]{2,1,0:T(8,128)(2,1)}, bf16[4,288,256]{2,1,0:T(8,128)(2,1)S(1)}, u32[]{:S(2)}, u32[]{:S(2)}) %collective-permute-start.13) | collective-permute-done | bytes 589856 | tf_op jit(solution)/shard_map/ppermute | solution.py:892
  313.8 12.7 %collective-permute-done.15.refs_3_ = bf16[4,288,256]{2,1,0:T(8,128)(2,1)S(1)} collective-permute-done((bf16[4,288,256]{2,1,0:T(8,128)(2,1)S(1)}, bf16[4,288,256]{2,1,0:T(8,128)(2,1)S(1)}, u32[]{:S(2)}, u32[]{:S(2)}) %collective-permute-start.15) | collective-permute-done | bytes 589856 | tf_op jit(solution)/shard_map/ppermute | solution.py:892
  328.8 3.0 copy-done.1
  331.8 3.9 shard_map.268.refs_1_
  337.7 3.8 collective-permute-done.18.refs_3_
  342.9 44.9 %shard_map.269 = (bf16[4,4,288,768]{3,2,1,0:T(8,128)(2,1)}, bf16[4,4,288,384]{3,2,1,0:T(8,128)(2,1)}, f32[4,4,288,1]{3,2,1,0:T(8,128)}, bf16[4,4,288,256]{3,2,1,...) custom-call(s32[2]{0:T(128)} %pad_add_fusion.4.me_ref, ...), custom_call_target="tpu_custom_call" | custom-call | flops 40000000 | bytes 1024 | tf_op jit(solution)/shard_map/pallas_call | solution.py:505
  388.3 13.3 %shard_map.270 = (bf16[4,4,288,768]{3,2,1,0:T(8,128)(2,1)}, bf16[4,288,768]{2,1,0:T(8,128)(2,1)}, bf16[4,288,768]{2,1,0:T(8,128)(2,1)}, bf16[4,288,768]{2,1,0:T(8,128)(2,1)}, bf16[4,288,768]{2,1,0:T(8,128)(2,1)}) custom-call(s32[2]{0:T(128)} %pad_add_fusion.4.me_ref, bf16[4,4,288,384]{3,2,1,0:T(8,128)(2,1)} %get-tuple-element.113.act_ref.refs_0_, ...), custom_call_target="tpu_custom_call" | custom-call | flops 12000000 | bytes 1024 | tf_op jit(solution)/shard_map/pallas_call | solution.py:688
  403.4 4.6 shard_map.271
  412.7 10.5 %collective-permute-done.22.refs_5_.refs_1_ = bf16[4,288,256]{2,1,0:T(8,128)(2,1)S(1)} collective-permute-done((bf16[4,288,256]{2,1,0:T(8,128)(2,1)}, bf16[4,288,256]{2,1,0:T(8,128)(2,1)S(1)}, u32[]{:S(2)}, u32[]{:S(2)}) %collective-permute-start.22) | collective-permute-done | bytes 589856 | tf_op jit(solution)/shard_map/ppermute | solution.py:892
  424.3 12.3 %collective-permute-done.24.refs_7_.refs_3_ = bf16[4,288,256]{2,1,0:T(8,128)(2,1)S(1)} collective-permute-done((bf16[4,288,256]{2,1,0:T(8,128)(2,1)}, bf16[4,288,256]{2,1,0:T(8,128)(2,1)S(1)}, u32[]{:S(2)}, u32[]{:S(2)}) %collective-permute-start.24) | collective-permute-done | bytes 589856 | tf_op jit(solution)/shard_map/ppermute | solution.py:892
  437.4 6.3 shard_map.272
  443.8 7.2 shard_map.273
  453.7 23.3 %collective-permute-done.25.refs_1_ = bf16[4,288,512]{2,1,0:T(8,128)(2,1)} collective-permute-done((bf16[4,288,512]{2,1,0:T(8,128)(2,1)S(1)}, bf16[4,288,512]{2,1,0:T(8,128)(2,1)}, u32[]{:S(2)}, u32[]{:S(2)}) %collective-permute-start.25) | collective-permute-done | bytes 1179680 | tf_op jit(solution)/shard_map/ppermute | solution.py:892
  477.5 25.3 %collective-permute-done.27.refs_3_ = bf16[4,288,512]{2,1,0:T(8,128)(2,1)} collective-permute-done((bf16[4,288,512]{2,1,0:T(8,128)(2,1)S(1)}, bf16[4,288,512]{2,1,0:T(8,128)(2,1)}, u32[]{:S(2)}, u32[]{:S(2)}) %collective-permute-start.27) | collective-permute-done | bytes 1179680 | tf_op jit(solution)/shard_map/ppermute | solution.py:892
  502.8 9.1 %shard_map.274 = (bf16[4,1024,512]{2,1,0:T(8,128)(2,1)}, f32[1,8,128]{2,1,0:T(8,128)}) custom-call(s32[1]{0:T(128)} %bitcast.20.line_ref, s32[4,1024,4]{2,1,0:T(8,128)} %bitcast.122, bf16[4,288,512]{2,1,0:T(8,128)(2,1)} %get-tuple-element.132.refs_0_, bf16[4,288,512]{2,1,0:T(8,128)(2,1)} %collective-permute-done.25.refs_1_, ...), custom_call_target="tpu_custom_call" | custom-call | flops 8000000 | bytes 1024 | tf_op jit(solution)/shard_map/pallas_call | solution.py:383
  523.4 8.6 %shard_map.276 = (bf16[4,288,768]{2,1,0:T(8,128)(2,1)}, bf16[4,288,768]{2,1,0:T(8,128)(2,1)}, bf16[4,288,768]{2,1,0:T(8,128)(2,1)}, bf16[4,288,768]{2,1,0:T(8,128)(2,1)}) custom-call(bf16[4,288,768]{2,1,0:T(8,128)(2,1)} %get-tuple-element.114.refs_0_, bf16[4,288,768]{2,1,0:T(8,128)(2,1)} %get-tuple-element.115.refs_1_, ...), custom_call_target="tpu_custom_call" | custom-call | flops 7000000 | bytes 1024 | tf_op jit(solution)/shard_map/pallas_call | solution.py:560
  534.0 5.1 select_reduce_fusion
  539.1 4.6 collective-permute-start.36
  544.9 7.2 convolution_bitcast_fusion.2
  552.1 3.0 broadcast_select_fusion.3
  556.3 5.1 collective-permute-start.39
  566.4 5.2 convolution_bitcast_fusion.5
  571.7 6.2 convolution_bitcast_fusion.1
  577.8 5.0 convolution_bitcast_fusion
  584.9 9.5 %reduce-scatter.6.cloned.1.call-done.refs_1_ = bf16[1024,512]{1,0:T(8,128)(2,1)} async-done(((bf16[4096,512]{1,0:T(8,128)(2,1)}), bf16[1024,512]{1,0:T(8,128)(2,1)}) %reduce-scatter.6.cloned.1.call-update) | async-done | bytes 1048592 | tf_op jit(solution)/shard_map/reduce_scatter | solution.py:899
  602.0 10.6 %shard_map.281 = (f32[1024,1536]{1,0:T(8,128)}, bf16[1024,1536]{1,0:T(8,128)(2,1)}, bf16[1024,128]{1,0:T(8,128)(2,1)}, f32[1,1536]{1,0:T(1,128)}) custom-call(s32[1]{0:T(128)} %bitcast.side_ref, bf16[1024,256]{1,0:T(8,128)(2,1)} %reduce-scatter.4.cloned.1.call-done.refs_1_.refs_0_, bf16[1024,512]{1,0:T(8,128)(2,1)} %reduce-scatter.6.cloned.1.call-done.refs_1_, ...), custom_call_target="tpu_custom_call" | custom-call | flops 10000000 | bytes 1024 | tf_op jit(solution)/shard_map/pallas_call | solution.py:619
  612.7 13.3 %shard_map.282 = (bf16[4,1024,768]{2,1,0:T(8,128)(2,1)}, f32[1,8,128]{2,1,0:T(8,128)}) custom-call(s32[1]{0:T(128)} %bitcast.20.line_ref, s32[4,1024,4]{2,1,0:T(8,128)} %bitcast.123, bf16[4,288,768]{2,1,0:T(8,128)(2,1)} %get-tuple-element.140.refs_0_, bf16[4,288,768]{2,1,0:T(8,128)(2,1)} %collective-permute-done.31.refs_1_, ...), custom_call_target="tpu_custom_call" | custom-call | flops 12000000 | bytes 1024 | tf_op jit(solution)/shard_map/pallas_call | solution.py:383
  626.0 8.4 %shard_map.284 = (f32[4,96,896]{2,1,0:T(8,128)}, bf16[4,96,896]{2,1,0:T(8,128)(2,1)}, bf16[4,96,896]{2,1,0:T(8,128)(2,1)}, bf16[4,96,896]{2,1,0:T(8,128)(2,1)}) custom-call(s32[1]{0:T(128)} %bitcast.59.spot_ref, bf16[1024,1536]{1,0:T(8,128)(2,1)} %get-tuple-element.149.refs_4_.left_ref.db_ref, bf16[1024,768]{1,0:T(8,128)(2,1)} %get-tuple-element.153.right_ref, ...), custom_call_target="tpu_custom_call" | custom-call | flops 6000000 | bytes 1024 | tf_op jit(solution)/shard_map/pallas_call | solution.py:869
  637.1 26.3 %shard_map.285.d_ref.refs_0_ = bf16[1024,1024]{1,0:T(8,128)(2,1)} custom-call(bf16[1024,768]{1,0:T(8,128)(2,1)} %get-tuple-element.89.q_ref, bf16[1024,128]{1,0:T(8,128)(2,1)} %get-tuple-element.90.k_ref, bf16[1024,128]{1,0:T(8,128)(2,1)} %get-tuple-element.91.v_ref, s32[1,1024]{1,0:T(1,128)} %segq_ref.3, s32[1024,1]{1,0:T(8,128)} %copy.130.segk_ref, ...), custom_call_target="tpu_custom_call" | custom-call | flops 28000000 | bytes 1024 | tf_op jit(solution)/shard_map/pallas_call | solution.py:777
  663.4 3.4 collective-permute-done.42
  668.2 7.8 shard_map.286.refs_1_.a_ref
  677.7 7.5 shard_map.288
  689.5 9.6 %shard_map.289.refs_1_ = f32[1024,1536]{1,0:T(8,128)} custom-call(bf16[1024,1536]{1,0:T(8,128)(2,1)} %shard_map.286.refs_1_.a_ref, bf16[1024,1536]{1,0:T(8,128)(2,1)} %copy-done.15, bf16[1024,1536]{1,0:T(8,128)(2,1)} %x_ref.5, f32[1024,1]{1,0:T(8,128)} %get-tuple-element.161.inv_ref, f32[1024,1536]{1,0:T(8,128)} %get-tuple-element.162.dh_ref, ...), custom_call_target="tpu_custom_call" | custom-call | flops 8000000 | bytes 1024 | tf_op jit(solution)/shard_map/pallas_call | solution.py:653
  699.1 5.6 collective-permute-done.44
  705.2 17.2 %collective-permute-done.46 = bf16[4,96,1024]{2,1,0:T(8,128)(2,1)} collective-permute-done((bf16[4,96,1024]{2,1,0:T(8,128)(2,1)}, bf16[4,96,1024]{2,1,0:T(8,128)(2,1)}, u32[]{:S(2)}, u32[]{:S(2)}) %collective-permute-start.46) | collective-permute-done | bytes 786464 | tf_op jit(solution)/shard_map/ppermute | solution.py:892
  722.4 2.6 convert_add_fusion.refs_1_
  726.3 2.4 collective-permute-start.49
  728.8 18.6 %reduce-scatter.8.cloned.1.call-done.refs_0_ = bf16[1024,768]{1,0:T(8,128)(2,1)} async-done(((bf16[4096,768]{1,0:T(8,128)(2,1)}), bf16[1024,768]{1,0:T(8,128)(2,1)}) %reduce-scatter.8.cloned.1.call-update) | async-done | bytes 1572880 | tf_op jit(solution)/shard_map/reduce_scatter | solution.py:899
  747.3 4.1 add_convert_fusion
  753.9 14.6 %collective-permute-done.50 = bf16[96,1920]{1,0:T(8,128)(2,1)} collective-permute-done((bf16[96,1920]{1,0:T(8,128)(2,1)S(1)}, bf16[96,1920]{1,0:T(8,128)(2,1)}, u32[]{:S(2)}, u32[]{:S(2)}) %collective-permute-start.50) | collective-permute-done | bytes 368672 | tf_op jit(solution)/shard_map/ppermute | solution.py:892
  776.5 2.1 broadcast_select_fusion.1
  (260 shorter events, 104.4 us)
Async XLA Ops:
  7.2 118.8 %all-gather.7.cloned.1.call-start = ((), (), s32[]{:S(2)}) async-start(), calls=%async_computation.6 | async-start | bytes 7864320 | tf_op jit(solution)/shard_map/all_gather | solution.py:895
  9.9 208.6 %all-gather.9.cloned.1.call-start = ((), (), s32[]{:S(2)}) async-start(), calls=%async_computation.7 | async-start | bytes 5242880 | tf_op jit(solution)/shard_map/all_gather | solution.py:895
  20.7 27.5 %copy-start.38 = (s32[1024,4]{0,1:T(4,128)S(1)}, s32[1024,4]{0,1:T(4,128)}, u32[]{:S(2)}) copy-start(s32[1024,4]{0,1:T(4,128)} %param.29) | copy-start | bytes 49156
  44.8 43.8 %collective-permute-start = (bf16[1024,1536]{1,0:T(8,128)(2,1)}, bf16[1024,1536]{1,0:T(8,128)(2,1)S(1)}, u32[]{:S(2)}, u32[]{:S(2)}) collective-permute-start(bf16[1024,1536]{1,0:T(8,128)(2,1)} %get-tuple-element.92.a_ref), channel_id=1, source_target_pairs={{0,1},{1,0},{2,3},{3,2},{4,5},{5,4},{6,7},{7,6},{8,9},{9,8},{10,11... | collective-permute-start | bytes 9437192 | tf_op jit(solution)/shard_map/ppermute | solution.py:929
  48.2 30.4 %copy-start.39 = (bf16[1536,16]{0,1:T(8,128)(2,1)S(1)}, bf16[1536,16]{0,1:T(8,128)(2,1)}, u32[]{:S(2)}) copy-start(bf16[1536,16]{0,1:T(8,128)(2,1)} %param.25) | copy-start | bytes 147460
  48.9 30.6 %copy-start.43 = (f32[1536]{0:T(1024)S(1)}, f32[1536]{0:T(1024)}, u32[]{:S(2)}) copy-start(f32[1536]{0:T(1024)} %param.20) | copy-start | bytes 18436
  58.6 4.1 collective-permute-start.1
  58.7 6.3 collective-permute-start.2
  61.2 4.8 collective-permute-start.3
  74.8 6.2 collective-permute-start.4
  76.1 8.9 %collective-permute-start.5 = (bf16[4,288,4]{2,1,0:T(8,128)(2,1)}, bf16[4,288,4]{2,1,0:T(8,128)(2,1)}, u32[]{:S(2)}, u32[]{:S(2)}) collective-permute-start(bf16[4,288,4]{2,1,0:T(8,128)(2,1)} %get-tuple-element.95), channel_id=1, source_target_pairs={{0,4},{2,6},{4,0},{6,2},{8,12},{10,14},{12,8},{14,10},{16,20},{18,... | collective-permute-start | bytes 27656 | tf_op jit(solution)/shard_map/ppermute | solution.py:892
  77.3 8.8 %collective-permute-start.6 = (bf16[4,288,4]{2,1,0:T(8,128)(2,1)}, bf16[4,288,4]{2,1,0:T(8,128)(2,1)}, u32[]{:S(2)}, u32[]{:S(2)}) collective-permute-start(bf16[4,288,4]{2,1,0:T(8,128)(2,1)} %get-tuple-element.96), channel_id=1, source_target_pairs={{0,6},{2,4},{4,2},{6,0},{8,14},{10,12},{12,10},{14,8},{16,22},{18,... | collective-permute-start | bytes 27656 | tf_op jit(solution)/shard_map/ppermute | solution.py:892
  126.0 151.0 %all-gather.11.cloned.1.call-start = ((), (), s32[]{:S(2)}) async-start(), calls=%async_computation.8 | async-start | bytes 2621440 | tf_op jit(solution)/shard_map/all_gather | solution.py:895
  139.8 39.9 %collective-permute-start.10 = (bf16[4,288,768]{2,1,0:T(8,128)(2,1)}, bf16[4,288,768]{2,1,0:T(8,128)(2,1)S(1)}, u32[]{:S(2)}, u32[]{:S(2)}) collective-permute-start(bf16[4,288,768]{2,1,0:T(8,128)(2,1)} %get-tuple-element.105), channel_id=1, source_target_pairs={{0,2},{2,0},{4,6},{6,4},{8,10},{10,8},{12,14},{14,12},{16,18},{18,... | collective-permute-start | bytes 5308424 | tf_op jit(solution)/shard_map/ppermute | solution.py:892
  141.0 39.4 %collective-permute-start.11 = (bf16[4,288,768]{2,1,0:T(8,128)(2,1)}, bf16[4,288,768]{2,1,0:T(8,128)(2,1)S(1)}, u32[]{:S(2)}, u32[]{:S(2)}) collective-permute-start(bf16[4,288,768]{2,1,0:T(8,128)(2,1)} %get-tuple-element.106), channel_id=1, source_target_pairs={{0,4},{2,6},{4,0},{6,2},{8,12},{10,14},{12,8},{14,10},{16,20},{18,... | collective-permute-start | bytes 5308424 | tf_op jit(solution)/shard_map/ppermute | solution.py:892
  142.2 76.3 %collective-permute-start.12 = (bf16[4,288,768]{2,1,0:T(8,128)(2,1)}, bf16[4,288,768]{2,1,0:T(8,128)(2,1)}, u32[]{:S(2)}, u32[]{:S(2)}) collective-permute-start(bf16[4,288,768]{2,1,0:T(8,128)(2,1)} %get-tuple-element.107), channel_id=1, source_target_pairs={{0,6},{2,4},{4,2},{6,0},{8,14},{10,12},{12,10},{14,8},{16,22},{18,... | collective-permute-start | bytes 5308424 | tf_op jit(solution)/shard_map/ppermute | solution.py:892
  179.6 38.9 %copy-start.11 = (bf16[4,288,768]{2,1,0:T(8,128)(2,1)}, bf16[4,288,768]{2,1,0:T(8,128)(2,1)S(1)}, u32[]{:S(2)}) copy-start(bf16[4,288,768]{2,1,0:T(8,128)(2,1)S(1)} %collective-permute-done.10.refs_2_.refs_1_) | copy-start | bytes 5308420
  180.4 38.1 %copy-start.12 = (bf16[4,288,768]{2,1,0:T(8,128)(2,1)}, bf16[4,288,768]{2,1,0:T(8,128)(2,1)S(1)}, u32[]{:S(2)}) copy-start(bf16[4,288,768]{2,1,0:T(8,128)(2,1)S(1)} %collective-permute-done.11.refs_3_.refs_2_) | copy-start | bytes 5308420
  218.5 293.3 %reduce-scatter.4.cloned.1.call-start = ((), (), s32[]{:S(2)}) async-start(), calls=%async_computation.3 | async-start | bytes 2621440 | tf_op jit(solution)/shard_map/reduce_scatter | solution.py:899
  226.5 25.2 %collective-permute-start.7 = (bf16[4,288,512]{2,1,0:T(8,128)(2,1)}, bf16[4,288,512]{2,1,0:T(8,128)(2,1)S(1)}, u32[]{:S(2)}, u32[]{:S(2)}) collective-permute-start(bf16[4,288,512]{2,1,0:T(8,128)(2,1)} %get-tuple-element.100), channel_id=1, source_target_pairs={{0,2},{2,0},{4,6},{6,4},{8,10},{10,8},{12,14},{14,12},{16,18},{18,... | collective-permute-start | bytes 3538952 | tf_op jit(solution)/shard_map/ppermute | solution.py:892
  227.7 28.8 %collective-permute-start.8 = (bf16[4,288,512]{2,1,0:T(8,128)(2,1)}, bf16[4,288,512]{2,1,0:T(8,128)(2,1)S(1)}, u32[]{:S(2)}, u32[]{:S(2)}) collective-permute-start(bf16[4,288,512]{2,1,0:T(8,128)(2,1)} %get-tuple-element.101), channel_id=1, source_target_pairs={{0,4},{2,6},{4,0},{6,2},{8,12},{10,14},{12,8},{14,10},{16,20},{18,... | collective-permute-start | bytes 3538952 | tf_op jit(solution)/shard_map/ppermute | solution.py:892
  228.0 49.0 %collective-permute-start.9 = (bf16[4,288,512]{2,1,0:T(8,128)(2,1)}, bf16[4,288,512]{2,1,0:T(8,128)(2,1)}, u32[]{:S(2)}, u32[]{:S(2)}) collective-permute-start(bf16[4,288,512]{2,1,0:T(8,128)(2,1)} %get-tuple-element.102), channel_id=1, source_target_pairs={{0,6},{2,4},{4,2},{6,0},{8,14},{10,12},{12,10},{14,8},{16,22},{18,... | collective-permute-start | bytes 3538952 | tf_op jit(solution)/shard_map/ppermute | solution.py:892
  288.5 38.0 %collective-permute-start.17 = (bf16[4,4,288,768]{3,2,1,0:T(8,128)(2,1)}, bf16[4,4,288,768]{3,2,1,0:T(8,128)(2,1)S(1)}, u32[]{:S(2)}, u32[]{:S(2)}) collective-permute-start(bf16[4,4,288,768]{3,2,1,0:T(8,128)(2,1)} %shard_map.266.refs_4_), channel_id=1, source_target_pairs={{0,1},{1,0},{2,3},{3,2},{4,5},{5,4},{6,7},{7,6},{8,9},{9,8},{10,11... | collective-permute-start | bytes 21233672 | tf_op jit(solution)/shard_map/ppermute | solution.py:929
  299.2 27.3 %collective-permute-start.16 = (bf16[4,4,288,512]{3,2,1,0:T(8,128)(2,1)}, bf16[4,4,288,512]{3,2,1,0:T(8,128)(2,1)S(1)}, u32[]{:S(2)}, u32[]{:S(2)}) collective-permute-start(bf16[4,4,288,512]{3,2,1,0:T(8,128)(2,1)} %shard_map.267.refs_0_), channel_id=1, source_target_pairs={{0,1},{1,0},{2,3},{3,2},{4,5},{5,4},{6,7},{7,6},{8,9},{9,8},{10,11... | collective-permute-start | bytes 14155784 | tf_op jit(solution)/shard_map/ppermute | solution.py:929
  299.2 14.6 %collective-permute-start.13 = (bf16[4,288,256]{2,1,0:T(8,128)(2,1)}, bf16[4,288,256]{2,1,0:T(8,128)(2,1)S(1)}, u32[]{:S(2)}, u32[]{:S(2)}) collective-permute-start(bf16[4,288,256]{2,1,0:T(8,128)(2,1)} %get-tuple-element.109.refs_4_), channel_id=1, source_target_pairs={{0,2},{2,0},{4,6},{6,4},{8,10},{10,8},{12,14},{14,12},{16,18},{18,... | collective-permute-start | bytes 1769480 | tf_op jit(solution)/shard_map/ppermute | solution.py:892
  299.5 14.3 %collective-permute-start.14 = (bf16[4,288,256]{2,1,0:T(8,128)(2,1)S(1)}, bf16[4,288,256]{2,1,0:T(8,128)(2,1)S(1)}, u32[]{:S(2)}, u32[]{:S(2)}) collective-permute-start(bf16[4,288,256]{2,1,0:T(8,128)(2,1)S(1)} %copy-done.30), channel_id=1, source_target_pairs={{0,4},{2,6},{4,0},{6,2},{8,12},{10,14},{12,8},{14,10},{16,20},{18,... | collective-permute-start | bytes 1769480 | tf_op jit(solution)/shard_map/ppermute | solution.py:892
  299.6 26.9 %collective-permute-start.15 = (bf16[4,288,256]{2,1,0:T(8,128)(2,1)S(1)}, bf16[4,288,256]{2,1,0:T(8,128)(2,1)S(1)}, u32[]{:S(2)}, u32[]{:S(2)}) collective-permute-start(bf16[4,288,256]{2,1,0:T(8,128)(2,1)S(1)} %copy-done.29), channel_id=1, source_target_pairs={{0,6},{2,4},{4,2},{6,0},{8,14},{10,12},{12,10},{14,8},{16,22},{18,... | collective-permute-start | bytes 1769480 | tf_op jit(solution)/shard_map/ppermute | solution.py:892
  335.7 5.8 collective-permute-start.18
  387.8 48.8 %collective-permute-start.20 = (bf16[4,4,288,512]{3,2,1,0:T(8,128)(2,1)}, bf16[4,4,288,512]{3,2,1,0:T(8,128)(2,1)}, u32[]{:S(2)}, u32[]{:S(2)}) collective-permute-start(bf16[4,4,288,512]{3,2,1,0:T(8,128)(2,1)} %get-tuple-element.123), channel_id=1, source_target_pairs={{0,1},{1,0},{2,3},{3,2},{4,5},{5,4},{6,7},{7,6},{8,9},{9,8},{10,11... | collective-permute-start | bytes 14155784 | tf_op jit(solution)/shard_map/ppermute | solution.py:929
  388.2 13.8 %collective-permute-start.21 = (bf16[4,4,288,256]{3,2,1,0:T(8,128)(2,1)}, bf16[4,4,288,256]{3,2,1,0:T(8,128)(2,1)S(1)}, u32[]{:S(2)}, u32[]{:S(2)}) collective-permute-start(bf16[4,4,288,256]{3,2,1,0:T(8,128)(2,1)} %get-tuple-element.128), channel_id=1, source_target_pairs={{0,1},{1,0},{2,3},{3,2},{4,5},{5,4},{6,7},{7,6},{8,9},{9,8},{10,11... | collective-permute-start | bytes 7077896 | tf_op jit(solution)/shard_map/ppermute | solution.py:929
  401.6 121.8 %collective-permute-start.19 = (bf16[4,4,288,768]{3,2,1,0:T(8,128)(2,1)}, bf16[4,4,288,768]{3,2,1,0:T(8,128)(2,1)}, u32[]{:S(2)}, u32[]{:S(2)}) collective-permute-start(bf16[4,4,288,768]{3,2,1,0:T(8,128)(2,1)} %get-tuple-element.118.refs_8_.refs_1_), channel_id=1, source_target_pairs={{0,1},{1,0},{2,3},{3,2},{4,5},{5,4},{6,7},{7,6},{8,9},{9,8},{10,11... | collective-permute-start | bytes 21233672 | tf_op jit(solution)/shard_map/ppermute | solution.py:929
  408.0 15.1 %collective-permute-start.22 = (bf16[4,288,256]{2,1,0:T(8,128)(2,1)}, bf16[4,288,256]{2,1,0:T(8,128)(2,1)S(1)}, u32[]{:S(2)}, u32[]{:S(2)}) collective-permute-start(bf16[4,288,256]{2,1,0:T(8,128)(2,1)} %get-tuple-element.129), channel_id=1, source_target_pairs={{0,2},{2,0},{4,6},{6,4},{8,10},{10,8},{12,14},{14,12},{16,18},{18,... | collective-permute-start | bytes 1769480 | tf_op jit(solution)/shard_map/ppermute | solution.py:892
  409.3 15.0 %collective-permute-start.23 = (bf16[4,288,256]{2,1,0:T(8,128)(2,1)}, bf16[4,288,256]{2,1,0:T(8,128)(2,1)S(1)}, u32[]{:S(2)}, u32[]{:S(2)}) collective-permute-start(bf16[4,288,256]{2,1,0:T(8,128)(2,1)} %get-tuple-element.130), channel_id=1, source_target_pairs={{0,4},{2,6},{4,0},{6,2},{8,12},{10,14},{12,8},{14,10},{16,20},{18,... | collective-permute-start | bytes 1769480 | tf_op jit(solution)/shard_map/ppermute | solution.py:892
  409.5 27.1 %collective-permute-start.24 = (bf16[4,288,256]{2,1,0:T(8,128)(2,1)}, bf16[4,288,256]{2,1,0:T(8,128)(2,1)S(1)}, u32[]{:S(2)}, u32[]{:S(2)}) collective-permute-start(bf16[4,288,256]{2,1,0:T(8,128)(2,1)} %get-tuple-element.131), channel_id=1, source_target_pairs={{0,6},{2,4},{4,2},{6,0},{8,14},{10,12},{12,10},{14,8},{16,22},{18,... | collective-permute-start | bytes 1769480 | tf_op jit(solution)/shard_map/ppermute | solution.py:892
  451.0 143.4 %reduce-scatter.6.cloned.1.call-start = ((), (), s32[]{:S(2)}) async-start(), calls=%async_computation.4 | async-start | bytes 5242880 | tf_op jit(solution)/shard_map/reduce_scatter | solution.py:899
  451.0 26.1 %collective-permute-start.25 = (bf16[4,288,512]{2,1,0:T(8,128)(2,1)S(1)}, bf16[4,288,512]{2,1,0:T(8,128)(2,1)}, u32[]{:S(2)}, u32[]{:S(2)}) collective-permute-start(bf16[4,288,512]{2,1,0:T(8,128)(2,1)S(1)} %copy-done.27), channel_id=1, source_target_pairs={{0,2},{2,0},{4,6},{6,4},{8,10},{10,8},{12,14},{14,12},{16,18},{18,... | collective-permute-start | bytes 3538952 | tf_op jit(solution)/shard_map/ppermute | solution.py:892
  451.5 26.0 %collective-permute-start.26 = (bf16[4,288,512]{2,1,0:T(8,128)(2,1)S(1)}, bf16[4,288,512]{2,1,0:T(8,128)(2,1)}, u32[]{:S(2)}, u32[]{:S(2)}) collective-permute-start(bf16[4,288,512]{2,1,0:T(8,128)(2,1)S(1)} %copy-done.26), channel_id=1, source_target_pairs={{0,4},{2,6},{4,0},{6,2},{8,12},{10,14},{12,8},{14,10},{16,20},{18,... | collective-permute-start | bytes 3538952 | tf_op jit(solution)/shard_map/ppermute | solution.py:892
  452.7 50.0 %collective-permute-start.27 = (bf16[4,288,512]{2,1,0:T(8,128)(2,1)S(1)}, bf16[4,288,512]{2,1,0:T(8,128)(2,1)}, u32[]{:S(2)}, u32[]{:S(2)}) collective-permute-start(bf16[4,288,512]{2,1,0:T(8,128)(2,1)S(1)} %copy-done.25), channel_id=1, source_target_pairs={{0,6},{2,4},{4,2},{6,0},{8,14},{10,12},{12,10},{14,8},{16,22},{18,... | collective-permute-start | bytes 3538952 | tf_op jit(solution)/shard_map/ppermute | solution.py:892
  511.9 235.4 %reduce-scatter.8.cloned.1.call-start = ((), (), s32[]{:S(2)}) async-start(), calls=%async_computation.5 | async-start | bytes 7864320 | tf_op jit(solution)/shard_map/reduce_scatter | solution.py:899
  516.1 4.8 collective-permute-start.28
  519.1 2.8 collective-permute-start.29
  519.4 3.4 collective-permute-start.30
  532.1 80.6 %collective-permute-start.31 = (bf16[4,288,768]{2,1,0:T(8,128)(2,1)}, bf16[4,288,768]{2,1,0:T(8,128)(2,1)}, u32[]{:S(2)}, u32[]{:S(2)}) collective-permute-start(bf16[4,288,768]{2,1,0:T(8,128)(2,1)} %get-tuple-element.141.refs_1_), channel_id=1, source_target_pairs={{0,2},{2,0},{4,6},{6,4},{8,10},{10,8},{12,14},{14,12},{16,18},{18,... | collective-permute-start | bytes 5308424 | tf_op jit(solution)/shard_map/ppermute | solution.py:892
  533.0 79.7 %collective-permute-start.32 = (bf16[4,288,768]{2,1,0:T(8,128)(2,1)}, bf16[4,288,768]{2,1,0:T(8,128)(2,1)}, u32[]{:S(2)}, u32[]{:S(2)}) collective-permute-start(bf16[4,288,768]{2,1,0:T(8,128)(2,1)} %get-tuple-element.142.refs_2_), channel_id=1, source_target_pairs={{0,4},{2,6},{4,0},{6,2},{8,12},{10,14},{12,8},{14,10},{16,20},{18,... | collective-permute-start | bytes 5308424 | tf_op jit(solution)/shard_map/ppermute | solution.py:892
  539.1 16.0 %collective-permute-start.36 = (f32[4,1024]{1,0:T(4,128)S(1)}, f32[4,1024]{1,0:T(4,128)S(1)}, u32[]{:S(2)}, u32[]{:S(2)}) collective-permute-start(f32[4,1024]{1,0:T(4,128)S(1)} %get-tuple-element.255), channel_id=1, source_target_pairs={{0,8},{2,10},{4,12},{6,14},{8,0},{10,2},{12,4},{14,6},{16,24},{18,... | collective-permute-start | bytes 49160 | tf_op jit(solution)/shard_map/ppermute | solution.py:892
  543.7 12.6 %collective-permute-start.37 = (f32[4,1024]{1,0:T(4,128)S(1)}, f32[4,1024]{1,0:T(4,128)S(1)}, u32[]{:S(2)}, u32[]{:S(2)}) collective-permute-start(f32[4,1024]{1,0:T(4,128)S(1)} %get-tuple-element.254), channel_id=1, source_target_pairs={{0,16},{2,18},{4,20},{6,22},{8,24},{10,26},{12,28},{14,30},{16,0},... | collective-permute-start | bytes 49160 | tf_op jit(solution)/shard_map/ppermute | solution.py:892
  543.7 12.6 %collective-permute-start.38 = (f32[4,1024]{1,0:T(4,128)S(1)}, f32[4,1024]{1,0:T(4,128)S(1)}, u32[]{:S(2)}, u32[]{:S(2)}) collective-permute-start(f32[4,1024]{1,0:T(4,128)S(1)} %get-tuple-element.253), channel_id=1, source_target_pairs={{0,24},{2,26},{4,28},{6,30},{8,16},{10,18},{12,20},{14,22},{16,8},... | collective-permute-start | bytes 49160 | tf_op jit(solution)/shard_map/ppermute | solution.py:892
  555.1 57.6 %collective-permute-start.33 = (bf16[4,288,768]{2,1,0:T(8,128)(2,1)}, bf16[4,288,768]{2,1,0:T(8,128)(2,1)}, u32[]{:S(2)}, u32[]{:S(2)}) collective-permute-start(bf16[4,288,768]{2,1,0:T(8,128)(2,1)} %get-tuple-element.143.refs_3_), channel_id=1, source_target_pairs={{0,6},{2,4},{4,2},{6,0},{8,14},{10,12},{12,10},{14,8},{16,22},{18,... | collective-permute-start | bytes 5308424 | tf_op jit(solution)/shard_map/ppermute | solution.py:892
  556.3 6.8 collective-permute-start.39
  594.4 6.5 collective-permute-start.35
  597.8 3.1 collective-permute-start.34
  634.4 29.0 %collective-permute-start.40 = (bf16[4,96,896]{2,1,0:T(8,128)(2,1)}, bf16[4,96,896]{2,1,0:T(8,128)(2,1)S(1)}, u32[]{:S(2)}, u32[]{:S(2)}) collective-permute-start(bf16[4,96,896]{2,1,0:T(8,128)(2,1)} %get-tuple-element.156.refs_0_), channel_id=1, source_target_pairs={{0,2},{2,0},{4,6},{6,4},{8,10},{10,8},{12,14},{14,12},{16,18},{18,... | collective-permute-start | bytes 2064392 | tf_op jit(solution)/shard_map/ppermute | solution.py:892
  635.6 27.8 %collective-permute-start.41 = (bf16[4,96,896]{2,1,0:T(8,128)(2,1)}, bf16[4,96,896]{2,1,0:T(8,128)(2,1)S(1)}, u32[]{:S(2)}, u32[]{:S(2)}) collective-permute-start(bf16[4,96,896]{2,1,0:T(8,128)(2,1)} %get-tuple-element.157.refs_1_), channel_id=1, source_target_pairs={{0,4},{2,6},{4,0},{6,2},{8,12},{10,14},{12,8},{14,10},{16,20},{18,... | collective-permute-start | bytes 2064392 | tf_op jit(solution)/shard_map/ppermute | solution.py:892
  636.8 30.0 %collective-permute-start.42 = (bf16[4,96,896]{2,1,0:T(8,128)(2,1)}, bf16[4,96,896]{2,1,0:T(8,128)(2,1)S(1)}, u32[]{:S(2)}, u32[]{:S(2)}) collective-permute-start(bf16[4,96,896]{2,1,0:T(8,128)(2,1)} %get-tuple-element.158.refs_2_), channel_id=1, source_target_pairs={{0,6},{2,4},{4,2},{6,0},{8,14},{10,12},{12,10},{14,8},{16,22},{18,... | collective-permute-start | bytes 2064392 | tf_op jit(solution)/shard_map/ppermute | solution.py:892
  637.1 29.7 %copy-start.22 = (f32[4,96,896]{2,1,0:T(8,128)S(1)}, f32[4,96,896]{2,1,0:T(8,128)}, u32[]{:S(2)}) copy-start(f32[4,96,896]{2,1,0:T(8,128)} %get-tuple-element.159) | copy-start | bytes 4128772
  676.0 11.8 %collective-permute-start.43 = (bf16[1024,1536]{1,0:T(8,128)(2,1)}, bf16[1024,1536]{1,0:T(8,128)(2,1)S(1)}, u32[]{:S(2)}, u32[]{:S(2)}) collective-permute-start(bf16[1024,1536]{1,0:T(8,128)(2,1)} %shard_map.286.refs_1_.a_ref), channel_id=1, source_target_pairs={{0,1},{1,0},{2,3},{3,2},{4,5},{5,4},{6,7},{7,6},{8,9},{9,8},{10,11... | collective-permute-start | bytes 9437192 | tf_op jit(solution)/shard_map/ppermute | solution.py:929
  685.2 19.5 %collective-permute-start.44 = (bf16[4,96,1024]{2,1,0:T(8,128)(2,1)}, bf16[4,96,1024]{2,1,0:T(8,128)(2,1)}, u32[]{:S(2)}, u32[]{:S(2)}) collective-permute-start(bf16[4,96,1024]{2,1,0:T(8,128)(2,1)} %get-tuple-element.163), channel_id=1, source_target_pairs={{0,2},{2,0},{4,6},{6,4},{8,10},{10,8},{12,14},{14,12},{16,18},{18,... | collective-permute-start | bytes 2359304 | tf_op jit(solution)/shard_map/ppermute | solution.py:892
  686.1 19.1 %collective-permute-start.45 = (bf16[4,96,1024]{2,1,0:T(8,128)(2,1)}, bf16[4,96,1024]{2,1,0:T(8,128)(2,1)}, u32[]{:S(2)}, u32[]{:S(2)}) collective-permute-start(bf16[4,96,1024]{2,1,0:T(8,128)(2,1)} %get-tuple-element.164), channel_id=1, source_target_pairs={{0,4},{2,6},{4,0},{6,2},{8,12},{10,14},{12,8},{14,10},{16,20},{18,... | collective-permute-start | bytes 2359304 | tf_op jit(solution)/shard_map/ppermute | solution.py:892
  686.7 35.7 %collective-permute-start.46 = (bf16[4,96,1024]{2,1,0:T(8,128)(2,1)}, bf16[4,96,1024]{2,1,0:T(8,128)(2,1)}, u32[]{:S(2)}, u32[]{:S(2)}) collective-permute-start(bf16[4,96,1024]{2,1,0:T(8,128)(2,1)} %get-tuple-element.165), channel_id=1, source_target_pairs={{0,6},{2,4},{4,2},{6,0},{8,14},{10,12},{12,10},{14,8},{16,22},{18,... | collective-permute-start | bytes 2359304 | tf_op jit(solution)/shard_map/ppermute | solution.py:892
  726.1 26.3 %collective-permute-start.48 = (bf16[96,1920]{1,0:T(8,128)(2,1)}, bf16[96,1920]{1,0:T(8,128)(2,1)}, u32[]{:S(2)}, u32[]{:S(2)}) collective-permute-start(bf16[96,1920]{1,0:T(8,128)(2,1)} %get-tuple-element.236), channel_id=1, source_target_pairs={{0,8},{2,10},{4,12},{6,14},{8,0},{10,2},{12,4},{14,6},{16,24},{18,... | collective-permute-start | bytes 1105928 | tf_op jit(solution)/shard_map/ppermute | solution.py:892
  726.3 27.6 %collective-permute-start.49 = (bf16[96,1920]{1,0:T(8,128)(2,1)}, bf16[96,1920]{1,0:T(8,128)(2,1)}, u32[]{:S(2)}, u32[]{:S(2)}) collective-permute-start(bf16[96,1920]{1,0:T(8,128)(2,1)} %get-tuple-element.237), channel_id=1, source_target_pairs={{0,16},{2,18},{4,20},{6,22},{8,24},{10,26},{12,28},{14,30},{16,0},... | collective-permute-start | bytes 1105928 | tf_op jit(solution)/shard_map/ppermute | solution.py:892
  728.7 39.9 %collective-permute-start.50 = (bf16[96,1920]{1,0:T(8,128)(2,1)S(1)}, bf16[96,1920]{1,0:T(8,128)(2,1)}, u32[]{:S(2)}, u32[]{:S(2)}) collective-permute-start(bf16[96,1920]{1,0:T(8,128)(2,1)S(1)} %get-tuple-element.238), channel_id=1, source_target_pairs={{0,24},{2,26},{4,28},{6,30},{8,16},{10,18},{12,20},{14,22},{16,8},... | collective-permute-start | bytes 1105928 | tf_op jit(solution)/shard_map/ppermute | solution.py:892
  751.4 25.1 %collective-permute-start.47 = (bf16[1024,768]{1,0:T(8,128)(2,1)}, bf16[1024,768]{1,0:T(8,128)(2,1)}, u32[]{:S(2)}, u32[]{:S(2)}) collective-permute-start(bf16[1024,768]{1,0:T(8,128)(2,1)} %add_convert_fusion), channel_id=1, source_target_pairs={{0,1},{1,0},{2,3},{3,2},{4,5},{5,4},{6,7},{7,6},{8,9},{9,8},{10,11... | collective-permute-start | bytes 4718600 | tf_op jit(solution)/shard_map/ppermute | solution.py:929
  774.1 1.9 collective-permute-start.51
  (42 other events, 320.7 us)
Sparse Core Ops, SparseCore 0:
  10.2 115.7 all-gather.6
  127.5 79.9 all-gather.8
  218.7 47.2 all-gather.10
  451.1 44.5 reduce-scatter.3
  512.0 82.3 reduce-scatter.5
  626.2 121.1 reduce-scatter.7

commit v6 on v5

--- a/solution.py
+++ b/solution.py
@@ -740,17 +740,18 @@
             span = slice(head * size, (head + 1) * size)
             query = q_ref[:, span]
             d_head = d_mixed[:, span]
-            scores = dot(keys, query, 1, 1) * scale - lse_ref[head : head + 1, :]
-            probs = jnp.where(allowed, jnp.exp(scores), 0.0)
+            offset = lse_ref[head : head + 1, :] * math.log2(math.e)
+            scores = dot(keys, query, 1, 1) * (scale * math.log2(math.e)) - offset
+            probs = jnp.where(allowed, jnp.exp2(scores), 0.0)
             d_probs = dot(values, d_head, 1, 1)
             scaled = probs * d_probs
             row_dot = jnp.sum(scaled, axis=0, keepdims=True)
-            d_scores = (scale * (scaled - probs * row_dot)).astype(jnp.bfloat16)
+            d_scores = (scaled - probs * row_dot).astype(jnp.bfloat16)
             dv_total = dv_total + dot(probs.astype(jnp.bfloat16), d_head)
             dk_total = dk_total + dot(d_scores, query)
-            d_query = dot(keys_t, d_scores).T
+            d_query = (dot(keys_t, d_scores) * scale).T
             put(here, head * size, turn(d_query, cosine, -sine))
-        dk_ref[:seen] += dk_total
+        dk_ref[:seen] += dk_total * scale
         dv_ref[:seen] += dv_total
 
     for at in range(length // tile):

time: 798 us -> 798 us (level)
  no operation moved by 1% of the time
where the time goes in v6:
time: 798 us; the launch traced here: 788 us
  waiting for transfers between devices  334 us (42%)
  Pallas kernels  274 us (34%)
  starting transfers between devices  56.5 us (7%)
  local copies, waits for them, and re-layouts  41.5 us (5%)
  other arithmetic  37.6 us (5%)
  matrix products  28.5 us (4%)
  between operations  15 us (2%)
    ppermute x39, waiting for transfers between devices, flip(): lax.ppermute(rows, 'expert', [(d, d ^ mask) for d in range(self.count)])  277 us
    pallas_call x1, Pallas kernels, expert_rows(): pl.pallas_call(functools.partial(expert_kernel, len(pieces) // 2, len(c_p...  44.9 us
    ppermute x39, starting transfers between devices, flip(): lax.ppermute(rows, 'expert', [(d, d ^ mask) for d in range(self.count)])  38.6 us
    pallas_call x3, Pallas kernels, combine(): pl.pallas_call(functools.partial(combine_kernel, width, capacity), grid_s...  29.5 us
    pallas_call x4, Pallas kernels, pick_rows(): pl.pallas_call(functools.partial(pick_kernel, width, capacity, len(out_sh...  29.1 us
    dot_general x6, matrix products, contract_rows(): lax.dot_general(left, right, (((0,), (0,)), ((), ())), preferred_element_...  28.5 us
    reduce_scatter x3, waiting for transfers between devices, collect(): lax.psum_scatter(flat, 'expert', scatter_dimension=0, axis_index_groups=s...  27.8 us
    pallas_call x1, Pallas kernels, attend_back(): pl.pallas_call(functools.partial(attend_back_kernel, heads, scale, tile,...  26.6 us
  transfers between devices with their start and end apart: 58, of which 32 were waited for; matrix products, arithmetic and copies ran while one was open for 10% of the time, Pallas kernels for 25%

profile of v6, /device:TPU:9, one launch (start us, length us, event | category | flops | bytes accessed | tf_op | source)
XLA Modules:
  0.0 787.6 jit_solution(12432942629374677605)
XLA Ops:
  7.3 2.7 constant_dynamic-slice_fusion
  11.7 9.0 %shard_map.256 = (bf16[1024,1536]{1,0:T(8,128)(2,1)}, bf16[1024,768]{1,0:T(8,128)(2,1)}, bf16[1024,128]{1,0:T(8,128)(2,1)}, bf16[1024,128]{1,0:T(8,128)(2,1)}, f32[1024,1]{1,0:T(8,128)}) custom-call(bf16[1024,1536]{1,0:T(8,128)(2,1)} %x_ref.5, f32[1,1536]{1,0:T(1,128)} %broadcast_in_dim.70.gain_ref, bf16[1536,768]{1,0:T(8,128)(2,1)} %wq_ref.3, ...), custom_call_target="tpu_custom_call" | custom-call | flops 9000000 | bytes 1024 | tf_op jit(solution)/shard_map/pallas_call | solution.py:162
  20.7 24.1 %shard_map.257 = (bf16[1024,768]{1,0:T(8,128)(2,1)}, f32[6,1024]{1,0:T(8,128)}, bf16[1024,1536]{1,0:T(8,128)(2,1)}) custom-call(bf16[1024,768]{1,0:T(8,128)(2,1)} %get-tuple-element.89.q_ref, bf16[1024,128]{1,0:T(8,128)(2,1)} %get-tuple-element.90.k_ref, bf16[1024,128]{1,0:T(8,128)(2,1)} %get-tuple-element.91.v_ref, s32[1,1024]{1,0:T(1,128)} %segq_ref.3, ...), custom_call_target="tpu_custom_call" | custom-call | flops 20000000 | bytes 1024 | tf_op jit(solution)/shard_map/pallas_call | solution.py:207
  48.9 8.9 %shard_map.258 = s32[16,1024]{1,0:T(8,128)} custom-call(s32[16,1024]{1,0:T(8,128)} %compare_select_fusion.keys_ref), custom_call_target="tpu_custom_call" | custom-call | flops 9000000 | bytes 1024 | tf_op jit(solution)/shard_map/pallas_call | solution.py:118
  58.7 2.5 collective-permute-start.2
  62.8 2.3 collective-permute-done.2
  69.5 5.3 shard_map.259
  81.0 3.9 collective-permute-done.5
  86.1 2.5 pad_maximum_fusion.4.refs_1_.refs_6_
  90.3 10.0 %shard_map.260 = (f32[1024,1536]{1,0:T(8,128)}, bf16[1024,1536]{1,0:T(8,128)(2,1)}, f32[1024,1]{1,0:T(8,128)}, f32[1024,16]{1,0:T(8,128)}, bf16[1024,512]{1,0:T(8,128)(2,1)}, /*index=5*/bf16[1024,256]{1,0:T(8,128)(2,1)}) custom-call(s32[1]{0:T(128)} %bitcast.side_ref, bf16[1024,1536]{1,0:T(8,128)(2,1)} %x_ref.5, bf16[1024,1536]{1,0:T(8,128)(2,1)} %get-tuple-element.92.a_ref, ...), custom_call_target="tpu_custom_call" | custom-call | flops 9000000 | bytes 1024 | tf_op jit(solution)/shard_map/pallas_call | solution.py:276
  100.3 25.7 %all-gather.7.cloned.1.call-done = bf16[4096,768]{1,0:T(8,128)(2,1)} async-done(((bf16[1024,768]{1,0:T(8,128)(2,1)}), bf16[4096,768]{1,0:T(8,128)(2,1)}) %all-gather.7.cloned.1.call-update) | async-done | bytes 6291472 | tf_op jit(solution)/shard_map/all_gather | solution.py:896
  129.2 10.6 %shard_map.263 = (bf16[4,288,768]{2,1,0:T(8,128)(2,1)}, bf16[4,288,768]{2,1,0:T(8,128)(2,1)}, bf16[4,288,768]{2,1,0:T(8,128)(2,1)}, bf16[4,288,768]{2,1,0:T(8,128)(2,1)}) custom-call(s32[1]{0:T(128)} %bitcast.20.line_ref, s32[4,4,1,1024]{3,2,1,0:T(1,128)} %broadcast_in_dim.75.tab_ref.refs_0_, bf16[4,1024,768]{2,1,0:T(8,128)(2,1)} %bitcast.125, ...), custom_call_target="tpu_custom_call" | custom-call | flops 12000000 | bytes 1024 | tf_op jit(solution)/shard_map/pallas_call | solution.py:341
  142.4 37.2 %collective-permute-done.10.refs_2_.refs_1_ = bf16[4,288,768]{2,1,0:T(8,128)(2,1)S(1)} collective-permute-done((bf16[4,288,768]{2,1,0:T(8,128)(2,1)}, bf16[4,288,768]{2,1,0:T(8,128)(2,1)S(1)}, u32[]{:S(2)}, u32[]{:S(2)}) %collective-permute-start.10) | collective-permute-done | bytes 1769504 | tf_op jit(solution)/shard_map/ppermute | solution.py:893
  180.4 38.1 %collective-permute-done.12.refs_4_.refs_3_ = bf16[4,288,768]{2,1,0:T(8,128)(2,1)} collective-permute-done((bf16[4,288,768]{2,1,0:T(8,128)(2,1)}, bf16[4,288,768]{2,1,0:T(8,128)(2,1)}, u32[]{:S(2)}, u32[]{:S(2)}) %collective-permute-start.12) | collective-permute-done | bytes 1769504 | tf_op jit(solution)/shard_map/ppermute | solution.py:893
  218.6 7.9 %shard_map.262 = (bf16[4,288,512]{2,1,0:T(8,128)(2,1)}, bf16[4,288,512]{2,1,0:T(8,128)(2,1)}, bf16[4,288,512]{2,1,0:T(8,128)(2,1)}, bf16[4,288,512]{2,1,0:T(8,128)(2,1)}) custom-call(s32[1]{0:T(128)} %bitcast.20.line_ref, s32[4,4,1,1024]{3,2,1,0:T(1,128)} %broadcast_in_dim.75.tab_ref.refs_0_, bf16[4,1024,512]{2,1,0:T(8,128)(2,1)} %bitcast.129), custom_call_target="tpu_custom_call" | custom-call | flops 8000000 | bytes 1024 | tf_op jit(solution)/shard_map/pallas_call | solution.py:341
  229.2 22.5 %collective-permute-done.7.refs_0_.refs_1_ = bf16[4,288,512]{2,1,0:T(8,128)(2,1)S(1)} collective-permute-done((bf16[4,288,512]{2,1,0:T(8,128)(2,1)}, bf16[4,288,512]{2,1,0:T(8,128)(2,1)S(1)}, u32[]{:S(2)}, u32[]{:S(2)}) %collective-permute-start.7) | collective-permute-done | bytes 1179680 | tf_op jit(solution)/shard_map/ppermute | solution.py:893
  251.7 4.8 collective-permute-done.8.refs_1_.refs_2_
  256.5 20.5 %collective-permute-done.9.refs_2_.refs_3_ = bf16[4,288,512]{2,1,0:T(8,128)(2,1)} collective-permute-done((bf16[4,288,512]{2,1,0:T(8,128)(2,1)}, bf16[4,288,512]{2,1,0:T(8,128)(2,1)}, u32[]{:S(2)}, u32[]{:S(2)}) %collective-permute-start.9) | collective-permute-done | bytes 1179680 | tf_op jit(solution)/shard_map/ppermute | solution.py:893
  277.0 5.3 shard_map.265
  282.2 6.3 shard_map.266.refs_4_
  288.5 5.6 collective-permute-start.17
  294.1 5.0 shard_map.267.refs_0_
  299.6 2.3 collective-permute-start.15
  301.9 12.0 %collective-permute-done.13.refs_1_ = bf16[4,288,256]{2,1,0:T(8,128)(2,1)S(1)} collective-permute-done((bf16[4,288,256]{2,1,0:T(8,128)(2,1)}, bf16[4,288,256]{2,1,0:T(8,128)(2,1)S(1)}, u32[]{:S(2)}, u32[]{:S(2)}) %collective-permute-start.13) | collective-permute-done | bytes 589856 | tf_op jit(solution)/shard_map/ppermute | solution.py:893
  313.8 12.7 %collective-permute-done.15.refs_3_ = bf16[4,288,256]{2,1,0:T(8,128)(2,1)S(1)} collective-permute-done((bf16[4,288,256]{2,1,0:T(8,128)(2,1)S(1)}, bf16[4,288,256]{2,1,0:T(8,128)(2,1)S(1)}, u32[]{:S(2)}, u32[]{:S(2)}) %collective-permute-start.15) | collective-permute-done | bytes 589856 | tf_op jit(solution)/shard_map/ppermute | solution.py:893
  328.8 3.0 copy-done.1
  331.8 3.9 shard_map.268.refs_1_
  337.7 3.8 collective-permute-done.18.refs_3_
  342.9 44.9 %shard_map.269 = (bf16[4,4,288,768]{3,2,1,0:T(8,128)(2,1)}, bf16[4,4,288,384]{3,2,1,0:T(8,128)(2,1)}, f32[4,4,288,1]{3,2,1,0:T(8,128)}, bf16[4,4,288,256]{3,2,1,...) custom-call(s32[2]{0:T(128)} %pad_add_fusion.4.me_ref, ...), custom_call_target="tpu_custom_call" | custom-call | flops 40000000 | bytes 1024 | tf_op jit(solution)/shard_map/pallas_call | solution.py:505
  388.3 13.3 %shard_map.270 = (bf16[4,4,288,768]{3,2,1,0:T(8,128)(2,1)}, bf16[4,288,768]{2,1,0:T(8,128)(2,1)}, bf16[4,288,768]{2,1,0:T(8,128)(2,1)}, bf16[4,288,768]{2,1,0:T(8,128)(2,1)}, bf16[4,288,768]{2,1,0:T(8,128)(2,1)}) custom-call(s32[2]{0:T(128)} %pad_add_fusion.4.me_ref, bf16[4,4,288,384]{3,2,1,0:T(8,128)(2,1)} %get-tuple-element.113.act_ref.refs_0_, ...), custom_call_target="tpu_custom_call" | custom-call | flops 12000000 | bytes 1024 | tf_op jit(solution)/shard_map/pallas_call | solution.py:688
  403.4 4.6 shard_map.271
  412.7 10.5 %collective-permute-done.22.refs_5_.refs_1_ = bf16[4,288,256]{2,1,0:T(8,128)(2,1)S(1)} collective-permute-done((bf16[4,288,256]{2,1,0:T(8,128)(2,1)}, bf16[4,288,256]{2,1,0:T(8,128)(2,1)S(1)}, u32[]{:S(2)}, u32[]{:S(2)}) %collective-permute-start.22) | collective-permute-done | bytes 589856 | tf_op jit(solution)/shard_map/ppermute | solution.py:893
  424.3 12.3 %collective-permute-done.24.refs_7_.refs_3_ = bf16[4,288,256]{2,1,0:T(8,128)(2,1)S(1)} collective-permute-done((bf16[4,288,256]{2,1,0:T(8,128)(2,1)}, bf16[4,288,256]{2,1,0:T(8,128)(2,1)S(1)}, u32[]{:S(2)}, u32[]{:S(2)}) %collective-permute-start.24) | collective-permute-done | bytes 589856 | tf_op jit(solution)/shard_map/ppermute | solution.py:893
  437.4 6.3 shard_map.272
  443.8 7.2 shard_map.273
  453.7 23.3 %collective-permute-done.25.refs_1_ = bf16[4,288,512]{2,1,0:T(8,128)(2,1)} collective-permute-done((bf16[4,288,512]{2,1,0:T(8,128)(2,1)S(1)}, bf16[4,288,512]{2,1,0:T(8,128)(2,1)}, u32[]{:S(2)}, u32[]{:S(2)}) %collective-permute-start.25) | collective-permute-done | bytes 1179680 | tf_op jit(solution)/shard_map/ppermute | solution.py:893
  477.5 25.3 %collective-permute-done.27.refs_3_ = bf16[4,288,512]{2,1,0:T(8,128)(2,1)} collective-permute-done((bf16[4,288,512]{2,1,0:T(8,128)(2,1)S(1)}, bf16[4,288,512]{2,1,0:T(8,128)(2,1)}, u32[]{:S(2)}, u32[]{:S(2)}) %collective-permute-start.27) | collective-permute-done | bytes 1179680 | tf_op jit(solution)/shard_map/ppermute | solution.py:893
  502.8 9.1 %shard_map.274 = (bf16[4,1024,512]{2,1,0:T(8,128)(2,1)}, f32[1,8,128]{2,1,0:T(8,128)}) custom-call(s32[1]{0:T(128)} %bitcast.20.line_ref, s32[4,1024,4]{2,1,0:T(8,128)} %bitcast.122, bf16[4,288,512]{2,1,0:T(8,128)(2,1)} %get-tuple-element.132.refs_0_, bf16[4,288,512]{2,1,0:T(8,128)(2,1)} %collective-permute-done.25.refs_1_, ...), custom_call_target="tpu_custom_call" | custom-call | flops 8000000 | bytes 1024 | tf_op jit(solution)/shard_map/pallas_call | solution.py:383
  523.4 8.6 %shard_map.276 = (bf16[4,288,768]{2,1,0:T(8,128)(2,1)}, bf16[4,288,768]{2,1,0:T(8,128)(2,1)}, bf16[4,288,768]{2,1,0:T(8,128)(2,1)}, bf16[4,288,768]{2,1,0:T(8,128)(2,1)}) custom-call(bf16[4,288,768]{2,1,0:T(8,128)(2,1)} %get-tuple-element.114.refs_0_, bf16[4,288,768]{2,1,0:T(8,128)(2,1)} %get-tuple-element.115.refs_1_, ...), custom_call_target="tpu_custom_call" | custom-call | flops 7000000 | bytes 1024 | tf_op jit(solution)/shard_map/pallas_call | solution.py:560
  534.0 5.1 select_reduce_fusion
  539.1 4.6 collective-permute-start.36
  544.9 7.2 convolution_bitcast_fusion.2
  552.1 3.0 broadcast_select_fusion.3
  556.3 5.1 collective-permute-start.39
  566.4 5.2 convolution_bitcast_fusion.5
  571.7 6.2 convolution_bitcast_fusion.1
  577.8 5.0 convolution_bitcast_fusion
  584.9 9.5 %reduce-scatter.6.cloned.1.call-done.refs_1_ = bf16[1024,512]{1,0:T(8,128)(2,1)} async-done(((bf16[4096,512]{1,0:T(8,128)(2,1)}), bf16[1024,512]{1,0:T(8,128)(2,1)}) %reduce-scatter.6.cloned.1.call-update) | async-done | bytes 1048592 | tf_op jit(solution)/shard_map/reduce_scatter | solution.py:900
  602.0 10.6 %shard_map.281 = (f32[1024,1536]{1,0:T(8,128)}, bf16[1024,1536]{1,0:T(8,128)(2,1)}, bf16[1024,128]{1,0:T(8,128)(2,1)}, f32[1,1536]{1,0:T(1,128)}) custom-call(s32[1]{0:T(128)} %bitcast.side_ref, bf16[1024,256]{1,0:T(8,128)(2,1)} %reduce-scatter.4.cloned.1.call-done.refs_1_.refs_0_, bf16[1024,512]{1,0:T(8,128)(2,1)} %reduce-scatter.6.cloned.1.call-done.refs_1_, ...), custom_call_target="tpu_custom_call" | custom-call | flops 10000000 | bytes 1024 | tf_op jit(solution)/shard_map/pallas_call | solution.py:619
  612.7 13.3 %shard_map.282 = (bf16[4,1024,768]{2,1,0:T(8,128)(2,1)}, f32[1,8,128]{2,1,0:T(8,128)}) custom-call(s32[1]{0:T(128)} %bitcast.20.line_ref, s32[4,1024,4]{2,1,0:T(8,128)} %bitcast.123, bf16[4,288,768]{2,1,0:T(8,128)(2,1)} %get-tuple-element.140.refs_0_, bf16[4,288,768]{2,1,0:T(8,128)(2,1)} %collective-permute-done.31.refs_1_, ...), custom_call_target="tpu_custom_call" | custom-call | flops 12000000 | bytes 1024 | tf_op jit(solution)/shard_map/pallas_call | solution.py:383
  626.0 8.4 %shard_map.284 = (f32[4,96,896]{2,1,0:T(8,128)}, bf16[4,96,896]{2,1,0:T(8,128)(2,1)}, bf16[4,96,896]{2,1,0:T(8,128)(2,1)}, bf16[4,96,896]{2,1,0:T(8,128)(2,1)}) custom-call(s32[1]{0:T(128)} %bitcast.59.spot_ref, bf16[1024,1536]{1,0:T(8,128)(2,1)} %get-tuple-element.149.refs_4_.left_ref.db_ref, bf16[1024,768]{1,0:T(8,128)(2,1)} %get-tuple-element.153.right_ref, ...), custom_call_target="tpu_custom_call" | custom-call | flops 6000000 | bytes 1024 | tf_op jit(solution)/shard_map/pallas_call | solution.py:870
  637.1 26.6 %shard_map.285.d_ref.refs_0_ = bf16[1024,1024]{1,0:T(8,128)(2,1)} custom-call(bf16[1024,768]{1,0:T(8,128)(2,1)} %get-tuple-element.89.q_ref, bf16[1024,128]{1,0:T(8,128)(2,1)} %get-tuple-element.90.k_ref, bf16[1024,128]{1,0:T(8,128)(2,1)} %get-tuple-element.91.v_ref, s32[1,1024]{1,0:T(1,128)} %segq_ref.3, s32[1024,1]{1,0:T(8,128)} %copy.130.segk_ref, ...), custom_call_target="tpu_custom_call" | custom-call | flops 28000000 | bytes 1024 | tf_op jit(solution)/shard_map/pallas_call | solution.py:778
  663.6 3.2 collective-permute-done.42
  668.2 7.8 shard_map.286.refs_1_.a_ref
  677.7 7.5 shard_map.288
  689.5 9.6 %shard_map.289.refs_1_ = f32[1024,1536]{1,0:T(8,128)} custom-call(bf16[1024,1536]{1,0:T(8,128)(2,1)} %shard_map.286.refs_1_.a_ref, bf16[1024,1536]{1,0:T(8,128)(2,1)} %copy-done.15, bf16[1024,1536]{1,0:T(8,128)(2,1)} %x_ref.5, f32[1024,1]{1,0:T(8,128)} %get-tuple-element.161.inv_ref, f32[1024,1536]{1,0:T(8,128)} %get-tuple-element.162.dh_ref, ...), custom_call_target="tpu_custom_call" | custom-call | flops 8000000 | bytes 1024 | tf_op jit(solution)/shard_map/pallas_call | solution.py:653
  699.1 5.6 collective-permute-done.44
  705.2 17.2 %collective-permute-done.46 = bf16[4,96,1024]{2,1,0:T(8,128)(2,1)} collective-permute-done((bf16[4,96,1024]{2,1,0:T(8,128)(2,1)}, bf16[4,96,1024]{2,1,0:T(8,128)(2,1)}, u32[]{:S(2)}, u32[]{:S(2)}) %collective-permute-start.46) | collective-permute-done | bytes 786464 | tf_op jit(solution)/shard_map/ppermute | solution.py:893
  722.4 2.6 convert_add_fusion.refs_1_
  726.6 2.2 collective-permute-start.49
  728.8 18.4 %reduce-scatter.8.cloned.1.call-done.refs_0_ = bf16[1024,768]{1,0:T(8,128)(2,1)} async-done(((bf16[4096,768]{1,0:T(8,128)(2,1)}), bf16[1024,768]{1,0:T(8,128)(2,1)}) %reduce-scatter.8.cloned.1.call-update) | async-done | bytes 1572880 | tf_op jit(solution)/shard_map/reduce_scatter | solution.py:900
  747.1 4.1 add_convert_fusion
  753.9 14.6 %collective-permute-done.50 = bf16[96,1920]{1,0:T(8,128)(2,1)} collective-permute-done((bf16[96,1920]{1,0:T(8,128)(2,1)S(1)}, bf16[96,1920]{1,0:T(8,128)(2,1)}, u32[]{:S(2)}, u32[]{:S(2)}) %collective-permute-start.50) | collective-permute-done | bytes 368672 | tf_op jit(solution)/shard_map/ppermute | solution.py:893
  776.5 2.1 broadcast_select_fusion.1
  (260 shorter events, 104.8 us)
Async XLA Ops:
  7.2 118.8 %all-gather.7.cloned.1.call-start = ((), (), s32[]{:S(2)}) async-start(), calls=%async_computation.6 | async-start | bytes 7864320 | tf_op jit(solution)/shard_map/all_gather | solution.py:896
  9.9 208.6 %all-gather.9.cloned.1.call-start = ((), (), s32[]{:S(2)}) async-start(), calls=%async_computation.7 | async-start | bytes 5242880 | tf_op jit(solution)/shard_map/all_gather | solution.py:896
  20.7 27.5 %copy-start.38 = (s32[1024,4]{0,1:T(4,128)S(1)}, s32[1024,4]{0,1:T(4,128)}, u32[]{:S(2)}) copy-start(s32[1024,4]{0,1:T(4,128)} %param.29) | copy-start | bytes 49156
  44.8 43.8 %collective-permute-start = (bf16[1024,1536]{1,0:T(8,128)(2,1)}, bf16[1024,1536]{1,0:T(8,128)(2,1)S(1)}, u32[]{:S(2)}, u32[]{:S(2)}) collective-permute-start(bf16[1024,1536]{1,0:T(8,128)(2,1)} %get-tuple-element.92.a_ref), channel_id=1, source_target_pairs={{0,1},{1,0},{2,3},{3,2},{4,5},{5,4},{6,7},{7,6},{8,9},{9,8},{10,11... | collective-permute-start | bytes 9437192 | tf_op jit(solution)/shard_map/ppermute | solution.py:930
  48.2 30.4 %copy-start.39 = (bf16[1536,16]{0,1:T(8,128)(2,1)S(1)}, bf16[1536,16]{0,1:T(8,128)(2,1)}, u32[]{:S(2)}) copy-start(bf16[1536,16]{0,1:T(8,128)(2,1)} %param.25) | copy-start | bytes 147460
  48.9 30.6 %copy-start.43 = (f32[1536]{0:T(1024)S(1)}, f32[1536]{0:T(1024)}, u32[]{:S(2)}) copy-start(f32[1536]{0:T(1024)} %param.20) | copy-start | bytes 18436
  58.6 4.1 collective-permute-start.1
  58.7 6.3 collective-permute-start.2
  61.2 4.8 collective-permute-start.3
  74.8 6.2 collective-permute-start.4
  76.1 8.9 %collective-permute-start.5 = (bf16[4,288,4]{2,1,0:T(8,128)(2,1)}, bf16[4,288,4]{2,1,0:T(8,128)(2,1)}, u32[]{:S(2)}, u32[]{:S(2)}) collective-permute-start(bf16[4,288,4]{2,1,0:T(8,128)(2,1)} %get-tuple-element.95), channel_id=1, source_target_pairs={{0,4},{2,6},{4,0},{6,2},{8,12},{10,14},{12,8},{14,10},{16,20},{18,... | collective-permute-start | bytes 27656 | tf_op jit(solution)/shard_map/ppermute | solution.py:893
  77.3 8.8 %collective-permute-start.6 = (bf16[4,288,4]{2,1,0:T(8,128)(2,1)}, bf16[4,288,4]{2,1,0:T(8,128)(2,1)}, u32[]{:S(2)}, u32[]{:S(2)}) collective-permute-start(bf16[4,288,4]{2,1,0:T(8,128)(2,1)} %get-tuple-element.96), channel_id=1, source_target_pairs={{0,6},{2,4},{4,2},{6,0},{8,14},{10,12},{12,10},{14,8},{16,22},{18,... | collective-permute-start | bytes 27656 | tf_op jit(solution)/shard_map/ppermute | solution.py:893
  126.0 151.0 %all-gather.11.cloned.1.call-start = ((), (), s32[]{:S(2)}) async-start(), calls=%async_computation.8 | async-start | bytes 2621440 | tf_op jit(solution)/shard_map/all_gather | solution.py:896
  139.8 39.9 %collective-permute-start.10 = (bf16[4,288,768]{2,1,0:T(8,128)(2,1)}, bf16[4,288,768]{2,1,0:T(8,128)(2,1)S(1)}, u32[]{:S(2)}, u32[]{:S(2)}) collective-permute-start(bf16[4,288,768]{2,1,0:T(8,128)(2,1)} %get-tuple-element.105), channel_id=1, source_target_pairs={{0,2},{2,0},{4,6},{6,4},{8,10},{10,8},{12,14},{14,12},{16,18},{18,... | collective-permute-start | bytes 5308424 | tf_op jit(solution)/shard_map/ppermute | solution.py:893
  141.0 39.4 %collective-permute-start.11 = (bf16[4,288,768]{2,1,0:T(8,128)(2,1)}, bf16[4,288,768]{2,1,0:T(8,128)(2,1)S(1)}, u32[]{:S(2)}, u32[]{:S(2)}) collective-permute-start(bf16[4,288,768]{2,1,0:T(8,128)(2,1)} %get-tuple-element.106), channel_id=1, source_target_pairs={{0,4},{2,6},{4,0},{6,2},{8,12},{10,14},{12,8},{14,10},{16,20},{18,... | collective-permute-start | bytes 5308424 | tf_op jit(solution)/shard_map/ppermute | solution.py:893
  142.2 76.3 %collective-permute-start.12 = (bf16[4,288,768]{2,1,0:T(8,128)(2,1)}, bf16[4,288,768]{2,1,0:T(8,128)(2,1)}, u32[]{:S(2)}, u32[]{:S(2)}) collective-permute-start(bf16[4,288,768]{2,1,0:T(8,128)(2,1)} %get-tuple-element.107), channel_id=1, source_target_pairs={{0,6},{2,4},{4,2},{6,0},{8,14},{10,12},{12,10},{14,8},{16,22},{18,... | collective-permute-start | bytes 5308424 | tf_op jit(solution)/shard_map/ppermute | solution.py:893
  179.6 38.9 %copy-start.11 = (bf16[4,288,768]{2,1,0:T(8,128)(2,1)}, bf16[4,288,768]{2,1,0:T(8,128)(2,1)S(1)}, u32[]{:S(2)}) copy-start(bf16[4,288,768]{2,1,0:T(8,128)(2,1)S(1)} %collective-permute-done.10.refs_2_.refs_1_) | copy-start | bytes 5308420
  180.4 38.1 %copy-start.12 = (bf16[4,288,768]{2,1,0:T(8,128)(2,1)}, bf16[4,288,768]{2,1,0:T(8,128)(2,1)S(1)}, u32[]{:S(2)}) copy-start(bf16[4,288,768]{2,1,0:T(8,128)(2,1)S(1)} %collective-permute-done.11.refs_3_.refs_2_) | copy-start | bytes 5308420
  218.5 293.3 %reduce-scatter.4.cloned.1.call-start = ((), (), s32[]{:S(2)}) async-start(), calls=%async_computation.3 | async-start | bytes 2621440 | tf_op jit(solution)/shard_map/reduce_scatter | solution.py:900
  226.5 25.2 %collective-permute-start.7 = (bf16[4,288,512]{2,1,0:T(8,128)(2,1)}, bf16[4,288,512]{2,1,0:T(8,128)(2,1)S(1)}, u32[]{:S(2)}, u32[]{:S(2)}) collective-permute-start(bf16[4,288,512]{2,1,0:T(8,128)(2,1)} %get-tuple-element.100), channel_id=1, source_target_pairs={{0,2},{2,0},{4,6},{6,4},{8,10},{10,8},{12,14},{14,12},{16,18},{18,... | collective-permute-start | bytes 3538952 | tf_op jit(solution)/shard_map/ppermute | solution.py:893
  227.7 28.8 %collective-permute-start.8 = (bf16[4,288,512]{2,1,0:T(8,128)(2,1)}, bf16[4,288,512]{2,1,0:T(8,128)(2,1)S(1)}, u32[]{:S(2)}, u32[]{:S(2)}) collective-permute-start(bf16[4,288,512]{2,1,0:T(8,128)(2,1)} %get-tuple-element.101), channel_id=1, source_target_pairs={{0,4},{2,6},{4,0},{6,2},{8,12},{10,14},{12,8},{14,10},{16,20},{18,... | collective-permute-start | bytes 3538952 | tf_op jit(solution)/shard_map/ppermute | solution.py:893
  228.0 49.0 %collective-permute-start.9 = (bf16[4,288,512]{2,1,0:T(8,128)(2,1)}, bf16[4,288,512]{2,1,0:T(8,128)(2,1)}, u32[]{:S(2)}, u32[]{:S(2)}) collective-permute-start(bf16[4,288,512]{2,1,0:T(8,128)(2,1)} %get-tuple-element.102), channel_id=1, source_target_pairs={{0,6},{2,4},{4,2},{6,0},{8,14},{10,12},{12,10},{14,8},{16,22},{18,... | collective-permute-start | bytes 3538952 | tf_op jit(solution)/shard_map/ppermute | solution.py:893
  288.5 38.0 %collective-permute-start.17 = (bf16[4,4,288,768]{3,2,1,0:T(8,128)(2,1)}, bf16[4,4,288,768]{3,2,1,0:T(8,128)(2,1)S(1)}, u32[]{:S(2)}, u32[]{:S(2)}) collective-permute-start(bf16[4,4,288,768]{3,2,1,0:T(8,128)(2,1)} %shard_map.266.refs_4_), channel_id=1, source_target_pairs={{0,1},{1,0},{2,3},{3,2},{4,5},{5,4},{6,7},{7,6},{8,9},{9,8},{10,11... | collective-permute-start | bytes 21233672 | tf_op jit(solution)/shard_map/ppermute | solution.py:930
  299.2 27.3 %collective-permute-start.16 = (bf16[4,4,288,512]{3,2,1,0:T(8,128)(2,1)}, bf16[4,4,288,512]{3,2,1,0:T(8,128)(2,1)S(1)}, u32[]{:S(2)}, u32[]{:S(2)}) collective-permute-start(bf16[4,4,288,512]{3,2,1,0:T(8,128)(2,1)} %shard_map.267.refs_0_), channel_id=1, source_target_pairs={{0,1},{1,0},{2,3},{3,2},{4,5},{5,4},{6,7},{7,6},{8,9},{9,8},{10,11... | collective-permute-start | bytes 14155784 | tf_op jit(solution)/shard_map/ppermute | solution.py:930
  299.2 14.6 %collective-permute-start.13 = (bf16[4,288,256]{2,1,0:T(8,128)(2,1)}, bf16[4,288,256]{2,1,0:T(8,128)(2,1)S(1)}, u32[]{:S(2)}, u32[]{:S(2)}) collective-permute-start(bf16[4,288,256]{2,1,0:T(8,128)(2,1)} %get-tuple-element.109.refs_4_), channel_id=1, source_target_pairs={{0,2},{2,0},{4,6},{6,4},{8,10},{10,8},{12,14},{14,12},{16,18},{18,... | collective-permute-start | bytes 1769480 | tf_op jit(solution)/shard_map/ppermute | solution.py:893
  299.5 14.3 %collective-permute-start.14 = (bf16[4,288,256]{2,1,0:T(8,128)(2,1)S(1)}, bf16[4,288,256]{2,1,0:T(8,128)(2,1)S(1)}, u32[]{:S(2)}, u32[]{:S(2)}) collective-permute-start(bf16[4,288,256]{2,1,0:T(8,128)(2,1)S(1)} %copy-done.30), channel_id=1, source_target_pairs={{0,4},{2,6},{4,0},{6,2},{8,12},{10,14},{12,8},{14,10},{16,20},{18,... | collective-permute-start | bytes 1769480 | tf_op jit(solution)/shard_map/ppermute | solution.py:893
  299.6 26.9 %collective-permute-start.15 = (bf16[4,288,256]{2,1,0:T(8,128)(2,1)S(1)}, bf16[4,288,256]{2,1,0:T(8,128)(2,1)S(1)}, u32[]{:S(2)}, u32[]{:S(2)}) collective-permute-start(bf16[4,288,256]{2,1,0:T(8,128)(2,1)S(1)} %copy-done.29), channel_id=1, source_target_pairs={{0,6},{2,4},{4,2},{6,0},{8,14},{10,12},{12,10},{14,8},{16,22},{18,... | collective-permute-start | bytes 1769480 | tf_op jit(solution)/shard_map/ppermute | solution.py:893
  335.7 5.8 collective-permute-start.18
  387.8 48.8 %collective-permute-start.20 = (bf16[4,4,288,512]{3,2,1,0:T(8,128)(2,1)}, bf16[4,4,288,512]{3,2,1,0:T(8,128)(2,1)}, u32[]{:S(2)}, u32[]{:S(2)}) collective-permute-start(bf16[4,4,288,512]{3,2,1,0:T(8,128)(2,1)} %get-tuple-element.123), channel_id=1, source_target_pairs={{0,1},{1,0},{2,3},{3,2},{4,5},{5,4},{6,7},{7,6},{8,9},{9,8},{10,11... | collective-permute-start | bytes 14155784 | tf_op jit(solution)/shard_map/ppermute | solution.py:930
  388.2 13.8 %collective-permute-start.21 = (bf16[4,4,288,256]{3,2,1,0:T(8,128)(2,1)}, bf16[4,4,288,256]{3,2,1,0:T(8,128)(2,1)S(1)}, u32[]{:S(2)}, u32[]{:S(2)}) collective-permute-start(bf16[4,4,288,256]{3,2,1,0:T(8,128)(2,1)} %get-tuple-element.128), channel_id=1, source_target_pairs={{0,1},{1,0},{2,3},{3,2},{4,5},{5,4},{6,7},{7,6},{8,9},{9,8},{10,11... | collective-permute-start | bytes 7077896 | tf_op jit(solution)/shard_map/ppermute | solution.py:930
  401.6 121.8 %collective-permute-start.19 = (bf16[4,4,288,768]{3,2,1,0:T(8,128)(2,1)}, bf16[4,4,288,768]{3,2,1,0:T(8,128)(2,1)}, u32[]{:S(2)}, u32[]{:S(2)}) collective-permute-start(bf16[4,4,288,768]{3,2,1,0:T(8,128)(2,1)} %get-tuple-element.118.refs_8_.refs_1_), channel_id=1, source_target_pairs={{0,1},{1,0},{2,3},{3,2},{4,5},{5,4},{6,7},{7,6},{8,9},{9,8},{10,11... | collective-permute-start | bytes 21233672 | tf_op jit(solution)/shard_map/ppermute | solution.py:930
  408.0 15.1 %collective-permute-start.22 = (bf16[4,288,256]{2,1,0:T(8,128)(2,1)}, bf16[4,288,256]{2,1,0:T(8,128)(2,1)S(1)}, u32[]{:S(2)}, u32[]{:S(2)}) collective-permute-start(bf16[4,288,256]{2,1,0:T(8,128)(2,1)} %get-tuple-element.129), channel_id=1, source_target_pairs={{0,2},{2,0},{4,6},{6,4},{8,10},{10,8},{12,14},{14,12},{16,18},{18,... | collective-permute-start | bytes 1769480 | tf_op jit(solution)/shard_map/ppermute | solution.py:893
  409.3 15.0 %collective-permute-start.23 = (bf16[4,288,256]{2,1,0:T(8,128)(2,1)}, bf16[4,288,256]{2,1,0:T(8,128)(2,1)S(1)}, u32[]{:S(2)}, u32[]{:S(2)}) collective-permute-start(bf16[4,288,256]{2,1,0:T(8,128)(2,1)} %get-tuple-element.130), channel_id=1, source_target_pairs={{0,4},{2,6},{4,0},{6,2},{8,12},{10,14},{12,8},{14,10},{16,20},{18,... | collective-permute-start | bytes 1769480 | tf_op jit(solution)/shard_map/ppermute | solution.py:893
  409.5 27.1 %collective-permute-start.24 = (bf16[4,288,256]{2,1,0:T(8,128)(2,1)}, bf16[4,288,256]{2,1,0:T(8,128)(2,1)S(1)}, u32[]{:S(2)}, u32[]{:S(2)}) collective-permute-start(bf16[4,288,256]{2,1,0:T(8,128)(2,1)} %get-tuple-element.131), channel_id=1, source_target_pairs={{0,6},{2,4},{4,2},{6,0},{8,14},{10,12},{12,10},{14,8},{16,22},{18,... | collective-permute-start | bytes 1769480 | tf_op jit(solution)/shard_map/ppermute | solution.py:893
  451.0 143.4 %reduce-scatter.6.cloned.1.call-start = ((), (), s32[]{:S(2)}) async-start(), calls=%async_computation.4 | async-start | bytes 5242880 | tf_op jit(solution)/shard_map/reduce_scatter | solution.py:900
  451.0 26.1 %collective-permute-start.25 = (bf16[4,288,512]{2,1,0:T(8,128)(2,1)S(1)}, bf16[4,288,512]{2,1,0:T(8,128)(2,1)}, u32[]{:S(2)}, u32[]{:S(2)}) collective-permute-start(bf16[4,288,512]{2,1,0:T(8,128)(2,1)S(1)} %copy-done.27), channel_id=1, source_target_pairs={{0,2},{2,0},{4,6},{6,4},{8,10},{10,8},{12,14},{14,12},{16,18},{18,... | collective-permute-start | bytes 3538952 | tf_op jit(solution)/shard_map/ppermute | solution.py:893
  451.5 26.0 %collective-permute-start.26 = (bf16[4,288,512]{2,1,0:T(8,128)(2,1)S(1)}, bf16[4,288,512]{2,1,0:T(8,128)(2,1)}, u32[]{:S(2)}, u32[]{:S(2)}) collective-permute-start(bf16[4,288,512]{2,1,0:T(8,128)(2,1)S(1)} %copy-done.26), channel_id=1, source_target_pairs={{0,4},{2,6},{4,0},{6,2},{8,12},{10,14},{12,8},{14,10},{16,20},{18,... | collective-permute-start | bytes 3538952 | tf_op jit(solution)/shard_map/ppermute | solution.py:893
  452.7 50.0 %collective-permute-start.27 = (bf16[4,288,512]{2,1,0:T(8,128)(2,1)S(1)}, bf16[4,288,512]{2,1,0:T(8,128)(2,1)}, u32[]{:S(2)}, u32[]{:S(2)}) collective-permute-start(bf16[4,288,512]{2,1,0:T(8,128)(2,1)S(1)} %copy-done.25), channel_id=1, source_target_pairs={{0,6},{2,4},{4,2},{6,0},{8,14},{10,12},{12,10},{14,8},{16,22},{18,... | collective-permute-start | bytes 3538952 | tf_op jit(solution)/shard_map/ppermute | solution.py:893
  511.9 235.2 %reduce-scatter.8.cloned.1.call-start = ((), (), s32[]{:S(2)}) async-start(), calls=%async_computation.5 | async-start | bytes 7864320 | tf_op jit(solution)/shard_map/reduce_scatter | solution.py:900
  516.1 4.8 collective-permute-start.28
  519.1 2.8 collective-permute-start.29
  519.4 3.4 collective-permute-start.30
  532.1 80.6 %collective-permute-start.31 = (bf16[4,288,768]{2,1,0:T(8,128)(2,1)}, bf16[4,288,768]{2,1,0:T(8,128)(2,1)}, u32[]{:S(2)}, u32[]{:S(2)}) collective-permute-start(bf16[4,288,768]{2,1,0:T(8,128)(2,1)} %get-tuple-element.141.refs_1_), channel_id=1, source_target_pairs={{0,2},{2,0},{4,6},{6,4},{8,10},{10,8},{12,14},{14,12},{16,18},{18,... | collective-permute-start | bytes 5308424 | tf_op jit(solution)/shard_map/ppermute | solution.py:893
  533.0 79.7 %collective-permute-start.32 = (bf16[4,288,768]{2,1,0:T(8,128)(2,1)}, bf16[4,288,768]{2,1,0:T(8,128)(2,1)}, u32[]{:S(2)}, u32[]{:S(2)}) collective-permute-start(bf16[4,288,768]{2,1,0:T(8,128)(2,1)} %get-tuple-element.142.refs_2_), channel_id=1, source_target_pairs={{0,4},{2,6},{4,0},{6,2},{8,12},{10,14},{12,8},{14,10},{16,20},{18,... | collective-permute-start | bytes 5308424 | tf_op jit(solution)/shard_map/ppermute | solution.py:893
  539.1 16.0 %collective-permute-start.36 = (f32[4,1024]{1,0:T(4,128)S(1)}, f32[4,1024]{1,0:T(4,128)S(1)}, u32[]{:S(2)}, u32[]{:S(2)}) collective-permute-start(f32[4,1024]{1,0:T(4,128)S(1)} %get-tuple-element.255), channel_id=1, source_target_pairs={{0,8},{2,10},{4,12},{6,14},{8,0},{10,2},{12,4},{14,6},{16,24},{18,... | collective-permute-start | bytes 49160 | tf_op jit(solution)/shard_map/ppermute | solution.py:893
  543.7 12.6 %collective-permute-start.37 = (f32[4,1024]{1,0:T(4,128)S(1)}, f32[4,1024]{1,0:T(4,128)S(1)}, u32[]{:S(2)}, u32[]{:S(2)}) collective-permute-start(f32[4,1024]{1,0:T(4,128)S(1)} %get-tuple-element.254), channel_id=1, source_target_pairs={{0,16},{2,18},{4,20},{6,22},{8,24},{10,26},{12,28},{14,30},{16,0},... | collective-permute-start | bytes 49160 | tf_op jit(solution)/shard_map/ppermute | solution.py:893
  543.7 12.6 %collective-permute-start.38 = (f32[4,1024]{1,0:T(4,128)S(1)}, f32[4,1024]{1,0:T(4,128)S(1)}, u32[]{:S(2)}, u32[]{:S(2)}) collective-permute-start(f32[4,1024]{1,0:T(4,128)S(1)} %get-tuple-element.253), channel_id=1, source_target_pairs={{0,24},{2,26},{4,28},{6,30},{8,16},{10,18},{12,20},{14,22},{16,8},... | collective-permute-start | bytes 49160 | tf_op jit(solution)/shard_map/ppermute | solution.py:893
  555.1 57.6 %collective-permute-start.33 = (bf16[4,288,768]{2,1,0:T(8,128)(2,1)}, bf16[4,288,768]{2,1,0:T(8,128)(2,1)}, u32[]{:S(2)}, u32[]{:S(2)}) collective-permute-start(bf16[4,288,768]{2,1,0:T(8,128)(2,1)} %get-tuple-element.143.refs_3_), channel_id=1, source_target_pairs={{0,6},{2,4},{4,2},{6,0},{8,14},{10,12},{12,10},{14,8},{16,22},{18,... | collective-permute-start | bytes 5308424 | tf_op jit(solution)/shard_map/ppermute | solution.py:893
  556.3 6.8 collective-permute-start.39
  594.4 6.5 collective-permute-start.35
  597.8 3.1 collective-permute-start.34
  634.4 29.2 %collective-permute-start.40 = (bf16[4,96,896]{2,1,0:T(8,128)(2,1)}, bf16[4,96,896]{2,1,0:T(8,128)(2,1)S(1)}, u32[]{:S(2)}, u32[]{:S(2)}) collective-permute-start(bf16[4,96,896]{2,1,0:T(8,128)(2,1)} %get-tuple-element.156.refs_0_), channel_id=1, source_target_pairs={{0,2},{2,0},{4,6},{6,4},{8,10},{10,8},{12,14},{14,12},{16,18},{18,... | collective-permute-start | bytes 2064392 | tf_op jit(solution)/shard_map/ppermute | solution.py:893
  635.6 28.0 %collective-permute-start.41 = (bf16[4,96,896]{2,1,0:T(8,128)(2,1)}, bf16[4,96,896]{2,1,0:T(8,128)(2,1)S(1)}, u32[]{:S(2)}, u32[]{:S(2)}) collective-permute-start(bf16[4,96,896]{2,1,0:T(8,128)(2,1)} %get-tuple-element.157.refs_1_), channel_id=1, source_target_pairs={{0,4},{2,6},{4,0},{6,2},{8,12},{10,14},{12,8},{14,10},{16,20},{18,... | collective-permute-start | bytes 2064392 | tf_op jit(solution)/shard_map/ppermute | solution.py:893
  636.8 30.0 %collective-permute-start.42 = (bf16[4,96,896]{2,1,0:T(8,128)(2,1)}, bf16[4,96,896]{2,1,0:T(8,128)(2,1)S(1)}, u32[]{:S(2)}, u32[]{:S(2)}) collective-permute-start(bf16[4,96,896]{2,1,0:T(8,128)(2,1)} %get-tuple-element.158.refs_2_), channel_id=1, source_target_pairs={{0,6},{2,4},{4,2},{6,0},{8,14},{10,12},{12,10},{14,8},{16,22},{18,... | collective-permute-start | bytes 2064392 | tf_op jit(solution)/shard_map/ppermute | solution.py:893
  637.1 29.7 %copy-start.22 = (f32[4,96,896]{2,1,0:T(8,128)S(1)}, f32[4,96,896]{2,1,0:T(8,128)}, u32[]{:S(2)}) copy-start(f32[4,96,896]{2,1,0:T(8,128)} %get-tuple-element.159) | copy-start | bytes 4128772
  676.0 11.8 %collective-permute-start.43 = (bf16[1024,1536]{1,0:T(8,128)(2,1)}, bf16[1024,1536]{1,0:T(8,128)(2,1)S(1)}, u32[]{:S(2)}, u32[]{:S(2)}) collective-permute-start(bf16[1024,1536]{1,0:T(8,128)(2,1)} %shard_map.286.refs_1_.a_ref), channel_id=1, source_target_pairs={{0,1},{1,0},{2,3},{3,2},{4,5},{5,4},{6,7},{7,6},{8,9},{9,8},{10,11... | collective-permute-start | bytes 9437192 | tf_op jit(solution)/shard_map/ppermute | solution.py:930
  685.2 19.5 %collective-permute-start.44 = (bf16[4,96,1024]{2,1,0:T(8,128)(2,1)}, bf16[4,96,1024]{2,1,0:T(8,128)(2,1)}, u32[]{:S(2)}, u32[]{:S(2)}) collective-permute-start(bf16[4,96,1024]{2,1,0:T(8,128)(2,1)} %get-tuple-element.163), channel_id=1, source_target_pairs={{0,2},{2,0},{4,6},{6,4},{8,10},{10,8},{12,14},{14,12},{16,18},{18,... | collective-permute-start | bytes 2359304 | tf_op jit(solution)/shard_map/ppermute | solution.py:893
  686.1 19.1 %collective-permute-start.45 = (bf16[4,96,1024]{2,1,0:T(8,128)(2,1)}, bf16[4,96,1024]{2,1,0:T(8,128)(2,1)}, u32[]{:S(2)}, u32[]{:S(2)}) collective-permute-start(bf16[4,96,1024]{2,1,0:T(8,128)(2,1)} %get-tuple-element.164), channel_id=1, source_target_pairs={{0,4},{2,6},{4,0},{6,2},{8,12},{10,14},{12,8},{14,10},{16,20},{18,... | collective-permute-start | bytes 2359304 | tf_op jit(solution)/shard_map/ppermute | solution.py:893
  686.7 35.7 %collective-permute-start.46 = (bf16[4,96,1024]{2,1,0:T(8,128)(2,1)}, bf16[4,96,1024]{2,1,0:T(8,128)(2,1)}, u32[]{:S(2)}, u32[]{:S(2)}) collective-permute-start(bf16[4,96,1024]{2,1,0:T(8,128)(2,1)} %get-tuple-element.165), channel_id=1, source_target_pairs={{0,6},{2,4},{4,2},{6,0},{8,14},{10,12},{12,10},{14,8},{16,22},{18,... | collective-permute-start | bytes 2359304 | tf_op jit(solution)/shard_map/ppermute | solution.py:893
  726.1 26.1 %collective-permute-start.48 = (bf16[96,1920]{1,0:T(8,128)(2,1)}, bf16[96,1920]{1,0:T(8,128)(2,1)}, u32[]{:S(2)}, u32[]{:S(2)}) collective-permute-start(bf16[96,1920]{1,0:T(8,128)(2,1)} %get-tuple-element.236), channel_id=1, source_target_pairs={{0,8},{2,10},{4,12},{6,14},{8,0},{10,2},{12,4},{14,6},{16,24},{18,... | collective-permute-start | bytes 1105928 | tf_op jit(solution)/shard_map/ppermute | solution.py:893
  726.6 27.4 %collective-permute-start.49 = (bf16[96,1920]{1,0:T(8,128)(2,1)}, bf16[96,1920]{1,0:T(8,128)(2,1)}, u32[]{:S(2)}, u32[]{:S(2)}) collective-permute-start(bf16[96,1920]{1,0:T(8,128)(2,1)} %get-tuple-element.237), channel_id=1, source_target_pairs={{0,16},{2,18},{4,20},{6,22},{8,24},{10,26},{12,28},{14,30},{16,0},... | collective-permute-start | bytes 1105928 | tf_op jit(solution)/shard_map/ppermute | solution.py:893
  728.7 39.9 %collective-permute-start.50 = (bf16[96,1920]{1,0:T(8,128)(2,1)S(1)}, bf16[96,1920]{1,0:T(8,128)(2,1)}, u32[]{:S(2)}, u32[]{:S(2)}) collective-permute-start(bf16[96,1920]{1,0:T(8,128)(2,1)S(1)} %get-tuple-element.238), channel_id=1, source_target_pairs={{0,24},{2,26},{4,28},{6,30},{8,16},{10,18},{12,20},{14,22},{16,8},... | collective-permute-start | bytes 1105928 | tf_op jit(solution)/shard_map/ppermute | solution.py:893
  751.2 25.3 %collective-permute-start.47 = (bf16[1024,768]{1,0:T(8,128)(2,1)}, bf16[1024,768]{1,0:T(8,128)(2,1)}, u32[]{:S(2)}, u32[]{:S(2)}) collective-permute-start(bf16[1024,768]{1,0:T(8,128)(2,1)} %add_convert_fusion), channel_id=1, source_target_pairs={{0,1},{1,0},{2,3},{3,2},{4,5},{5,4},{6,7},{7,6},{8,9},{9,8},{10,11... | collective-permute-start | bytes 4718600 | tf_op jit(solution)/shard_map/ppermute | solution.py:930
  774.1 1.9 collective-permute-start.51
  (42 other events, 320.7 us)
Sparse Core Ops, SparseCore 0:
  10.2 115.7 all-gather.6
  127.5 79.9 all-gather.8
  218.7 47.2 all-gather.10
  451.1 44.5 reduce-scatter.3
  512.0 82.3 reduce-scatter.5
  626.2 120.9 reduce-scatter.7
